TPU v7x, 128 devices: a whole 4x4x4 slice. The times are simulated.
128 devices in a mesh: seq: 16 (over x, y_hi, core), grp: 8 (over y_lo, z).
Axes of the slice: x: 4, y: 4 (y_hi: 2, y_lo: 2; y = y_hi * 2 + y_lo), z: 4, core: 2. Of those that a mesh axis runs over, the one named last changes fastest.
Arguments:
- inputs: bfloat16 [32768, 1024], P('seq'), may hold values from -13 to 13
- latents: bfloat16 [8192, 1024], P('seq'), may hold values from -27 to 27
- w_query: bfloat16 [1024, 1024], P(None, 'grp')
- w_key: bfloat16 [1024, 1024], P(None, 'grp')
- w_value: bfloat16 [1024, 1024], P(None, 'grp'), may hold values from -0.1875 to 0.1875
- w_out: bfloat16 [1024, 1024], P('grp'), may hold values from -6 to 6
- positions: int32 [8192], replicated, may hold values from 8192 to 32767, as said below
- block_mask: int32 [64, 256], replicated, may hold values 0 or 1
Outputs:
- latent_update: bfloat16 [8192, 1024], P(('seq', 'grp'))
Inputs may be any that keep to these rules, and one draw needn't show every extreme that they name: `positions`: each latent's position in the input sequence.
All inputs are finite; a program needn't handle non-finite values.
Results may differ from a plain program's by a relative error of at most 0.035.
Values may be sent and summed in bfloat16 or wider, within the bound.
No kernel may reach another device: no remote copies, remote signals or barrier semaphores. Data moves between devices by JAX's collectives and lax.ppermute only.
A program may use at most 128 MiB of HBM per device.

v0:
```python
import jax
import jax.numpy as jnp
from jax import lax
from jax.sharding import PartitionSpec as P

HS = 64
BLOCK = 128


masked_score = -1e30


def from_behind(block, axis, distance):
    devices = range(lax.axis_size(axis))
    route = [((i - distance) % len(devices), i) for i in devices]
    return lax.ppermute(block, axis, route)


def allowed_pairs(row_spots, mask_rows, key_first, key_total):
    key_index = key_first + jnp.arange(key_total, dtype=jnp.int32)
    causal = key_index[None, :] <= row_spots[:, None]
    own_block = (key_index // BLOCK)[None, :] == (row_spots // BLOCK)[:, None]
    listed = jnp.repeat(jnp.repeat(mask_rows, BLOCK, axis=0), BLOCK, axis=1) == 1
    return causal & (listed | own_block)


def attend(state_tuple, queries, key_proj, value_proj, allowed):
    running_max, denominator, summed = state_tuple
    groups = running_max.shape[0]
    row_count = queries.shape[0]
    query_heads = queries.reshape(row_count, groups, HS)
    key_heads = key_proj.reshape(key_proj.shape[0], groups, HS)
    value_heads = value_proj.reshape(value_proj.shape[0], groups, HS)
    scores = jnp.einsum(
        "rgd,kgd->grk", query_heads, key_heads, preferred_element_type=jnp.float32
    ) * HS ** (-0.5)
    masked = jnp.where(allowed[None], scores, masked_score)
    new_max = jnp.maximum(running_max, jnp.max(masked, axis=2))
    weights = jnp.where(allowed[None], jnp.exp(masked - new_max[..., None]), 0.0)
    shrink = jnp.exp(running_max - new_max)
    denominator = denominator * shrink + jnp.sum(weights, axis=2)
    weighted = jnp.einsum(
        "grk,kgd->grd",
        weights.astype(jnp.bfloat16),
        value_heads,
        preferred_element_type=jnp.float32,
    )
    summed = summed * shrink[..., None] + weighted
    return (new_max, denominator, summed)


def body(inputs, latents, w_query, w_key, w_value, w_out, positions, block_mask):
    seq_count = lax.axis_size("seq")
    my_index = lax.axis_index("seq")
    row_count = latents.shape[0]
    key_total = inputs.shape[0]
    groups = w_query.shape[1] // HS
    key_proj = jnp.dot(inputs, w_key, preferred_element_type=jnp.float32).astype(jnp.bfloat16)
    value_proj = jnp.dot(inputs, w_value, preferred_element_type=jnp.float32).astype(jnp.bfloat16)
    queries = jnp.dot(latents, w_query, preferred_element_type=jnp.float32).astype(jnp.bfloat16)
    key_first = my_index * key_total
    mask_cols = lax.dynamic_slice_in_dim(
        block_mask, my_index * (key_total // BLOCK), key_total // BLOCK, 1
    )

    def rows_allowed(source):
        row_spots = lax.dynamic_slice_in_dim(positions, source * row_count, row_count, 0)
        mask_rows = lax.dynamic_slice_in_dim(
            mask_cols, source * (row_count // BLOCK), row_count // BLOCK, 0
        )
        return allowed_pairs(row_spots, mask_rows, key_first, key_total)

    start_state = (
        jnp.full((groups, row_count), masked_score, jnp.float32),
        jnp.zeros((groups, row_count), jnp.float32),
        jnp.zeros((groups, row_count, HS), jnp.float32),
    )

    def one_turn(turn_index, state_tuple):
        travelling, running_max, denominator, summed = state_tuple
        source = (my_index - turn_index + seq_count) % seq_count
        running_max, denominator, summed = attend(
            (running_max, denominator, summed),
            travelling,
            key_proj,
            value_proj,
            rows_allowed(source),
        )
        travelling = from_behind(travelling, "seq", 1)
        running_max, denominator, flat_acc = (
            from_behind(running_max.astype(jnp.bfloat16), "seq", 1).astype(running_max.dtype),
            from_behind(denominator.astype(jnp.bfloat16), "seq", 1).astype(denominator.dtype),
            from_behind(
                summed.reshape(groups, row_count * HS).astype(jnp.bfloat16), "seq", 1
            ).astype(jnp.float32),
        )
        return (travelling, running_max, denominator, flat_acc.reshape(groups, row_count, HS))

    travelling, running_max, denominator, summed = lax.fori_loop(
        0, seq_count, one_turn, (queries,) + start_state
    )
    attention = (summed / denominator[..., None]).transpose(1, 0, 2).reshape(row_count, groups * HS)
    attention = attention.astype(jnp.bfloat16)
    return lax.psum_scatter(
        jnp.dot(attention, w_out, preferred_element_type=jnp.float32).astype(jnp.bfloat16),
        "grp",
        scatter_dimension=0,
        tiled=True,
    )


def solution(mesh):
    return jax.shard_map(
        body,
        mesh=mesh,
        in_specs=(
            P("seq", None),
            P("seq", None),
            P(None, "grp"),
            P(None, "grp"),
            P(None, "grp"),
            P("grp", None),
            P(),
            P(),
        ),
        out_specs=P(("seq", "grp"), None),
        check_vma=False,
    )
```

profile of v0, /device:TPU:3, one launch (start us, length us, event | category | flops | bytes accessed | tf_op | source)
XLA Modules:
  0.0 435.2 jit_solution(6508004269423914862)
XLA Ops:
  9.3 3.5 convolution_convert_fusion.1
  13.0 3.4 convolution_convert_fusion
  16.8 365.0 %while.23 = (s32[]{:T(128)}, bf16[512,128]{0,1:T(8,128)(2,1)S(1)}, f32[2,512]{1,0:T(2,128)S(1)}, f32[2,512]{1,0:T(2,128)S(1)}, f32[2,512,64]{2,1,0:T(8,128)S(1)}...) while((s32[]{:T(128)}, bf16[512,128]{0,1:T(8,128)(2,1)S(1)}, ...), condition=%wide.region_3.4_spmd.clone, body=%wide.region_0.3_spmd.clone.sunk | while | flops 568574592 | bytes 35929028 | solution.py:99
  17.9 3.5 broadcast_in_dim.155
  25.1 2.8 fusion.54
  30.6 3.5 collective-permute-start.3
  38.8 3.5 broadcast_in_dim.155
  46.1 2.8 fusion.54
  51.6 4.0 collective-permute-start.3
  60.9 3.5 broadcast_in_dim.155
  68.1 2.8 fusion.54
  73.7 3.5 collective-permute-start.3
  77.2 3.6 collective-permute-start.2
  83.3 3.5 broadcast_in_dim.155
  90.5 2.8 fusion.54
  96.0 3.5 collective-permute-start.3
  99.6 3.6 collective-permute-start.2
  105.6 3.5 broadcast_in_dim.155
  112.9 2.8 fusion.54
  118.4 3.5 collective-permute-start.3
  122.0 3.6 collective-permute-start.2
  128.0 3.5 broadcast_in_dim.155
  135.2 2.8 fusion.54
  140.7 3.5 collective-permute-start.3
  144.3 3.6 collective-permute-start.2
  150.3 3.5 broadcast_in_dim.155
  157.6 2.8 fusion.54
  163.1 3.5 collective-permute-start.3
  166.7 3.6 collective-permute-start.2
  172.7 3.5 broadcast_in_dim.155
  179.9 2.8 fusion.54
  185.4 3.5 collective-permute-start.3
  189.0 3.6 collective-permute-start.2
  195.0 3.5 broadcast_in_dim.155
  202.3 2.8 fusion.54
  207.8 3.5 collective-permute-start.3
  211.4 4.1 collective-permute-start.2
  218.0 3.5 broadcast_in_dim.155
  225.2 2.8 fusion.54
  230.7 3.7 collective-permute-start.3
  234.7 4.3 collective-permute-start.2
  241.5 3.5 broadcast_in_dim.155
  248.7 2.8 fusion.54
  254.2 3.7 collective-permute-start.3
  258.3 4.3 collective-permute-start.2
  265.1 3.5 broadcast_in_dim.155
  272.3 2.8 fusion.54
  277.8 3.7 collective-permute-start.3
  281.8 4.3 collective-permute-start.2
  288.6 3.5 broadcast_in_dim.155
  295.9 2.8 fusion.54
  301.4 3.7 collective-permute-start.3
  305.4 4.3 collective-permute-start.2
  312.2 3.5 broadcast_in_dim.155
  319.4 2.8 fusion.54
  324.9 3.7 collective-permute-start.3
  329.0 4.3 collective-permute-start.2
  335.8 3.5 broadcast_in_dim.155
  348.5 3.7 collective-permute-start.3
  352.5 4.3 collective-permute-start.2
  359.3 3.5 broadcast_in_dim.155
  372.1 3.7 collective-permute-start.3
  376.1 4.3 collective-permute-start.2
  383.5 44.9 %reduce-scatter.2.cloned.1.call-done = bf16[64,1024]{1,0:T(8,128)(2,1)} async-done(((bf16[512,1024]{1,0:T(8,128)(2,1)}), bf16[64,1024]{1,0:T(8,128)(2,1)}) %reduce-scatter.2.cloned.1.call-update) | async-done | bytes 131088 | tf_op jit(solution)/shard_map/reduce_scatter | solution.py:104
  (377 shorter events, 158.8 us)
Async XLA Ops:
  6.5 421.8 %reduce-scatter.2.cloned.1.call-start = ((), (), s32[]{:S(2)}) async-start(), calls=%async_computation.1 | async-start | bytes 1179648 | tf_op jit(solution)/shard_map/reduce_scatter | solution.py:104
  30.6 6.9 %collective-permute-start.3 = (bf16[2,32768]{1,0:T(2,128)(2,1)S(1)}, bf16[2,32768]{1,0:T(2,128)(2,1)S(1)}, u32[]{:S(2)}, u32[]{:S(2)}) collective-permute-start(bf16[2,32768]{1,0:T(2,128)(2,1)S(1)} %convert_element_type.140), channel_id=1, source_target_pairs={{120,0},{0,8},{8,16},{16,24},{24,32},{32,40},{40,48},{48,56},{56,6... | collective-permute-start | bytes 393224 | tf_op jit(solution)/shard_map/while/body/eval_jaxpr/ppermute | solution.py:16
  34.2 3.6 collective-permute-start
  34.3 3.3 collective-permute-start.2
  35.6 2.0 collective-permute-start.1
  51.6 8.0 %collective-permute-start.3 = (bf16[2,32768]{1,0:T(2,128)(2,1)S(1)}, bf16[2,32768]{1,0:T(2,128)(2,1)S(1)}, u32[]{:S(2)}, u32[]{:S(2)}) collective-permute-start(bf16[2,32768]{1,0:T(2,128)(2,1)S(1)} %convert_element_type.140), channel_id=1, source_target_pairs={{120,0},{0,8},{8,16},{16,24},{24,32},{32,40},{40,48},{48,56},{56,6... | collective-permute-start | bytes 393224 | tf_op jit(solution)/shard_map/while/body/eval_jaxpr/ppermute | solution.py:16
  55.6 4.2 collective-permute-start
  55.7 3.5 collective-permute-start.2
  58.5 1.2 collective-permute-start.1
  73.7 8.3 %collective-permute-start.3 = (bf16[2,32768]{1,0:T(2,128)(2,1)S(1)}, bf16[2,32768]{1,0:T(2,128)(2,1)S(1)}, u32[]{:S(2)}, u32[]{:S(2)}) collective-permute-start(bf16[2,32768]{1,0:T(2,128)(2,1)S(1)} %convert_element_type.140), channel_id=1, source_target_pairs={{120,0},{0,8},{8,16},{16,24},{24,32},{32,40},{40,48},{48,56},{56,6... | collective-permute-start | bytes 393224 | tf_op jit(solution)/shard_map/while/body/eval_jaxpr/ppermute | solution.py:16
  77.2 5.0 %collective-permute-start = (bf16[512,128]{0,1:T(8,128)(2,1)S(1)}, bf16[512,128]{0,1:T(8,128)(2,1)S(1)}, u32[]{:S(2)}, u32[]{:S(2)}) collective-permute-start(bf16[512,128]{0,1:T(8,128)(2,1)S(1)} %copy.33), channel_id=1, source_target_pairs={{120,0},{0,8},{8,16},{16,24},{24,32},{32,40},{40,48},{48,56},{56,6... | collective-permute-start | bytes 393224 | tf_op jit(solution)/shard_map/while/body/eval_jaxpr/ppermute | solution.py:16
  77.2 4.3 collective-permute-start.2
  80.8 1.2 collective-permute-start.1
  96.0 8.3 %collective-permute-start.3 = (bf16[2,32768]{1,0:T(2,128)(2,1)S(1)}, bf16[2,32768]{1,0:T(2,128)(2,1)S(1)}, u32[]{:S(2)}, u32[]{:S(2)}) collective-permute-start(bf16[2,32768]{1,0:T(2,128)(2,1)S(1)} %convert_element_type.140), channel_id=1, source_target_pairs={{120,0},{0,8},{8,16},{16,24},{24,32},{32,40},{40,48},{48,56},{56,6... | collective-permute-start | bytes 393224 | tf_op jit(solution)/shard_map/while/body/eval_jaxpr/ppermute | solution.py:16
  99.5 5.0 %collective-permute-start = (bf16[512,128]{0,1:T(8,128)(2,1)S(1)}, bf16[512,128]{0,1:T(8,128)(2,1)S(1)}, u32[]{:S(2)}, u32[]{:S(2)}) collective-permute-start(bf16[512,128]{0,1:T(8,128)(2,1)S(1)} %copy.33), channel_id=1, source_target_pairs={{120,0},{0,8},{8,16},{16,24},{24,32},{32,40},{40,48},{48,56},{56,6... | collective-permute-start | bytes 393224 | tf_op jit(solution)/shard_map/while/body/eval_jaxpr/ppermute | solution.py:16
  99.6 4.3 collective-permute-start.2
  103.2 1.2 collective-permute-start.1
  118.4 8.3 %collective-permute-start.3 = (bf16[2,32768]{1,0:T(2,128)(2,1)S(1)}, bf16[2,32768]{1,0:T(2,128)(2,1)S(1)}, u32[]{:S(2)}, u32[]{:S(2)}) collective-permute-start(bf16[2,32768]{1,0:T(2,128)(2,1)S(1)} %convert_element_type.140), channel_id=1, source_target_pairs={{120,0},{0,8},{8,16},{16,24},{24,32},{32,40},{40,48},{48,56},{56,6... | collective-permute-start | bytes 393224 | tf_op jit(solution)/shard_map/while/body/eval_jaxpr/ppermute | solution.py:16
  121.9 5.0 %collective-permute-start = (bf16[512,128]{0,1:T(8,128)(2,1)S(1)}, bf16[512,128]{0,1:T(8,128)(2,1)S(1)}, u32[]{:S(2)}, u32[]{:S(2)}) collective-permute-start(bf16[512,128]{0,1:T(8,128)(2,1)S(1)} %copy.33), channel_id=1, source_target_pairs={{120,0},{0,8},{8,16},{16,24},{24,32},{32,40},{40,48},{48,56},{56,6... | collective-permute-start | bytes 393224 | tf_op jit(solution)/shard_map/while/body/eval_jaxpr/ppermute | solution.py:16
  122.0 4.3 collective-permute-start.2
  125.5 1.2 collective-permute-start.1
  140.7 8.3 %collective-permute-start.3 = (bf16[2,32768]{1,0:T(2,128)(2,1)S(1)}, bf16[2,32768]{1,0:T(2,128)(2,1)S(1)}, u32[]{:S(2)}, u32[]{:S(2)}) collective-permute-start(bf16[2,32768]{1,0:T(2,128)(2,1)S(1)} %convert_element_type.140), channel_id=1, source_target_pairs={{120,0},{0,8},{8,16},{16,24},{24,32},{32,40},{40,48},{48,56},{56,6... | collective-permute-start | bytes 393224 | tf_op jit(solution)/shard_map/while/body/eval_jaxpr/ppermute | solution.py:16
  144.2 5.0 %collective-permute-start = (bf16[512,128]{0,1:T(8,128)(2,1)S(1)}, bf16[512,128]{0,1:T(8,128)(2,1)S(1)}, u32[]{:S(2)}, u32[]{:S(2)}) collective-permute-start(bf16[512,128]{0,1:T(8,128)(2,1)S(1)} %copy.33), channel_id=1, source_target_pairs={{120,0},{0,8},{8,16},{16,24},{24,32},{32,40},{40,48},{48,56},{56,6... | collective-permute-start | bytes 393224 | tf_op jit(solution)/shard_map/while/body/eval_jaxpr/ppermute | solution.py:16
  144.3 4.3 collective-permute-start.2
  147.9 1.2 collective-permute-start.1
  163.1 8.3 %collective-permute-start.3 = (bf16[2,32768]{1,0:T(2,128)(2,1)S(1)}, bf16[2,32768]{1,0:T(2,128)(2,1)S(1)}, u32[]{:S(2)}, u32[]{:S(2)}) collective-permute-start(bf16[2,32768]{1,0:T(2,128)(2,1)S(1)} %convert_element_type.140), channel_id=1, source_target_pairs={{120,0},{0,8},{8,16},{16,24},{24,32},{32,40},{40,48},{48,56},{56,6... | collective-permute-start | bytes 393224 | tf_op jit(solution)/shard_map/while/body/eval_jaxpr/ppermute | solution.py:16
  166.6 5.0 %collective-permute-start = (bf16[512,128]{0,1:T(8,128)(2,1)S(1)}, bf16[512,128]{0,1:T(8,128)(2,1)S(1)}, u32[]{:S(2)}, u32[]{:S(2)}) collective-permute-start(bf16[512,128]{0,1:T(8,128)(2,1)S(1)} %copy.33), channel_id=1, source_target_pairs={{120,0},{0,8},{8,16},{16,24},{24,32},{32,40},{40,48},{48,56},{56,6... | collective-permute-start | bytes 393224 | tf_op jit(solution)/shard_map/while/body/eval_jaxpr/ppermute | solution.py:16
  166.7 4.3 collective-permute-start.2
  170.2 1.2 collective-permute-start.1
  185.4 8.3 %collective-permute-start.3 = (bf16[2,32768]{1,0:T(2,128)(2,1)S(1)}, bf16[2,32768]{1,0:T(2,128)(2,1)S(1)}, u32[]{:S(2)}, u32[]{:S(2)}) collective-permute-start(bf16[2,32768]{1,0:T(2,128)(2,1)S(1)} %convert_element_type.140), channel_id=1, source_target_pairs={{120,0},{0,8},{8,16},{16,24},{24,32},{32,40},{40,48},{48,56},{56,6... | collective-permute-start | bytes 393224 | tf_op jit(solution)/shard_map/while/body/eval_jaxpr/ppermute | solution.py:16
  188.9 5.0 %collective-permute-start = (bf16[512,128]{0,1:T(8,128)(2,1)S(1)}, bf16[512,128]{0,1:T(8,128)(2,1)S(1)}, u32[]{:S(2)}, u32[]{:S(2)}) collective-permute-start(bf16[512,128]{0,1:T(8,128)(2,1)S(1)} %copy.33), channel_id=1, source_target_pairs={{120,0},{0,8},{8,16},{16,24},{24,32},{32,40},{40,48},{48,56},{56,6... | collective-permute-start | bytes 393224 | tf_op jit(solution)/shard_map/while/body/eval_jaxpr/ppermute | solution.py:16
  189.0 4.3 collective-permute-start.2
  192.6 1.2 collective-permute-start.1
  207.8 8.9 %collective-permute-start.3 = (bf16[2,32768]{1,0:T(2,128)(2,1)S(1)}, bf16[2,32768]{1,0:T(2,128)(2,1)S(1)}, u32[]{:S(2)}, u32[]{:S(2)}) collective-permute-start(bf16[2,32768]{1,0:T(2,128)(2,1)S(1)} %convert_element_type.140), channel_id=1, source_target_pairs={{120,0},{0,8},{8,16},{16,24},{24,32},{32,40},{40,48},{48,56},{56,6... | collective-permute-start | bytes 393224 | tf_op jit(solution)/shard_map/while/body/eval_jaxpr/ppermute | solution.py:16
  211.3 5.6 %collective-permute-start = (bf16[512,128]{0,1:T(8,128)(2,1)S(1)}, bf16[512,128]{0,1:T(8,128)(2,1)S(1)}, u32[]{:S(2)}, u32[]{:S(2)}) collective-permute-start(bf16[512,128]{0,1:T(8,128)(2,1)S(1)} %copy.33), channel_id=1, source_target_pairs={{120,0},{0,8},{8,16},{16,24},{24,32},{32,40},{40,48},{48,56},{56,6... | collective-permute-start | bytes 393224 | tf_op jit(solution)/shard_map/while/body/eval_jaxpr/ppermute | solution.py:16
  211.4 4.9 %collective-permute-start.2 = (bf16[2,512]{1,0:T(2,128)(2,1)S(1)}, bf16[2,512]{1,0:T(2,128)(2,1)S(1)}, u32[]{:S(2)}, u32[]{:S(2)}) collective-permute-start(bf16[2,512]{1,0:T(2,128)(2,1)S(1)} %get-tuple-element.484), channel_id=1, source_target_pairs={{120,0},{0,8},{8,16},{16,24},{24,32},{32,40},{40,48},{48,56},{56,6... | collective-permute-start | bytes 6152 | tf_op jit(solution)/shard_map/while/body/eval_jaxpr/ppermute | solution.py:16
  215.5 1.2 collective-permute-start.1
  230.7 9.5 %collective-permute-start.3 = (bf16[2,32768]{1,0:T(2,128)(2,1)S(1)}, bf16[2,32768]{1,0:T(2,128)(2,1)S(1)}, u32[]{:S(2)}, u32[]{:S(2)}) collective-permute-start(bf16[2,32768]{1,0:T(2,128)(2,1)S(1)} %convert_element_type.140), channel_id=1, source_target_pairs={{120,0},{0,8},{8,16},{16,24},{24,32},{32,40},{40,48},{48,56},{56,6... | collective-permute-start | bytes 393224 | tf_op jit(solution)/shard_map/while/body/eval_jaxpr/ppermute | solution.py:16
  234.4 6.0 %collective-permute-start = (bf16[512,128]{0,1:T(8,128)(2,1)S(1)}, bf16[512,128]{0,1:T(8,128)(2,1)S(1)}, u32[]{:S(2)}, u32[]{:S(2)}) collective-permute-start(bf16[512,128]{0,1:T(8,128)(2,1)S(1)} %copy.33), channel_id=1, source_target_pairs={{120,0},{0,8},{8,16},{16,24},{24,32},{32,40},{40,48},{48,56},{56,6... | collective-permute-start | bytes 393224 | tf_op jit(solution)/shard_map/while/body/eval_jaxpr/ppermute | solution.py:16
  234.7 5.1 %collective-permute-start.2 = (bf16[2,512]{1,0:T(2,128)(2,1)S(1)}, bf16[2,512]{1,0:T(2,128)(2,1)S(1)}, u32[]{:S(2)}, u32[]{:S(2)}) collective-permute-start(bf16[2,512]{1,0:T(2,128)(2,1)S(1)} %get-tuple-element.484), channel_id=1, source_target_pairs={{120,0},{0,8},{8,16},{16,24},{24,32},{32,40},{40,48},{48,56},{56,6... | collective-permute-start | bytes 6152 | tf_op jit(solution)/shard_map/while/body/eval_jaxpr/ppermute | solution.py:16
  239.1 1.2 collective-permute-start.1
  254.2 9.5 %collective-permute-start.3 = (bf16[2,32768]{1,0:T(2,128)(2,1)S(1)}, bf16[2,32768]{1,0:T(2,128)(2,1)S(1)}, u32[]{:S(2)}, u32[]{:S(2)}) collective-permute-start(bf16[2,32768]{1,0:T(2,128)(2,1)S(1)} %convert_element_type.140), channel_id=1, source_target_pairs={{120,0},{0,8},{8,16},{16,24},{24,32},{32,40},{40,48},{48,56},{56,6... | collective-permute-start | bytes 393224 | tf_op jit(solution)/shard_map/while/body/eval_jaxpr/ppermute | solution.py:16
  258.0 6.0 %collective-permute-start = (bf16[512,128]{0,1:T(8,128)(2,1)S(1)}, bf16[512,128]{0,1:T(8,128)(2,1)S(1)}, u32[]{:S(2)}, u32[]{:S(2)}) collective-permute-start(bf16[512,128]{0,1:T(8,128)(2,1)S(1)} %copy.33), channel_id=1, source_target_pairs={{120,0},{0,8},{8,16},{16,24},{24,32},{32,40},{40,48},{48,56},{56,6... | collective-permute-start | bytes 393224 | tf_op jit(solution)/shard_map/while/body/eval_jaxpr/ppermute | solution.py:16
  258.3 5.1 %collective-permute-start.2 = (bf16[2,512]{1,0:T(2,128)(2,1)S(1)}, bf16[2,512]{1,0:T(2,128)(2,1)S(1)}, u32[]{:S(2)}, u32[]{:S(2)}) collective-permute-start(bf16[2,512]{1,0:T(2,128)(2,1)S(1)} %get-tuple-element.484), channel_id=1, source_target_pairs={{120,0},{0,8},{8,16},{16,24},{24,32},{32,40},{40,48},{48,56},{56,6... | collective-permute-start | bytes 6152 | tf_op jit(solution)/shard_map/while/body/eval_jaxpr/ppermute | solution.py:16
  262.6 1.2 collective-permute-start.1
  277.8 9.5 %collective-permute-start.3 = (bf16[2,32768]{1,0:T(2,128)(2,1)S(1)}, bf16[2,32768]{1,0:T(2,128)(2,1)S(1)}, u32[]{:S(2)}, u32[]{:S(2)}) collective-permute-start(bf16[2,32768]{1,0:T(2,128)(2,1)S(1)} %convert_element_type.140), channel_id=1, source_target_pairs={{120,0},{0,8},{8,16},{16,24},{24,32},{32,40},{40,48},{48,56},{56,6... | collective-permute-start | bytes 393224 | tf_op jit(solution)/shard_map/while/body/eval_jaxpr/ppermute | solution.py:16
  281.5 6.0 %collective-permute-start = (bf16[512,128]{0,1:T(8,128)(2,1)S(1)}, bf16[512,128]{0,1:T(8,128)(2,1)S(1)}, u32[]{:S(2)}, u32[]{:S(2)}) collective-permute-start(bf16[512,128]{0,1:T(8,128)(2,1)S(1)} %copy.33), channel_id=1, source_target_pairs={{120,0},{0,8},{8,16},{16,24},{24,32},{32,40},{40,48},{48,56},{56,6... | collective-permute-start | bytes 393224 | tf_op jit(solution)/shard_map/while/body/eval_jaxpr/ppermute | solution.py:16
  281.8 5.1 %collective-permute-start.2 = (bf16[2,512]{1,0:T(2,128)(2,1)S(1)}, bf16[2,512]{1,0:T(2,128)(2,1)S(1)}, u32[]{:S(2)}, u32[]{:S(2)}) collective-permute-start(bf16[2,512]{1,0:T(2,128)(2,1)S(1)} %get-tuple-element.484), channel_id=1, source_target_pairs={{120,0},{0,8},{8,16},{16,24},{24,32},{32,40},{40,48},{48,56},{56,6... | collective-permute-start | bytes 6152 | tf_op jit(solution)/shard_map/while/body/eval_jaxpr/ppermute | solution.py:16
  286.2 1.2 collective-permute-start.1
  301.4 9.5 %collective-permute-start.3 = (bf16[2,32768]{1,0:T(2,128)(2,1)S(1)}, bf16[2,32768]{1,0:T(2,128)(2,1)S(1)}, u32[]{:S(2)}, u32[]{:S(2)}) collective-permute-start(bf16[2,32768]{1,0:T(2,128)(2,1)S(1)} %convert_element_type.140), channel_id=1, source_target_pairs={{120,0},{0,8},{8,16},{16,24},{24,32},{32,40},{40,48},{48,56},{56,6... | collective-permute-start | bytes 393224 | tf_op jit(solution)/shard_map/while/body/eval_jaxpr/ppermute | solution.py:16
  305.1 6.0 %collective-permute-start = (bf16[512,128]{0,1:T(8,128)(2,1)S(1)}, bf16[512,128]{0,1:T(8,128)(2,1)S(1)}, u32[]{:S(2)}, u32[]{:S(2)}) collective-permute-start(bf16[512,128]{0,1:T(8,128)(2,1)S(1)} %copy.33), channel_id=1, source_target_pairs={{120,0},{0,8},{8,16},{16,24},{24,32},{32,40},{40,48},{48,56},{56,6... | collective-permute-start | bytes 393224 | tf_op jit(solution)/shard_map/while/body/eval_jaxpr/ppermute | solution.py:16
  305.4 5.1 %collective-permute-start.2 = (bf16[2,512]{1,0:T(2,128)(2,1)S(1)}, bf16[2,512]{1,0:T(2,128)(2,1)S(1)}, u32[]{:S(2)}, u32[]{:S(2)}) collective-permute-start(bf16[2,512]{1,0:T(2,128)(2,1)S(1)} %get-tuple-element.484), channel_id=1, source_target_pairs={{120,0},{0,8},{8,16},{16,24},{24,32},{32,40},{40,48},{48,56},{56,6... | collective-permute-start | bytes 6152 | tf_op jit(solution)/shard_map/while/body/eval_jaxpr/ppermute | solution.py:16
  309.7 1.2 collective-permute-start.1
  324.9 9.5 %collective-permute-start.3 = (bf16[2,32768]{1,0:T(2,128)(2,1)S(1)}, bf16[2,32768]{1,0:T(2,128)(2,1)S(1)}, u32[]{:S(2)}, u32[]{:S(2)}) collective-permute-start(bf16[2,32768]{1,0:T(2,128)(2,1)S(1)} %convert_element_type.140), channel_id=1, source_target_pairs={{120,0},{0,8},{8,16},{16,24},{24,32},{32,40},{40,48},{48,56},{56,6... | collective-permute-start | bytes 393224 | tf_op jit(solution)/shard_map/while/body/eval_jaxpr/ppermute | solution.py:16
  328.6 6.0 %collective-permute-start = (bf16[512,128]{0,1:T(8,128)(2,1)S(1)}, bf16[512,128]{0,1:T(8,128)(2,1)S(1)}, u32[]{:S(2)}, u32[]{:S(2)}) collective-permute-start(bf16[512,128]{0,1:T(8,128)(2,1)S(1)} %copy.33), channel_id=1, source_target_pairs={{120,0},{0,8},{8,16},{16,24},{24,32},{32,40},{40,48},{48,56},{56,6... | collective-permute-start | bytes 393224 | tf_op jit(solution)/shard_map/while/body/eval_jaxpr/ppermute | solution.py:16
  329.0 5.1 %collective-permute-start.2 = (bf16[2,512]{1,0:T(2,128)(2,1)S(1)}, bf16[2,512]{1,0:T(2,128)(2,1)S(1)}, u32[]{:S(2)}, u32[]{:S(2)}) collective-permute-start(bf16[2,512]{1,0:T(2,128)(2,1)S(1)} %get-tuple-element.484), channel_id=1, source_target_pairs={{120,0},{0,8},{8,16},{16,24},{24,32},{32,40},{40,48},{48,56},{56,6... | collective-permute-start | bytes 6152 | tf_op jit(solution)/shard_map/while/body/eval_jaxpr/ppermute | solution.py:16
  333.3 1.2 collective-permute-start.1
  348.5 9.5 %collective-permute-start.3 = (bf16[2,32768]{1,0:T(2,128)(2,1)S(1)}, bf16[2,32768]{1,0:T(2,128)(2,1)S(1)}, u32[]{:S(2)}, u32[]{:S(2)}) collective-permute-start(bf16[2,32768]{1,0:T(2,128)(2,1)S(1)} %convert_element_type.140), channel_id=1, source_target_pairs={{120,0},{0,8},{8,16},{16,24},{24,32},{32,40},{40,48},{48,56},{56,6... | collective-permute-start | bytes 393224 | tf_op jit(solution)/shard_map/while/body/eval_jaxpr/ppermute | solution.py:16
  352.2 6.0 %collective-permute-start = (bf16[512,128]{0,1:T(8,128)(2,1)S(1)}, bf16[512,128]{0,1:T(8,128)(2,1)S(1)}, u32[]{:S(2)}, u32[]{:S(2)}) collective-permute-start(bf16[512,128]{0,1:T(8,128)(2,1)S(1)} %copy.33), channel_id=1, source_target_pairs={{120,0},{0,8},{8,16},{16,24},{24,32},{32,40},{40,48},{48,56},{56,6... | collective-permute-start | bytes 393224 | tf_op jit(solution)/shard_map/while/body/eval_jaxpr/ppermute | solution.py:16
  352.5 5.1 %collective-permute-start.2 = (bf16[2,512]{1,0:T(2,128)(2,1)S(1)}, bf16[2,512]{1,0:T(2,128)(2,1)S(1)}, u32[]{:S(2)}, u32[]{:S(2)}) collective-permute-start(bf16[2,512]{1,0:T(2,128)(2,1)S(1)} %get-tuple-element.484), channel_id=1, source_target_pairs={{120,0},{0,8},{8,16},{16,24},{24,32},{32,40},{40,48},{48,56},{56,6... | collective-permute-start | bytes 6152 | tf_op jit(solution)/shard_map/while/body/eval_jaxpr/ppermute | solution.py:16
  372.1 9.5 %collective-permute-start.3 = (bf16[2,32768]{1,0:T(2,128)(2,1)S(1)}, bf16[2,32768]{1,0:T(2,128)(2,1)S(1)}, u32[]{:S(2)}, u32[]{:S(2)}) collective-permute-start(bf16[2,32768]{1,0:T(2,128)(2,1)S(1)} %convert_element_type.140), channel_id=1, source_target_pairs={{120,0},{0,8},{8,16},{16,24},{24,32},{32,40},{40,48},{48,56},{56,6... | collective-permute-start | bytes 393224 | tf_op jit(solution)/shard_map/while/body/eval_jaxpr/ppermute | solution.py:16
  375.8 6.0 %collective-permute-start = (bf16[512,128]{0,1:T(8,128)(2,1)S(1)}, bf16[512,128]{0,1:T(8,128)(2,1)S(1)}, u32[]{:S(2)}, u32[]{:S(2)}) collective-permute-start(bf16[512,128]{0,1:T(8,128)(2,1)S(1)} %copy.33), channel_id=1, source_target_pairs={{120,0},{0,8},{8,16},{16,24},{24,32},{32,40},{40,48},{48,56},{56,6... | collective-permute-start | bytes 393224 | tf_op jit(solution)/shard_map/while/body/eval_jaxpr/ppermute | solution.py:16
  376.1 5.1 %collective-permute-start.2 = (bf16[2,512]{1,0:T(2,128)(2,1)S(1)}, bf16[2,512]{1,0:T(2,128)(2,1)S(1)}, u32[]{:S(2)}, u32[]{:S(2)}) collective-permute-start(bf16[2,512]{1,0:T(2,128)(2,1)S(1)} %get-tuple-element.484), channel_id=1, source_target_pairs={{120,0},{0,8},{8,16},{16,24},{24,32},{32,40},{40,48},{48,56},{56,6... | collective-permute-start | bytes 6152 | tf_op jit(solution)/shard_map/while/body/eval_jaxpr/ppermute | solution.py:16
  380.4 1.2 collective-permute-start.1
  (5 other events, 384.2 us)
Sparse Core Ops, SparseCore 0:
  383.6 44.7 reduce-scatter.1
where the time goes:
time: 441 us; the launch traced here: 435 us
  starting transfers between devices  124 us (28%)
  other arithmetic  86.3 us (20%)
  matrix products  77.1 us (17%)
  local copies, waits for them, and re-layouts  70.6 us (16%)
  waiting for transfers between devices  61.4 us (14%)
  between operations  13.5 us (3%)
    ppermute x64, starting transfers between devices, from_behind(): return lax.ppermute(block, axis, route)  124 us
    broadcast_in_dim x16, local copies, waits for them, and re-layouts, allowed_pairs(): jnp.repeat(jnp.repeat(mask_rows, BLOCK, axis=0), BLOCK, axis=1) == 1  55.5 us
    reduce_scatter x1, waiting for transfers between devices, body(): lax.psum_scatter(jnp.dot(attention, w_out, preferred_element_type=jnp.flo...  44.9 us
    reduce_sum x16, other arithmetic, attend(): denominator = denominator * shrink + jnp.sum(weights, axis=2)  44.7 us
    dot_general x16, matrix products, attend(): jnp.einsum('grk,kgd->grd', weights.astype(jnp.bfloat16), value_heads, pre...  36 us
    dot_general x16, matrix products, attend(): jnp.einsum('rgd,kgd->grk', query_heads, key_heads, preferred_element_type...  31.4 us
    and x16, other arithmetic, allowed_pairs(): return causal & (listed | own_block)  28.3 us
    ppermute x64, waiting for transfers between devices, from_behind(): return lax.ppermute(block, axis, route)  16.5 us
  transfers between devices with their start and end apart: 65, of which 32 were waited for; matrix products, arithmetic and copies ran while one was open for 1% of the time, Pallas kernels for 0%

commit v1 on v0

v1 whole, which is shorter than its diff:
```python
import functools

import jax
import jax.numpy as jnp
from jax import lax
from jax.experimental import pallas as pl
from jax.experimental.pallas import tpu as pltpu
from jax.sharding import PartitionSpec as P

HS = 64
BLOCK = 128
CHUNK = 8
KEY_BLOCKS = 32
ACC_ROWS = 72
LOG2E = 1.4426950408889634
masked_score = -1e30
lowest_max = -1e29


def attention_kernel(n_ref, code_ref, base_ref, q_ref, pos_ref, kv_ref, o_ref, s_a, s_b, acc, vt):
    row_blocks = n_ref.shape[0]
    per_shard = q_ref.shape[2] // BLOCK
    own_base = base_ref[0]
    partner_base = base_ref[1]
    key_iota = lax.broadcasted_iota(jnp.int32, (BLOCK, BLOCK), 0)

    for t in range(KEY_BLOCKS):
        tile = kv_ref[t * BLOCK : (t + 1) * BLOCK, :].T
        vt[:HS, t * BLOCK : (t + 1) * BLOCK] = tile[HS:, :]
    vt[HS:, :] = jnp.ones((ACC_ROWS - HS, KEY_BLOCKS * BLOCK), jnp.bfloat16)

    def clamp(r):
        return jnp.minimum(r, row_blocks - 1)

    def advance(r, c):
        last = c + 1 >= n_ref[clamp(r)]
        return jnp.where(last, jnp.minimum(r + 1, row_blocks), r), jnp.where(last, 0, c + 1)

    def key_offset(r, c, t):
        return pl.multiple_of(jnp.bitwise_and(code_ref[r, c * CHUNK + t], 31) * BLOCK, BLOCK)

    def scores(s_ref, r, c, max_before):
        r = clamp(r)
        cols = pl.ds(pl.multiple_of(lax.rem(r, per_shard) * BLOCK, BLOCK), BLOCK)
        q = q_ref[lax.div(r, per_shard), :, cols]
        q = jnp.concatenate([q, jnp.zeros_like(q)], 0)
        pos = pos_ref[pl.ds(r, 1), :]
        keys = jnp.concatenate([kv_ref[pl.ds(key_offset(r, c, t), BLOCK), :] for t in range(CHUNK)], 0)
        s_all = jnp.dot(keys, q, preferred_element_type=jnp.float32)
        best = None
        for t in range(CHUNK):
            code = code_ref[r, c * CHUNK + t]
            k = jnp.bitwise_and(code, 31)
            base = jnp.where(k < 16, own_base, partner_base - 16 * BLOCK) + k * BLOCK
            reach = jnp.where(jnp.bitwise_and(code, 32) > 0, 1 << 30, BLOCK)
            reach = jnp.where(code >= 64, reach, -(1 << 30))
            ahead = pos - base
            last_key = jnp.where(ahead < reach, ahead, -1)
            s = jnp.where(key_iota <= last_key, s_all[t * BLOCK : (t + 1) * BLOCK], masked_score)
            s_ref[t * BLOCK : (t + 1) * BLOCK, :] = s
            part = jnp.max(s.reshape(16, 8, BLOCK), 0)
            best = part if best is None else jnp.maximum(best, part)
        before = jnp.where(c == 0, lowest_max, max_before)
        now = jnp.maximum(before, jnp.max(best, 0, keepdims=True))
        return now.astype(jnp.bfloat16).astype(jnp.float32)

    def weigh(s_ref, r, c, max_before, max_now):
        p = jnp.exp2((s_ref[...] - max_now) * LOG2E).astype(jnp.bfloat16)
        shrink = jnp.where(c == 0, 0.0, jnp.exp2((max_before - max_now) * LOG2E))
        rr = clamp(r)
        values = jnp.concatenate([vt[:, pl.ds(key_offset(rr, c, t), BLOCK)] for t in range(CHUNK)], 1)
        a = acc[...] * shrink + jnp.dot(values, p, preferred_element_type=jnp.float32)
        acc[...] = a
        total = a[HS : HS + 1]
        low = total - total.astype(jnp.bfloat16).astype(jnp.float32)
        out = jnp.concatenate([a[: HS + 1], max_now, low, a[HS + 3 :]], 0).astype(jnp.bfloat16)
        cols = pl.ds(pl.multiple_of(lax.rem(r, per_shard) * BLOCK, BLOCK), BLOCK)
        o_ref[lax.div(r, per_shard), :, cols] = out

    acc[...] = jnp.zeros_like(acc)
    items = lax.fori_loop(0, row_blocks, lambda r, total: total + n_ref[r], jnp.int32(0))
    start = jnp.full((1, BLOCK), lowest_max, jnp.float32)
    first = scores(s_a, jnp.int32(0), jnp.int32(0), start)

    def two_items(_, state):
        r, c, max_before, max_now = state
        r1, c1 = advance(r, c)
        max_1 = scores(s_b, r1, c1, max_now)
        weigh(s_a, r, c, max_before, max_now)
        r2, c2 = advance(r1, c1)
        max_2 = scores(s_a, r2, c2, max_1)
        weigh(s_b, r1, c1, max_now, max_1)
        return r2, c2, max_1, max_2

    lax.fori_loop(0, lax.div(items + 1, 2), two_items, (jnp.int32(0), jnp.int32(0), start, first))


def attend(chunks, codes, bases, queries, spots, kv):
    shards, _, rows = queries.shape
    smem = pl.BlockSpec(memory_space=pltpu.SMEM)
    vmem = pl.BlockSpec(memory_space=pltpu.VMEM)
    return pl.pallas_call(
        attention_kernel,
        in_specs=[smem] * 3 + [vmem] * 3,
        out_specs=vmem,
        out_shape=jax.ShapeDtypeStruct((shards + 1, ACC_ROWS, rows), jnp.bfloat16),
        scratch_shapes=[
            pltpu.VMEM((CHUNK * BLOCK, BLOCK), jnp.float32),
            pltpu.VMEM((CHUNK * BLOCK, BLOCK), jnp.float32),
            pltpu.VMEM((ACC_ROWS, BLOCK), jnp.float32),
            pltpu.VMEM((ACC_ROWS, KEY_BLOCKS * BLOCK), jnp.bfloat16),
        ],
        compiler_params=pltpu.CompilerParams(vmem_limit_bytes=40 * 2**20),
        cost_estimate=pl.CostEstimate(flops=10**10, bytes_accessed=4 * 2**20, transcendentals=2**24),
    )(chunks, codes, bases, queries, spots, kv)


def work_list(spots, block_mask, key_blocks):
    listed = jnp.concatenate(
        [lax.dynamic_slice_in_dim(block_mask, first, 16, 1) for first in (key_blocks[0], key_blocks[16])], 1
    ) == 1
    own = jnp.any((spots // BLOCK)[:, :, None] == key_blocks[None, None, :], axis=1)
    reached = (key_blocks * BLOCK)[None, :] <= jnp.max(spots, axis=1)[:, None]
    active = (listed & reached) | own
    index = jnp.arange(KEY_BLOCKS, dtype=jnp.int32)
    earlier = index[None, :] < index[:, None]
    place = jnp.sum(active[:, None, :] & earlier[None], axis=2, dtype=jnp.int32)
    value = index[None, :] + 32 * listed.astype(jnp.int32) + 64
    chosen = active[:, None, :] & (place[:, None, :] == index[None, :, None])
    codes = jnp.sum(jnp.where(chosen, value[:, None, :], 0), axis=2, dtype=jnp.int32)
    count = jnp.sum(active, axis=1, dtype=jnp.int32)
    return jnp.maximum((count + CHUNK - 1) // CHUNK, 1), codes


def gather_groups(block):
    me = lax.axis_index("grp")
    other = lax.ppermute(block, "grp", [(g, g ^ 4) for g in range(8)])
    low = me < 4
    pair = jnp.stack([jnp.where(low, block, other), jnp.where(low, other, block)])
    turns = [pair] + [
        lax.ppermute(pair, "grp", [(g, (g & 4) | ((g + k) & 3)) for g in range(8)]) for k in (1, 2, 3)
    ]
    z = me % 4
    stacked = jnp.stack(turns)
    ordered = jnp.stack([lax.dynamic_index_in_dim(stacked, (z - i) % 4, 0, False) for i in range(4)], 1)
    return ordered.reshape(8 * block.shape[0], block.shape[1])


def body(inputs, latents, w_query, w_key, w_value, w_out, positions, block_mask):
    s = lax.axis_index("seq")
    core = s % 2
    spots = positions.reshape(-1, BLOCK)
    index = jnp.arange(16, dtype=jnp.int32)
    key_blocks = jnp.concatenate([s * 16 + index, (s ^ 1) * 16 + index])

    queries = lax.dot_general(
        w_query, latents, (((0,), (1,)), ((), ())), preferred_element_type=jnp.float32
    ).astype(jnp.bfloat16) * jnp.bfloat16(HS ** -0.5)
    halves = queries.reshape(2, HS, queries.shape[1])
    queries = lax.all_to_all(jnp.tile(halves, (8, 1, 1)), "seq", 0, 0)

    def head_weights(head):
        return jnp.concatenate(
            [lax.dynamic_slice_in_dim(w, head * HS, HS, 1) for w in (w_key, w_value)], 1
        )

    kv_own = jnp.dot(inputs, head_weights(core), preferred_element_type=jnp.float32).astype(jnp.bfloat16)
    kv_other = jnp.dot(inputs, head_weights(1 - core), preferred_element_type=jnp.float32).astype(jnp.bfloat16)
    kv_partner = lax.ppermute(kv_other, "seq", [(i, i ^ 1) for i in range(16)])
    kv = jnp.concatenate([kv_own, kv_partner], 0)

    chunks, codes = work_list(spots, block_mask, key_blocks)
    bases = jnp.stack([key_blocks[0] * BLOCK, key_blocks[16] * BLOCK])
    parts = attend(chunks, codes, bases, queries, spots, kv)[:16]
    parts = lax.all_to_all(parts, "seq", 0, 0).astype(jnp.float32)

    parts = parts.reshape(8, 2, ACC_ROWS, parts.shape[2])
    maxima = parts[:, :, HS + 1]
    scale = jnp.exp(maxima - jnp.max(maxima, axis=0, keepdims=True))
    total = jnp.sum((parts[:, :, HS] + parts[:, :, HS + 2]) * scale, axis=0)
    summed = jnp.sum(parts[:, :, :HS] * scale[:, :, None], axis=0)
    attention = (summed / total[:, None]).astype(jnp.bfloat16)
    attention = attention.reshape(2 * HS, -1).T.reshape(8, -1, 2 * HS)
    attention = lax.all_to_all(attention, "grp", 0, 0).transpose(1, 0, 2)
    attention = attention.reshape(attention.shape[0], -1)
    w_all = gather_groups(w_out)
    return jnp.dot(attention, w_all, preferred_element_type=jnp.float32).astype(jnp.bfloat16)


def solution(mesh):
    return jax.shard_map(
        body,
        mesh=mesh,
        in_specs=(
            P("seq", None),
            P("seq", None),
            P(None, "grp"),
            P(None, "grp"),
            P(None, "grp"),
            P("grp", None),
            P(),
            P(),
        ),
        out_specs=P(("seq", "grp"), None),
        check_vma=False,
    )
```

time: 441 us -> 163 us (0.37)
  starting transfers between devices: 124 us -> 23.9 us
  Pallas kernels: 0 us -> 79 us
  other arithmetic: 86.3 us -> 8.53 us
  matrix products: 77.1 us -> 9.54 us
  local copies, waits for them, and re-layouts: 70.6 us -> 6.27 us
  waiting for transfers between devices: 61.4 us -> 33.4 us
  between operations: 13.5 us -> 0.46 us
    ppermute x64 -> x5, starting transfers between devices: 124 us -> 6.89 us  [the longest x3 5.74 us: gather_groups(): lax.ppermute(pair, 'grp', [(g, g & 4 | g + k & 3) for g in range(8)])]
    pallas_call x0 -> x1, Pallas kernels: none -> 79 us  [attend(): pl.pallas_call(attention_kernel, in_specs=[smem] * 3 + [vmem] * 3, out_sp...]
    dot_general x36 -> x4, matrix products: 77.1 us -> 9.54 us  [the longest x1 4.38 us: body(): jnp.dot(inputs, head_weights(1 - core), preferred_element_type=jnp.float32)]
    broadcast_in_dim x33 -> x0, local copies, waits for them, and re-layouts: 55.9 us -> none  [the longest x16 55.5 us: allowed_pairs(): jnp.repeat(jnp.repeat(mask_rows, BLOCK, axis=0), BLOCK, axis=1) == 1]
    reduce_scatter x1 -> x0, waiting for transfers between devices: 44.9 us -> none  [body(): lax.psum_scatter(jnp.dot(attention, w_out, preferred_element_type=jnp.flo...]
    reduce_sum x16 -> x5, other arithmetic: 44.7 us -> 0.87 us  [the longest x1 0.27 us: body(): summed = jnp.sum(parts[:, :, :HS] * scale[:, :, None], axis=0)]
    and x16 -> x0, other arithmetic: 28.3 us -> none  [allowed_pairs(): return causal & (listed | own_block)]
    all_to_all x0 -> x3, starting transfers between devices: none -> 17 us  [the longest x1 7.23 us: body(): queries = lax.all_to_all(jnp.tile(halves, (8, 1, 1)), 'seq', 0, 0)]
  transfers between devices with their start and end apart: 65 -> 8, of which waited for: 32 -> 4; matrix products, arithmetic and copies ran while one was open for 1% -> 10% of each run, Pallas kernels for 0% -> 49%
where the time goes in v1:
time: 163 us; the launch traced here: 161 us
  Pallas kernels  79 us (48%)
  waiting for transfers between devices  33.4 us (20%)
  starting transfers between devices  23.9 us (15%)
  matrix products  9.54 us (6%)
  other arithmetic  8.53 us (5%)
  local copies, waits for them, and re-layouts  6.27 us (4%)
    pallas_call x1, Pallas kernels, attend(): pl.pallas_call(attention_kernel, in_specs=[smem] * 3 + [vmem] * 3, out_sp...  79 us
    ppermute x3, waiting for transfers between devices, gather_groups(): lax.ppermute(pair, 'grp', [(g, g & 4 | g + k & 3) for g in range(8)])  22.3 us
    all_to_all x1, waiting for transfers between devices, body(): queries = lax.all_to_all(jnp.tile(halves, (8, 1, 1)), 'seq', 0, 0)  7.44 us
    all_to_all x1, starting transfers between devices, body(): queries = lax.all_to_all(jnp.tile(halves, (8, 1, 1)), 'seq', 0, 0)  7.23 us
    all_to_all x1, starting transfers between devices, body(): parts = lax.all_to_all(parts, 'seq', 0, 0).astype(jnp.float32)  5.85 us
    ppermute x3, starting transfers between devices, gather_groups(): lax.ppermute(pair, 'grp', [(g, g & 4 | g + k & 3) for g in range(8)])  5.74 us
    dot_general x1, matrix products, body(): jnp.dot(inputs, head_weights(1 - core), preferred_element_type=jnp.float32)  4.38 us
    all_to_all x1, starting transfers between devices, body(): attention = lax.all_to_all(attention, 'grp', 0, 0).transpose(1, 0, 2)  3.96 us
  transfers between devices with their start and end apart: 8, of which 4 were waited for; matrix products, arithmetic and copies ran while one was open for 10% of the time, Pallas kernels for 49%

profile of v1, /device:TPU:3, one launch (start us, length us, event | category | flops | bytes accessed | tf_op | source)
XLA Modules:
  0.0 161.1 jit_solution(13492252990541296026)
XLA Ops:
  0.0 0.0 copy-start
  0.0 1.6 %constant_dynamic-slice_fusion.2 = (bf16[1024,64]{1,0:T(8,128)(2,1)S(1)}, bf16[1024,64]{1,0:T(8,128)(2,1)S(1)}, bf16[1024,64]{1,0:T(8,128)(2,1)S(1)}, bf16[1024,64]{1,0:T(8,128)(2,1)S(1)}) fusion(bf16[1024,128]{1,0:T(8,128)(2,1)} %param.12, s32[]{:T(128)S(6)} %select_n.90, s32[]{:T(128)S(6)} %select_n.91, bf16[1024,128]{1,0:T(8,128)(2,1)} %param.11), kind=kLoop, calls=%fused_computation.53 | loop fusion | bytes 1048584 | tf_op jit(solution)/shard_map/dynamic_slice | solution.py:164
  1.6 0.0 copy-start.2
  1.6 4.4 %fusion.1 = bf16[2048,128]{1,0:T(8,128)(2,1)} fusion(bf16[2048,1024]{1,0:T(8,128)(2,1)} %param.8, bf16[1024,64]{1,0:T(8,128)(2,1)S(1)} %get-tuple-element.25, bf16[1024,64]{1,0:T(8,128)(2,1)S(1)} %get-tuple-element.32), kind=kOutput, calls=%fused_computation.3 | convolution fusion | flops 537657344 | bytes 4980736 | tf_op jit(solution)/shard_map/dot_general | solution.py:168
  6.0 0.0 copy-start.3
  6.0 0.0 copy-start.1
  6.0 0.0 copy-start.4
  6.0 0.7 collective-permute-start
  6.7 0.0 copy-done
  6.7 0.0 copy-done.2
  6.7 0.5 fusion.3
  7.2 1.1 tile.11
  8.3 7.2 %all-to-all-start = ((bf16[16,64,512]{2,1,0:T(8,128)(2,1)}), bf16[16,64,512]{2,1,0:T(8,128)(2,1)S(1)}, u32[]{:S(2)}, u32[]{:S(2)}) async-start(bf16[16,64,512]{2,1,0:T(8,128)(2,1)} %bitcast.6), calls=%async_computation | async-start | bytes 2097152 | tf_op jit(solution)/shard_map/all_to_all | solution.py:160
  15.5 0.0 copy-done.3
  15.5 0.5 collective-permute-start.1
  16.2 0.1 broadcast_multiply_fusion
  16.2 0.0 copy-done.1
  16.3 0.1 bitcast_reduce_fusion
  16.4 0.0 copy-done.4
  16.5 0.1 constant_dynamic-slice_fusion.5
  16.5 0.1 add_add_fusion
  16.6 1.2 compare_reduce_fusion
  17.9 0.2 convert_reduce_fusion.1
  18.1 0.1 copy.21
  18.2 0.1 copy.22
  18.3 0.2 convert_reduce_fusion
  18.5 0.1 select_reduce_fusion
  18.7 0.1 copy.25.code_ref
  18.8 0.1 pad_add_fusion.1.base_ref
  18.9 3.5 %fusion = bf16[2048,128]{1,0:T(8,128)(2,1)S(1)} fusion(bf16[2048,1024]{1,0:T(8,128)(2,1)} %param.8, bf16[1024,64]{1,0:T(8,128)(2,1)S(1)} %get-tuple-element.24, bf16[1024,64]{1,0:T(8,128)(2,1)S(1)} %get-tuple-element.33), kind=kOutput, calls=%fused_computation.2 | convolution fusion | flops 537657344 | bytes 4980736 | tf_op jit(solution)/shard_map/dot_general | solution.py:167
  22.4 0.0 collective-permute-done
  22.4 1.1 pad_maximum_fusion.2.kv_ref
  23.5 7.4 %all-to-all-done.q_ref = bf16[16,64,512]{2,1,0:T(8,128)(2,1)S(1)} async-done(((bf16[16,64,512]{2,1,0:T(8,128)(2,1)}), bf16[16,64,512]{2,1,0:T(8,128)(2,1)S(1)}, u32[]{:S(2)}, u32[]{:S(2)}) %all-to-all-start) | async-done | bytes 1048608 | tf_op jit(solution)/shard_map/all_to_all | solution.py:160
  31.0 79.0 %shard_map.82 = bf16[17,72,512]{2,1,0:T(8,128)(2,1)S(1)} custom-call(s32[64]{0:T(128)S(1)} %fusion.17.n_ref, s32[64,32]{1,0:T(8,128)S(1)} %copy.25.code_ref, s32[2]{0:T(128)S(1)} %pad_add_fusion.1.base_ref, bf16[16,64,512]{2,1,0:T(8,128)(2,1)S(1)} %all-to-all-done.q_ref, s32[64,128]{1,0:T(8,128)S(1)} %bitcast.65, bf16[4096,128]{1,0:T(8,128)(2,1)S(1)} %pad_maximum_fusion.2.kv_ref), custom_call_target="tpu_custom_call" | custom-call | flops 10000000000 | bytes 4194304 | tf_op jit(solution)/shard_map/pallas_call | solution.py:102
  110.0 1.1 slice.30
  111.1 5.8 %all-to-all-start.1 = ((bf16[16,72,512]{2,1,0:T(8,128)(2,1)}), bf16[16,72,512]{2,1,0:T(8,128)(2,1)S(1)}, u32[]{:S(2)}, u32[]{:S(2)}) async-start(bf16[16,72,512]{2,1,0:T(8,128)(2,1)} %slice.30), calls=%async_computation.1 | async-start | bytes 2359296 | tf_op jit(solution)/shard_map/all_to_all | solution.py:175
  116.9 0.0 collective-permute-done.1
  116.9 1.0 select_bitcast_fusion.1
  117.9 0.1 fusion.20
  118.0 1.7 %collective-permute-start.2 = (bf16[2,128,1024]{2,1,0:T(8,128)(2,1)S(1)}, bf16[2,128,1024]{2,1,0:T(8,128)(2,1)}, u32[]{:S(2)}, u32[]{:S(2)}) collective-permute-start(bf16[2,128,1024]{2,1,0:T(8,128)(2,1)S(1)} %get-tuple-element.19), channel_id=1, source_target_pairs={{0,1},{1,2},{2,3},{3,0},{4,5},{5,6},{6,7},{7,4},{8,9},{9,10},{10,1... | collective-permute-start | bytes 1572872 | tf_op jit(solution)/shard_map/ppermute | solution.py:141
  119.7 3.3 %collective-permute-start.3 = (bf16[2,128,1024]{2,1,0:T(8,128)(2,1)S(1)}, bf16[2,128,1024]{2,1,0:T(8,128)(2,1)}, u32[]{:S(2)}, u32[]{:S(2)}) collective-permute-start(bf16[2,128,1024]{2,1,0:T(8,128)(2,1)S(1)} %get-tuple-element.19), channel_id=1, source_target_pairs={{0,2},{1,3},{2,0},{3,1},{4,6},{5,7},{6,4},{7,5},{8,10},{9,11},{10,... | collective-permute-start | bytes 1572872 | tf_op jit(solution)/shard_map/ppermute | solution.py:141
  123.0 0.7 collective-permute-start.4
  123.7 10.2 %collective-permute-done.2 = bf16[2,128,1024]{2,1,0:T(8,128)(2,1)} collective-permute-done((bf16[2,128,1024]{2,1,0:T(8,128)(2,1)S(1)}, bf16[2,128,1024]{2,1,0:T(8,128)(2,1)}, u32[]{:S(2)}, u32[]{:S(2)}) %collective-permute-start.2) | collective-permute-done | bytes 524320 | tf_op jit(solution)/shard_map/ppermute | solution.py:141
  133.9 12.1 %collective-permute-done.3 = bf16[2,128,1024]{2,1,0:T(8,128)(2,1)} collective-permute-done((bf16[2,128,1024]{2,1,0:T(8,128)(2,1)S(1)}, bf16[2,128,1024]{2,1,0:T(8,128)(2,1)}, u32[]{:S(2)}, u32[]{:S(2)}) %collective-permute-start.3) | collective-permute-done | bytes 524320 | tf_op jit(solution)/shard_map/ppermute | solution.py:141
  146.0 0.0 collective-permute-done.4
  146.0 1.6 %pad_maximum_fusion = bf16[4,2,128,1024]{3,2,1,0:T(8,128)(2,1)S(1)} fusion(bf16[1,2,128,1024]{3,2,1,0:T(8,128)(2,1)} %bitcast.22, bf16[1,2,128,1024]{3,2,1,0:T(8,128)(2,1)} %bitcast.21, bf16[1,2,128,1024]{3,2,1,0:T(8,128)(2,1)} %bitcast.20, bf16[1,2,128,1024]{3,2,1,0:T(8,128)(2,1)S(1)} %get-tuple-element.18), kind=kLoop, calls=%fused_computation.6 | loop fusion | flops 3145728 | bytes 4194304 | tf_op jit(solution)/shard_map/stack | solution.py:144
  147.7 1.4 dynamic-slice_bitcast_fusion.3
  149.0 0.0 all-to-all-done.1
  149.0 0.3 bitcast_convert_fusion
  149.3 0.1 slice_add_fusion
  149.5 0.1 fusion.14
  149.5 0.3 fusion.2
  149.8 0.8 copy.27
  150.6 4.0 %all-to-all-start.2 = ((bf16[8,64,128]{2,1,0:T(8,128)(2,1)}), bf16[8,64,128]{2,1,0:T(8,128)(2,1)S(1)}, u32[]{:S(2)}, u32[]{:S(2)}) async-start(bf16[8,64,128]{2,1,0:T(8,128)(2,1)} %bitcast.15), calls=%async_computation.2 | async-start | bytes 262144 | tf_op jit(solution)/shard_map/all_to_all | solution.py:184
  154.5 1.8 %pad_maximum_fusion.1 = bf16[2,4,128,1024]{3,2,1,0:T(8,128)(2,1)S(1)} fusion(bf16[2,1,128,1024]{3,2,1,0:T(8,128)(2,1)} %get-tuple-element.15, bf16[2,1,128,1024]{3,2,1,0:T(8,128)(2,1)} %get-tuple-element.16, bf16[2,1,128,1024]{3,2,1,0:T(8,128)(2,1)} %get-tuple-element.17, bf16[2,1,128,1024]{3,2,1,0:T(8,128)(2,1)} %get-tuple-element.14), kind=kLoop, calls=%fused_computation.7 | loop fusion | flops 3145728 | bytes 4194304 | tf_op jit(solution)/shard_map/stack | solution.py:145
  156.3 3.7 %all-to-all-done.2 = bf16[8,64,128]{2,1,0:T(8,128)(2,1)S(1)} async-done(((bf16[8,64,128]{2,1,0:T(8,128)(2,1)}), bf16[8,64,128]{2,1,0:T(8,128)(2,1)S(1)}, u32[]{:S(2)}, u32[]{:S(2)}) %all-to-all-start.2) | async-done | bytes 131104 | tf_op jit(solution)/shard_map/all_to_all | solution.py:184
  160.0 1.1 convolution_convert_fusion.2
  (5 shorter events, 0.1 us)
Async XLA Ops:
  0.0 6.7 %copy-start = (bf16[512,1024]{1,0:T(8,128)(2,1)S(1)}, bf16[512,1024]{1,0:T(8,128)(2,1)}, u32[]{:S(2)}) copy-start(bf16[512,1024]{1,0:T(8,128)(2,1)} %param.9) | copy-start | bytes 3145732
  1.6 5.1 %copy-start.2 = (bf16[1024,128]{1,0:T(8,128)(2,1)S(1)}, bf16[1024,128]{1,0:T(8,128)(2,1)}, u32[]{:S(2)}) copy-start(bf16[1024,128]{1,0:T(8,128)(2,1)} %param.10) | copy-start | bytes 786436
  6.0 9.5 %copy-start.3 = (bf16[128,1024]{1,0:T(8,128)(2,1)S(1)}, bf16[128,1024]{1,0:T(8,128)(2,1)}, u32[]{:S(2)}) copy-start(bf16[128,1024]{1,0:T(8,128)(2,1)} %param.13) | copy-start | bytes 786436
  6.0 10.2 %copy-start.1 = (s32[8192]{0:T(1024)S(1)}, s32[8192]{0:T(1024)}, u32[]{:S(2)}) copy-start(s32[8192]{0:T(1024)} %param.14) | copy-start | bytes 98308
  6.0 10.4 %copy-start.4 = (s32[64,256]{1,0:T(8,128)S(1)}, s32[64,256]{1,0:T(8,128)}, u32[]{:S(2)}) copy-start(s32[64,256]{1,0:T(8,128)} %param.15) | copy-start | bytes 196612
  6.0 16.4 %collective-permute-start = (bf16[2048,128]{1,0:T(8,128)(2,1)}, bf16[2048,128]{1,0:T(8,128)(2,1)}, u32[]{:S(2)}, u32[]{:S(2)}) collective-permute-start(bf16[2048,128]{1,0:T(8,128)(2,1)} %fusion.1), channel_id=1, source_target_pairs={{0,8},{8,0},{16,24},{24,16},{32,40},{40,32},{48,56},{56,48},{64,72... | collective-permute-start | bytes 1572872 | tf_op jit(solution)/shard_map/ppermute | solution.py:169
  8.3 22.7 %all-to-all-start = ((bf16[16,64,512]{2,1,0:T(8,128)(2,1)}), bf16[16,64,512]{2,1,0:T(8,128)(2,1)S(1)}, u32[]{:S(2)}, u32[]{:S(2)}) async-start(bf16[16,64,512]{2,1,0:T(8,128)(2,1)} %bitcast.6), calls=%async_computation | async-start | bytes 2097152 | tf_op jit(solution)/shard_map/all_to_all | solution.py:160
  15.5 101.4 %collective-permute-start.1 = (bf16[128,1024]{1,0:T(8,128)(2,1)S(1)}, bf16[128,1024]{1,0:T(8,128)(2,1)}, u32[]{:S(2)}, u32[]{:S(2)}) collective-permute-start(bf16[128,1024]{1,0:T(8,128)(2,1)S(1)} %copy-done.3), channel_id=1, source_target_pairs={{0,4},{1,5},{2,6},{3,7},{4,0},{5,1},{6,2},{7,3},{8,12},{9,13},{10,... | collective-permute-start | bytes 786440 | tf_op jit(solution)/shard_map/ppermute | solution.py:137
  111.1 38.0 %all-to-all-start.1 = ((bf16[16,72,512]{2,1,0:T(8,128)(2,1)}), bf16[16,72,512]{2,1,0:T(8,128)(2,1)S(1)}, u32[]{:S(2)}, u32[]{:S(2)}) async-start(bf16[16,72,512]{2,1,0:T(8,128)(2,1)} %slice.30), calls=%async_computation.1 | async-start | bytes 2359296 | tf_op jit(solution)/shard_map/all_to_all | solution.py:175
  118.0 15.9 %collective-permute-start.2 = (bf16[2,128,1024]{2,1,0:T(8,128)(2,1)S(1)}, bf16[2,128,1024]{2,1,0:T(8,128)(2,1)}, u32[]{:S(2)}, u32[]{:S(2)}) collective-permute-start(bf16[2,128,1024]{2,1,0:T(8,128)(2,1)S(1)} %get-tuple-element.19), channel_id=1, source_target_pairs={{0,1},{1,2},{2,3},{3,0},{4,5},{5,6},{6,7},{7,4},{8,9},{9,10},{10,1... | collective-permute-start | bytes 1572872 | tf_op jit(solution)/shard_map/ppermute | solution.py:141
  119.7 26.3 %collective-permute-start.3 = (bf16[2,128,1024]{2,1,0:T(8,128)(2,1)S(1)}, bf16[2,128,1024]{2,1,0:T(8,128)(2,1)}, u32[]{:S(2)}, u32[]{:S(2)}) collective-permute-start(bf16[2,128,1024]{2,1,0:T(8,128)(2,1)S(1)} %get-tuple-element.19), channel_id=1, source_target_pairs={{0,2},{1,3},{2,0},{3,1},{4,6},{5,7},{6,4},{7,5},{8,10},{9,11},{10,... | collective-permute-start | bytes 1572872 | tf_op jit(solution)/shard_map/ppermute | solution.py:141
  123.0 23.0 %collective-permute-start.4 = (bf16[2,128,1024]{2,1,0:T(8,128)(2,1)S(1)}, bf16[2,128,1024]{2,1,0:T(8,128)(2,1)}, u32[]{:S(2)}, u32[]{:S(2)}) collective-permute-start(bf16[2,128,1024]{2,1,0:T(8,128)(2,1)S(1)} %get-tuple-element.19), channel_id=1, source_target_pairs={{0,3},{1,0},{2,1},{3,2},{4,7},{5,4},{6,5},{7,6},{8,11},{9,8},{10,9... | collective-permute-start | bytes 1572872 | tf_op jit(solution)/shard_map/ppermute | solution.py:141
  150.6 9.4 %all-to-all-start.2 = ((bf16[8,64,128]{2,1,0:T(8,128)(2,1)}), bf16[8,64,128]{2,1,0:T(8,128)(2,1)S(1)}, u32[]{:S(2)}, u32[]{:S(2)}) async-start(bf16[8,64,128]{2,1,0:T(8,128)(2,1)} %bitcast.15), calls=%async_computation.2 | async-start | bytes 262144 | tf_op jit(solution)/shard_map/all_to_all | solution.py:184

commit v2 on v0

v2 whole, which is shorter than its diff:
```python
import functools

import jax
import jax.numpy as jnp
from jax import lax
from jax.experimental import pallas as pl
from jax.experimental.pallas import tpu as pltpu
from jax.sharding import PartitionSpec as P

HS = 64
BLOCK = 128
TILES = 4
SLOTS = 4
KEY_BLOCKS = 32
ACC_ROWS = 72
LOG2E = 1.4426950408889634
SAFE_SCORE = 60.0
masked_score = -1e30
lowest_max = -1e29
SMEM = pl.BlockSpec(memory_space=pltpu.SMEM)
VMEM = pl.BlockSpec(memory_space=pltpu.VMEM)


def project_kernel(core_ref, x_ref, wk_ref, wv_ref, own_ref, other_ref, w_own, w_other):
    @pl.when(pl.program_id(0) == 0)
    def _():
        first = core_ref[0] == 0
        wk, wv = wk_ref[...], wv_ref[...]
        head_0 = jnp.concatenate([wk[:, :HS], wv[:, :HS]], 1)
        head_1 = jnp.concatenate([wk[:, HS:], wv[:, HS:]], 1)
        w_own[...] = jnp.where(first, head_0, head_1)
        w_other[...] = jnp.where(first, head_1, head_0)

    x = x_ref[...]
    own_ref[...] = jnp.dot(x, w_own[...], preferred_element_type=jnp.float32).astype(jnp.bfloat16)
    other_ref[...] = jnp.dot(x, w_other[...], preferred_element_type=jnp.float32).astype(jnp.bfloat16)


def project(core, inputs, w_key, w_value):
    keys, width = inputs.shape
    rows = 256
    out = jax.ShapeDtypeStruct((keys, 2 * HS), jnp.bfloat16)
    tile = pl.BlockSpec((rows, 2 * HS), lambda i: (i, 0))
    whole = pl.BlockSpec((width, 2 * HS), lambda i: (0, 0))
    return pl.pallas_call(
        project_kernel,
        grid=(keys // rows,),
        in_specs=[SMEM, pl.BlockSpec((rows, width), lambda i: (i, 0)), whole, whole],
        out_specs=[tile, tile],
        out_shape=[out, out],
        scratch_shapes=[pltpu.VMEM((width, 2 * HS), jnp.bfloat16)] * 2,
        compiler_params=pltpu.CompilerParams(vmem_limit_bytes=32 * 2**20),
        cost_estimate=pl.CostEstimate(flops=2 * keys * width * 4 * HS, bytes_accessed=5 * 2**20, transcendentals=0),
    )(core, inputs, w_key, w_value)


def prepare_kernel(own_ref, partner_ref, kv_ref, vt_ref, norm_ref):
    most = None
    for t in range(KEY_BLOCKS):
        source, at = (own_ref, t) if t < KEY_BLOCKS // 2 else (partner_ref, t - KEY_BLOCKS // 2)
        tile = source[at * BLOCK : (at + 1) * BLOCK, :]
        kv_ref[t * BLOCK : (t + 1) * BLOCK, :] = tile
        turned = tile.T
        vt_ref[:HS, t * BLOCK : (t + 1) * BLOCK] = turned[HS:, :]
        k = turned[:HS, :].astype(jnp.float32)
        squares = jnp.sum(k * k, axis=0, keepdims=True)
        most = squares if most is None else jnp.maximum(most, squares)
    vt_ref[HS:, :] = jnp.ones((ACC_ROWS - HS, KEY_BLOCKS * BLOCK), jnp.bfloat16)
    norm_ref[0] = jnp.max(most)


def prepare(own, partner):
    keys = 2 * own.shape[0]
    return pl.pallas_call(
        prepare_kernel,
        in_specs=[VMEM, VMEM],
        out_specs=[VMEM, VMEM, SMEM],
        out_shape=[
            jax.ShapeDtypeStruct((keys, 2 * HS), jnp.bfloat16),
            jax.ShapeDtypeStruct((ACC_ROWS, keys), jnp.bfloat16),
            jax.ShapeDtypeStruct((1,), jnp.float32),
        ],
        compiler_params=pltpu.CompilerParams(vmem_limit_bytes=32 * 2**20),
    )(own, partner)


def attention_kernel(chips, count_ref, code_ref, base_ref, shard_ref, norm_ref, pos_ref, kv_ref, vt_ref, *rest):
    q_refs, o_refs = rest[:chips], rest[chips : 2 * chips]
    q_all, p_a, p_b, s_all, acc = rest[2 * chips :]
    blocks = 8 * chips
    own_base = base_ref[0]
    partner_base = base_ref[1]
    iota = lax.broadcasted_iota(jnp.int32, (BLOCK, BLOCK), 0)
    iota_half = iota.astype(jnp.float32).astype(jnp.bfloat16)

    most = None
    for i in range(chips):
        for j in range(2):
            q = q_refs[i][j]
            q_all[2 * i + j] = q
            q = q.astype(jnp.float32)
            squares = jnp.sum(q * q, axis=0, keepdims=True)
            most = squares if most is None else jnp.maximum(most, squares)
    safe = jnp.max(most) * norm_ref[0] <= SAFE_SCORE * SAFE_SCORE

    def clamp(r):
        return jnp.minimum(r, blocks - 1)

    def whole_block(r):
        return shard_ref[lax.div(r, 4)] * 4 + lax.rem(r, 4)

    def offset(i):
        return pl.multiple_of(i * BLOCK, BLOCK)

    def query(r):
        q = q_all[lax.div(r, 4), :, pl.ds(offset(lax.rem(r, 4)), BLOCK)]
        return jnp.concatenate([q, jnp.zeros_like(q)], 0)

    def key_blocks(row, c):
        return [jnp.bitwise_and(code_ref[row, c * TILES + t], KEY_BLOCKS - 1) for t in range(TILES)]

    def products(row, r, c):
        keys = jnp.concatenate([kv_ref[pl.ds(offset(k), BLOCK), :] for k in key_blocks(row, c)], 0)
        return jnp.dot(keys, query(r), preferred_element_type=jnp.float32)

    def values(row, c):
        return jnp.concatenate([vt_ref[:, pl.ds(offset(k), BLOCK)] for k in key_blocks(row, c)], 1)

    def last_key(row, c, t, pos, real):
        code = code_ref[row, c * TILES + t]
        k = jnp.bitwise_and(code, KEY_BLOCKS - 1)
        half = KEY_BLOCKS // 2
        base = jnp.where(k < half, own_base, partner_base - half * BLOCK) + k * BLOCK
        reach = jnp.where(jnp.bitwise_and(code, KEY_BLOCKS) > 0, 1 << 30, BLOCK)
        reach = jnp.where(jnp.logical_and(real, code >= 2 * KEY_BLOCKS), reach, -(1 << 30))
        ahead = pos - base
        return jnp.where(ahead < reach, jnp.minimum(ahead, BLOCK - 1), -1)

    def store(r, a, top):
        total = a[HS : HS + 1]
        low = total - total.astype(jnp.bfloat16).astype(jnp.float32)
        out = jnp.concatenate([a[: HS + 1], top, low, a[HS + 3 :]], 0).astype(jnp.bfloat16)
        return out

    def put(i, rr, out):
        o_refs[i][lax.div(rr, 4), :, pl.ds(offset(lax.rem(rr, 4)), BLOCK)] = out

    def advance(r, c):
        last = c + 1 >= count_ref[whole_block(clamp(r))]
        return jnp.where(last, jnp.minimum(r + 1, blocks), r), jnp.where(last, 0, c + 1)

    def step_slots(r, c):
        slots = []
        for _ in range(SLOTS):
            slots.append((r, c))
            r, c = advance(r, c)
        return slots, r, c

    @pl.when(safe)
    def _():
        acc[...] = jnp.zeros_like(acc)

        def weigh(p_ref, slots):
            for g, (r, c) in enumerate(slots):
                rr = clamp(r)
                row = whole_block(rr)
                s = products(row, rr, c)
                pos = pos_ref[pl.ds(row, 1), :]
                for t in range(TILES):
                    p = jnp.exp2(s[t * BLOCK : (t + 1) * BLOCK] * LOG2E).astype(jnp.bfloat16)
                    last = last_key(row, c, t, pos, r < blocks).astype(jnp.float32).astype(jnp.bfloat16)
                    at = (g * TILES + t) * BLOCK
                    p_ref[at : at + BLOCK, :] = jnp.where(iota_half <= last, p, jnp.zeros_like(p))

        def add(p_ref, slots):
            for g, (r, c) in enumerate(slots):
                v = values(whole_block(clamp(r)), c)
                at = g * TILES * BLOCK
                acc[r] += jnp.dot(v, p_ref[at : at + TILES * BLOCK, :], preferred_element_type=jnp.float32)

        slots_0, r0, c0 = step_slots(jnp.int32(0), jnp.int32(0))
        weigh(p_a, slots_0)

        def two_steps(_, state):
            r, c, r1, c1 = state
            slots, _, _ = step_slots(r, c)
            slots_1, r2, c2 = step_slots(r1, c1)
            weigh(p_b, slots_1)
            add(p_a, slots)
            slots_2, r3, c3 = step_slots(r2, c2)
            weigh(p_a, slots_2)
            add(p_b, slots_1)
            return r2, c2, r3, c3

        items = lax.fori_loop(0, blocks, lambda r, n: n + count_ref[whole_block(r)], jnp.int32(0))
        steps = lax.div(items + (2 * SLOTS - 1), 2 * SLOTS)
        lax.fori_loop(0, steps, two_steps, (jnp.int32(0), jnp.int32(0), r0, c0))

        for i in range(chips):
            def finish(rr, _, i=i):
                a = acc[i * 8 + rr]
                put(i, rr, store(rr, a, jnp.where(a[HS : HS + 1] > 0, 0.0, lowest_max)))
                return 0

            lax.fori_loop(0, 8, finish, 0)

    @pl.when(jnp.logical_not(safe))
    def _():
        for i in range(chips):
            def one_block(rr, _, i=i):
                r = i * 8 + rr
                row = whole_block(r)
                pos = pos_ref[pl.ds(row, 1), :]
                acc[0] = jnp.zeros((ACC_ROWS, BLOCK), jnp.float32)

                def one_slot(c, top):
                    s = products(row, r, c)
                    best = top
                    for t in range(TILES):
                        tile = s[t * BLOCK : (t + 1) * BLOCK]
                        tile = jnp.where(iota <= last_key(row, c, t, pos, True), tile, masked_score)
                        s_all[t * BLOCK : (t + 1) * BLOCK, :] = tile
                        best = jnp.maximum(best, jnp.max(tile, 0, keepdims=True))
                    best = best.astype(jnp.bfloat16).astype(jnp.float32)
                    p = jnp.exp2((s_all[...] - best) * LOG2E).astype(jnp.bfloat16)
                    shrink = jnp.exp2((top - best) * LOG2E)
                    acc[0] = acc[0] * shrink + jnp.dot(values(row, c), p, preferred_element_type=jnp.float32)
                    return best

                start = jnp.full((1, BLOCK), lowest_max, jnp.bfloat16).astype(jnp.float32)
                top = lax.fori_loop(0, count_ref[row], one_slot, start)
                put(i, rr, store(rr, acc[0], top))
                return 0

            lax.fori_loop(0, 8, one_block, 0)


def attend(counts, codes, bases, shards, norm, spots, kv, vt, queries):
    chips = len(queries)
    out = jax.ShapeDtypeStruct((2, ACC_ROWS, queries[0].shape[2]), jnp.bfloat16)
    return pl.pallas_call(
        functools.partial(attention_kernel, chips),
        in_specs=[SMEM] * 5 + [VMEM] * (3 + chips),
        out_specs=[VMEM] * chips,
        out_shape=[out] * chips,
        scratch_shapes=[
            pltpu.VMEM((2 * chips, HS, queries[0].shape[2]), jnp.bfloat16),
            pltpu.VMEM((SLOTS * TILES * BLOCK, BLOCK), jnp.bfloat16),
            pltpu.VMEM((SLOTS * TILES * BLOCK, BLOCK), jnp.bfloat16),
            pltpu.VMEM((TILES * BLOCK, BLOCK), jnp.float32),
            pltpu.VMEM((8 * chips + 1, ACC_ROWS, BLOCK), jnp.float32),
        ],
        compiler_params=pltpu.CompilerParams(vmem_limit_bytes=32 * 2**20),
        cost_estimate=pl.CostEstimate(
            flops=chips * 6 * 10**9, bytes_accessed=4 * 2**20, transcendentals=chips * 2**20
        ),
    )(counts, codes, bases, shards, norm, spots, kv, vt, *queries)


def combine_kernel(*refs):
    parts, out_ref = refs[:-1], refs[-1]
    for j in range(2):
        tops = [p[j, HS + 1 : HS + 2, :].astype(jnp.float32) for p in parts]
        top = functools.reduce(jnp.maximum, tops)
        scales = [jnp.exp(t - top) for t in tops]
        total = sum(
            (p[j, HS : HS + 1, :].astype(jnp.float32) + p[j, HS + 2 : HS + 3, :].astype(jnp.float32)) * scale
            for p, scale in zip(parts, scales)
        )
        summed = sum(p[j, :HS, :].astype(jnp.float32) * scale for p, scale in zip(parts, scales))
        out_ref[j] = (summed / total).astype(jnp.bfloat16)


def combine(parts):
    return pl.pallas_call(
        combine_kernel,
        in_specs=[VMEM] * len(parts),
        out_specs=VMEM,
        out_shape=jax.ShapeDtypeStruct((2, HS, parts[0].shape[2]), jnp.bfloat16),
        compiler_params=pltpu.CompilerParams(vmem_limit_bytes=32 * 2**20),
    )(*parts)


def work_list(spots, block_mask, first_own, first_partner):
    half = KEY_BLOCKS // 2
    index = jnp.arange(KEY_BLOCKS, dtype=jnp.int32)
    key_blocks = jnp.where(index < half, first_own, first_partner - half) + index
    listed = jnp.concatenate(
        [lax.dynamic_slice_in_dim(block_mask, first, half, 1) for first in (first_own, first_partner)], 1
    ) == 1
    own = jnp.any((spots // BLOCK)[:, :, None] == key_blocks[None, None, :], axis=1)
    reached = (key_blocks * BLOCK)[None, :] <= jnp.max(spots, axis=1)[:, None]
    active = (listed & reached) | own
    earlier = index[None, :] < index[:, None]
    place = jnp.sum(active[:, None, :] & earlier[None], axis=2, dtype=jnp.int32)
    value = index[None, :] + KEY_BLOCKS * listed.astype(jnp.int32) + 2 * KEY_BLOCKS
    chosen = active[:, None, :] & (place[:, None, :] == index[None, :, None])
    codes = jnp.sum(jnp.where(chosen, value[:, None, :], 0), axis=2, dtype=jnp.int32)
    count = jnp.sum(active, axis=1, dtype=jnp.int32)
    return jnp.maximum((count + TILES - 1) // TILES, 1), codes


def shifted(x_by, y_by):
    return [(s, ((s // 4 + x_by) % 4) * 4 + (s % 4 ^ 2 * y_by)) for s in range(16)]


def back(route):
    return [(b, a) for a, b in route]


CALLS = (((0, 1), (1, 0)), ((3, 0), (1, 1)), ((3, 1), (2, 0)), ((2, 1),), ((0, 0),))
SWAP = [(i, i ^ 1) for i in range(16)]


def body(inputs, latents, w_query, w_key, w_value, w_out, positions, block_mask):
    s = lax.axis_index("seq")
    core = s % 2
    me = lax.axis_index("grp")

    queries = lax.dot_general(
        w_query, latents, (((0,), (1,)), ((), ())), preferred_element_type=jnp.float32
    ).astype(jnp.bfloat16) * jnp.bfloat16(HS ** -0.5)
    first, second = queries[:HS], queries[HS:]
    mine = jnp.where(core == 0, first, second)
    theirs = jnp.where(core == 0, second, first)
    q_chip = jnp.stack([mine, lax.ppermute(theirs, "seq", SWAP)])
    arrived = {
        step: q_chip if step == (0, 0) else lax.ppermute(q_chip, "seq", shifted(*step))
        for call in CALLS
        for step in call
    }

    w_other = lax.ppermute(w_out, "grp", [(g, g ^ 4) for g in range(8)])
    w_pair = jnp.concatenate([w_out, w_other], 0)
    w_turns = [w_pair] + [
        lax.ppermute(w_pair, "grp", [(g, (g & 4) | ((g + k) & 3)) for g in range(8)]) for k in (1, 2, 3)
    ]

    kv_own, kv_other = project(core[None], inputs, w_key, w_value)
    kv, vt, norm = prepare(kv_own, lax.ppermute(kv_other, "seq", SWAP))

    per_device = inputs.shape[0] // BLOCK
    spots = positions.reshape(-1, BLOCK)
    counts, codes = work_list(spots, block_mask, s * per_device, (s ^ 1) * per_device)
    bases = jnp.stack([s, s ^ 1]) * inputs.shape[0]

    parts = []
    for n, call in enumerate(CALLS):
        came_from = [(((s // 4 + 4 - x_by) % 4) * 4 + (s % 4 ^ 2 * y_by)) for x_by, y_by in call]
        shards = jnp.stack([shard for c in came_from for shard in (c, c ^ 1)])
        blocks = [arrived[step] for step in call]
        if 1 <= n <= 3:
            blocks[0], w_turns[n] = lax.optimization_barrier((blocks[0], w_turns[n]))
        done = attend(counts, codes, bases, shards, norm, spots, kv, vt, blocks)
        for step, part in zip(call, done):
            parts.append(part if step == (0, 0) else lax.ppermute(part, "seq", back(shifted(*step))))

    attention = combine(parts)
    rows = attention.shape[2]
    swapped = lax.ppermute(attention[1], "seq", SWAP)
    attention = jnp.where(
        core == 0, jnp.concatenate([attention[0], swapped], 0), jnp.concatenate([swapped, attention[0]], 0)
    )
    attention = attention.T.reshape(8, rows // 8, 2 * HS)
    attention = lax.all_to_all(attention, "grp", 0, 0)
    result = 0.0
    for k, w in enumerate(w_turns):
        group = (me & 4) | ((me - k) & 3)
        heads = jnp.concatenate([attention[group], attention[group ^ 4]], 1)
        result += jnp.dot(heads, w, preferred_element_type=jnp.float32)
    return result.astype(jnp.bfloat16)


def solution(mesh):
    return jax.shard_map(
        body,
        mesh=mesh,
        in_specs=(
            P("seq", None),
            P("seq", None),
            P(None, "grp"),
            P(None, "grp"),
            P(None, "grp"),
            P("grp", None),
            P(),
            P(),
        ),
        out_specs=P(("seq", "grp"), None),
        check_vma=False,
    )
```

time: 441 us -> 235 us (0.53)
  Pallas kernels: 0 us -> 169 us
  other arithmetic: 86.3 us -> 2.53 us
  starting transfers between devices: 124 us -> 42.7 us
  matrix products: 77.1 us -> 2.92 us
  local copies, waits for them, and re-layouts: 70.6 us -> 8.78 us
  waiting for transfers between devices: 61.4 us -> 6.28 us
  between operations: 13.5 us -> 0.39 us
    pallas_call x0 -> x8, Pallas kernels: none -> 169 us  [the longest x5 164 us: attend(): pl.pallas_call(functools.partial(attention_kernel, chips), in_specs=[SMEM...]
    ppermute x64 -> x21, starting transfers between devices: 124 us -> 39.3 us  [the longest x7 13.5 us: body(): lax.ppermute(part, 'seq', back(shifted(*step)))]
    dot_general x36 -> x5, matrix products: 77.1 us -> 2.92 us  [the longest x4 1.49 us: body(): result += jnp.dot(heads, w, preferred_element_type=jnp.float32)]
    broadcast_in_dim x33 -> x0, local copies, waits for them, and re-layouts: 55.9 us -> none  [the longest x16 55.5 us: allowed_pairs(): jnp.repeat(jnp.repeat(mask_rows, BLOCK, axis=0), BLOCK, axis=1) == 1]
    reduce_scatter x1 -> x0, waiting for transfers between devices: 44.9 us -> none  [body(): lax.psum_scatter(jnp.dot(attention, w_out, preferred_element_type=jnp.flo...]
    reduce_sum x16 -> x3, other arithmetic: 44.7 us -> 0.54 us  [the longest x1 0.22 us: work_list(): place = jnp.sum(active[:, None, :] & earlier[None], axis=2, dtype=jnp.int32)]
    and x16 -> x0, other arithmetic: 28.3 us -> none  [allowed_pairs(): return causal & (listed | own_block)]
    ppermute x64 -> x21, waiting for transfers between devices: 16.5 us -> 0.95 us  [the longest x1 0.9 us: body(): swapped = lax.ppermute(attention[1], 'seq', SWAP)]
  transfers between devices with their start and end apart: 65 -> 22, of which waited for: 32 -> 2; matrix products, arithmetic and copies ran while one was open for 1% -> 2% of each run, Pallas kernels for 0% -> 73%
where the time goes in v2:
time: 235 us; the launch traced here: 233 us
  Pallas kernels  169 us (72%)
  starting transfers between devices  42.7 us (18%)
  local copies, waits for them, and re-layouts  8.78 us (4%)
  waiting for transfers between devices  6.28 us (3%)
  matrix products  2.92 us (1%)
  other arithmetic  2.53 us (1%)
    pallas_call x5, Pallas kernels, attend(): pl.pallas_call(functools.partial(attention_kernel, chips), in_specs=[SMEM...  164 us
    ppermute x7, starting transfers between devices, body(): lax.ppermute(part, 'seq', back(shifted(*step)))  13.5 us
    ppermute x7, starting transfers between devices, body(): lax.ppermute(q_chip, 'seq', shifted(*step))  13.5 us
    unnamed x17, local copies, waits for them, and re-layouts  6.01 us
    all_to_all x1, waiting for transfers between devices, body(): attention = lax.all_to_all(attention, 'grp', 0, 0)  5.32 us
    ppermute x3, starting transfers between devices, body(): lax.ppermute(w_pair, 'grp', [(g, g & 4 | g + k & 3) for g in range(8)])  5.07 us
    ppermute x1, starting transfers between devices, body(): swapped = lax.ppermute(attention[1], 'seq', SWAP)  4.73 us
  transfers between devices with their start and end apart: 22, of which 2 were waited for; matrix products, arithmetic and copies ran while one was open for 2% of the time, Pallas kernels for 73%

profile of v2, /device:TPU:3, one launch (start us, length us, event | category | flops | bytes accessed | tf_op | source)
XLA Modules:
  0.0 233.0 jit_solution(8403541813080118689)
XLA Ops:
  0.0 1.2 copy-done
  1.2 1.4 fusion.3
  2.7 0.8 collective-permute-start.1
  3.4 1.3 collective-permute-start.7
  4.8 2.2 copy-done.1
  6.9 0.9 copy-done.2
  7.9 0.9 copy-done.3
  8.8 3.7 %shard_map.82 = (bf16[2048,128]{1,0:T(8,128)(2,1)S(1)}, bf16[2048,128]{1,0:T(8,128)(2,1)S(1)}) custom-call(s32[1]{0:T(128)} %bitcast.7.core_ref, bf16[2048,1024]{1,0:T(8,128)(2,1)S(1)} %copy-done.1, bf16[1024,128]{1,0:T(8,128)(2,1)S(1)} %copy-done.2, bf16[1024,128]{1,0:T(8,128)(2,1)S(1)} %copy-done.3), custom_call_target="tpu_custom_call" | custom-call | flops 1073741824 | bytes 5242880 | tf_op jit(solution)/shard_map/pallas_call | solution.py:45
  12.5 0.4 collective-permute-start
  12.9 0.7 constant_dynamic-update-slice_fusion.1
  13.7 0.1 bitcast_reduce_fusion
  13.8 1.2 compare_reduce_fusion
  15.1 0.1 constant_dynamic-slice_fusion.1
  15.2 0.1 add_add_fusion
  15.2 0.2 convert_reduce_fusion.1
  15.4 0.1 copy.11
  15.5 0.1 copy.10
  15.6 0.2 convert_reduce_fusion
  15.8 0.1 select_reduce_fusion
  16.0 0.1 add_multiply_fusion.base_ref
  16.1 0.1 pad_add_fusion.3.shard_ref
  16.2 0.1 pad_add_fusion.4.shard_ref
  16.2 0.1 pad_add_fusion.shard_ref
  16.3 0.1 pad_add_fusion.1.shard_ref
  16.4 0.0 collective-permute-done.1
  16.4 2.7 %collective-permute-start.2 = (bf16[2,64,512]{2,1,0:T(8,128)(2,1)S(1)}, bf16[2,64,512]{2,1,0:T(8,128)(2,1)S(1)}, u32[]{:S(2)}, u32[]{:S(2)}) collective-permute-start(bf16[2,64,512]{2,1,0:T(8,128)(2,1)S(1)} %pad_maximum_fusion.rest_0_), channel_id=1, source_target_pairs={{0,16},{8,24},{16,0},{24,8},{32,48},{40,56},{48,32},{56,40},{64,80... | collective-permute-start | bytes 393224 | tf_op jit(solution)/shard_map/ppermute | solution.py:328
  19.1 1.2 collective-permute-start.3
  20.3 0.1 pad_add_fusion.2.shard_ref
  20.4 0.1 copy.12.code_ref
  20.5 0.9 collective-permute-start.17
  21.4 1.9 collective-permute-start.6
  23.3 1.7 constant_dynamic-update-slice_fusion
  25.0 0.0 collective-permute-done.partner_ref
  25.0 1.9 collective-permute-start.9
  26.9 1.0 shard_map.83
  27.9 0.0 collective-permute-done.2.rest_0_
  27.9 2.0 collective-permute-start.12
  30.0 1.6 collective-permute-start.8
  31.6 40.4 %shard_map.84 = (bf16[2,72,512]{2,1,0:T(8,128)(2,1)S(1)}, bf16[2,72,512]{2,1,0:T(8,128)(2,1)S(1)}) custom-call(s32[64]{0:T(128)S(1)} %fusion.24.count_ref, s32[64,32]{1,0:T(8,128)S(1)} %copy.12.code_ref, s32[2]{0:T(128)S(1)} %add_multiply_fusion.base_ref, s32[4]{0:T(128)S(1)} %pad_add_fusion.shard_ref, f32[1]{0:T(128)} %get-tuple-element.24.norm_ref, ...), custom_call_target="tpu_custom_call" | custom-call | flops 12000000000 | bytes 4194304 | tf_op jit(solution)/shard_map/pallas_call | solution.py:241
  72.0 2.8 %collective-permute-start.14 = (bf16[2,64,512]{2,1,0:T(8,128)(2,1)S(1)}, bf16[2,64,512]{2,1,0:T(8,128)(2,1)S(1)}, u32[]{:S(2)}, u32[]{:S(2)}) collective-permute-start(bf16[2,64,512]{2,1,0:T(8,128)(2,1)S(1)} %pad_maximum_fusion.rest_0_), channel_id=1, source_target_pairs={{0,64},{8,72},{16,80},{24,88},{32,96},{40,104},{48,112},{56,120},{... | collective-permute-start | bytes 393224 | tf_op jit(solution)/shard_map/ppermute | solution.py:328
  74.8 2.1 collective-permute-start.18
  76.9 0.0 collective-permute-done.9.rest_1_
  76.9 1.3 collective-permute-start.13
  78.2 41.1 %shard_map.85 = (bf16[2,72,512]{2,1,0:T(8,128)(2,1)S(1)}, bf16[2,72,512]{2,1,0:T(8,128)(2,1)S(1)}) custom-call(s32[64]{0:T(128)S(1)} %fusion.24.count_ref, s32[64,32]{1,0:T(8,128)S(1)} %copy.12.code_ref, s32[2]{0:T(128)S(1)} %add_multiply_fusion.base_ref, s32[4]{0:T(128)S(1)} %pad_add_fusion.1.shard_ref, f32[1]{0:T(128)} %get-tuple-element.24.norm_ref, ...), custom_call_target="tpu_custom_call" | custom-call | flops 12000000000 | bytes 4194304 | tf_op jit(solution)/shard_map/pallas_call | solution.py:241
  119.3 0.0 collective-permute-done.17.rest_0_
  119.3 2.0 collective-permute-start.4
  121.3 1.5 collective-permute-start.10
  122.8 1.9 collective-permute-start.11
  124.7 39.9 %shard_map.86 = (bf16[2,72,512]{2,1,0:T(8,128)(2,1)S(1)}, bf16[2,72,512]{2,1,0:T(8,128)(2,1)S(1)}) custom-call(s32[64]{0:T(128)S(1)} %fusion.24.count_ref, s32[64,32]{1,0:T(8,128)S(1)} %copy.12.code_ref, s32[2]{0:T(128)S(1)} %add_multiply_fusion.base_ref, s32[4]{0:T(128)S(1)} %pad_add_fusion.2.shard_ref, f32[1]{0:T(128)} %get-tuple-element.24.norm_ref, ...), custom_call_target="tpu_custom_call" | custom-call | flops 12000000000 | bytes 4194304 | tf_op jit(solution)/shard_map/pallas_call | solution.py:241
  164.7 3.6 %collective-permute-start.15 = (bf16[2,72,512]{2,1,0:T(8,128)(2,1)S(1)}, bf16[2,72,512]{2,1,0:T(8,128)(2,1)S(1)}, u32[]{:S(2)}, u32[]{:S(2)}) collective-permute-start(bf16[2,72,512]{2,1,0:T(8,128)(2,1)S(1)} %get-tuple-element.33), channel_id=1, source_target_pairs={{112,0},{120,8},{96,16},{104,24},{16,32},{24,40},{0,48},{8,56},{48... | collective-permute-start | bytes 442376 | tf_op jit(solution)/shard_map/ppermute | solution.py:356
  168.3 21.9 %shard_map.87 = bf16[2,72,512]{2,1,0:T(8,128)(2,1)S(1)} custom-call(s32[64]{0:T(128)S(1)} %fusion.24.count_ref, s32[64,32]{1,0:T(8,128)S(1)} %copy.12.code_ref, s32[2]{0:T(128)S(1)} %add_multiply_fusion.base_ref, s32[2]{0:T(128)S(1)} %pad_add_fusion.3.shard_ref, f32[1]{0:T(128)} %get-tuple-element.24.norm_ref, s32[64,128]{1,0:T(8,128)S(1)} %bitcast.57, ...), custom_call_target="tpu_custom_call" | custom-call | flops 6000000000 | bytes 4194304 | tf_op jit(solution)/shard_map/pallas_call | solution.py:241
  190.2 0.1 collective-permute-start.16
  190.3 4.4 %collective-permute-start.19 = (bf16[2,72,512]{2,1,0:T(8,128)(2,1)S(1)}, bf16[2,72,512]{2,1,0:T(8,128)(2,1)S(1)}, u32[]{:S(2)}, u32[]{:S(2)}) collective-permute-start(bf16[2,72,512]{2,1,0:T(8,128)(2,1)S(1)} %shard_map.87), channel_id=1, source_target_pairs={{80,0},{88,8},{64,16},{72,24},{112,32},{120,40},{96,48},{104,56},{... | collective-permute-start | bytes 442376 | tf_op jit(solution)/shard_map/ppermute | solution.py:356
  194.8 21.1 %shard_map.88.refs_7_ = bf16[2,72,512]{2,1,0:T(8,128)(2,1)S(1)} custom-call(s32[64]{0:T(128)S(1)} %fusion.24.count_ref, s32[64,32]{1,0:T(8,128)S(1)} %copy.12.code_ref, s32[2]{0:T(128)S(1)} %add_multiply_fusion.base_ref, s32[2]{0:T(128)S(1)} %pad_add_fusion.4.shard_ref, f32[1]{0:T(128)} %get-tuple-element.24.norm_ref, s32[64,128]{1,0:T(8,128)S(1)} %bitcast.58, ...), custom_call_target="tpu_custom_call" | custom-call | flops 6000000000 | bytes 4194304 | tf_op jit(solution)/shard_map/pallas_call | solution.py:241
  215.9 0.3 shard_map.89
  216.3 4.7 %collective-permute-start.20 = (bf16[64,512]{1,0:T(8,128)(2,1)S(1)}, bf16[64,512]{1,0:T(8,128)(2,1)S(1)}, u32[]{:S(2)}, u32[]{:S(2)}) collective-permute-start(bf16[64,512]{1,0:T(8,128)(2,1)S(1)} %get-tuple-element.54), channel_id=1, source_target_pairs={{0,8},{8,0},{16,24},{24,16},{32,40},{40,32},{48,56},{56,48},{64,72... | collective-permute-start | bytes 196616 | tf_op jit(solution)/shard_map/ppermute | solution.py:360
  221.0 0.9 collective-permute-done.20
  221.9 0.8 copy.17
  222.7 3.4 %all-to-all-start = ((bf16[8,64,128]{2,1,0:T(8,128)(2,1)}), bf16[8,64,128]{2,1,0:T(8,128)(2,1)S(1)}, u32[]{:S(2)}, u32[]{:S(2)}) async-start(bf16[8,64,128]{2,1,0:T(8,128)(2,1)} %bitcast.25), calls=%async_computation | async-start | bytes 262144 | tf_op jit(solution)/shard_map/all_to_all | solution.py:365
  226.1 5.3 %all-to-all-done = bf16[8,64,128]{2,1,0:T(8,128)(2,1)S(1)} async-done(((bf16[8,64,128]{2,1,0:T(8,128)(2,1)}), bf16[8,64,128]{2,1,0:T(8,128)(2,1)S(1)}, u32[]{:S(2)}, u32[]{:S(2)}) %all-to-all-start) | async-done | bytes 131104 | tf_op jit(solution)/shard_map/all_to_all | solution.py:365
  231.5 0.2 fusion.18
  231.7 0.2 fusion.14
  231.9 0.2 fusion.10
  232.1 0.9 fusion.2
  (36 shorter events, 0.2 us)
Async XLA Ops:
  0.0 1.2 copy-start
  0.0 12.9 %copy-start.6 = (bf16[128,1024]{1,0:T(8,128)(2,1)S(1)}, bf16[128,1024]{1,0:T(8,128)(2,1)}, u32[]{:S(2)}) copy-start(bf16[128,1024]{1,0:T(8,128)(2,1)} %param.13) | copy-start | bytes 786436
  0.0 13.7 %copy-start.4 = (s32[8192]{0:T(1024)S(1)}, s32[8192]{0:T(1024)}, u32[]{:S(2)}) copy-start(s32[8192]{0:T(1024)} %param.14) | copy-start | bytes 98308
  0.0 15.0 %copy-start.7 = (s32[64,256]{1,0:T(8,128)S(1)}, s32[64,256]{1,0:T(8,128)}, u32[]{:S(2)}) copy-start(s32[64,256]{1,0:T(8,128)} %param.15) | copy-start | bytes 196612
  2.7 13.7 %collective-permute-start.1 = (bf16[64,512]{1,0:T(8,128)(2,1)S(1)}, bf16[64,512]{1,0:T(8,128)(2,1)S(1)}, u32[]{:S(2)}, u32[]{:S(2)}) collective-permute-start(bf16[64,512]{1,0:T(8,128)(2,1)S(1)} %get-tuple-element.56), channel_id=1, source_target_pairs={{0,8},{8,0},{16,24},{24,16},{32,40},{40,32},{48,56},{56,48},{64,72... | collective-permute-start | bytes 196616 | tf_op jit(solution)/shard_map/ppermute | solution.py:326
  3.4 18.0 %collective-permute-start.7 = (bf16[128,1024]{1,0:T(8,128)(2,1)}, bf16[128,1024]{1,0:T(8,128)(2,1)}, u32[]{:S(2)}, u32[]{:S(2)}) collective-permute-start(bf16[128,1024]{1,0:T(8,128)(2,1)} %param.13), channel_id=1, source_target_pairs={{0,4},{1,5},{2,6},{3,7},{4,0},{5,1},{6,2},{7,3},{8,12},{9,13},{10,... | collective-permute-start | bytes 786440 | tf_op jit(solution)/shard_map/ppermute | solution.py:333
  4.8 2.2 copy-start.1
  6.9 0.9 copy-start.2
  7.9 0.9 copy-start.3
  12.5 12.5 %collective-permute-start = (bf16[2048,128]{1,0:T(8,128)(2,1)S(1)}, bf16[2048,128]{1,0:T(8,128)(2,1)S(1)}, u32[]{:S(2)}, u32[]{:S(2)}) collective-permute-start(bf16[2048,128]{1,0:T(8,128)(2,1)S(1)} %get-tuple-element.23), channel_id=1, source_target_pairs={{0,8},{8,0},{16,24},{24,16},{32,40},{40,32},{48,56},{56,48},{64,72... | collective-permute-start | bytes 1572872 | tf_op jit(solution)/shard_map/ppermute | solution.py:340
  16.4 11.5 %collective-permute-start.2 = (bf16[2,64,512]{2,1,0:T(8,128)(2,1)S(1)}, bf16[2,64,512]{2,1,0:T(8,128)(2,1)S(1)}, u32[]{:S(2)}, u32[]{:S(2)}) collective-permute-start(bf16[2,64,512]{2,1,0:T(8,128)(2,1)S(1)} %pad_maximum_fusion.rest_0_), channel_id=1, source_target_pairs={{0,16},{8,24},{16,0},{24,8},{32,48},{40,56},{48,32},{56,40},{64,80... | collective-permute-start | bytes 393224 | tf_op jit(solution)/shard_map/ppermute | solution.py:328
  19.1 10.8 %collective-permute-start.3 = (bf16[2,64,512]{2,1,0:T(8,128)(2,1)S(1)}, bf16[2,64,512]{2,1,0:T(8,128)(2,1)S(1)}, u32[]{:S(2)}, u32[]{:S(2)}) collective-permute-start(bf16[2,64,512]{2,1,0:T(8,128)(2,1)S(1)} %pad_maximum_fusion.rest_0_), channel_id=1, source_target_pairs={{0,32},{8,40},{16,48},{24,56},{32,64},{40,72},{48,80},{56,88},{64,... | collective-permute-start | bytes 393224 | tf_op jit(solution)/shard_map/ppermute | solution.py:328
  20.5 98.8 %collective-permute-start.17 = (bf16[2,64,512]{2,1,0:T(8,128)(2,1)S(1)}, bf16[2,64,512]{2,1,0:T(8,128)(2,1)S(1)}, u32[]{:S(2)}, u32[]{:S(2)}) collective-permute-start(bf16[2,64,512]{2,1,0:T(8,128)(2,1)S(1)} %pad_maximum_fusion.rest_0_), channel_id=1, source_target_pairs={{0,80},{8,88},{16,64},{24,72},{32,112},{40,120},{48,96},{56,104},{... | collective-permute-start | bytes 393224 | tf_op jit(solution)/shard_map/ppermute | solution.py:328
  21.4 50.5 %collective-permute-start.6 = (bf16[2,64,512]{2,1,0:T(8,128)(2,1)S(1)}, bf16[2,64,512]{2,1,0:T(8,128)(2,1)S(1)}, u32[]{:S(2)}, u32[]{:S(2)}) collective-permute-start(bf16[2,64,512]{2,1,0:T(8,128)(2,1)S(1)} %pad_maximum_fusion.rest_0_), channel_id=1, source_target_pairs={{0,96},{8,104},{16,112},{24,120},{32,0},{40,8},{48,16},{56,24},{64... | collective-permute-start | bytes 393224 | tf_op jit(solution)/shard_map/ppermute | solution.py:328
  25.0 51.9 %collective-permute-start.9 = (bf16[2,64,512]{2,1,0:T(8,128)(2,1)S(1)}, bf16[2,64,512]{2,1,0:T(8,128)(2,1)S(1)}, u32[]{:S(2)}, u32[]{:S(2)}) collective-permute-start(bf16[2,64,512]{2,1,0:T(8,128)(2,1)S(1)} %pad_maximum_fusion.rest_0_), channel_id=1, source_target_pairs={{0,48},{8,56},{16,32},{24,40},{32,80},{40,88},{48,64},{56,72},{64,... | collective-permute-start | bytes 393224 | tf_op jit(solution)/shard_map/ppermute | solution.py:328
  27.9 93.4 %collective-permute-start.12 = (bf16[2,64,512]{2,1,0:T(8,128)(2,1)S(1)}, bf16[2,64,512]{2,1,0:T(8,128)(2,1)S(1)}, u32[]{:S(2)}, u32[]{:S(2)}) collective-permute-start(bf16[2,64,512]{2,1,0:T(8,128)(2,1)S(1)} %pad_maximum_fusion.rest_0_), channel_id=1, source_target_pairs={{0,112},{8,120},{16,96},{24,104},{32,16},{40,24},{48,0},{56,8},{64... | collective-permute-start | bytes 393224 | tf_op jit(solution)/shard_map/ppermute | solution.py:328
  30.0 44.8 %collective-permute-start.8 = (bf16[256,1024]{1,0:T(8,128)(2,1)}, bf16[256,1024]{1,0:T(8,128)(2,1)S(1)}, u32[]{:S(2)}, u32[]{:S(2)}) collective-permute-start(bf16[256,1024]{1,0:T(8,128)(2,1)} %constant_dynamic-update-slice_fusion), channel_id=1, source_target_pairs={{0,1},{1,2},{2,3},{3,0},{4,5},{5,6},{6,7},{7,4},{8,9},{9,10},{10,1... | collective-permute-start | bytes 1572872 | tf_op jit(solution)/shard_map/ppermute | solution.py:336
  31.6 43.2 %copy-start.5 = (bf16[256,1024]{1,0:T(8,128)(2,1)S(1)}, bf16[256,1024]{1,0:T(8,128)(2,1)}, u32[]{:S(2)}) copy-start(bf16[256,1024]{1,0:T(8,128)(2,1)} %constant_dynamic-update-slice_fusion) | copy-start | bytes 1572868
  72.0 52.8 %collective-permute-start.14 = (bf16[2,64,512]{2,1,0:T(8,128)(2,1)S(1)}, bf16[2,64,512]{2,1,0:T(8,128)(2,1)S(1)}, u32[]{:S(2)}, u32[]{:S(2)}) collective-permute-start(bf16[2,64,512]{2,1,0:T(8,128)(2,1)S(1)} %pad_maximum_fusion.rest_0_), channel_id=1, source_target_pairs={{0,64},{8,72},{16,80},{24,88},{32,96},{40,104},{48,112},{56,120},{... | collective-permute-start | bytes 393224 | tf_op jit(solution)/shard_map/ppermute | solution.py:328
  74.8 46.6 %collective-permute-start.18 = (bf16[256,1024]{1,0:T(8,128)(2,1)S(1)}, bf16[256,1024]{1,0:T(8,128)(2,1)S(1)}, u32[]{:S(2)}, u32[]{:S(2)}) collective-permute-start(bf16[256,1024]{1,0:T(8,128)(2,1)S(1)} %copy-done.5), channel_id=1, source_target_pairs={{0,3},{1,0},{2,1},{3,2},{4,7},{5,4},{6,5},{7,6},{8,11},{9,8},{10,9... | collective-permute-start | bytes 1572872 | tf_op jit(solution)/shard_map/ppermute | solution.py:336
  76.9 45.9 %collective-permute-start.13 = (bf16[256,1024]{1,0:T(8,128)(2,1)S(1)}, bf16[256,1024]{1,0:T(8,128)(2,1)S(1)}, u32[]{:S(2)}, u32[]{:S(2)}) collective-permute-start(bf16[256,1024]{1,0:T(8,128)(2,1)S(1)} %copy-done.5), channel_id=1, source_target_pairs={{0,2},{1,3},{2,0},{3,1},{4,6},{5,7},{6,4},{7,5},{8,10},{9,11},{10,... | collective-permute-start | bytes 1572872 | tf_op jit(solution)/shard_map/ppermute | solution.py:336
  119.3 70.9 %collective-permute-start.4 = (bf16[2,72,512]{2,1,0:T(8,128)(2,1)S(1)}, bf16[2,72,512]{2,1,0:T(8,128)(2,1)S(1)}, u32[]{:S(2)}, u32[]{:S(2)}) collective-permute-start(bf16[2,72,512]{2,1,0:T(8,128)(2,1)S(1)} %get-tuple-element.27), channel_id=1, source_target_pairs={{16,0},{24,8},{0,16},{8,24},{48,32},{56,40},{32,48},{40,56},{80,64... | collective-permute-start | bytes 442376 | tf_op jit(solution)/shard_map/ppermute | solution.py:356
  121.3 69.0 %collective-permute-start.5 = (bf16[2,72,512]{2,1,0:T(8,128)(2,1)S(1)}, bf16[2,72,512]{2,1,0:T(8,128)(2,1)S(1)}, u32[]{:S(2)}, u32[]{:S(2)}) collective-permute-start(bf16[2,72,512]{2,1,0:T(8,128)(2,1)S(1)} %get-tuple-element.28), channel_id=1, source_target_pairs={{32,0},{40,8},{48,16},{56,24},{64,32},{72,40},{80,48},{88,56},{96,... | collective-permute-start | bytes 442376 | tf_op jit(solution)/shard_map/ppermute | solution.py:356
  121.3 94.5 %collective-permute-start.10 = (bf16[2,72,512]{2,1,0:T(8,128)(2,1)S(1)}, bf16[2,72,512]{2,1,0:T(8,128)(2,1)S(1)}, u32[]{:S(2)}, u32[]{:S(2)}) collective-permute-start(bf16[2,72,512]{2,1,0:T(8,128)(2,1)S(1)} %get-tuple-element.30), channel_id=1, source_target_pairs={{96,0},{104,8},{112,16},{120,24},{0,32},{8,40},{16,48},{24,56},{32... | collective-permute-start | bytes 442376 | tf_op jit(solution)/shard_map/ppermute | solution.py:356
  122.8 93.1 %collective-permute-start.11 = (bf16[2,72,512]{2,1,0:T(8,128)(2,1)S(1)}, bf16[2,72,512]{2,1,0:T(8,128)(2,1)S(1)}, u32[]{:S(2)}, u32[]{:S(2)}) collective-permute-start(bf16[2,72,512]{2,1,0:T(8,128)(2,1)S(1)} %get-tuple-element.31), channel_id=1, source_target_pairs={{48,0},{56,8},{32,16},{40,24},{80,32},{88,40},{64,48},{72,56},{112... | collective-permute-start | bytes 442376 | tf_op jit(solution)/shard_map/ppermute | solution.py:356
  164.7 51.2 %collective-permute-start.15 = (bf16[2,72,512]{2,1,0:T(8,128)(2,1)S(1)}, bf16[2,72,512]{2,1,0:T(8,128)(2,1)S(1)}, u32[]{:S(2)}, u32[]{:S(2)}) collective-permute-start(bf16[2,72,512]{2,1,0:T(8,128)(2,1)S(1)} %get-tuple-element.33), channel_id=1, source_target_pairs={{112,0},{120,8},{96,16},{104,24},{16,32},{24,40},{0,48},{8,56},{48... | collective-permute-start | bytes 442376 | tf_op jit(solution)/shard_map/ppermute | solution.py:356
  190.2 25.7 %collective-permute-start.16 = (bf16[2,72,512]{2,1,0:T(8,128)(2,1)S(1)}, bf16[2,72,512]{2,1,0:T(8,128)(2,1)S(1)}, u32[]{:S(2)}, u32[]{:S(2)}) collective-permute-start(bf16[2,72,512]{2,1,0:T(8,128)(2,1)S(1)} %get-tuple-element.34), channel_id=1, source_target_pairs={{64,0},{72,8},{80,16},{88,24},{96,32},{104,40},{112,48},{120,56},{... | collective-permute-start | bytes 442376 | tf_op jit(solution)/shard_map/ppermute | solution.py:356
  190.3 25.6 %collective-permute-start.19 = (bf16[2,72,512]{2,1,0:T(8,128)(2,1)S(1)}, bf16[2,72,512]{2,1,0:T(8,128)(2,1)S(1)}, u32[]{:S(2)}, u32[]{:S(2)}) collective-permute-start(bf16[2,72,512]{2,1,0:T(8,128)(2,1)S(1)} %shard_map.87), channel_id=1, source_target_pairs={{80,0},{88,8},{64,16},{72,24},{112,32},{120,40},{96,48},{104,56},{... | collective-permute-start | bytes 442376 | tf_op jit(solution)/shard_map/ppermute | solution.py:356
  216.3 5.6 %collective-permute-start.20 = (bf16[64,512]{1,0:T(8,128)(2,1)S(1)}, bf16[64,512]{1,0:T(8,128)(2,1)S(1)}, u32[]{:S(2)}, u32[]{:S(2)}) collective-permute-start(bf16[64,512]{1,0:T(8,128)(2,1)S(1)} %get-tuple-element.54), channel_id=1, source_target_pairs={{0,8},{8,0},{16,24},{24,16},{32,40},{40,32},{48,56},{56,48},{64,72... | collective-permute-start | bytes 196616 | tf_op jit(solution)/shard_map/ppermute | solution.py:360
  222.7 8.7 %all-to-all-start = ((bf16[8,64,128]{2,1,0:T(8,128)(2,1)}), bf16[8,64,128]{2,1,0:T(8,128)(2,1)S(1)}, u32[]{:S(2)}, u32[]{:S(2)}) async-start(bf16[8,64,128]{2,1,0:T(8,128)(2,1)} %bitcast.25), calls=%async_computation | async-start | bytes 262144 | tf_op jit(solution)/shard_map/all_to_all | solution.py:365

commit v3 on v2

--- a/solution.py
+++ b/solution.py
@@ -10,7 +10,8 @@
 HS = 64
 BLOCK = 128
 TILES = 4
-SLOTS = 4
+SLOTS = 2
+ROWS = 2 * BLOCK
 KEY_BLOCKS = 32
 ACC_ROWS = 72
 LOG2E = 1.4426950408889634
@@ -21,19 +22,19 @@
 VMEM = pl.BlockSpec(memory_space=pltpu.VMEM)
 
 
-def project_kernel(core_ref, x_ref, wk_ref, wv_ref, own_ref, other_ref, w_own, w_other):
+def project_kernel(core_ref, x_ref, wk_ref, wv_ref, own_ref, other_ref, w_all):
     @pl.when(pl.program_id(0) == 0)
     def _():
         first = core_ref[0] == 0
         wk, wv = wk_ref[...], wv_ref[...]
         head_0 = jnp.concatenate([wk[:, :HS], wv[:, :HS]], 1)
         head_1 = jnp.concatenate([wk[:, HS:], wv[:, HS:]], 1)
-        w_own[...] = jnp.where(first, head_0, head_1)
-        w_other[...] = jnp.where(first, head_1, head_0)
-
-    x = x_ref[...]
-    own_ref[...] = jnp.dot(x, w_own[...], preferred_element_type=jnp.float32).astype(jnp.bfloat16)
-    other_ref[...] = jnp.dot(x, w_other[...], preferred_element_type=jnp.float32).astype(jnp.bfloat16)
+        w_all[:, : 2 * HS] = jnp.where(first, head_0, head_1)
+        w_all[:, 2 * HS :] = jnp.where(first, head_1, head_0)
+
+    both = jnp.dot(x_ref[...], w_all[...], preferred_element_type=jnp.float32).astype(jnp.bfloat16)
+    own_ref[...] = both[:, : 2 * HS]
+    other_ref[...] = both[:, 2 * HS :]
 
 
 def project(core, inputs, w_key, w_value):
@@ -48,8 +49,8 @@
         in_specs=[SMEM, pl.BlockSpec((rows, width), lambda i: (i, 0)), whole, whole],
         out_specs=[tile, tile],
         out_shape=[out, out],
-        scratch_shapes=[pltpu.VMEM((width, 2 * HS), jnp.bfloat16)] * 2,
-        compiler_params=pltpu.CompilerParams(vmem_limit_bytes=32 * 2**20),
+        scratch_shapes=[pltpu.VMEM((width, 4 * HS), jnp.bfloat16)],
+        compiler_params=pltpu.CompilerParams(vmem_limit_bytes=60 * 2**20),
         cost_estimate=pl.CostEstimate(flops=2 * keys * width * 4 * HS, bytes_accessed=5 * 2**20, transcendentals=0),
     )(core, inputs, w_key, w_value)
 
@@ -87,10 +88,11 @@
 def attention_kernel(chips, count_ref, code_ref, base_ref, shard_ref, norm_ref, pos_ref, kv_ref, vt_ref, *rest):
     q_refs, o_refs = rest[:chips], rest[chips : 2 * chips]
     q_all, p_a, p_b, s_all, acc = rest[2 * chips :]
-    blocks = 8 * chips
+    blocks = 4 * chips
     own_base = base_ref[0]
     partner_base = base_ref[1]
-    iota = lax.broadcasted_iota(jnp.int32, (BLOCK, BLOCK), 0)
+    iota = lax.broadcasted_iota(jnp.int32, (BLOCK, ROWS), 0)
+    in_first = lax.broadcasted_iota(jnp.int32, (1, ROWS), 1) < BLOCK
     iota_half = iota.astype(jnp.float32).astype(jnp.bfloat16)
 
     most = None
@@ -107,13 +109,16 @@
         return jnp.minimum(r, blocks - 1)
 
     def whole_block(r):
-        return shard_ref[lax.div(r, 4)] * 4 + lax.rem(r, 4)
+        return shard_ref[lax.div(r, 2)] * 2 + lax.rem(r, 2)
 
     def offset(i):
         return pl.multiple_of(i * BLOCK, BLOCK)
 
+    def row_offset(i):
+        return pl.multiple_of(i * ROWS, ROWS)
+
     def query(r):
-        q = q_all[lax.div(r, 4), :, pl.ds(offset(lax.rem(r, 4)), BLOCK)]
+        q = q_all[lax.div(r, 2), :, pl.ds(row_offset(lax.rem(r, 2)), ROWS)]
         return jnp.concatenate([q, jnp.zeros_like(q)], 0)
 
     def key_blocks(row, c):
@@ -131,8 +136,9 @@
         k = jnp.bitwise_and(code, KEY_BLOCKS - 1)
         half = KEY_BLOCKS // 2
         base = jnp.where(k < half, own_base, partner_base - half * BLOCK) + k * BLOCK
-        reach = jnp.where(jnp.bitwise_and(code, KEY_BLOCKS) > 0, 1 << 30, BLOCK)
-        reach = jnp.where(jnp.logical_and(real, code >= 2 * KEY_BLOCKS), reach, -(1 << 30))
+        real = jnp.logical_and(real, code >= 4 * KEY_BLOCKS)
+        reach = [jnp.where(jnp.bitwise_and(code, n * KEY_BLOCKS) > 0, 1 << 30, BLOCK) for n in (1, 2)]
+        reach = jnp.where(in_first, *[jnp.where(real, n, -(1 << 30)) for n in reach])
         ahead = pos - base
         return jnp.where(ahead < reach, jnp.minimum(ahead, BLOCK - 1), -1)
 
@@ -143,7 +149,7 @@
         return out
 
     def put(i, rr, out):
-        o_refs[i][lax.div(rr, 4), :, pl.ds(offset(lax.rem(rr, 4)), BLOCK)] = out
+        o_refs[i][lax.div(rr, 2), :, pl.ds(row_offset(lax.rem(rr, 2)), ROWS)] = out
 
     def advance(r, c):
         last = c + 1 >= count_ref[whole_block(clamp(r))]
@@ -198,20 +204,20 @@
 
         for i in range(chips):
             def finish(rr, _, i=i):
-                a = acc[i * 8 + rr]
+                a = acc[i * 4 + rr]
                 put(i, rr, store(rr, a, jnp.where(a[HS : HS + 1] > 0, 0.0, lowest_max)))
                 return 0
 
-            lax.fori_loop(0, 8, finish, 0)
+            lax.fori_loop(0, 4, finish, 0)
 
     @pl.when(jnp.logical_not(safe))
     def _():
         for i in range(chips):
             def one_block(rr, _, i=i):
-                r = i * 8 + rr
+                r = i * 4 + rr
                 row = whole_block(r)
                 pos = pos_ref[pl.ds(row, 1), :]
-                acc[0] = jnp.zeros((ACC_ROWS, BLOCK), jnp.float32)
+                acc[0] = jnp.zeros((ACC_ROWS, ROWS), jnp.float32)
 
                 def one_slot(c, top):
                     s = products(row, r, c)
@@ -227,12 +233,12 @@
                     acc[0] = acc[0] * shrink + jnp.dot(values(row, c), p, preferred_element_type=jnp.float32)
                     return best
 
-                start = jnp.full((1, BLOCK), lowest_max, jnp.bfloat16).astype(jnp.float32)
+                start = jnp.full((1, ROWS), lowest_max, jnp.bfloat16).astype(jnp.float32)
                 top = lax.fori_loop(0, count_ref[row], one_slot, start)
                 put(i, rr, store(rr, acc[0], top))
                 return 0
 
-            lax.fori_loop(0, 8, one_block, 0)
+            lax.fori_loop(0, 4, one_block, 0)
 
 
 def attend(counts, codes, bases, shards, norm, spots, kv, vt, queries):
@@ -245,10 +251,10 @@
         out_shape=[out] * chips,
         scratch_shapes=[
             pltpu.VMEM((2 * chips, HS, queries[0].shape[2]), jnp.bfloat16),
-            pltpu.VMEM((SLOTS * TILES * BLOCK, BLOCK), jnp.bfloat16),
-            pltpu.VMEM((SLOTS * TILES * BLOCK, BLOCK), jnp.bfloat16),
-            pltpu.VMEM((TILES * BLOCK, BLOCK), jnp.float32),
-            pltpu.VMEM((8 * chips + 1, ACC_ROWS, BLOCK), jnp.float32),
+            pltpu.VMEM((SLOTS * TILES * BLOCK, ROWS), jnp.bfloat16),
+            pltpu.VMEM((SLOTS * TILES * BLOCK, ROWS), jnp.bfloat16),
+            pltpu.VMEM((TILES * BLOCK, ROWS), jnp.float32),
+            pltpu.VMEM((4 * chips + 1, ACC_ROWS, ROWS), jnp.float32),
         ],
         compiler_params=pltpu.CompilerParams(vmem_limit_bytes=32 * 2**20),
         cost_estimate=pl.CostEstimate(
@@ -257,8 +263,10 @@
     )(counts, codes, bases, shards, norm, spots, kv, vt, *queries)
 
 
-def combine_kernel(*refs):
+def combine_kernel(core_ref, *refs):
     parts, out_ref = refs[:-1], refs[-1]
+    groups = out_ref.shape[0] // 2
+    half = out_ref.shape[1]
     for j in range(2):
         tops = [p[j, HS + 1 : HS + 2, :].astype(jnp.float32) for p in parts]
         top = functools.reduce(jnp.maximum, tops)
@@ -268,21 +276,47 @@
             for p, scale in zip(parts, scales)
         )
         summed = sum(p[j, :HS, :].astype(jnp.float32) * scale for p, scale in zip(parts, scales))
-        out_ref[j] = (summed / total).astype(jnp.bfloat16)
-
-
-def combine(parts):
+        rows = (summed / total).T.astype(jnp.bfloat16)
+        first = jnp.bitwise_xor(core_ref[0], j) * groups
+        for g in range(groups):
+            upper = rows[2 * g * half : (2 * g + 1) * half]
+            lower = rows[(2 * g + 1) * half : (2 * g + 2) * half]
+            out_ref[first + g] = jnp.concatenate([upper, lower], 1)
+
+
+def combine(core, parts):
+    half = parts[0].shape[2] // 16
     return pl.pallas_call(
         combine_kernel,
-        in_specs=[VMEM] * len(parts),
+        in_specs=[SMEM] + [VMEM] * len(parts),
         out_specs=VMEM,
-        out_shape=jax.ShapeDtypeStruct((2, HS, parts[0].shape[2]), jnp.bfloat16),
+        out_shape=jax.ShapeDtypeStruct((16, half, 2 * HS), jnp.bfloat16),
         compiler_params=pltpu.CompilerParams(vmem_limit_bytes=32 * 2**20),
-    )(*parts)
-
-
-def work_list(spots, block_mask, first_own, first_partner):
+    )(core, *parts)
+
+
+def finish_kernel(pieces_ref, w_ref, out_ref):
+    groups = pieces_ref.shape[0] // 2
+    order = [c * groups + g for g in range(groups) for c in range(2)]
+    upper = jnp.concatenate([pieces_ref[i][:, :HS] for i in order], 1)
+    lower = jnp.concatenate([pieces_ref[i][:, HS:] for i in order], 1)
+    attention = jnp.concatenate([upper, lower], 0)
+    out_ref[...] = jnp.dot(attention, w_ref[...], preferred_element_type=jnp.float32).astype(jnp.bfloat16)
+
+
+def finish(pieces, w_all):
+    return pl.pallas_call(
+        finish_kernel,
+        in_specs=[VMEM, VMEM],
+        out_specs=VMEM,
+        out_shape=jax.ShapeDtypeStruct((2 * pieces.shape[1], w_all.shape[1]), jnp.bfloat16),
+        compiler_params=pltpu.CompilerParams(vmem_limit_bytes=32 * 2**20),
+    )(pieces, w_all)
+
+
+def work_list(positions, block_mask, first_own, first_partner):
     half = KEY_BLOCKS // 2
+    spots = positions.reshape(-1, BLOCK)
     index = jnp.arange(KEY_BLOCKS, dtype=jnp.int32)
     key_blocks = jnp.where(index < half, first_own, first_partner - half) + index
     listed = jnp.concatenate(
@@ -290,10 +324,12 @@
     ) == 1
     own = jnp.any((spots // BLOCK)[:, :, None] == key_blocks[None, None, :], axis=1)
     reached = (key_blocks * BLOCK)[None, :] <= jnp.max(spots, axis=1)[:, None]
-    active = (listed & reached) | own
+    active = ((listed & reached) | own).reshape(-1, 2, KEY_BLOCKS)
+    active = active[:, 0] | active[:, 1]
+    listed = listed.reshape(-1, 2, KEY_BLOCKS).astype(jnp.int32)
     earlier = index[None, :] < index[:, None]
     place = jnp.sum(active[:, None, :] & earlier[None], axis=2, dtype=jnp.int32)
-    value = index[None, :] + KEY_BLOCKS * listed.astype(jnp.int32) + 2 * KEY_BLOCKS
+    value = index[None, :] + KEY_BLOCKS * (listed[:, 0] + 2 * listed[:, 1] + 4)
     chosen = active[:, None, :] & (place[:, None, :] == index[None, :, None])
     codes = jnp.sum(jnp.where(chosen, value[:, None, :], 0), axis=2, dtype=jnp.int32)
     count = jnp.sum(active, axis=1, dtype=jnp.int32)
@@ -315,7 +351,7 @@
 def body(inputs, latents, w_query, w_key, w_value, w_out, positions, block_mask):
     s = lax.axis_index("seq")
     core = s % 2
-    me = lax.axis_index("grp")
+    w_all = lax.all_gather(w_out, "grp", axis=0, tiled=True)
 
     queries = lax.dot_general(
         w_query, latents, (((0,), (1,)), ((), ())), preferred_element_type=jnp.float32
@@ -324,51 +360,34 @@
     mine = jnp.where(core == 0, first, second)
     theirs = jnp.where(core == 0, second, first)
     q_chip = jnp.stack([mine, lax.ppermute(theirs, "seq", SWAP)])
+    q_chip, inputs = lax.optimization_barrier((q_chip, inputs))
     arrived = {
         step: q_chip if step == (0, 0) else lax.ppermute(q_chip, "seq", shifted(*step))
         for call in CALLS
         for step in call
     }
 
-    w_other = lax.ppermute(w_out, "grp", [(g, g ^ 4) for g in range(8)])
-    w_pair = jnp.concatenate([w_out, w_other], 0)
-    w_turns = [w_pair] + [
-        lax.ppermute(w_pair, "grp", [(g, (g & 4) | ((g + k) & 3)) for g in range(8)]) for k in (1, 2, 3)
-    ]
-
     kv_own, kv_other = project(core[None], inputs, w_key, w_value)
     kv, vt, norm = prepare(kv_own, lax.ppermute(kv_other, "seq", SWAP))
 
     per_device = inputs.shape[0] // BLOCK
-    spots = positions.reshape(-1, BLOCK)
-    counts, codes = work_list(spots, block_mask, s * per_device, (s ^ 1) * per_device)
+    counts, codes = work_list(positions, block_mask, s * per_device, (s ^ 1) * per_device)
     bases = jnp.stack([s, s ^ 1]) * inputs.shape[0]
+    spots = positions.reshape(-1, ROWS)
 
     parts = []
-    for n, call in enumerate(CALLS):
+    for call in CALLS:
         came_from = [(((s // 4 + 4 - x_by) % 4) * 4 + (s % 4 ^ 2 * y_by)) for x_by, y_by in call]
         shards = jnp.stack([shard for c in came_from for shard in (c, c ^ 1)])
         blocks = [arrived[step] for step in call]
-        if 1 <= n <= 3:
-            blocks[0], w_turns[n] = lax.optimization_barrier((blocks[0], w_turns[n]))
         done = attend(counts, codes, bases, shards, norm, spots, kv, vt, blocks)
         for step, part in zip(call, done):
             parts.append(part if step == (0, 0) else lax.ppermute(part, "seq", back(shifted(*step))))
 
-    attention = combine(parts)
-    rows = attention.shape[2]
-    swapped = lax.ppermute(attention[1], "seq", SWAP)
-    attention = jnp.where(
-        core == 0, jnp.concatenate([attention[0], swapped], 0), jnp.concatenate([swapped, attention[0]], 0)
-    )
-    attention = attention.T.reshape(8, rows // 8, 2 * HS)
-    attention = lax.all_to_all(attention, "grp", 0, 0)
-    result = 0.0
-    for k, w in enumerate(w_turns):
-        group = (me & 4) | ((me - k) & 3)
-        heads = jnp.concatenate([attention[group], attention[group ^ 4]], 1)
-        result += jnp.dot(heads, w, preferred_element_type=jnp.float32)
-    return result.astype(jnp.bfloat16)
+    pieces = combine(core[None], parts)
+    owners = [[(4 * x + 2 * y + c) * 8 + g for c in range(2) for g in range(8)] for x in range(4) for y in range(2)]
+    pieces = lax.all_to_all(pieces, ("seq", "grp"), 0, 0, axis_index_groups=owners)
+    return finish(pieces, w_all)
 
 
 def solution(mesh):

time: 235 us -> 209 us (0.89)
  Pallas kernels: 169 us -> 137 us
  blocking collectives: 0 us -> 16.4 us
  starting transfers between devices: 42.7 us -> 27.9 us
  between operations: 0.39 us -> 13.7 us
  waiting for transfers between devices: 6.28 us -> 0.06 us
  local copies, waits for them, and re-layouts: 8.78 us -> 4.92 us
    pallas_call x5, Pallas kernels: 164 us -> 127 us  [attend(): pl.pallas_call(functools.partial(attention_kernel, chips), in_specs=[SMEM...]
    all_to_all x0 -> x1, blocking collectives: none -> 16.4 us  [body(): lax.all_to_all(pieces, ('seq', 'grp'), 0, 0, axis_index_groups=owners)]
    ppermute x5 -> x0, starting transfers between devices: 11.1 us -> none  [the longest x3 5.07 us: body(): lax.ppermute(w_pair, 'grp', [(g, g & 4 | g + k & 3) for g in range(8)])]
    all_to_all x1 -> x0, waiting for transfers between devices: 5.32 us -> none  [body(): attention = lax.all_to_all(attention, 'grp', 0, 0)]
    pallas_call x1, Pallas kernels: 3.66 us -> 7.36 us  [project(): pl.pallas_call(project_kernel, grid=(keys // rows,), in_specs=[SMEM, pl.B...]
    all_to_all x1 -> x0, starting transfers between devices: 3.37 us -> none  [body(): attention = lax.all_to_all(attention, 'grp', 0, 0)]
    unnamed x17 -> x9, local copies, waits for them, and re-layouts: 6.01 us -> 3.87 us
  transfers between devices with their start and end apart: 22 -> 17, of which waited for: 2 -> 0; matrix products, arithmetic and copies ran while one was open for 2% -> 3% of each run, Pallas kernels for 73% -> 66%
where the time goes in v3:
time: 209 us; the launch traced here: 207 us
  Pallas kernels  137 us (66%)
  starting transfers between devices  27.9 us (13%)
  blocking collectives  16.4 us (8%)
  between operations  13.7 us (7%)
  local copies, waits for them, and re-layouts  4.92 us (2%)
  other arithmetic  4.8 us (2%)
    pallas_call x5, Pallas kernels, attend(): pl.pallas_call(functools.partial(attention_kernel, chips), in_specs=[SMEM...  127 us
    all_to_all x1, blocking collectives, body(): lax.all_to_all(pieces, ('seq', 'grp'), 0, 0, axis_index_groups=owners)  16.4 us
    ppermute x7, starting transfers between devices, body(): lax.ppermute(part, 'seq', back(shifted(*step)))  15.7 us
    ppermute x7, starting transfers between devices, body(): lax.ppermute(q_chip, 'seq', shifted(*step))  11.5 us
    pallas_call x1, Pallas kernels, project(): pl.pallas_call(project_kernel, grid=(keys // rows,), in_specs=[SMEM, pl.B...  7.36 us
  transfers between devices with their start and end apart: 17, of which 0 were waited for; matrix products, arithmetic and copies ran while one was open for 3% of the time, Pallas kernels for 66%

profile of v3, /device:TPU:3, one launch (start us, length us, event | category | flops | bytes accessed | tf_op | source)
XLA Modules:
  0.0 206.8 jit_solution(10030556417275628269)
XLA Ops:
  6.5 0.0 copy-start
  6.5 0.0 all-gather.2.cloned.1.call-start
  6.5 1.2 copy-done
  7.8 1.4 fusion
  9.2 0.8 collective-permute-start
  10.0 0.0 all-gather.2.cloned.1.call-update
  10.1 0.9 bitcast_reduce_fusion
  11.0 1.2 compare_reduce_fusion
  12.3 0.1 le.17
  12.4 0.9 constant_dynamic-slice_fusion.1
  13.3 0.1 fusion.8
  13.4 0.1 and_or_fusion
  13.6 0.7 convert_reduce_fusion.1
  14.3 0.6 convert_reduce_fusion
  14.9 0.1 add_multiply_fusion.base_ref
  15.0 0.1 pad_add_fusion.3.shard_ref
  15.0 0.1 pad_add_fusion.4.shard_ref
  15.1 0.1 pad_add_fusion.shard_ref
  15.2 0.0 collective-permute-done
  15.2 7.4 %shard_map.82 = (bf16[2048,128]{1,0:T(8,128)(2,1)}, bf16[2048,128]{1,0:T(8,128)(2,1)}) custom-call(s32[1]{0:T(128)} %bitcast.core_ref, bf16[2048,1024]{1,0:T(8,128)(2,1)} %x_ref, bf16[1024,128]{1,0:T(8,128)(2,1)} %wk_ref.1, bf16[1024,128]{1,0:T(8,128)(2,1)} %wv_ref.1), custom_call_target="tpu_custom_call" | custom-call | flops 1073741824 | bytes 5242880 | tf_op jit(solution)/shard_map/pallas_call | solution.py:46
  22.6 0.0 collective-permute-start.1
  22.6 0.1 pad_add_fusion.1.shard_ref
  22.7 3.0 %collective-permute-start.2 = (bf16[2,64,512]{2,1,0:T(8,128)(2,1)S(1)}, bf16[2,64,512]{2,1,0:T(8,128)(2,1)S(1)}, u32[]{:S(2)}, u32[]{:S(2)}) collective-permute-start(bf16[2,64,512]{2,1,0:T(8,128)(2,1)S(1)} %pad_maximum_fusion.rest_0_), channel_id=1, source_target_pairs={{0,16},{8,24},{16,0},{24,8},{32,48},{40,56},{48,32},{56,40},{64,80... | collective-permute-start | bytes 393224 | tf_op jit(solution)/shard_map/ppermute | solution.py:365
  25.7 1.2 collective-permute-start.3
  26.9 0.1 pad_add_fusion.2.shard_ref
  27.0 0.6 select_reduce_fusion.code_ref
  27.6 0.3 collective-permute-start.6
  28.0 1.0 collective-permute-start.7
  29.0 0.0 collective-permute-done.1.partner_ref
  29.0 2.9 %collective-permute-start.10 = (bf16[2,64,512]{2,1,0:T(8,128)(2,1)S(1)}, bf16[2,64,512]{2,1,0:T(8,128)(2,1)S(1)}, u32[]{:S(2)}, u32[]{:S(2)}) collective-permute-start(bf16[2,64,512]{2,1,0:T(8,128)(2,1)S(1)} %pad_maximum_fusion.rest_0_), channel_id=1, source_target_pairs={{0,112},{8,120},{16,96},{24,104},{32,16},{40,24},{48,0},{56,8},{64... | collective-permute-start | bytes 393224 | tf_op jit(solution)/shard_map/ppermute | solution.py:365
  31.8 1.1 copy-done.2
  32.9 1.0 shard_map.83
  33.9 0.0 collective-permute-done.2.rest_0_
  33.9 1.9 collective-permute-start.11
  35.8 0.0 collective-permute-done.3.rest_1_
  35.8 1.1 collective-permute-start.14
  37.0 30.5 %shard_map.84 = (bf16[2,72,512]{2,1,0:T(8,128)(2,1)S(1)}, bf16[2,72,512]{2,1,0:T(8,128)(2,1)S(1)}) custom-call(s32[32]{0:T(128)S(1)} %fusion.7.count_ref, s32[32,32]{1,0:T(8,128)S(1)} %select_reduce_fusion.code_ref, s32[2]{0:T(128)S(1)} %add_multiply_fusion.base_ref, s32[4]{0:T(128)S(1)} %pad_add_fusion.shard_ref, f32[1]{0:T(128)} %get-tuple-element.21.norm_ref, ...), custom_call_target="tpu_custom_call" | custom-call | flops 12000000000 | bytes 4194304 | tf_op jit(solution)/shard_map/pallas_call | solution.py:247
  67.5 0.0 collective-permute-done.6.rest_0_
  67.5 3.7 %collective-permute-start.4 = (bf16[2,72,512]{2,1,0:T(8,128)(2,1)S(1)}, bf16[2,72,512]{2,1,0:T(8,128)(2,1)S(1)}, u32[]{:S(2)}, u32[]{:S(2)}) collective-permute-start(bf16[2,72,512]{2,1,0:T(8,128)(2,1)S(1)} %get-tuple-element.25), channel_id=1, source_target_pairs={{16,0},{24,8},{0,16},{8,24},{48,32},{56,40},{32,48},{40,56},{80,64... | collective-permute-start | bytes 442376 | tf_op jit(solution)/shard_map/ppermute | solution.py:385
  71.2 0.0 collective-permute-done.7.rest_1_
  71.2 0.0 collective-permute-start.5
  71.2 31.0 %shard_map.85 = (bf16[2,72,512]{2,1,0:T(8,128)(2,1)S(1)}, bf16[2,72,512]{2,1,0:T(8,128)(2,1)S(1)}) custom-call(s32[32]{0:T(128)S(1)} %fusion.7.count_ref, s32[32,32]{1,0:T(8,128)S(1)} %select_reduce_fusion.code_ref, s32[2]{0:T(128)S(1)} %add_multiply_fusion.base_ref, s32[4]{0:T(128)S(1)} %pad_add_fusion.1.shard_ref, f32[1]{0:T(128)} %get-tuple-element.21.norm_ref, ...), custom_call_target="tpu_custom_call" | custom-call | flops 12000000000 | bytes 4194304 | tf_op jit(solution)/shard_map/pallas_call | solution.py:247
  102.2 0.0 collective-permute-done.10.rest_0_
  102.2 2.4 %collective-permute-start.8 = (bf16[2,72,512]{2,1,0:T(8,128)(2,1)S(1)}, bf16[2,72,512]{2,1,0:T(8,128)(2,1)S(1)}, u32[]{:S(2)}, u32[]{:S(2)}) collective-permute-start(bf16[2,72,512]{2,1,0:T(8,128)(2,1)S(1)} %get-tuple-element.27), channel_id=1, source_target_pairs={{96,0},{104,8},{112,16},{120,24},{0,32},{8,40},{16,48},{24,56},{32... | collective-permute-start | bytes 442376 | tf_op jit(solution)/shard_map/ppermute | solution.py:385
  104.7 0.0 collective-permute-done.11.rest_1_
  104.7 0.0 collective-permute-start.9
  104.7 30.7 %shard_map.86 = (bf16[2,72,512]{2,1,0:T(8,128)(2,1)S(1)}, bf16[2,72,512]{2,1,0:T(8,128)(2,1)S(1)}) custom-call(s32[32]{0:T(128)S(1)} %fusion.7.count_ref, s32[32,32]{1,0:T(8,128)S(1)} %select_reduce_fusion.code_ref, s32[2]{0:T(128)S(1)} %add_multiply_fusion.base_ref, s32[4]{0:T(128)S(1)} %pad_add_fusion.2.shard_ref, f32[1]{0:T(128)} %get-tuple-element.21.norm_ref, ...), custom_call_target="tpu_custom_call" | custom-call | flops 12000000000 | bytes 4194304 | tf_op jit(solution)/shard_map/pallas_call | solution.py:247
  135.4 0.0 collective-permute-done.14.rest_0_
  135.4 5.0 %collective-permute-start.12 = (bf16[2,72,512]{2,1,0:T(8,128)(2,1)S(1)}, bf16[2,72,512]{2,1,0:T(8,128)(2,1)S(1)}, u32[]{:S(2)}, u32[]{:S(2)}) collective-permute-start(bf16[2,72,512]{2,1,0:T(8,128)(2,1)S(1)} %get-tuple-element.29), channel_id=1, source_target_pairs={{112,0},{120,8},{96,16},{104,24},{16,32},{24,40},{0,48},{8,56},{48... | collective-permute-start | bytes 442376 | tf_op jit(solution)/shard_map/ppermute | solution.py:385
  140.4 17.8 %shard_map.87 = bf16[2,72,512]{2,1,0:T(8,128)(2,1)S(1)} custom-call(s32[32]{0:T(128)S(1)} %fusion.7.count_ref, s32[32,32]{1,0:T(8,128)S(1)} %select_reduce_fusion.code_ref, s32[2]{0:T(128)S(1)} %add_multiply_fusion.base_ref, s32[2]{0:T(128)S(1)} %pad_add_fusion.3.shard_ref, f32[1]{0:T(128)} %get-tuple-element.21.norm_ref, s32[32,256]{1,0:T(8,128)S(1)} %reshape.86.pos_ref, ...), custom_call_target="tpu_custom_call" | custom-call | flops 6000000000 | bytes 4194304 | tf_op jit(solution)/shard_map/pallas_call | solution.py:247
  158.3 0.0 collective-permute-done.4.refs_0_
  158.3 0.8 collective-permute-start.13
  159.1 0.0 collective-permute-done.5.refs_1_
  159.1 3.7 %collective-permute-start.15 = (bf16[2,72,512]{2,1,0:T(8,128)(2,1)S(1)}, bf16[2,72,512]{2,1,0:T(8,128)(2,1)S(1)}, u32[]{:S(2)}, u32[]{:S(2)}) collective-permute-start(bf16[2,72,512]{2,1,0:T(8,128)(2,1)S(1)} %shard_map.87), channel_id=1, source_target_pairs={{80,0},{88,8},{64,16},{72,24},{112,32},{120,40},{96,48},{104,56},{... | collective-permute-start | bytes 442376 | tf_op jit(solution)/shard_map/ppermute | solution.py:385
  162.8 17.3 %shard_map.88.refs_7_ = bf16[2,72,512]{2,1,0:T(8,128)(2,1)S(1)} custom-call(s32[32]{0:T(128)S(1)} %fusion.7.count_ref, s32[32,32]{1,0:T(8,128)S(1)} %select_reduce_fusion.code_ref, s32[2]{0:T(128)S(1)} %add_multiply_fusion.base_ref, s32[2]{0:T(128)S(1)} %pad_add_fusion.4.shard_ref, f32[1]{0:T(128)} %get-tuple-element.21.norm_ref, ...), custom_call_target="tpu_custom_call" | custom-call | flops 6000000000 | bytes 4194304 | tf_op jit(solution)/shard_map/pallas_call | solution.py:247
  180.2 0.0 collective-permute-done.8.refs_2_
  180.2 0.0 collective-permute-done.9.refs_3_
  180.2 0.0 collective-permute-done.12.refs_4_
  180.2 0.0 collective-permute-done.13.refs_5_
  180.2 0.0 collective-permute-done.15.refs_6_
  180.2 0.5 shard_map.89
  180.7 16.4 %all_to_all.5.pieces_ref = bf16[16,32,128]{2,1,0:T(8,128)(2,1)S(1)} all-to-all(bf16[16,32,128]{2,1,0:T(8,128)(2,1)S(1)} %shard_map.89), channel_id=1, replica_groups={{0,1,2,3,4,5,6,7,8,9,10,11,12,13,14,15},{16,17,18,19,20,21,22,23,24,25,..., dimensions={0} | all-to-all | bytes 262144 | tf_op jit(solution)/shard_map/all_to_all | solution.py:389
  197.2 1.6 copy-done.1
  198.7 1.2 shard_map.90
  (14 shorter events, 0.1 us)
Async XLA Ops:
  6.5 1.2 copy-start
  6.5 20.5 %copy-start.3 = (s32[8192]{0:T(1024)S(1)}, s32[8192]{0:T(1024)}, u32[]{:S(2)}) copy-start(s32[8192]{0:T(1024)} %param.14) | copy-start | bytes 98308
  6.5 190.6 %all-gather.2.cloned.1.call-start = ((), (), s32[]{:S(2)}) async-start(), calls=%async_computation.1 | async-start | bytes 2359296 | tf_op jit(solution)/shard_map/all_gather | solution.py:354
  9.2 6.0 %collective-permute-start = (bf16[64,512]{1,0:T(8,128)(2,1)S(1)}, bf16[64,512]{1,0:T(8,128)(2,1)S(1)}, u32[]{:S(2)}, u32[]{:S(2)}) collective-permute-start(bf16[64,512]{1,0:T(8,128)(2,1)S(1)} %get-tuple-element.38), channel_id=1, source_target_pairs={{0,8},{8,0},{16,24},{24,16},{32,40},{40,32},{48,56},{56,48},{64,72... | collective-permute-start | bytes 196616 | tf_op jit(solution)/shard_map/ppermute | solution.py:362
  22.6 6.4 %collective-permute-start.1 = (bf16[2048,128]{1,0:T(8,128)(2,1)}, bf16[2048,128]{1,0:T(8,128)(2,1)S(1)}, u32[]{:S(2)}, u32[]{:S(2)}) collective-permute-start(bf16[2048,128]{1,0:T(8,128)(2,1)} %get-tuple-element.20), channel_id=1, source_target_pairs={{0,8},{8,0},{16,24},{24,16},{32,40},{40,32},{48,56},{56,48},{64,72... | collective-permute-start | bytes 1572872 | tf_op jit(solution)/shard_map/ppermute | solution.py:371
  22.7 11.2 %collective-permute-start.2 = (bf16[2,64,512]{2,1,0:T(8,128)(2,1)S(1)}, bf16[2,64,512]{2,1,0:T(8,128)(2,1)S(1)}, u32[]{:S(2)}, u32[]{:S(2)}) collective-permute-start(bf16[2,64,512]{2,1,0:T(8,128)(2,1)S(1)} %pad_maximum_fusion.rest_0_), channel_id=1, source_target_pairs={{0,16},{8,24},{16,0},{24,8},{32,48},{40,56},{48,32},{56,40},{64,80... | collective-permute-start | bytes 393224 | tf_op jit(solution)/shard_map/ppermute | solution.py:365
  25.7 10.1 %collective-permute-start.3 = (bf16[2,64,512]{2,1,0:T(8,128)(2,1)S(1)}, bf16[2,64,512]{2,1,0:T(8,128)(2,1)S(1)}, u32[]{:S(2)}, u32[]{:S(2)}) collective-permute-start(bf16[2,64,512]{2,1,0:T(8,128)(2,1)S(1)} %pad_maximum_fusion.rest_0_), channel_id=1, source_target_pairs={{0,32},{8,40},{16,48},{24,56},{32,64},{40,72},{48,80},{56,88},{64,... | collective-permute-start | bytes 393224 | tf_op jit(solution)/shard_map/ppermute | solution.py:365
  27.6 39.9 %collective-permute-start.6 = (bf16[2,64,512]{2,1,0:T(8,128)(2,1)S(1)}, bf16[2,64,512]{2,1,0:T(8,128)(2,1)S(1)}, u32[]{:S(2)}, u32[]{:S(2)}) collective-permute-start(bf16[2,64,512]{2,1,0:T(8,128)(2,1)S(1)} %pad_maximum_fusion.rest_0_), channel_id=1, source_target_pairs={{0,96},{8,104},{16,112},{24,120},{32,0},{40,8},{48,16},{56,24},{64... | collective-permute-start | bytes 393224 | tf_op jit(solution)/shard_map/ppermute | solution.py:365
  28.0 43.3 %collective-permute-start.7 = (bf16[2,64,512]{2,1,0:T(8,128)(2,1)S(1)}, bf16[2,64,512]{2,1,0:T(8,128)(2,1)S(1)}, u32[]{:S(2)}, u32[]{:S(2)}) collective-permute-start(bf16[2,64,512]{2,1,0:T(8,128)(2,1)S(1)} %pad_maximum_fusion.rest_0_), channel_id=1, source_target_pairs={{0,48},{8,56},{16,32},{24,40},{32,80},{40,88},{48,64},{56,72},{64,... | collective-permute-start | bytes 393224 | tf_op jit(solution)/shard_map/ppermute | solution.py:365
  29.0 73.3 %collective-permute-start.10 = (bf16[2,64,512]{2,1,0:T(8,128)(2,1)S(1)}, bf16[2,64,512]{2,1,0:T(8,128)(2,1)S(1)}, u32[]{:S(2)}, u32[]{:S(2)}) collective-permute-start(bf16[2,64,512]{2,1,0:T(8,128)(2,1)S(1)} %pad_maximum_fusion.rest_0_), channel_id=1, source_target_pairs={{0,112},{8,120},{16,96},{24,104},{32,16},{40,24},{48,0},{56,8},{64... | collective-permute-start | bytes 393224 | tf_op jit(solution)/shard_map/ppermute | solution.py:365
  31.8 1.1 copy-start.2
  33.9 70.8 %collective-permute-start.11 = (bf16[2,64,512]{2,1,0:T(8,128)(2,1)S(1)}, bf16[2,64,512]{2,1,0:T(8,128)(2,1)S(1)}, u32[]{:S(2)}, u32[]{:S(2)}) collective-permute-start(bf16[2,64,512]{2,1,0:T(8,128)(2,1)S(1)} %pad_maximum_fusion.rest_0_), channel_id=1, source_target_pairs={{0,64},{8,72},{16,80},{24,88},{32,96},{40,104},{48,112},{56,120},{... | collective-permute-start | bytes 393224 | tf_op jit(solution)/shard_map/ppermute | solution.py:365
  35.8 99.6 %collective-permute-start.14 = (bf16[2,64,512]{2,1,0:T(8,128)(2,1)S(1)}, bf16[2,64,512]{2,1,0:T(8,128)(2,1)S(1)}, u32[]{:S(2)}, u32[]{:S(2)}) collective-permute-start(bf16[2,64,512]{2,1,0:T(8,128)(2,1)S(1)} %pad_maximum_fusion.rest_0_), channel_id=1, source_target_pairs={{0,80},{8,88},{16,64},{24,72},{32,112},{40,120},{48,96},{56,104},{... | collective-permute-start | bytes 393224 | tf_op jit(solution)/shard_map/ppermute | solution.py:365
  67.5 90.8 %collective-permute-start.4 = (bf16[2,72,512]{2,1,0:T(8,128)(2,1)S(1)}, bf16[2,72,512]{2,1,0:T(8,128)(2,1)S(1)}, u32[]{:S(2)}, u32[]{:S(2)}) collective-permute-start(bf16[2,72,512]{2,1,0:T(8,128)(2,1)S(1)} %get-tuple-element.25), channel_id=1, source_target_pairs={{16,0},{24,8},{0,16},{8,24},{48,32},{56,40},{32,48},{40,56},{80,64... | collective-permute-start | bytes 442376 | tf_op jit(solution)/shard_map/ppermute | solution.py:385
  71.2 87.9 %collective-permute-start.5 = (bf16[2,72,512]{2,1,0:T(8,128)(2,1)S(1)}, bf16[2,72,512]{2,1,0:T(8,128)(2,1)S(1)}, u32[]{:S(2)}, u32[]{:S(2)}) collective-permute-start(bf16[2,72,512]{2,1,0:T(8,128)(2,1)S(1)} %get-tuple-element.26), channel_id=1, source_target_pairs={{32,0},{40,8},{48,16},{56,24},{64,32},{72,40},{80,48},{88,56},{96,... | collective-permute-start | bytes 442376 | tf_op jit(solution)/shard_map/ppermute | solution.py:385
  102.2 77.9 %collective-permute-start.8 = (bf16[2,72,512]{2,1,0:T(8,128)(2,1)S(1)}, bf16[2,72,512]{2,1,0:T(8,128)(2,1)S(1)}, u32[]{:S(2)}, u32[]{:S(2)}) collective-permute-start(bf16[2,72,512]{2,1,0:T(8,128)(2,1)S(1)} %get-tuple-element.27), channel_id=1, source_target_pairs={{96,0},{104,8},{112,16},{120,24},{0,32},{8,40},{16,48},{24,56},{32... | collective-permute-start | bytes 442376 | tf_op jit(solution)/shard_map/ppermute | solution.py:385
  104.7 75.5 %collective-permute-start.9 = (bf16[2,72,512]{2,1,0:T(8,128)(2,1)S(1)}, bf16[2,72,512]{2,1,0:T(8,128)(2,1)S(1)}, u32[]{:S(2)}, u32[]{:S(2)}) collective-permute-start(bf16[2,72,512]{2,1,0:T(8,128)(2,1)S(1)} %get-tuple-element.28), channel_id=1, source_target_pairs={{48,0},{56,8},{32,16},{40,24},{80,32},{88,40},{64,48},{72,56},{112... | collective-permute-start | bytes 442376 | tf_op jit(solution)/shard_map/ppermute | solution.py:385
  135.4 44.8 %collective-permute-start.12 = (bf16[2,72,512]{2,1,0:T(8,128)(2,1)S(1)}, bf16[2,72,512]{2,1,0:T(8,128)(2,1)S(1)}, u32[]{:S(2)}, u32[]{:S(2)}) collective-permute-start(bf16[2,72,512]{2,1,0:T(8,128)(2,1)S(1)} %get-tuple-element.29), channel_id=1, source_target_pairs={{112,0},{120,8},{96,16},{104,24},{16,32},{24,40},{0,48},{8,56},{48... | collective-permute-start | bytes 442376 | tf_op jit(solution)/shard_map/ppermute | solution.py:385
  158.3 21.9 %collective-permute-start.13 = (bf16[2,72,512]{2,1,0:T(8,128)(2,1)S(1)}, bf16[2,72,512]{2,1,0:T(8,128)(2,1)S(1)}, u32[]{:S(2)}, u32[]{:S(2)}) collective-permute-start(bf16[2,72,512]{2,1,0:T(8,128)(2,1)S(1)} %get-tuple-element.30), channel_id=1, source_target_pairs={{64,0},{72,8},{80,16},{88,24},{96,32},{104,40},{112,48},{120,56},{... | collective-permute-start | bytes 442376 | tf_op jit(solution)/shard_map/ppermute | solution.py:385
  159.1 21.1 %collective-permute-start.15 = (bf16[2,72,512]{2,1,0:T(8,128)(2,1)S(1)}, bf16[2,72,512]{2,1,0:T(8,128)(2,1)S(1)}, u32[]{:S(2)}, u32[]{:S(2)}) collective-permute-start(bf16[2,72,512]{2,1,0:T(8,128)(2,1)S(1)} %shard_map.87), channel_id=1, source_target_pairs={{80,0},{88,8},{64,16},{72,24},{112,32},{120,40},{96,48},{104,56},{... | collective-permute-start | bytes 442376 | tf_op jit(solution)/shard_map/ppermute | solution.py:385
  197.2 1.6 copy-start.1
Sparse Core Ops, SparseCore 0:
  10.1 47.3 all-gather.1

commit v4 on v3

--- a/solution.py
+++ b/solution.py
@@ -22,37 +22,116 @@
 VMEM = pl.BlockSpec(memory_space=pltpu.VMEM)
 
 
-def project_kernel(core_ref, x_ref, wk_ref, wv_ref, own_ref, other_ref, w_all):
-    @pl.when(pl.program_id(0) == 0)
-    def _():
-        first = core_ref[0] == 0
-        wk, wv = wk_ref[...], wv_ref[...]
-        head_0 = jnp.concatenate([wk[:, :HS], wv[:, :HS]], 1)
-        head_1 = jnp.concatenate([wk[:, HS:], wv[:, HS:]], 1)
-        w_all[:, : 2 * HS] = jnp.where(first, head_0, head_1)
-        w_all[:, 2 * HS :] = jnp.where(first, head_1, head_0)
-
-    both = jnp.dot(x_ref[...], w_all[...], preferred_element_type=jnp.float32).astype(jnp.bfloat16)
-    own_ref[...] = both[:, : 2 * HS]
-    other_ref[...] = both[:, 2 * HS :]
-
-
-def project(core, inputs, w_key, w_value):
-    keys, width = inputs.shape
-    rows = 256
-    out = jax.ShapeDtypeStruct((keys, 2 * HS), jnp.bfloat16)
-    tile = pl.BlockSpec((rows, 2 * HS), lambda i: (i, 0))
-    whole = pl.BlockSpec((width, 2 * HS), lambda i: (0, 0))
+def list_work(me, pos_ref, mask_ref, code_ref, listed_all):
+    half = KEY_BLOCKS // 2
+    pairs = code_ref.shape[0]
+
+    def held(t):
+        return jnp.where(t < half, me * half, jnp.bitwise_xor(me, 1) * half - half) + t
+
+    columns = mask_ref.shape[1]
+    at = lax.broadcasted_iota(jnp.int32, (columns, BLOCK), 0)
+    lane = lax.broadcasted_iota(jnp.int32, (columns, BLOCK), 1)
+    pick = ((at == held(lane)) & (lane < KEY_BLOCKS)).astype(jnp.float32).astype(jnp.bfloat16)
+    listed = (mask_ref[...] == 1).astype(jnp.float32).astype(jnp.bfloat16)
+    listed_all[...] = jnp.dot(listed, pick, preferred_element_type=jnp.float32)
+
+    lane = lax.broadcasted_iota(jnp.int32, (pairs, BLOCK), 1)
+    value = jnp.full((pairs, BLOCK), 4 * KEY_BLOCKS, jnp.int32) + lane
+    active = jnp.zeros((pairs, BLOCK), jnp.bool_)
+    for n in range(2):
+        spots = pos_ref[pl.ds(n, pairs, stride=2), :]
+        listed = listed_all[pl.ds(n, pairs, stride=2), :] > 0.5
+        blocks = lax.shift_right_logical(spots, 7)
+        own = jnp.zeros((pairs, BLOCK), jnp.int32)
+        for t in range(KEY_BLOCKS):
+            any_own = jnp.max((blocks == held(t)).astype(jnp.int32), axis=1, keepdims=True)
+            own = jnp.where(lane == t, any_own, own)
+        reached = held(lane) * BLOCK <= jnp.max(spots, axis=1, keepdims=True)
+        active = active | (own > 0) | (listed & reached)
+        value = value + jnp.where(listed, (n + 1) * KEY_BLOCKS, 0)
+    active = active & (lane < KEY_BLOCKS)
+    ones = active.astype(jnp.float32)
+    row = lax.broadcasted_iota(jnp.int32, (BLOCK, BLOCK), 0)
+    col = lax.broadcasted_iota(jnp.int32, (BLOCK, BLOCK), 1)
+    earlier = (row < col).astype(jnp.float32).astype(jnp.bfloat16)
+    place = jnp.dot(ones.astype(jnp.bfloat16), earlier, preferred_element_type=jnp.float32).astype(jnp.int32)
+    packed = jnp.where(active, place * 512 + value, -1)
+    codes = jnp.zeros((pairs, BLOCK), jnp.int32)
+    for t in range(KEY_BLOCKS):
+        one = packed[:, t : t + 1]
+        codes = jnp.where(lax.shift_right_arithmetic(one, 9) == lane, jnp.bitwise_and(one, 511), codes)
+    count = jnp.sum(ones, axis=1, keepdims=True).astype(jnp.int32)
+    slots = jnp.maximum(lax.shift_right_logical(count + (TILES - 1), 2), 1)
+    code_ref[...] = jnp.where(lane == KEY_BLOCKS, slots, codes)
+
+
+def front_kernel(seq_ref, lat_hbm, x_hbm, wq_hbm, wk_hbm, wv_hbm, pos_hbm, mask_hbm, *rest):
+    mine_ref, theirs_ref, own_ref, other_ref, code_ref = rest[:5]
+    lat, x, wq, wk, wv, pos, mask, w_all, listed_all, sems, x_sems = rest[5:]
+    small = [
+        pltpu.make_async_copy(source, target, sems.at[i])
+        for i, (source, target) in enumerate(
+            [(pos_hbm, pos), (mask_hbm, mask), (wq_hbm, wq), (lat_hbm, lat), (wk_hbm, wk), (wv_hbm, wv)]
+        )
+    ]
+    rows = x.shape[0] // x_sems.shape[0]
+    parts = [pl.ds(i * rows, rows) for i in range(x_sems.shape[0])]
+    large = [pltpu.make_async_copy(x_hbm.at[p], x.at[p], x_sems.at[i]) for i, p in enumerate(parts)]
+    for copy in small + large:
+        copy.start()
+    got_pos, got_mask, got_wq, got_lat, got_wk, got_wv = small
+    first = jnp.bitwise_and(seq_ref[0], 1) == 0
+
+    got_pos.wait()
+    got_mask.wait()
+    list_work(seq_ref[0], pos, mask, code_ref, listed_all)
+
+    got_wq.wait()
+    got_lat.wait()
+    q = jnp.dot(lat[...], wq[...], preferred_element_type=jnp.float32).T
+    q = q.astype(jnp.bfloat16) * jnp.bfloat16(HS ** -0.5)
+    mine_ref[...] = jnp.where(first, q[:HS], q[HS:])
+    theirs_ref[...] = jnp.where(first, q[HS:], q[:HS])
+
+    got_wk.wait()
+    got_wv.wait()
+    k, v = wk[...], wv[...]
+    head_0 = jnp.concatenate([k[:, :HS], v[:, :HS]], 1)
+    head_1 = jnp.concatenate([k[:, HS:], v[:, HS:]], 1)
+    w_all[:, : 2 * HS] = jnp.where(first, head_0, head_1)
+    w_all[:, 2 * HS :] = jnp.where(first, head_1, head_0)
+    for copy, part in zip(large, parts):
+        copy.wait()
+        both = jnp.dot(x[part, :], w_all[...], preferred_element_type=jnp.float32).astype(jnp.bfloat16)
+        own_ref[part, :] = both[:, : 2 * HS]
+        other_ref[part, :] = both[:, 2 * HS :]
+
+
+def front(seq, latents, inputs, w_query, w_key, w_value, positions, block_mask):
+    rows, width = latents.shape
+    keys = inputs.shape[0]
+    spots = positions.reshape(-1, BLOCK)
+    operands = (latents, inputs, w_query, w_key, w_value, spots, block_mask)
+    q = jax.ShapeDtypeStruct((HS, rows), jnp.bfloat16)
+    kv = jax.ShapeDtypeStruct((keys, 2 * HS), jnp.bfloat16)
     return pl.pallas_call(
-        project_kernel,
-        grid=(keys // rows,),
-        in_specs=[SMEM, pl.BlockSpec((rows, width), lambda i: (i, 0)), whole, whole],
-        out_specs=[tile, tile],
-        out_shape=[out, out],
-        scratch_shapes=[pltpu.VMEM((width, 4 * HS), jnp.bfloat16)],
-        compiler_params=pltpu.CompilerParams(vmem_limit_bytes=60 * 2**20),
-        cost_estimate=pl.CostEstimate(flops=2 * keys * width * 4 * HS, bytes_accessed=5 * 2**20, transcendentals=0),
-    )(core, inputs, w_key, w_value)
+        front_kernel,
+        in_specs=[SMEM] + [pl.BlockSpec(memory_space=pl.ANY)] * len(operands),
+        out_specs=[VMEM] * 5,
+        out_shape=[q, q, kv, kv, jax.ShapeDtypeStruct((spots.shape[0] // 2, BLOCK), jnp.int32)],
+        scratch_shapes=[pltpu.VMEM(a.shape, a.dtype) for a in operands]
+        + [
+            pltpu.VMEM((width, 4 * HS), jnp.bfloat16),
+            pltpu.VMEM(spots.shape, jnp.float32),
+            pltpu.SemaphoreType.DMA((6,)),
+            pltpu.SemaphoreType.DMA((4,)),
+        ],
+        compiler_params=pltpu.CompilerParams(vmem_limit_bytes=61 * 2**20),
+        cost_estimate=pl.CostEstimate(
+            flops=2 * (keys * 4 + rows * 2) * width * HS, bytes_accessed=6 * 2**20, transcendentals=0
+        ),
+    )(seq, *operands)
 
 
 def prepare_kernel(own_ref, partner_ref, kv_ref, vt_ref, norm_ref):
@@ -85,21 +164,24 @@
     )(own, partner)
 
 
-def attention_kernel(chips, count_ref, code_ref, base_ref, shard_ref, norm_ref, pos_ref, kv_ref, vt_ref, *rest):
-    q_refs, o_refs = rest[:chips], rest[chips : 2 * chips]
-    q_all, p_a, p_b, s_all, acc = rest[2 * chips :]
+def attention_kernel(steps, takes, seq_ref, code_ref, norm_ref, pos_ref, kv_ref, vt_ref, *rest):
+    chips = len(steps)
+    q_refs, o_refs = rest[:takes], rest[takes : takes + chips]
+    q_all, p_a, p_b, s_all, acc = rest[takes + chips :]
     blocks = 4 * chips
-    own_base = base_ref[0]
-    partner_base = base_ref[1]
+    me = seq_ref[0]
+    own_base = me * (KEY_BLOCKS // 2 * BLOCK)
+    partner_base = jnp.bitwise_xor(me, 1) * (KEY_BLOCKS // 2 * BLOCK)
+    sources = [came_from(me, *step) for step in steps]
     iota = lax.broadcasted_iota(jnp.int32, (BLOCK, ROWS), 0)
     in_first = lax.broadcasted_iota(jnp.int32, (1, ROWS), 1) < BLOCK
     iota_half = iota.astype(jnp.float32).astype(jnp.bfloat16)
 
     most = None
-    for i in range(chips):
-        for j in range(2):
-            q = q_refs[i][j]
-            q_all[2 * i + j] = q
+    for i, ref in enumerate(q_refs):
+        for j in range(ref.shape[0]):
+            q = ref[j]
+            q_all[i * ref.shape[0] + j] = q
             q = q.astype(jnp.float32)
             squares = jnp.sum(q * q, axis=0, keepdims=True)
             most = squares if most is None else jnp.maximum(most, squares)
@@ -109,7 +191,10 @@
         return jnp.minimum(r, blocks - 1)
 
     def whole_block(r):
-        return shard_ref[lax.div(r, 2)] * 2 + lax.rem(r, 2)
+        shard = sources[-1]
+        for i in range(chips - 1):
+            shard = jnp.where(lax.div(r, 4) == i, sources[i], shard)
+        return jnp.bitwise_xor(shard, jnp.bitwise_and(lax.div(r, 2), 1)) * 2 + lax.rem(r, 2)
 
     def offset(i):
         return pl.multiple_of(i * BLOCK, BLOCK)
@@ -152,7 +237,7 @@
         o_refs[i][lax.div(rr, 2), :, pl.ds(row_offset(lax.rem(rr, 2)), ROWS)] = out
 
     def advance(r, c):
-        last = c + 1 >= count_ref[whole_block(clamp(r))]
+        last = c + 1 >= code_ref[whole_block(clamp(r)), KEY_BLOCKS]
         return jnp.where(last, jnp.minimum(r + 1, blocks), r), jnp.where(last, 0, c + 1)
 
     def step_slots(r, c):
@@ -198,9 +283,9 @@
             add(p_b, slots_1)
             return r2, c2, r3, c3
 
-        items = lax.fori_loop(0, blocks, lambda r, n: n + count_ref[whole_block(r)], jnp.int32(0))
-        steps = lax.div(items + (2 * SLOTS - 1), 2 * SLOTS)
-        lax.fori_loop(0, steps, two_steps, (jnp.int32(0), jnp.int32(0), r0, c0))
+        items = lax.fori_loop(0, blocks, lambda r, n: n + code_ref[whole_block(r), KEY_BLOCKS], jnp.int32(0))
+        turns = lax.div(items + (2 * SLOTS - 1), 2 * SLOTS)
+        lax.fori_loop(0, turns, two_steps, (jnp.int32(0), jnp.int32(0), r0, c0))
 
         for i in range(chips):
             def finish(rr, _, i=i):
@@ -234,19 +319,19 @@
                     return best
 
                 start = jnp.full((1, ROWS), lowest_max, jnp.bfloat16).astype(jnp.float32)
-                top = lax.fori_loop(0, count_ref[row], one_slot, start)
+                top = lax.fori_loop(0, code_ref[row, KEY_BLOCKS], one_slot, start)
                 put(i, rr, store(rr, acc[0], top))
                 return 0
 
             lax.fori_loop(0, 4, one_block, 0)
 
 
-def attend(counts, codes, bases, shards, norm, spots, kv, vt, queries):
-    chips = len(queries)
+def attend(steps, seq, codes, norm, spots, kv, vt, queries):
+    chips = len(steps)
     out = jax.ShapeDtypeStruct((2, ACC_ROWS, queries[0].shape[2]), jnp.bfloat16)
     return pl.pallas_call(
-        functools.partial(attention_kernel, chips),
-        in_specs=[SMEM] * 5 + [VMEM] * (3 + chips),
+        functools.partial(attention_kernel, steps, len(queries)),
+        in_specs=[SMEM] * 3 + [VMEM] * (3 + len(queries)),
         out_specs=[VMEM] * chips,
         out_shape=[out] * chips,
         scratch_shapes=[
@@ -260,7 +345,7 @@
         cost_estimate=pl.CostEstimate(
             flops=chips * 6 * 10**9, bytes_accessed=4 * 2**20, transcendentals=chips * 2**20
         ),
-    )(counts, codes, bases, shards, norm, spots, kv, vt, *queries)
+    )(seq, codes, norm, spots, kv, vt, *queries)
 
 
 def combine_kernel(core_ref, *refs):
@@ -295,45 +380,31 @@
     )(core, *parts)
 
 
-def finish_kernel(pieces_ref, w_ref, out_ref):
+def finish_kernel(grp_ref, pieces_ref, *refs):
+    w_refs, out_ref = refs[:-1], refs[-1]
     groups = pieces_ref.shape[0] // 2
-    order = [c * groups + g for g in range(groups) for c in range(2)]
-    upper = jnp.concatenate([pieces_ref[i][:, :HS] for i in order], 1)
-    lower = jnp.concatenate([pieces_ref[i][:, HS:] for i in order], 1)
-    attention = jnp.concatenate([upper, lower], 0)
-    out_ref[...] = jnp.dot(attention, w_ref[...], preferred_element_type=jnp.float32).astype(jnp.bfloat16)
-
-
-def finish(pieces, w_all):
+    me = grp_ref[0]
+    result = None
+    for k, w_ref in enumerate(w_refs):
+        near = jnp.bitwise_or(jnp.bitwise_and(me, 4), jnp.bitwise_and(me - k, 3))
+        order = [c * groups + g for g in (near, jnp.bitwise_xor(near, 4)) for c in range(2)]
+        blocks = [pieces_ref[i] for i in order]
+        upper = jnp.concatenate([p[:, :HS] for p in blocks], 1)
+        lower = jnp.concatenate([p[:, HS:] for p in blocks], 1)
+        attention = jnp.concatenate([upper, lower], 0)
+        term = jnp.dot(attention, w_ref[...], preferred_element_type=jnp.float32)
+        result = term if result is None else result + term
+    out_ref[...] = result.astype(jnp.bfloat16)
+
+
+def finish(grp, pieces, w_turns):
     return pl.pallas_call(
         finish_kernel,
-        in_specs=[VMEM, VMEM],
+        in_specs=[SMEM] + [VMEM] * (1 + len(w_turns)),
         out_specs=VMEM,
-        out_shape=jax.ShapeDtypeStruct((2 * pieces.shape[1], w_all.shape[1]), jnp.bfloat16),
-        compiler_params=pltpu.CompilerParams(vmem_limit_bytes=32 * 2**20),
-    )(pieces, w_all)
-
-
-def work_list(positions, block_mask, first_own, first_partner):
-    half = KEY_BLOCKS // 2
-    spots = positions.reshape(-1, BLOCK)
-    index = jnp.arange(KEY_BLOCKS, dtype=jnp.int32)
-    key_blocks = jnp.where(index < half, first_own, first_partner - half) + index
-    listed = jnp.concatenate(
-        [lax.dynamic_slice_in_dim(block_mask, first, half, 1) for first in (first_own, first_partner)], 1
-    ) == 1
-    own = jnp.any((spots // BLOCK)[:, :, None] == key_blocks[None, None, :], axis=1)
-    reached = (key_blocks * BLOCK)[None, :] <= jnp.max(spots, axis=1)[:, None]
-    active = ((listed & reached) | own).reshape(-1, 2, KEY_BLOCKS)
-    active = active[:, 0] | active[:, 1]
-    listed = listed.reshape(-1, 2, KEY_BLOCKS).astype(jnp.int32)
-    earlier = index[None, :] < index[:, None]
-    place = jnp.sum(active[:, None, :] & earlier[None], axis=2, dtype=jnp.int32)
-    value = index[None, :] + KEY_BLOCKS * (listed[:, 0] + 2 * listed[:, 1] + 4)
-    chosen = active[:, None, :] & (place[:, None, :] == index[None, :, None])
-    codes = jnp.sum(jnp.where(chosen, value[:, None, :], 0), axis=2, dtype=jnp.int32)
-    count = jnp.sum(active, axis=1, dtype=jnp.int32)
-    return jnp.maximum((count + TILES - 1) // TILES, 1), codes
+        out_shape=jax.ShapeDtypeStruct((2 * pieces.shape[1], w_turns[0].shape[1]), jnp.bfloat16),
+        compiler_params=pltpu.CompilerParams(vmem_limit_bytes=24 * 2**20),
+    )(grp, pieces, *w_turns)
 
 
 def shifted(x_by, y_by):
@@ -344,50 +415,55 @@
     return [(b, a) for a, b in route]
 
 
-CALLS = (((0, 1), (1, 0)), ((3, 0), (1, 1)), ((3, 1), (2, 0)), ((2, 1),), ((0, 0),))
+def came_from(s, x_by, y_by):
+    moved = jnp.bitwise_and(s - 4 * x_by, 12)
+    return moved + jnp.bitwise_xor(jnp.bitwise_and(s, 3), 2 * y_by)
+
+
+CALLS = (((0, 1),), ((1, 0), (1, 1), (3, 0), (3, 1)), ((2, 0), (2, 1)), ((0, 0),))
 SWAP = [(i, i ^ 1) for i in range(16)]
 
 
 def body(inputs, latents, w_query, w_key, w_value, w_out, positions, block_mask):
-    s = lax.axis_index("seq")
-    core = s % 2
-    w_all = lax.all_gather(w_out, "grp", axis=0, tiled=True)
-
-    queries = lax.dot_general(
-        w_query, latents, (((0,), (1,)), ((), ())), preferred_element_type=jnp.float32
-    ).astype(jnp.bfloat16) * jnp.bfloat16(HS ** -0.5)
-    first, second = queries[:HS], queries[HS:]
-    mine = jnp.where(core == 0, first, second)
-    theirs = jnp.where(core == 0, second, first)
+    seq = lax.axis_index("seq")[None]
+    grp = lax.axis_index("grp")[None]
+    core = jnp.bitwise_and(seq, 1)
+
+    w_other = lax.ppermute(w_out, "grp", [(g, g ^ 4) for g in range(8)])
+    mine, theirs, kv_own, kv_other, codes = front(
+        seq, latents, inputs, w_query, w_key, w_value, positions, block_mask
+    )
     q_chip = jnp.stack([mine, lax.ppermute(theirs, "seq", SWAP)])
-    q_chip, inputs = lax.optimization_barrier((q_chip, inputs))
     arrived = {
         step: q_chip if step == (0, 0) else lax.ppermute(q_chip, "seq", shifted(*step))
         for call in CALLS
         for step in call
     }
-
-    kv_own, kv_other = project(core[None], inputs, w_key, w_value)
     kv, vt, norm = prepare(kv_own, lax.ppermute(kv_other, "seq", SWAP))
 
-    per_device = inputs.shape[0] // BLOCK
-    counts, codes = work_list(positions, block_mask, s * per_device, (s ^ 1) * per_device)
-    bases = jnp.stack([s, s ^ 1]) * inputs.shape[0]
+    w_pair = jnp.concatenate([w_out, w_other], 0)
+    w_turns = [w_pair] + [
+        lax.ppermute(w_pair, "grp", [(g, (g & 4) | ((g + k) & 3)) for g in range(8)]) for k in (1, 2, 3)
+    ]
+    arrived[2, 0], w_turns = lax.optimization_barrier((arrived[2, 0], w_turns))
+
     spots = positions.reshape(-1, ROWS)
-
     parts = []
     for call in CALLS:
-        came_from = [(((s // 4 + 4 - x_by) % 4) * 4 + (s % 4 ^ 2 * y_by)) for x_by, y_by in call]
-        shards = jnp.stack([shard for c in came_from for shard in (c, c ^ 1)])
-        blocks = [arrived[step] for step in call]
-        done = attend(counts, codes, bases, shards, norm, spots, kv, vt, blocks)
-        for step, part in zip(call, done):
-            parts.append(part if step == (0, 0) else lax.ppermute(part, "seq", back(shifted(*step))))
-
-    pieces = combine(core[None], parts)
+        if parts:
+            arrived[call[0]], parts[-1] = lax.optimization_barrier((arrived[call[0]], parts[-1]))
+        done = attend(call, seq, codes, norm, spots, kv, vt, [arrived[step] for step in call])
+        parts += done
+
+    order = [step for call in CALLS for step in call]
+    parts = [
+        part if step == (0, 0) else lax.ppermute(part, "seq", back(shifted(*step)))
+        for step, part in zip(order, parts)
+    ]
+    pieces = combine(core, parts)
     owners = [[(4 * x + 2 * y + c) * 8 + g for c in range(2) for g in range(8)] for x in range(4) for y in range(2)]
     pieces = lax.all_to_all(pieces, ("seq", "grp"), 0, 0, axis_index_groups=owners)
-    return finish(pieces, w_all)
+    return finish(grp, pieces, w_turns)
 
 
 def solution(mesh):

time: 209 us -> 190 us (0.909)
  blocking collectives: 16.4 us -> 0 us
  between operations: 13.7 us -> 0.19 us
  starting transfers between devices: 27.9 us -> 40.1 us
  waiting for transfers between devices: 0.06 us -> 8.79 us
  other arithmetic: 4.8 us -> 0.85 us
  local copies, waits for them, and re-layouts: 4.92 us -> 1.81 us
    all_to_all x1 -> x0, blocking collectives: 16.4 us -> none  [body(): lax.all_to_all(pieces, ('seq', 'grp'), 0, 0, axis_index_groups=owners)]
    all_to_all x0 -> x1, starting transfers between devices: none -> 8.75 us  [body(): lax.all_to_all(pieces, ('seq', 'grp'), 0, 0, axis_index_groups=owners)]
    ppermute x0 -> x4, starting transfers between devices: none -> 7.04 us  [the longest x3 5.74 us: body(): lax.ppermute(w_pair, 'grp', [(g, g & 4 | g + k & 3) for g in range(8)])]
    all_to_all x0 -> x1, waiting for transfers between devices: none -> 6.35 us  [body(): lax.all_to_all(pieces, ('seq', 'grp'), 0, 0, axis_index_groups=owners)]
    ppermute x7, starting transfers between devices: 15.7 us -> 11.3 us  [body(): lax.ppermute(part, 'seq', back(shifted(*step)))]
    pallas_call x7 -> x6, Pallas kernels: 136 us -> 135 us  [the longest x4 127 us: attend(): pl.pallas_call(functools.partial(attention_kernel, steps, len(queries)),...]
  transfers between devices with their start and end apart: 17 -> 21, of which waited for: 0 -> 3; matrix products, arithmetic and copies ran while one was open for 3% -> 0% of each run, Pallas kernels for 66% -> 68%
where the time goes in v4:
time: 190 us; the launch traced here: 189 us
  Pallas kernels  137 us (72%)
  starting transfers between devices  40.1 us (21%)
  waiting for transfers between devices  8.79 us (5%)
    pallas_call x4, Pallas kernels, attend(): pl.pallas_call(functools.partial(attention_kernel, steps, len(queries)),...  127 us
    ppermute x7, starting transfers between devices, body(): lax.ppermute(q_chip, 'seq', shifted(*step))  12.2 us
    ppermute x7, starting transfers between devices, body(): lax.ppermute(part, 'seq', back(shifted(*step)))  11.3 us
    all_to_all x1, starting transfers between devices, body(): lax.all_to_all(pieces, ('seq', 'grp'), 0, 0, axis_index_groups=owners)  8.75 us
    pallas_call x1, Pallas kernels, front(): pl.pallas_call(front_kernel, in_specs=[SMEM] + [pl.BlockSpec(memory_space...  6.78 us
    all_to_all x1, waiting for transfers between devices, body(): lax.all_to_all(pieces, ('seq', 'grp'), 0, 0, axis_index_groups=owners)  6.35 us
    ppermute x3, starting transfers between devices, body(): lax.ppermute(w_pair, 'grp', [(g, g & 4 | g + k & 3) for g in range(8)])  5.74 us
  transfers between devices with their start and end apart: 21, of which 3 were waited for; matrix products, arithmetic and copies ran while one was open for 0% of the time, Pallas kernels for 68%

profile of v4, /device:TPU:3, one launch (start us, length us, event | category | flops | bytes accessed | tf_op | source)
XLA Modules:
  0.0 188.9 jit_solution(4908264802754138939)
XLA Ops:
  0.0 0.0 copy-start.3
  0.0 0.0 copy-start.2
  0.0 6.8 %shard_map.82 = (bf16[64,512]{1,0:T(8,128)(2,1)}, bf16[64,512]{1,0:T(8,128)(2,1)}, bf16[2048,128]{1,0:T(8,128)(2,1)}, bf16[2048,128]{1,0:T(8,128)(2,1)}, s32[32,128]{1,0:T(8,128)}) custom-call(s32[1]{0:T(128)} %bitcast.1.seq_ref, bf16[512,1024]{1,0:T(8,128)(2,1)} %lat_hbm.1, bf16[2048,1024]{1,0:T(8,128)(2,1)} %x_hbm.1, bf16[1024,128]{1,0:T(8,128)(2,1)} %wq_hbm.1, ...), custom_call_target="tpu_custom_call" | custom-call | flops 1207959552 | bytes 6291456 | tf_op jit(solution)/shard_map/pallas_call | solution.py:118
  6.8 0.8 collective-permute-start.2
  7.5 0.1 collective-permute-start
  7.6 0.0 copy-done.2
  7.6 1.3 collective-permute-start.12
  8.9 0.4 collective-permute-done
  9.4 0.9 pad_maximum_fusion.rest_0_
  10.2 3.0 %collective-permute-start.3 = (bf16[2,64,512]{2,1,0:T(8,128)(2,1)S(1)}, bf16[2,64,512]{2,1,0:T(8,128)(2,1)S(1)}, u32[]{:S(2)}, u32[]{:S(2)}) collective-permute-start(bf16[2,64,512]{2,1,0:T(8,128)(2,1)S(1)} %pad_maximum_fusion.rest_0_), channel_id=1, source_target_pairs={{0,16},{8,24},{16,0},{24,8},{32,48},{40,56},{48,32},{56,40},{64,80... | collective-permute-start | bytes 393224 | tf_op jit(solution)/shard_map/ppermute | solution.py:438
  13.3 0.0 copy-done.3
  13.3 1.3 collective-permute-start.1
  14.6 0.7 collective-permute-start.5
  15.3 0.0 collective-permute-done.12
  15.3 0.5 collective-permute-start.6
  15.8 0.0 collective-permute-done.2.partner_ref
  15.8 4.7 %collective-permute-start.7 = (bf16[2,64,512]{2,1,0:T(8,128)(2,1)S(1)}, bf16[2,64,512]{2,1,0:T(8,128)(2,1)S(1)}, u32[]{:S(2)}, u32[]{:S(2)}) collective-permute-start(bf16[2,64,512]{2,1,0:T(8,128)(2,1)S(1)} %pad_maximum_fusion.rest_0_), channel_id=1, source_target_pairs={{0,112},{8,120},{16,96},{24,104},{32,16},{40,24},{48,0},{56,8},{64... | collective-permute-start | bytes 393224 | tf_op jit(solution)/shard_map/ppermute | solution.py:438
  20.6 0.0 copy-start
  20.6 1.0 copy-done
  21.6 1.0 shard_map.83
  22.6 1.9 %collective-permute-done.3.rest_0_ = bf16[2,64,512]{2,1,0:T(8,128)(2,1)S(1)} collective-permute-done((bf16[2,64,512]{2,1,0:T(8,128)(2,1)S(1)}, bf16[2,64,512]{2,1,0:T(8,128)(2,1)S(1)}, u32[]{:S(2)}, u32[]{:S(2)}) %collective-permute-start.3) | collective-permute-done | bytes 131104 | tf_op jit(solution)/shard_map/ppermute | solution.py:438
  24.6 1.8 collective-permute-start.11
  26.4 0.0 copy-start.1
  26.4 0.7 copy-done.1
  27.1 17.8 %shard_map.84 = bf16[2,72,512]{2,1,0:T(8,128)(2,1)S(1)} custom-call(s32[1]{0:T(128)} %bitcast.1.seq_ref, s32[32,128]{1,0:T(8,128)S(1)} %copy-done.1, f32[1]{0:T(128)} %get-tuple-element.35.norm_ref, s32[32,256]{1,0:T(8,128)S(1)} %reshape.7.pos_ref, bf16[4096,128]{1,0:T(8,128)(2,1)S(1)} %get-tuple-element.36.kv_ref, ...), custom_call_target="tpu_custom_call" | custom-call | flops 6000000000 | bytes 4194304 | tf_op jit(solution)/shard_map/pallas_call | solution.py:332
  45.0 0.0 collective-permute-done.1.rest_0_
  45.0 0.1 collective-permute-start.17
  45.1 0.0 collective-permute-done.5.rest_1_
  45.1 1.7 collective-permute-start.13
  46.8 0.0 collective-permute-done.6.rest_2_
  46.8 3.3 %collective-permute-start.14 = (bf16[256,1024]{1,0:T(8,128)(2,1)S(1)}, bf16[256,1024]{1,0:T(8,128)(2,1)S(1)}, u32[]{:S(2)}, u32[]{:S(2)}) collective-permute-start(bf16[256,1024]{1,0:T(8,128)(2,1)S(1)} %constant_dynamic-update-slice_fusion.refs_0_), channel_id=1, source_target_pairs={{0,2},{1,3},{2,0},{3,1},{4,6},{5,7},{6,4},{7,5},{8,10},{9,11},{10,... | collective-permute-start | bytes 1572872 | tf_op jit(solution)/shard_map/ppermute | solution.py:446
  50.1 0.0 collective-permute-done.7.rest_3_
  50.1 0.7 collective-permute-start.15
  50.8 60.9 %shard_map.85 = (bf16[2,72,512]{2,1,0:T(8,128)(2,1)S(1)}, bf16[2,72,512]{2,1,0:T(8,128)(2,1)S(1)}, bf16[2,72,512]{2,1,0:T(8,128)(2,1)S(1)}, bf16[2,72,512]{2,1,0:T(8,128)(2,1)S(1)}) custom-call(s32[1]{0:T(128)} %bitcast.1.seq_ref, s32[32,128]{1,0:T(8,128)S(1)} %copy-done.1, f32[1]{0:T(128)} %get-tuple-element.35.norm_ref, s32[32,256]{1,0:T(8,128)S(1)} %reshape.7.pos_ref, ...), custom_call_target="tpu_custom_call" | custom-call | flops 24000000000 | bytes 4194304 | tf_op jit(solution)/shard_map/pallas_call | solution.py:332
  111.8 0.0 collective-permute-done.11.rest_0_
  111.8 0.1 collective-permute-start.10
  111.8 0.0 collective-permute-done.13.refs_1_
  111.9 1.4 collective-permute-start.8
  113.3 0.0 collective-permute-done.14.refs_2_
  113.3 4.0 %collective-permute-start.9 = (bf16[2,72,512]{2,1,0:T(8,128)(2,1)S(1)}, bf16[2,72,512]{2,1,0:T(8,128)(2,1)S(1)}, u32[]{:S(2)}, u32[]{:S(2)}) collective-permute-start(bf16[2,72,512]{2,1,0:T(8,128)(2,1)S(1)} %get-tuple-element.41), channel_id=1, source_target_pairs={{48,0},{56,8},{32,16},{40,24},{80,32},{88,40},{64,48},{72,56},{112... | collective-permute-start | bytes 442376 | tf_op jit(solution)/shard_map/ppermute | solution.py:460
  117.3 0.0 collective-permute-done.15.refs_3_
  117.3 0.0 collective-permute-start.4
  117.3 0.0 collective-permute-done.17.rest_1_
  117.3 31.0 %shard_map.86 = (bf16[2,72,512]{2,1,0:T(8,128)(2,1)S(1)}, bf16[2,72,512]{2,1,0:T(8,128)(2,1)S(1)}) custom-call(s32[1]{0:T(128)} %bitcast.1.seq_ref, s32[32,128]{1,0:T(8,128)S(1)} %copy-done.1, f32[1]{0:T(128)} %get-tuple-element.35.norm_ref, s32[32,256]{1,0:T(8,128)S(1)} %reshape.7.pos_ref, bf16[4096,128]{1,0:T(8,128)(2,1)S(1)} %get-tuple-element.36.kv_ref, ...), custom_call_target="tpu_custom_call" | custom-call | flops 12000000000 | bytes 4194304 | tf_op jit(solution)/shard_map/pallas_call | solution.py:332
  148.3 2.7 %collective-permute-start.19 = (bf16[2,72,512]{2,1,0:T(8,128)(2,1)S(1)}, bf16[2,72,512]{2,1,0:T(8,128)(2,1)S(1)}, u32[]{:S(2)}, u32[]{:S(2)}) collective-permute-start(bf16[2,72,512]{2,1,0:T(8,128)(2,1)S(1)} %get-tuple-element.49), channel_id=1, source_target_pairs={{80,0},{88,8},{64,16},{72,24},{112,32},{120,40},{96,48},{104,56},{... | collective-permute-start | bytes 442376 | tf_op jit(solution)/shard_map/ppermute | solution.py:460
  151.0 0.0 collective-permute-done.10.refs_3_
  151.0 3.1 %collective-permute-start.18 = (bf16[2,72,512]{2,1,0:T(8,128)(2,1)S(1)}, bf16[2,72,512]{2,1,0:T(8,128)(2,1)S(1)}, u32[]{:S(2)}, u32[]{:S(2)}) collective-permute-start(bf16[2,72,512]{2,1,0:T(8,128)(2,1)S(1)} %get-tuple-element.47), channel_id=1, source_target_pairs={{64,0},{72,8},{80,16},{88,24},{96,32},{104,40},{112,48},{120,56},{... | collective-permute-start | bytes 442376 | tf_op jit(solution)/shard_map/ppermute | solution.py:460
  154.1 0.0 collective-permute-done.8.refs_1_
  154.1 0.0 collective-permute-start.16
  154.1 17.3 %shard_map.87.refs_7_ = bf16[2,72,512]{2,1,0:T(8,128)(2,1)S(1)} custom-call(s32[1]{0:T(128)} %bitcast.1.seq_ref, s32[32,128]{1,0:T(8,128)S(1)} %copy-done.1, f32[1]{0:T(128)} %get-tuple-element.35.norm_ref, s32[32,256]{1,0:T(8,128)S(1)} %reshape.7.pos_ref, bf16[4096,128]{1,0:T(8,128)(2,1)S(1)} %get-tuple-element.36.kv_ref, ...), custom_call_target="tpu_custom_call" | custom-call | flops 6000000000 | bytes 4194304 | tf_op jit(solution)/shard_map/pallas_call | solution.py:332
  171.4 0.0 collective-permute-done.9.refs_2_
  171.4 0.0 collective-permute-done.4.refs_0_
  171.4 0.0 collective-permute-done.19.refs_6_
  171.4 0.0 collective-permute-done.18.refs_5_
  171.5 0.0 collective-permute-done.16.refs_4_
  171.5 1.1 shard_map.88
  172.6 8.7 %all-to-all-start = ((bf16[16,32,128]{2,1,0:T(8,128)(2,1)}), bf16[16,32,128]{2,1,0:T(8,128)(2,1)S(1)}, u32[]{:S(2)}, u32[]{:S(2)}) async-start(bf16[16,32,128]{2,1,0:T(8,128)(2,1)} %shard_map.88), calls=%async_computation | async-start | bytes 262144 | tf_op jit(solution)/shard_map/all_to_all | solution.py:465
  181.4 6.4 %all-to-all-done.pieces_ref = bf16[16,32,128]{2,1,0:T(8,128)(2,1)S(1)} async-done(((bf16[16,32,128]{2,1,0:T(8,128)(2,1)}), bf16[16,32,128]{2,1,0:T(8,128)(2,1)S(1)}, u32[]{:S(2)}, u32[]{:S(2)}) %all-to-all-start) | async-done | bytes 131104 | tf_op jit(solution)/shard_map/all_to_all | solution.py:465
  187.7 1.2 shard_map.89
  (3 shorter events, 0.0 us)
Async XLA Ops:
  0.0 13.3 %copy-start.3 = (s32[8192]{0:T(1024)S(1)}, s32[8192]{0:T(1024)}, u32[]{:S(2)}) copy-start(s32[8192]{0:T(1024)} %param.14) | copy-start | bytes 98308
  0.0 7.6 %copy-start.2 = (bf16[128,1024]{1,0:T(8,128)(2,1)S(1)}, bf16[128,1024]{1,0:T(8,128)(2,1)}, u32[]{:S(2)}) copy-start(bf16[128,1024]{1,0:T(8,128)(2,1)} %param.13) | copy-start | bytes 786436
  6.8 9.0 %collective-permute-start.2 = (bf16[2048,128]{1,0:T(8,128)(2,1)}, bf16[2048,128]{1,0:T(8,128)(2,1)S(1)}, u32[]{:S(2)}, u32[]{:S(2)}) collective-permute-start(bf16[2048,128]{1,0:T(8,128)(2,1)} %get-tuple-element.34), channel_id=1, source_target_pairs={{0,8},{8,0},{16,24},{24,16},{32,40},{40,32},{48,56},{56,48},{64,72... | collective-permute-start | bytes 1572872 | tf_op jit(solution)/shard_map/ppermute | solution.py:442
  7.5 1.8 collective-permute-start
  7.6 7.6 %collective-permute-start.12 = (bf16[128,1024]{1,0:T(8,128)(2,1)S(1)}, bf16[128,1024]{1,0:T(8,128)(2,1)S(1)}, u32[]{:S(2)}, u32[]{:S(2)}) collective-permute-start(bf16[128,1024]{1,0:T(8,128)(2,1)S(1)} %copy-done.2), channel_id=1, source_target_pairs={{0,4},{1,5},{2,6},{3,7},{4,0},{5,1},{6,2},{7,3},{8,12},{9,13},{10,... | collective-permute-start | bytes 786440 | tf_op jit(solution)/shard_map/ppermute | solution.py:432
  10.2 14.3 %collective-permute-start.3 = (bf16[2,64,512]{2,1,0:T(8,128)(2,1)S(1)}, bf16[2,64,512]{2,1,0:T(8,128)(2,1)S(1)}, u32[]{:S(2)}, u32[]{:S(2)}) collective-permute-start(bf16[2,64,512]{2,1,0:T(8,128)(2,1)S(1)} %pad_maximum_fusion.rest_0_), channel_id=1, source_target_pairs={{0,16},{8,24},{16,0},{24,8},{32,48},{40,56},{48,32},{56,40},{64,80... | collective-permute-start | bytes 393224 | tf_op jit(solution)/shard_map/ppermute | solution.py:438
  13.3 31.7 %collective-permute-start.1 = (bf16[2,64,512]{2,1,0:T(8,128)(2,1)S(1)}, bf16[2,64,512]{2,1,0:T(8,128)(2,1)S(1)}, u32[]{:S(2)}, u32[]{:S(2)}) collective-permute-start(bf16[2,64,512]{2,1,0:T(8,128)(2,1)S(1)} %pad_maximum_fusion.rest_0_), channel_id=1, source_target_pairs={{0,32},{8,40},{16,48},{24,56},{32,64},{40,72},{48,80},{56,88},{64,... | collective-permute-start | bytes 393224 | tf_op jit(solution)/shard_map/ppermute | solution.py:438
  14.6 30.5 %collective-permute-start.5 = (bf16[2,64,512]{2,1,0:T(8,128)(2,1)S(1)}, bf16[2,64,512]{2,1,0:T(8,128)(2,1)S(1)}, u32[]{:S(2)}, u32[]{:S(2)}) collective-permute-start(bf16[2,64,512]{2,1,0:T(8,128)(2,1)S(1)} %pad_maximum_fusion.rest_0_), channel_id=1, source_target_pairs={{0,48},{8,56},{16,32},{24,40},{32,80},{40,88},{48,64},{56,72},{64,... | collective-permute-start | bytes 393224 | tf_op jit(solution)/shard_map/ppermute | solution.py:438
  15.3 31.5 %collective-permute-start.6 = (bf16[2,64,512]{2,1,0:T(8,128)(2,1)S(1)}, bf16[2,64,512]{2,1,0:T(8,128)(2,1)S(1)}, u32[]{:S(2)}, u32[]{:S(2)}) collective-permute-start(bf16[2,64,512]{2,1,0:T(8,128)(2,1)S(1)} %pad_maximum_fusion.rest_0_), channel_id=1, source_target_pairs={{0,96},{8,104},{16,112},{24,120},{32,0},{40,8},{48,16},{56,24},{64... | collective-permute-start | bytes 393224 | tf_op jit(solution)/shard_map/ppermute | solution.py:438
  15.8 34.3 %collective-permute-start.7 = (bf16[2,64,512]{2,1,0:T(8,128)(2,1)S(1)}, bf16[2,64,512]{2,1,0:T(8,128)(2,1)S(1)}, u32[]{:S(2)}, u32[]{:S(2)}) collective-permute-start(bf16[2,64,512]{2,1,0:T(8,128)(2,1)S(1)} %pad_maximum_fusion.rest_0_), channel_id=1, source_target_pairs={{0,112},{8,120},{16,96},{24,104},{32,16},{40,24},{48,0},{56,8},{64... | collective-permute-start | bytes 393224 | tf_op jit(solution)/shard_map/ppermute | solution.py:438
  20.6 1.0 copy-start
  24.6 87.2 %collective-permute-start.11 = (bf16[2,64,512]{2,1,0:T(8,128)(2,1)S(1)}, bf16[2,64,512]{2,1,0:T(8,128)(2,1)S(1)}, u32[]{:S(2)}, u32[]{:S(2)}) collective-permute-start(bf16[2,64,512]{2,1,0:T(8,128)(2,1)S(1)} %pad_maximum_fusion.rest_0_), channel_id=1, source_target_pairs={{0,64},{8,72},{16,80},{24,88},{32,96},{40,104},{48,112},{56,120},{... | collective-permute-start | bytes 393224 | tf_op jit(solution)/shard_map/ppermute | solution.py:438
  26.4 0.7 copy-start.1
  45.0 72.3 %collective-permute-start.17 = (bf16[2,64,512]{2,1,0:T(8,128)(2,1)S(1)}, bf16[2,64,512]{2,1,0:T(8,128)(2,1)S(1)}, u32[]{:S(2)}, u32[]{:S(2)}) collective-permute-start(bf16[2,64,512]{2,1,0:T(8,128)(2,1)S(1)} %pad_maximum_fusion.rest_0_), channel_id=1, source_target_pairs={{0,80},{8,88},{16,64},{24,72},{32,112},{40,120},{48,96},{56,104},{... | collective-permute-start | bytes 393224 | tf_op jit(solution)/shard_map/ppermute | solution.py:438
  45.1 66.8 %collective-permute-start.13 = (bf16[256,1024]{1,0:T(8,128)(2,1)S(1)}, bf16[256,1024]{1,0:T(8,128)(2,1)S(1)}, u32[]{:S(2)}, u32[]{:S(2)}) collective-permute-start(bf16[256,1024]{1,0:T(8,128)(2,1)S(1)} %constant_dynamic-update-slice_fusion.refs_0_), channel_id=1, source_target_pairs={{0,1},{1,2},{2,3},{3,0},{4,5},{5,6},{6,7},{7,4},{8,9},{9,10},{10,1... | collective-permute-start | bytes 1572872 | tf_op jit(solution)/shard_map/ppermute | solution.py:446
  46.8 66.5 %collective-permute-start.14 = (bf16[256,1024]{1,0:T(8,128)(2,1)S(1)}, bf16[256,1024]{1,0:T(8,128)(2,1)S(1)}, u32[]{:S(2)}, u32[]{:S(2)}) collective-permute-start(bf16[256,1024]{1,0:T(8,128)(2,1)S(1)} %constant_dynamic-update-slice_fusion.refs_0_), channel_id=1, source_target_pairs={{0,2},{1,3},{2,0},{3,1},{4,6},{5,7},{6,4},{7,5},{8,10},{9,11},{10,... | collective-permute-start | bytes 1572872 | tf_op jit(solution)/shard_map/ppermute | solution.py:446
  50.1 67.2 %collective-permute-start.15 = (bf16[256,1024]{1,0:T(8,128)(2,1)S(1)}, bf16[256,1024]{1,0:T(8,128)(2,1)S(1)}, u32[]{:S(2)}, u32[]{:S(2)}) collective-permute-start(bf16[256,1024]{1,0:T(8,128)(2,1)S(1)} %constant_dynamic-update-slice_fusion.refs_0_), channel_id=1, source_target_pairs={{0,3},{1,0},{2,1},{3,2},{4,7},{5,4},{6,5},{7,6},{8,11},{9,8},{10,9... | collective-permute-start | bytes 1572872 | tf_op jit(solution)/shard_map/ppermute | solution.py:446
  111.8 39.3 %collective-permute-start.10 = (bf16[2,72,512]{2,1,0:T(8,128)(2,1)S(1)}, bf16[2,72,512]{2,1,0:T(8,128)(2,1)S(1)}, u32[]{:S(2)}, u32[]{:S(2)}) collective-permute-start(bf16[2,72,512]{2,1,0:T(8,128)(2,1)S(1)} %get-tuple-element.42), channel_id=1, source_target_pairs={{96,0},{104,8},{112,16},{120,24},{0,32},{8,40},{16,48},{24,56},{32... | collective-permute-start | bytes 442376 | tf_op jit(solution)/shard_map/ppermute | solution.py:460
  111.9 42.2 %collective-permute-start.8 = (bf16[2,72,512]{2,1,0:T(8,128)(2,1)S(1)}, bf16[2,72,512]{2,1,0:T(8,128)(2,1)S(1)}, u32[]{:S(2)}, u32[]{:S(2)}) collective-permute-start(bf16[2,72,512]{2,1,0:T(8,128)(2,1)S(1)} %get-tuple-element.40), channel_id=1, source_target_pairs={{32,0},{40,8},{48,16},{56,24},{64,32},{72,40},{80,48},{88,56},{96,... | collective-permute-start | bytes 442376 | tf_op jit(solution)/shard_map/ppermute | solution.py:460
  113.3 58.1 %collective-permute-start.9 = (bf16[2,72,512]{2,1,0:T(8,128)(2,1)S(1)}, bf16[2,72,512]{2,1,0:T(8,128)(2,1)S(1)}, u32[]{:S(2)}, u32[]{:S(2)}) collective-permute-start(bf16[2,72,512]{2,1,0:T(8,128)(2,1)S(1)} %get-tuple-element.41), channel_id=1, source_target_pairs={{48,0},{56,8},{32,16},{40,24},{80,32},{88,40},{64,48},{72,56},{112... | collective-permute-start | bytes 442376 | tf_op jit(solution)/shard_map/ppermute | solution.py:460
  117.3 54.1 %collective-permute-start.4 = (bf16[2,72,512]{2,1,0:T(8,128)(2,1)S(1)}, bf16[2,72,512]{2,1,0:T(8,128)(2,1)S(1)}, u32[]{:S(2)}, u32[]{:S(2)}) collective-permute-start(bf16[2,72,512]{2,1,0:T(8,128)(2,1)S(1)} %shard_map.84), channel_id=1, source_target_pairs={{16,0},{24,8},{0,16},{8,24},{48,32},{56,40},{32,48},{40,56},{80,64... | collective-permute-start | bytes 442376 | tf_op jit(solution)/shard_map/ppermute | solution.py:460
  148.3 23.1 %collective-permute-start.19 = (bf16[2,72,512]{2,1,0:T(8,128)(2,1)S(1)}, bf16[2,72,512]{2,1,0:T(8,128)(2,1)S(1)}, u32[]{:S(2)}, u32[]{:S(2)}) collective-permute-start(bf16[2,72,512]{2,1,0:T(8,128)(2,1)S(1)} %get-tuple-element.49), channel_id=1, source_target_pairs={{80,0},{88,8},{64,16},{72,24},{112,32},{120,40},{96,48},{104,56},{... | collective-permute-start | bytes 442376 | tf_op jit(solution)/shard_map/ppermute | solution.py:460
  151.0 20.4 %collective-permute-start.18 = (bf16[2,72,512]{2,1,0:T(8,128)(2,1)S(1)}, bf16[2,72,512]{2,1,0:T(8,128)(2,1)S(1)}, u32[]{:S(2)}, u32[]{:S(2)}) collective-permute-start(bf16[2,72,512]{2,1,0:T(8,128)(2,1)S(1)} %get-tuple-element.47), channel_id=1, source_target_pairs={{64,0},{72,8},{80,16},{88,24},{96,32},{104,40},{112,48},{120,56},{... | collective-permute-start | bytes 442376 | tf_op jit(solution)/shard_map/ppermute | solution.py:460
  154.1 17.4 %collective-permute-start.16 = (bf16[2,72,512]{2,1,0:T(8,128)(2,1)S(1)}, bf16[2,72,512]{2,1,0:T(8,128)(2,1)S(1)}, u32[]{:S(2)}, u32[]{:S(2)}) collective-permute-start(bf16[2,72,512]{2,1,0:T(8,128)(2,1)S(1)} %get-tuple-element.45), channel_id=1, source_target_pairs={{112,0},{120,8},{96,16},{104,24},{16,32},{24,40},{0,48},{8,56},{48... | collective-permute-start | bytes 442376 | tf_op jit(solution)/shard_map/ppermute | solution.py:460
  172.6 15.1 %all-to-all-start = ((bf16[16,32,128]{2,1,0:T(8,128)(2,1)}), bf16[16,32,128]{2,1,0:T(8,128)(2,1)S(1)}, u32[]{:S(2)}, u32[]{:S(2)}) async-start(bf16[16,32,128]{2,1,0:T(8,128)(2,1)} %shard_map.88), calls=%async_computation | async-start | bytes 262144 | tf_op jit(solution)/shard_map/all_to_all | solution.py:465

commit v5 on v4

--- a/solution.py
+++ b/solution.py
@@ -12,6 +12,7 @@
 TILES = 4
 SLOTS = 2
 ROWS = 2 * BLOCK
+FAR = 64
 KEY_BLOCKS = 32
 ACC_ROWS = 72
 LOG2E = 1.4426950408889634
@@ -22,53 +23,67 @@
 VMEM = pl.BlockSpec(memory_space=pltpu.VMEM)
 
 
-def list_work(me, pos_ref, mask_ref, code_ref, listed_all):
+def list_work(me, pos_ref, mask_ref, code_ref):
     half = KEY_BLOCKS // 2
-    pairs = code_ref.shape[0]
+    both = 2 * KEY_BLOCKS
+    blocks = pos_ref.shape[0]
 
     def held(t):
-        return jnp.where(t < half, me * half, jnp.bitwise_xor(me, 1) * half - half) + t
+        source = jnp.bitwise_xor(me, lax.shift_right_logical(t, 4))
+        return source * half + jnp.bitwise_and(t, half - 1)
+
+    spots = pos_ref[...].T
+    own_block = lax.shift_right_logical(spots, 7)
+    furthest = jnp.max(own_block, axis=0, keepdims=True)
+    t_rows = lax.broadcasted_iota(jnp.int32, (both, blocks), 0)
+    own = jnp.zeros((both, blocks), jnp.int32)
+    for t in range(both):
+        found = jnp.max((own_block == held(jnp.int32(t))).astype(jnp.int32), axis=0, keepdims=True)
+        own = jnp.where(t_rows == t, found, own)
+
+    def exact(condition):
+        return condition.astype(jnp.float32).astype(jnp.bfloat16)
 
     columns = mask_ref.shape[1]
-    at = lax.broadcasted_iota(jnp.int32, (columns, BLOCK), 0)
-    lane = lax.broadcasted_iota(jnp.int32, (columns, BLOCK), 1)
-    pick = ((at == held(lane)) & (lane < KEY_BLOCKS)).astype(jnp.float32).astype(jnp.bfloat16)
-    listed = (mask_ref[...] == 1).astype(jnp.float32).astype(jnp.bfloat16)
-    listed_all[...] = jnp.dot(listed, pick, preferred_element_type=jnp.float32)
-
-    lane = lax.broadcasted_iota(jnp.int32, (pairs, BLOCK), 1)
-    value = jnp.full((pairs, BLOCK), 4 * KEY_BLOCKS, jnp.int32) + lane
-    active = jnp.zeros((pairs, BLOCK), jnp.bool_)
+    pick = exact(
+        lax.broadcasted_iota(jnp.int32, (both, columns), 1)
+        == held(lax.broadcasted_iota(jnp.int32, (both, columns), 0))
+    )
+    listed = lax.dot_general(
+        pick, exact(mask_ref[...] == 1), (((1,), (1,)), ((), ())), preferred_element_type=jnp.float32
+    )
+    active = exact((own > 0) | ((listed > 0.5) & (held(t_rows) <= furthest)))
+    listed = exact(listed > 0.5)
+
+    row = lax.broadcasted_iota(jnp.int32, (blocks, BLOCK), 0)
+    col = lax.broadcasted_iota(jnp.int32, (blocks, BLOCK), 1)
+    first, second = exact(row == 2 * col), exact(row == 2 * col + 1)
+    active = jnp.dot(active, first + second, preferred_element_type=jnp.float32) > 0.5
+    listed = [jnp.dot(listed, pairs, preferred_element_type=jnp.float32).astype(jnp.int32) for pairs in (first, second)]
+    row = lax.broadcasted_iota(jnp.int32, (both, both), 0)
+    col = lax.broadcasted_iota(jnp.int32, (both, both), 1)
+    earlier = exact((col < row) & (lax.shift_right_logical(row, 5) == lax.shift_right_logical(col, 5)))
+    place = jnp.dot(earlier, exact(active), preferred_element_type=jnp.float32).astype(jnp.int32)
+    t_rows = lax.broadcasted_iota(jnp.int32, (both, BLOCK), 0)
+    value = jnp.bitwise_and(t_rows, KEY_BLOCKS - 1) + KEY_BLOCKS * (listed[0] + 2 * listed[1] + 4)
+    packed = jnp.where(active, place * 512 + value, -1)
+    ones = active.astype(jnp.int32)
+    slot_rows = lax.broadcasted_iota(jnp.int32, (KEY_BLOCKS, BLOCK), 0)
+    tables = []
     for n in range(2):
-        spots = pos_ref[pl.ds(n, pairs, stride=2), :]
-        listed = listed_all[pl.ds(n, pairs, stride=2), :] > 0.5
-        blocks = lax.shift_right_logical(spots, 7)
-        own = jnp.zeros((pairs, BLOCK), jnp.int32)
-        for t in range(KEY_BLOCKS):
-            any_own = jnp.max((blocks == held(t)).astype(jnp.int32), axis=1, keepdims=True)
-            own = jnp.where(lane == t, any_own, own)
-        reached = held(lane) * BLOCK <= jnp.max(spots, axis=1, keepdims=True)
-        active = active | (own > 0) | (listed & reached)
-        value = value + jnp.where(listed, (n + 1) * KEY_BLOCKS, 0)
-    active = active & (lane < KEY_BLOCKS)
-    ones = active.astype(jnp.float32)
-    row = lax.broadcasted_iota(jnp.int32, (BLOCK, BLOCK), 0)
-    col = lax.broadcasted_iota(jnp.int32, (BLOCK, BLOCK), 1)
-    earlier = (row < col).astype(jnp.float32).astype(jnp.bfloat16)
-    place = jnp.dot(ones.astype(jnp.bfloat16), earlier, preferred_element_type=jnp.float32).astype(jnp.int32)
-    packed = jnp.where(active, place * 512 + value, -1)
-    codes = jnp.zeros((pairs, BLOCK), jnp.int32)
-    for t in range(KEY_BLOCKS):
-        one = packed[:, t : t + 1]
-        codes = jnp.where(lax.shift_right_arithmetic(one, 9) == lane, jnp.bitwise_and(one, 511), codes)
-    count = jnp.sum(ones, axis=1, keepdims=True).astype(jnp.int32)
-    slots = jnp.maximum(lax.shift_right_logical(count + (TILES - 1), 2), 1)
-    code_ref[...] = jnp.where(lane == KEY_BLOCKS, slots, codes)
+        codes = jnp.zeros((KEY_BLOCKS, BLOCK), jnp.int32)
+        for t in range(n * KEY_BLOCKS, (n + 1) * KEY_BLOCKS):
+            one = packed[t : t + 1, :]
+            codes = jnp.where(lax.shift_right_arithmetic(one, 9) == slot_rows, jnp.bitwise_and(one, 511), codes)
+        count = jnp.sum(ones[n * KEY_BLOCKS : (n + 1) * KEY_BLOCKS], axis=0, keepdims=True)
+        slots = jnp.maximum(lax.shift_right_logical(count + (TILES - 1), 2), 1)
+        tables += [codes, jnp.broadcast_to(slots, (FAR - KEY_BLOCKS, BLOCK))]
+    code_ref[...] = jnp.concatenate(tables, 0).T[: code_ref.shape[0]]
 
 
 def front_kernel(seq_ref, lat_hbm, x_hbm, wq_hbm, wk_hbm, wv_hbm, pos_hbm, mask_hbm, *rest):
     mine_ref, theirs_ref, own_ref, other_ref, code_ref = rest[:5]
-    lat, x, wq, wk, wv, pos, mask, w_all, listed_all, sems, x_sems = rest[5:]
+    lat, x, wq, wk, wv, pos, mask, w_all, sems, x_sems = rest[5:]
     small = [
         pltpu.make_async_copy(source, target, sems.at[i])
         for i, (source, target) in enumerate(
@@ -85,7 +100,7 @@
 
     got_pos.wait()
     got_mask.wait()
-    list_work(seq_ref[0], pos, mask, code_ref, listed_all)
+    list_work(seq_ref[0], pos, mask, code_ref)
 
     got_wq.wait()
     got_lat.wait()
@@ -123,7 +138,6 @@
         scratch_shapes=[pltpu.VMEM(a.shape, a.dtype) for a in operands]
         + [
             pltpu.VMEM((width, 4 * HS), jnp.bfloat16),
-            pltpu.VMEM(spots.shape, jnp.float32),
             pltpu.SemaphoreType.DMA((6,)),
             pltpu.SemaphoreType.DMA((4,)),
         ],
@@ -134,11 +148,13 @@
     )(seq, *operands)
 
 
-def prepare_kernel(own_ref, partner_ref, kv_ref, vt_ref, norm_ref):
+def prepare_kernel(*refs):
+    sources, (kv_ref, vt_ref, norm_ref) = refs[:-3], refs[-3:]
+    each = KEY_BLOCKS // len(sources)
     most = None
     for t in range(KEY_BLOCKS):
-        source, at = (own_ref, t) if t < KEY_BLOCKS // 2 else (partner_ref, t - KEY_BLOCKS // 2)
-        tile = source[at * BLOCK : (at + 1) * BLOCK, :]
+        at = t % each
+        tile = sources[t // each][at * BLOCK : (at + 1) * BLOCK, :]
         kv_ref[t * BLOCK : (t + 1) * BLOCK, :] = tile
         turned = tile.T
         vt_ref[:HS, t * BLOCK : (t + 1) * BLOCK] = turned[HS:, :]
@@ -149,30 +165,33 @@
     norm_ref[0] = jnp.max(most)
 
 
-def prepare(own, partner):
-    keys = 2 * own.shape[0]
+def prepare(*sources):
+    keys = sum(source.shape[0] for source in sources)
     return pl.pallas_call(
         prepare_kernel,
-        in_specs=[VMEM, VMEM],
+        in_specs=[VMEM] * len(sources),
         out_specs=[VMEM, VMEM, SMEM],
         out_shape=[
             jax.ShapeDtypeStruct((keys, 2 * HS), jnp.bfloat16),
             jax.ShapeDtypeStruct((ACC_ROWS, keys), jnp.bfloat16),
             jax.ShapeDtypeStruct((1,), jnp.float32),
         ],
-        compiler_params=pltpu.CompilerParams(vmem_limit_bytes=32 * 2**20),
-    )(own, partner)
-
-
-def attention_kernel(steps, takes, seq_ref, code_ref, norm_ref, pos_ref, kv_ref, vt_ref, *rest):
+        compiler_params=pltpu.CompilerParams(vmem_limit_bytes=24 * 2**20),
+    )(*sources)
+
+
+def attention_kernel(steps, far, seq_ref, code_ref, norm_ref, pos_ref, kv_ref, vt_ref, *rest):
     chips = len(steps)
-    q_refs, o_refs = rest[:takes], rest[takes : takes + chips]
-    q_all, p_a, p_b, s_all, acc = rest[takes + chips :]
+    q_refs, rest = rest[:chips], rest[chips:]
+    before_refs, rest = (rest[:chips], rest[chips:]) if far else (None, rest)
+    o_refs, (q_all, p_a, p_b, s_all, acc) = rest[:chips], rest[chips:]
+    table = FAR if far else 0
     blocks = 4 * chips
     me = seq_ref[0]
-    own_base = me * (KEY_BLOCKS // 2 * BLOCK)
-    partner_base = jnp.bitwise_xor(me, 1) * (KEY_BLOCKS // 2 * BLOCK)
-    sources = [came_from(me, *step) for step in steps]
+    keys_of = jnp.bitwise_xor(me, 2) if far else me
+    own_base = keys_of * (KEY_BLOCKS // 2 * BLOCK)
+    partner_base = jnp.bitwise_xor(keys_of, 1) * (KEY_BLOCKS // 2 * BLOCK)
+    sources = [came_from(me, step) for step in steps]
     iota = lax.broadcasted_iota(jnp.int32, (BLOCK, ROWS), 0)
     in_first = lax.broadcasted_iota(jnp.int32, (1, ROWS), 1) < BLOCK
     iota_half = iota.astype(jnp.float32).astype(jnp.bfloat16)
@@ -207,7 +226,7 @@
         return jnp.concatenate([q, jnp.zeros_like(q)], 0)
 
     def key_blocks(row, c):
-        return [jnp.bitwise_and(code_ref[row, c * TILES + t], KEY_BLOCKS - 1) for t in range(TILES)]
+        return [jnp.bitwise_and(code_ref[row, table + c * TILES + t], KEY_BLOCKS - 1) for t in range(TILES)]
 
     def products(row, r, c):
         keys = jnp.concatenate([kv_ref[pl.ds(offset(k), BLOCK), :] for k in key_blocks(row, c)], 0)
@@ -217,7 +236,7 @@
         return jnp.concatenate([vt_ref[:, pl.ds(offset(k), BLOCK)] for k in key_blocks(row, c)], 1)
 
     def last_key(row, c, t, pos, real):
-        code = code_ref[row, c * TILES + t]
+        code = code_ref[row, table + c * TILES + t]
         k = jnp.bitwise_and(code, KEY_BLOCKS - 1)
         half = KEY_BLOCKS // 2
         base = jnp.where(k < half, own_base, partner_base - half * BLOCK) + k * BLOCK
@@ -227,17 +246,23 @@
         ahead = pos - base
         return jnp.where(ahead < reach, jnp.minimum(ahead, BLOCK - 1), -1)
 
-    def store(r, a, top):
-        total = a[HS : HS + 1]
+    def put(i, rr, a, top):
+        at = (lax.div(rr, 2), slice(None), pl.ds(row_offset(lax.rem(rr, 2)), ROWS))
+        if far:
+            before = before_refs[i][at].astype(jnp.float32)
+            top_before, top_now = before[HS + 1 : HS + 2], top
+            top = jnp.maximum(top_before, top_now)
+            shrink, shrink_before = jnp.exp(top_now - top), jnp.exp(top_before - top)
+            total = a[HS : HS + 1] * shrink + (before[HS : HS + 1] + before[HS + 2 : HS + 3]) * shrink_before
+            a = a * shrink + before * shrink_before
+        else:
+            total = a[HS : HS + 1]
         low = total - total.astype(jnp.bfloat16).astype(jnp.float32)
-        out = jnp.concatenate([a[: HS + 1], top, low, a[HS + 3 :]], 0).astype(jnp.bfloat16)
-        return out
-
-    def put(i, rr, out):
-        o_refs[i][lax.div(rr, 2), :, pl.ds(row_offset(lax.rem(rr, 2)), ROWS)] = out
+        out = jnp.concatenate([a[:HS], total, top, low, a[HS + 3 :]], 0)
+        o_refs[i][at] = out.astype(jnp.bfloat16)
 
     def advance(r, c):
-        last = c + 1 >= code_ref[whole_block(clamp(r)), KEY_BLOCKS]
+        last = c + 1 >= code_ref[whole_block(clamp(r)), table + KEY_BLOCKS]
         return jnp.where(last, jnp.minimum(r + 1, blocks), r), jnp.where(last, 0, c + 1)
 
     def step_slots(r, c):
@@ -283,14 +308,14 @@
             add(p_b, slots_1)
             return r2, c2, r3, c3
 
-        items = lax.fori_loop(0, blocks, lambda r, n: n + code_ref[whole_block(r), KEY_BLOCKS], jnp.int32(0))
+        items = lax.fori_loop(0, blocks, lambda r, n: n + code_ref[whole_block(r), table + KEY_BLOCKS], jnp.int32(0))
         turns = lax.div(items + (2 * SLOTS - 1), 2 * SLOTS)
         lax.fori_loop(0, turns, two_steps, (jnp.int32(0), jnp.int32(0), r0, c0))
 
         for i in range(chips):
             def finish(rr, _, i=i):
                 a = acc[i * 4 + rr]
-                put(i, rr, store(rr, a, jnp.where(a[HS : HS + 1] > 0, 0.0, lowest_max)))
+                put(i, rr, a, jnp.where(a[HS : HS + 1] > 0, 0.0, lowest_max))
                 return 0
 
             lax.fori_loop(0, 4, finish, 0)
@@ -319,19 +344,20 @@
                     return best
 
                 start = jnp.full((1, ROWS), lowest_max, jnp.bfloat16).astype(jnp.float32)
-                top = lax.fori_loop(0, code_ref[row, KEY_BLOCKS], one_slot, start)
-                put(i, rr, store(rr, acc[0], top))
+                top = lax.fori_loop(0, code_ref[row, table + KEY_BLOCKS], one_slot, start)
+                put(i, rr, acc[0], top)
                 return 0
 
             lax.fori_loop(0, 4, one_block, 0)
 
 
-def attend(steps, seq, codes, norm, spots, kv, vt, queries):
+def attend(steps, seq, codes, spots, held, queries, before=()):
+    kv, vt, norm = held
     chips = len(steps)
     out = jax.ShapeDtypeStruct((2, ACC_ROWS, queries[0].shape[2]), jnp.bfloat16)
     return pl.pallas_call(
-        functools.partial(attention_kernel, steps, len(queries)),
-        in_specs=[SMEM] * 3 + [VMEM] * (3 + len(queries)),
+        functools.partial(attention_kernel, steps, bool(before)),
+        in_specs=[SMEM] * 3 + [VMEM] * (3 + len(queries) + len(before)),
         out_specs=[VMEM] * chips,
         out_shape=[out] * chips,
         scratch_shapes=[
@@ -345,7 +371,7 @@
         cost_estimate=pl.CostEstimate(
             flops=chips * 6 * 10**9, bytes_accessed=4 * 2**20, transcendentals=chips * 2**20
         ),
-    )(seq, codes, norm, spots, kv, vt, *queries)
+    )(seq, codes, norm, spots, kv, vt, *queries, *before)
 
 
 def combine_kernel(core_ref, *refs):
@@ -407,21 +433,18 @@
     )(grp, pieces, *w_turns)
 
 
-def shifted(x_by, y_by):
-    return [(s, ((s // 4 + x_by) % 4) * 4 + (s % 4 ^ 2 * y_by)) for s in range(16)]
-
-
-def back(route):
-    return [(b, a) for a, b in route]
-
-
-def came_from(s, x_by, y_by):
-    moved = jnp.bitwise_and(s - 4 * x_by, 12)
-    return moved + jnp.bitwise_xor(jnp.bitwise_and(s, 3), 2 * y_by)
-
-
-CALLS = (((0, 1),), ((1, 0), (1, 1), (3, 0), (3, 1)), ((2, 0), (2, 1)), ((0, 0),))
-SWAP = [(i, i ^ 1) for i in range(16)]
+def along_x(by):
+    return [(s, (s + 4 * by) % 16) for s in range(16)]
+
+
+def came_from(s, by):
+    return jnp.bitwise_and(s - 4 * by, 15)
+
+
+NEAR_CALLS = ((0,), (1, 3, 2))
+FAR_CALLS = ((2, 1, 3), (0,))
+CORE_SWAP = [(s, s ^ 1) for s in range(16)]
+Y_SWAP = [(s, s ^ 2) for s in range(16)]
 
 
 def body(inputs, latents, w_query, w_key, w_value, w_out, positions, block_mask):
@@ -429,37 +452,44 @@
     grp = lax.axis_index("grp")[None]
     core = jnp.bitwise_and(seq, 1)
 
-    w_other = lax.ppermute(w_out, "grp", [(g, g ^ 4) for g in range(8)])
     mine, theirs, kv_own, kv_other, codes = front(
         seq, latents, inputs, w_query, w_key, w_value, positions, block_mask
     )
-    q_chip = jnp.stack([mine, lax.ppermute(theirs, "seq", SWAP)])
-    arrived = {
-        step: q_chip if step == (0, 0) else lax.ppermute(q_chip, "seq", shifted(*step))
-        for call in CALLS
-        for step in call
-    }
-    kv, vt, norm = prepare(kv_own, lax.ppermute(kv_other, "seq", SWAP))
-
-    w_pair = jnp.concatenate([w_out, w_other], 0)
+    q_chip = jnp.stack([mine, lax.ppermute(theirs, "seq", CORE_SWAP)])
+    queries = {by: q_chip if by == 0 else lax.ppermute(q_chip, "seq", along_x(by)) for by in (0, 1, 3, 2)}
+    kv_partner = lax.ppermute(kv_other, "seq", CORE_SWAP)
+    near = prepare(kv_own, kv_partner)
+    kv_far = [lax.ppermute(kv, "seq", Y_SWAP) for kv in (kv_own, kv_partner)]
+
+    w_other = lax.ppermute(w_out, "grp", [(g, g ^ 4) for g in range(8)])
+    spots = positions.reshape(-1, ROWS)
+    near_parts = dict(zip(NEAR_CALLS[0], attend(NEAR_CALLS[0], seq, codes, spots, near, [q_chip])))
+    w_pair, near_parts[0] = lax.optimization_barrier((jnp.concatenate([w_out, w_other], 0), near_parts[0]))
     w_turns = [w_pair] + [
         lax.ppermute(w_pair, "grp", [(g, (g & 4) | ((g + k) & 3)) for g in range(8)]) for k in (1, 2, 3)
     ]
-    arrived[2, 0], w_turns = lax.optimization_barrier((arrived[2, 0], w_turns))
-
-    spots = positions.reshape(-1, ROWS)
-    parts = []
-    for call in CALLS:
-        if parts:
-            arrived[call[0]], parts[-1] = lax.optimization_barrier((arrived[call[0]], parts[-1]))
-        done = attend(call, seq, codes, norm, spots, kv, vt, [arrived[step] for step in call])
-        parts += done
-
-    order = [step for call in CALLS for step in call]
-    parts = [
-        part if step == (0, 0) else lax.ppermute(part, "seq", back(shifted(*step)))
-        for step, part in zip(order, parts)
-    ]
+
+    parts = {}
+    last = 0
+    for call in NEAR_CALLS[1:]:
+        queries[call[0]], near_parts[last], kv_far[0] = lax.optimization_barrier(
+            (queries[call[0]], near_parts[last], kv_far[0])
+        )
+        near_parts.update(zip(call, attend(call, seq, codes, spots, near, [queries[by] for by in call])))
+        last = call[-1]
+    kv_far, w_turns, near_parts[last] = lax.optimization_barrier((kv_far, w_turns, near_parts[last]))
+    far = prepare(*kv_far)
+    last = None
+    for call in FAR_CALLS:
+        if last is not None:
+            queries[call[0]], parts[last] = lax.optimization_barrier((queries[call[0]], parts[last]))
+        done = attend(
+            call, seq, codes, spots, far, [queries[by] for by in call], [near_parts[by] for by in call]
+        )
+        parts.update(zip(call, done))
+        last = call[-1]
+
+    parts = [part if by == 0 else lax.ppermute(part, "seq", along_x(-by)) for by, part in parts.items()]
     pieces = combine(core, parts)
     owners = [[(4 * x + 2 * y + c) * 8 + g for c in range(2) for g in range(8)] for x in range(4) for y in range(2)]
     pieces = lax.all_to_all(pieces, ("seq", "grp"), 0, 0, axis_index_groups=owners)

time: 190 us -> 175 us (0.921)
  starting transfers between devices: 40.1 us -> 28.3 us
    ppermute x16 -> x10, starting transfers between devices: 24.3 us -> 14.3 us  [the longest x2 6 us: body(): kv_far = [lax.ppermute(kv, 'seq', Y_SWAP) for kv in (kv_own, kv_partner)]]
    ppermute x16 -> x10, waiting for transfers between devices: 2.43 us -> 0.03 us  [the longest x3 0.01 us: body(): lax.ppermute(q_chip, 'seq', along_x(by))]
    pallas_call x5 -> x6, Pallas kernels: 128 us -> 127 us  [the longest x4 125 us: attend(): pl.pallas_call(functools.partial(attention_kernel, steps, bool(before)),...]
  transfers between devices with their start and end apart: 21 -> 15, of which waited for: 3 -> 2; matrix products, arithmetic and copies ran while one was open for 0% -> 1% of each run, Pallas kernels for 68% -> 47%
where the time goes in v5:
time: 175 us; the launch traced here: 174 us
  Pallas kernels  136 us (78%)
  starting transfers between devices  28.3 us (16%)
  waiting for transfers between devices  6.95 us (4%)
  local copies, waits for them, and re-layouts  1.76 us (1%)
    pallas_call x4, Pallas kernels, attend(): pl.pallas_call(functools.partial(attention_kernel, steps, bool(before)),...  125 us
    all_to_all x1, starting transfers between devices, body(): lax.all_to_all(pieces, ('seq', 'grp'), 0, 0, axis_index_groups=owners)  6.98 us
    pallas_call x1, Pallas kernels, front(): pl.pallas_call(front_kernel, in_specs=[SMEM] + [pl.BlockSpec(memory_space...  6.81 us
    all_to_all x1, waiting for transfers between devices, body(): lax.all_to_all(pieces, ('seq', 'grp'), 0, 0, axis_index_groups=owners)  6.35 us
    ppermute x2, starting transfers between devices, body(): kv_far = [lax.ppermute(kv, 'seq', Y_SWAP) for kv in (kv_own, kv_partner)]  6 us
    ppermute x3, starting transfers between devices, body(): lax.ppermute(w_pair, 'grp', [(g, g & 4 | g + k & 3) for g in range(8)])  5.74 us
    ppermute x3, starting transfers between devices, body(): lax.ppermute(part, 'seq', along_x(-by))  3.72 us
  transfers between devices with their start and end apart: 15, of which 2 were waited for; matrix products, arithmetic and copies ran while one was open for 1% of the time, Pallas kernels for 47%

profile of v5, /device:TPU:3, one launch (start us, length us, event | category | flops | bytes accessed | tf_op | source)
XLA Modules:
  0.0 173.6 jit_solution(14129889467153347642)
XLA Ops:
  0.0 0.0 copy-start.3
  0.0 0.0 copy-start.2
  0.0 6.8 %shard_map.82 = (bf16[64,512]{1,0:T(8,128)(2,1)}, bf16[64,512]{1,0:T(8,128)(2,1)}, bf16[2048,128]{1,0:T(8,128)(2,1)}, bf16[2048,128]{1,0:T(8,128)(2,1)}, s32[32,128]{1,0:T(8,128)}) custom-call(s32[1]{0:T(128)} %bitcast.1.seq_ref, bf16[512,1024]{1,0:T(8,128)(2,1)} %lat_hbm.1, bf16[2048,1024]{1,0:T(8,128)(2,1)} %x_hbm.1, bf16[1024,128]{1,0:T(8,128)(2,1)} %wq_hbm.1, ...), custom_call_target="tpu_custom_call" | custom-call | flops 1207959552 | bytes 6291456 | tf_op jit(solution)/shard_map/pallas_call | solution.py:133
  6.8 0.8 collective-permute-start.3
  7.6 0.0 copy-done.2
  7.6 1.3 collective-permute-start.2
  8.9 0.4 collective-permute-start
  9.3 2.6 %collective-permute-start.4 = (bf16[2048,128]{1,0:T(8,128)(2,1)}, bf16[2048,128]{1,0:T(8,128)(2,1)S(1)}, u32[]{:S(2)}, u32[]{:S(2)}) collective-permute-start(bf16[2048,128]{1,0:T(8,128)(2,1)} %get-tuple-element.39.refs_0_), channel_id=1, source_target_pairs={{0,16},{8,24},{16,0},{24,8},{32,48},{40,56},{48,32},{56,40},{64,80... | collective-permute-start | bytes 1572872 | tf_op jit(solution)/shard_map/ppermute | solution.py:462
  11.9 0.0 copy-done.3
  11.9 0.0 collective-permute-done
  11.9 0.9 pad_maximum_fusion.1.rest_0_
  12.8 1.3 collective-permute-start.1
  14.0 0.8 collective-permute-start.10
  14.9 0.6 collective-permute-done.2
  15.4 1.3 collective-permute-start.9
  16.8 0.0 collective-permute-done.3.refs_1_
  16.8 0.0 copy-start
  16.8 1.0 copy-done
  17.8 1.0 shard_map.83
  18.9 0.0 copy-start.1
  18.9 0.7 copy-done.1
  19.6 16.3 %shard_map.84.rest_1_ = bf16[2,72,512]{2,1,0:T(8,128)(2,1)S(1)} custom-call(s32[1]{0:T(128)} %bitcast.1.seq_ref, s32[32,128]{1,0:T(8,128)S(1)} %copy-done.1, f32[1]{0:T(128)} %get-tuple-element.41.norm_ref, s32[32,256]{1,0:T(8,128)S(1)} %reshape.7.pos_ref, bf16[4096,128]{1,0:T(8,128)(2,1)S(1)} %get-tuple-element.42.kv_ref, ...), custom_call_target="tpu_custom_call" | custom-call | flops 6000000000 | bytes 4194304 | tf_op jit(solution)/shard_map/pallas_call | solution.py:358
  35.9 1.7 collective-permute-start.6
  37.6 0.0 collective-permute-done.1.rest_0_.rest_1_
  37.6 3.3 %collective-permute-start.7 = (bf16[256,1024]{1,0:T(8,128)(2,1)S(1)}, bf16[256,1024]{1,0:T(8,128)(2,1)S(1)}, u32[]{:S(2)}, u32[]{:S(2)}) collective-permute-start(bf16[256,1024]{1,0:T(8,128)(2,1)S(1)} %pad_maximum_fusion.refs_0_), channel_id=1, source_target_pairs={{0,2},{1,3},{2,0},{3,1},{4,6},{5,7},{6,4},{7,5},{8,10},{9,11},{10,... | collective-permute-start | bytes 1572872 | tf_op jit(solution)/shard_map/ppermute | solution.py:469
  40.9 0.0 collective-permute-done.4.refs_0_
  40.9 0.7 collective-permute-start.8
  41.6 0.0 collective-permute-done.10.rest_2_.rest_0_
  41.6 3.4 %collective-permute-start.5 = (bf16[2048,128]{1,0:T(8,128)(2,1)S(1)}, bf16[2048,128]{1,0:T(8,128)(2,1)S(1)}, u32[]{:S(2)}, u32[]{:S(2)}) collective-permute-start(bf16[2048,128]{1,0:T(8,128)(2,1)S(1)} %collective-permute-done.3.refs_1_), channel_id=1, source_target_pairs={{0,16},{8,24},{16,0},{24,8},{32,48},{40,56},{48,32},{56,40},{64,80... | collective-permute-start | bytes 1572872 | tf_op jit(solution)/shard_map/ppermute | solution.py:462
  45.0 0.0 collective-permute-done.9.rest_1_.rest_2_
  45.0 46.0 %shard_map.85 = (bf16[2,72,512]{2,1,0:T(8,128)(2,1)S(1)}, bf16[2,72,512]{2,1,0:T(8,128)(2,1)S(1)}, bf16[2,72,512]{2,1,0:T(8,128)(2,1)S(1)}) custom-call(s32[1]{0:T(128)} %bitcast.1.seq_ref, s32[32,128]{1,0:T(8,128)S(1)} %copy-done.1, f32[1]{0:T(128)} %get-tuple-element.41.norm_ref, s32[32,256]{1,0:T(8,128)S(1)} %reshape.7.pos_ref, ...), custom_call_target="tpu_custom_call" | custom-call | flops 17999998976 | bytes 4194304 | tf_op jit(solution)/shard_map/pallas_call | solution.py:358
  91.0 0.0 collective-permute-done.6.refs_1_
  91.0 0.0 collective-permute-done.7.refs_2_
  91.0 0.0 collective-permute-done.8.refs_3_
  91.0 0.0 collective-permute-done.5.refs_1_
  91.0 1.0 shard_map.86
  92.1 44.3 %shard_map.87 = (bf16[2,72,512]{2,1,0:T(8,128)(2,1)S(1)}, bf16[2,72,512]{2,1,0:T(8,128)(2,1)S(1)}, bf16[2,72,512]{2,1,0:T(8,128)(2,1)S(1)}) custom-call(s32[1]{0:T(128)} %bitcast.1.seq_ref, s32[32,128]{1,0:T(8,128)S(1)} %copy-done.1, f32[1]{0:T(128)} %get-tuple-element.51.norm_ref, s32[32,256]{1,0:T(8,128)S(1)} %reshape.7.pos_ref, ...), custom_call_target="tpu_custom_call" | custom-call | flops 17999998976 | bytes 4194304 | tf_op jit(solution)/shard_map/pallas_call | solution.py:358
  136.4 1.7 %collective-permute-start.13 = (bf16[2,72,512]{2,1,0:T(8,128)(2,1)S(1)}, bf16[2,72,512]{2,1,0:T(8,128)(2,1)S(1)}, u32[]{:S(2)}, u32[]{:S(2)}) collective-permute-start(bf16[2,72,512]{2,1,0:T(8,128)(2,1)S(1)} %get-tuple-element.60), channel_id=1, source_target_pairs={{0,32},{8,40},{16,48},{24,56},{32,64},{40,72},{48,80},{56,88},{64,... | collective-permute-start | bytes 442376 | tf_op jit(solution)/shard_map/ppermute | solution.py:492
  138.2 0.0 collective-permute-start.11
  138.2 2.0 %collective-permute-start.12 = (bf16[2,72,512]{2,1,0:T(8,128)(2,1)S(1)}, bf16[2,72,512]{2,1,0:T(8,128)(2,1)S(1)}, u32[]{:S(2)}, u32[]{:S(2)}) collective-permute-start(bf16[2,72,512]{2,1,0:T(8,128)(2,1)S(1)} %get-tuple-element.58), channel_id=1, source_target_pairs={{0,96},{8,104},{16,112},{24,120},{32,0},{40,8},{48,16},{56,24},{64... | collective-permute-start | bytes 442376 | tf_op jit(solution)/shard_map/ppermute | solution.py:492
  140.1 17.9 %shard_map.88.refs_3_ = bf16[2,72,512]{2,1,0:T(8,128)(2,1)S(1)} custom-call(s32[1]{0:T(128)} %bitcast.1.seq_ref, s32[32,128]{1,0:T(8,128)S(1)} %copy-done.1, f32[1]{0:T(128)} %get-tuple-element.51.norm_ref, s32[32,256]{1,0:T(8,128)S(1)} %reshape.7.pos_ref, bf16[4096,128]{1,0:T(8,128)(2,1)S(1)} %get-tuple-element.52.kv_ref, ...), custom_call_target="tpu_custom_call" | custom-call | flops 6000000000 | bytes 4194304 | tf_op jit(solution)/shard_map/pallas_call | solution.py:358
  158.1 0.0 collective-permute-done.13.refs_2_
  158.1 0.0 collective-permute-done.11.refs_0_
  158.1 0.0 collective-permute-done.12.refs_1_
  158.1 1.0 shard_map.89
  159.1 7.0 %all-to-all-start = ((bf16[16,32,128]{2,1,0:T(8,128)(2,1)}), bf16[16,32,128]{2,1,0:T(8,128)(2,1)S(1)}, u32[]{:S(2)}, u32[]{:S(2)}) async-start(bf16[16,32,128]{2,1,0:T(8,128)(2,1)} %shard_map.89), calls=%async_computation | async-start | bytes 262144 | tf_op jit(solution)/shard_map/all_to_all | solution.py:495
  166.1 6.4 %all-to-all-done.pieces_ref = bf16[16,32,128]{2,1,0:T(8,128)(2,1)S(1)} async-done(((bf16[16,32,128]{2,1,0:T(8,128)(2,1)}), bf16[16,32,128]{2,1,0:T(8,128)(2,1)S(1)}, u32[]{:S(2)}, u32[]{:S(2)}) %all-to-all-start) | async-done | bytes 131104 | tf_op jit(solution)/shard_map/all_to_all | solution.py:495
  172.4 1.2 shard_map.90
  (2 shorter events, 0.0 us)
Async XLA Ops:
  0.0 11.9 %copy-start.3 = (s32[8192]{0:T(1024)S(1)}, s32[8192]{0:T(1024)}, u32[]{:S(2)}) copy-start(s32[8192]{0:T(1024)} %param.14) | copy-start | bytes 98308
  0.0 7.6 %copy-start.2 = (bf16[128,1024]{1,0:T(8,128)(2,1)S(1)}, bf16[128,1024]{1,0:T(8,128)(2,1)}, u32[]{:S(2)}) copy-start(bf16[128,1024]{1,0:T(8,128)(2,1)} %param.13) | copy-start | bytes 786436
  6.8 10.0 %collective-permute-start.3 = (bf16[2048,128]{1,0:T(8,128)(2,1)}, bf16[2048,128]{1,0:T(8,128)(2,1)S(1)}, u32[]{:S(2)}, u32[]{:S(2)}) collective-permute-start(bf16[2048,128]{1,0:T(8,128)(2,1)} %get-tuple-element.40), channel_id=1, source_target_pairs={{0,8},{8,0},{16,24},{24,16},{32,40},{40,32},{48,56},{56,48},{64,72... | collective-permute-start | bytes 1572872 | tf_op jit(solution)/shard_map/ppermute | solution.py:460
  7.6 7.9 %collective-permute-start.2 = (bf16[128,1024]{1,0:T(8,128)(2,1)S(1)}, bf16[128,1024]{1,0:T(8,128)(2,1)S(1)}, u32[]{:S(2)}, u32[]{:S(2)}) collective-permute-start(bf16[128,1024]{1,0:T(8,128)(2,1)S(1)} %copy-done.2), channel_id=1, source_target_pairs={{0,4},{1,5},{2,6},{3,7},{4,0},{5,1},{6,2},{7,3},{8,12},{9,13},{10,... | collective-permute-start | bytes 786440 | tf_op jit(solution)/shard_map/ppermute | solution.py:464
  8.9 3.0 %collective-permute-start = (bf16[64,512]{1,0:T(8,128)(2,1)}, bf16[64,512]{1,0:T(8,128)(2,1)S(1)}, u32[]{:S(2)}, u32[]{:S(2)}) collective-permute-start(bf16[64,512]{1,0:T(8,128)(2,1)} %get-tuple-element.38), channel_id=1, source_target_pairs={{0,8},{8,0},{16,24},{24,16},{32,40},{40,32},{48,56},{56,48},{64,72... | collective-permute-start | bytes 196616 | tf_op jit(solution)/shard_map/ppermute | solution.py:458
  9.3 31.7 %collective-permute-start.4 = (bf16[2048,128]{1,0:T(8,128)(2,1)}, bf16[2048,128]{1,0:T(8,128)(2,1)S(1)}, u32[]{:S(2)}, u32[]{:S(2)}) collective-permute-start(bf16[2048,128]{1,0:T(8,128)(2,1)} %get-tuple-element.39.refs_0_), channel_id=1, source_target_pairs={{0,16},{8,24},{16,0},{24,8},{32,48},{40,56},{48,32},{56,40},{64,80... | collective-permute-start | bytes 1572872 | tf_op jit(solution)/shard_map/ppermute | solution.py:462
  12.8 24.8 %collective-permute-start.1 = (bf16[2,64,512]{2,1,0:T(8,128)(2,1)S(1)}, bf16[2,64,512]{2,1,0:T(8,128)(2,1)S(1)}, u32[]{:S(2)}, u32[]{:S(2)}) collective-permute-start(bf16[2,64,512]{2,1,0:T(8,128)(2,1)S(1)} %pad_maximum_fusion.1.rest_0_), channel_id=1, source_target_pairs={{0,32},{8,40},{16,48},{24,56},{32,64},{40,72},{48,80},{56,88},{64,... | collective-permute-start | bytes 393224 | tf_op jit(solution)/shard_map/ppermute | solution.py:459
  14.0 27.6 %collective-permute-start.10 = (bf16[2,64,512]{2,1,0:T(8,128)(2,1)S(1)}, bf16[2,64,512]{2,1,0:T(8,128)(2,1)S(1)}, u32[]{:S(2)}, u32[]{:S(2)}) collective-permute-start(bf16[2,64,512]{2,1,0:T(8,128)(2,1)S(1)} %pad_maximum_fusion.1.rest_0_), channel_id=1, source_target_pairs={{0,64},{8,72},{16,80},{24,88},{32,96},{40,104},{48,112},{56,120},{... | collective-permute-start | bytes 393224 | tf_op jit(solution)/shard_map/ppermute | solution.py:459
  15.4 29.6 %collective-permute-start.9 = (bf16[2,64,512]{2,1,0:T(8,128)(2,1)S(1)}, bf16[2,64,512]{2,1,0:T(8,128)(2,1)S(1)}, u32[]{:S(2)}, u32[]{:S(2)}) collective-permute-start(bf16[2,64,512]{2,1,0:T(8,128)(2,1)S(1)} %pad_maximum_fusion.1.rest_0_), channel_id=1, source_target_pairs={{0,96},{8,104},{16,112},{24,120},{32,0},{40,8},{48,16},{56,24},{64... | collective-permute-start | bytes 393224 | tf_op jit(solution)/shard_map/ppermute | solution.py:459
  16.8 1.0 copy-start
  18.9 0.7 copy-start.1
  35.9 55.1 %collective-permute-start.6 = (bf16[256,1024]{1,0:T(8,128)(2,1)S(1)}, bf16[256,1024]{1,0:T(8,128)(2,1)S(1)}, u32[]{:S(2)}, u32[]{:S(2)}) collective-permute-start(bf16[256,1024]{1,0:T(8,128)(2,1)S(1)} %pad_maximum_fusion.refs_0_), channel_id=1, source_target_pairs={{0,1},{1,2},{2,3},{3,0},{4,5},{5,6},{6,7},{7,4},{8,9},{9,10},{10,1... | collective-permute-start | bytes 1572872 | tf_op jit(solution)/shard_map/ppermute | solution.py:469
  37.6 53.4 %collective-permute-start.7 = (bf16[256,1024]{1,0:T(8,128)(2,1)S(1)}, bf16[256,1024]{1,0:T(8,128)(2,1)S(1)}, u32[]{:S(2)}, u32[]{:S(2)}) collective-permute-start(bf16[256,1024]{1,0:T(8,128)(2,1)S(1)} %pad_maximum_fusion.refs_0_), channel_id=1, source_target_pairs={{0,2},{1,3},{2,0},{3,1},{4,6},{5,7},{6,4},{7,5},{8,10},{9,11},{10,... | collective-permute-start | bytes 1572872 | tf_op jit(solution)/shard_map/ppermute | solution.py:469
  40.9 50.1 %collective-permute-start.8 = (bf16[256,1024]{1,0:T(8,128)(2,1)S(1)}, bf16[256,1024]{1,0:T(8,128)(2,1)S(1)}, u32[]{:S(2)}, u32[]{:S(2)}) collective-permute-start(bf16[256,1024]{1,0:T(8,128)(2,1)S(1)} %pad_maximum_fusion.refs_0_), channel_id=1, source_target_pairs={{0,3},{1,0},{2,1},{3,2},{4,7},{5,4},{6,5},{7,6},{8,11},{9,8},{10,9... | collective-permute-start | bytes 1572872 | tf_op jit(solution)/shard_map/ppermute | solution.py:469
  41.6 49.4 %collective-permute-start.5 = (bf16[2048,128]{1,0:T(8,128)(2,1)S(1)}, bf16[2048,128]{1,0:T(8,128)(2,1)S(1)}, u32[]{:S(2)}, u32[]{:S(2)}) collective-permute-start(bf16[2048,128]{1,0:T(8,128)(2,1)S(1)} %collective-permute-done.3.refs_1_), channel_id=1, source_target_pairs={{0,16},{8,24},{16,0},{24,8},{32,48},{40,56},{48,32},{56,40},{64,80... | collective-permute-start | bytes 1572872 | tf_op jit(solution)/shard_map/ppermute | solution.py:462
  136.4 21.6 %collective-permute-start.13 = (bf16[2,72,512]{2,1,0:T(8,128)(2,1)S(1)}, bf16[2,72,512]{2,1,0:T(8,128)(2,1)S(1)}, u32[]{:S(2)}, u32[]{:S(2)}) collective-permute-start(bf16[2,72,512]{2,1,0:T(8,128)(2,1)S(1)} %get-tuple-element.60), channel_id=1, source_target_pairs={{0,32},{8,40},{16,48},{24,56},{32,64},{40,72},{48,80},{56,88},{64,... | collective-permute-start | bytes 442376 | tf_op jit(solution)/shard_map/ppermute | solution.py:492
  138.2 19.9 %collective-permute-start.11 = (bf16[2,72,512]{2,1,0:T(8,128)(2,1)S(1)}, bf16[2,72,512]{2,1,0:T(8,128)(2,1)S(1)}, u32[]{:S(2)}, u32[]{:S(2)}) collective-permute-start(bf16[2,72,512]{2,1,0:T(8,128)(2,1)S(1)} %get-tuple-element.57), channel_id=1, source_target_pairs={{0,64},{8,72},{16,80},{24,88},{32,96},{40,104},{48,112},{56,120},{... | collective-permute-start | bytes 442376 | tf_op jit(solution)/shard_map/ppermute | solution.py:492
  138.2 19.9 %collective-permute-start.12 = (bf16[2,72,512]{2,1,0:T(8,128)(2,1)S(1)}, bf16[2,72,512]{2,1,0:T(8,128)(2,1)S(1)}, u32[]{:S(2)}, u32[]{:S(2)}) collective-permute-start(bf16[2,72,512]{2,1,0:T(8,128)(2,1)S(1)} %get-tuple-element.58), channel_id=1, source_target_pairs={{0,96},{8,104},{16,112},{24,120},{32,0},{40,8},{48,16},{56,24},{64... | collective-permute-start | bytes 442376 | tf_op jit(solution)/shard_map/ppermute | solution.py:492
  159.1 13.3 %all-to-all-start = ((bf16[16,32,128]{2,1,0:T(8,128)(2,1)}), bf16[16,32,128]{2,1,0:T(8,128)(2,1)S(1)}, u32[]{:S(2)}, u32[]{:S(2)}) async-start(bf16[16,32,128]{2,1,0:T(8,128)(2,1)} %shard_map.89), calls=%async_computation | async-start | bytes 262144 | tf_op jit(solution)/shard_map/all_to_all | solution.py:495

commit v6 on v5

--- a/solution.py
+++ b/solution.py
@@ -464,7 +464,8 @@
     w_other = lax.ppermute(w_out, "grp", [(g, g ^ 4) for g in range(8)])
     spots = positions.reshape(-1, ROWS)
     near_parts = dict(zip(NEAR_CALLS[0], attend(NEAR_CALLS[0], seq, codes, spots, near, [q_chip])))
-    w_pair, near_parts[0] = lax.optimization_barrier((jnp.concatenate([w_out, w_other], 0), near_parts[0]))
+    w_other, near_parts[0] = lax.optimization_barrier((w_other, near_parts[0]))
+    w_pair = jnp.concatenate([w_out, w_other], 0)
     w_turns = [w_pair] + [
         lax.ppermute(w_pair, "grp", [(g, (g & 4) | ((g + k) & 3)) for g in range(8)]) for k in (1, 2, 3)
     ]
@@ -477,7 +478,9 @@
         )
         near_parts.update(zip(call, attend(call, seq, codes, spots, near, [queries[by] for by in call])))
         last = call[-1]
-    kv_far, w_turns, near_parts[last] = lax.optimization_barrier((kv_far, w_turns, near_parts[last]))
+    w_early = w_turns[1], w_turns[3]
+    kv_far, w_early, near_parts[last] = lax.optimization_barrier((kv_far, w_early, near_parts[last]))
+    w_turns[1], w_turns[3] = w_early
     far = prepare(*kv_far)
     last = None
     for call in FAR_CALLS:
@@ -490,6 +493,7 @@
         last = call[-1]
 
     parts = [part if by == 0 else lax.ppermute(part, "seq", along_x(-by)) for by, part in parts.items()]
+    parts, w_turns[2] = lax.optimization_barrier((parts, w_turns[2]))
     pieces = combine(core, parts)
     owners = [[(4 * x + 2 * y + c) * 8 + g for c in range(2) for g in range(8)] for x in range(4) for y in range(2)]
     pieces = lax.all_to_all(pieces, ("seq", "grp"), 0, 0, axis_index_groups=owners)

time: 175 us -> 172 us (0.983); the launches traced: 174 us -> 173 us
  starting transfers between devices: 28.3 us -> 24.9 us
  Pallas kernels: 136 us -> 138 us
    pallas_call x4, Pallas kernels: 125 us -> 127 us  [attend(): pl.pallas_call(functools.partial(attention_kernel, steps, bool(before)),...]
    ppermute x2, starting transfers between devices: 6 us -> 3.81 us  [body(): kv_far = [lax.ppermute(kv, 'seq', Y_SWAP) for kv in (kv_own, kv_partner)]]
  transfers between devices with their start and end apart: 15 -> 15, of which waited for: 2 -> 1; matrix products, arithmetic and copies ran while one was open for 1% -> 1% of each run, Pallas kernels for 47% -> 75%
where the time goes in v6:
time: 172 us; the launch traced here: 173 us
  Pallas kernels  138 us (80%)
  starting transfers between devices  24.9 us (14%)
  waiting for transfers between devices  6.39 us (4%)
  local copies, waits for them, and re-layouts  1.81 us (1%)
    pallas_call x4, Pallas kernels, attend(): pl.pallas_call(functools.partial(attention_kernel, steps, bool(before)),...  127 us
    pallas_call x1, Pallas kernels, front(): pl.pallas_call(front_kernel, in_specs=[SMEM] + [pl.BlockSpec(memory_space...  6.81 us
    all_to_all x1, starting transfers between devices, body(): lax.all_to_all(pieces, ('seq', 'grp'), 0, 0, axis_index_groups=owners)  6.74 us
    all_to_all x1, waiting for transfers between devices, body(): lax.all_to_all(pieces, ('seq', 'grp'), 0, 0, axis_index_groups=owners)  6.35 us
    ppermute x3, starting transfers between devices, body(): lax.ppermute(w_pair, 'grp', [(g, g & 4 | g + k & 3) for g in range(8)])  5.13 us
    ppermute x2, starting transfers between devices, body(): kv_far = [lax.ppermute(kv, 'seq', Y_SWAP) for kv in (kv_own, kv_partner)]  3.81 us
    ppermute x3, starting transfers between devices, body(): lax.ppermute(part, 'seq', along_x(-by))  3.74 us
  transfers between devices with their start and end apart: 15, of which 1 were waited for; matrix products, arithmetic and copies ran while one was open for 1% of the time, Pallas kernels for 75%

profile of v6, /device:TPU:3, one launch (start us, length us, event | category | flops | bytes accessed | tf_op | source)
XLA Modules:
  0.0 172.6 jit_solution(1524128561645280820)
XLA Ops:
  0.0 0.0 copy-start.3
  0.0 0.0 copy-start.2
  0.0 6.8 %shard_map.82 = (bf16[64,512]{1,0:T(8,128)(2,1)}, bf16[64,512]{1,0:T(8,128)(2,1)}, bf16[2048,128]{1,0:T(8,128)(2,1)}, bf16[2048,128]{1,0:T(8,128)(2,1)}, s32[32,128]{1,0:T(8,128)}) custom-call(s32[1]{0:T(128)} %bitcast.1.seq_ref, bf16[512,1024]{1,0:T(8,128)(2,1)} %lat_hbm.1, bf16[2048,1024]{1,0:T(8,128)(2,1)} %x_hbm.1, bf16[1024,128]{1,0:T(8,128)(2,1)} %wq_hbm.1, ...), custom_call_target="tpu_custom_call" | custom-call | flops 1207959552 | bytes 6291456 | tf_op jit(solution)/shard_map/pallas_call | solution.py:133
  6.8 0.8 collective-permute-start.3
  7.6 0.1 collective-permute-start
  7.7 0.0 copy-done.2
  7.7 1.3 collective-permute-start.2
  9.0 2.6 %collective-permute-start.4 = (bf16[2048,128]{1,0:T(8,128)(2,1)}, bf16[2048,128]{1,0:T(8,128)(2,1)S(1)}, u32[]{:S(2)}, u32[]{:S(2)}) collective-permute-start(bf16[2048,128]{1,0:T(8,128)(2,1)} %get-tuple-element.42.refs_0_), channel_id=1, source_target_pairs={{0,16},{8,24},{16,0},{24,8},{32,48},{40,56},{48,32},{56,40},{64,80... | collective-permute-start | bytes 1572872 | tf_op jit(solution)/shard_map/ppermute | solution.py:462
  11.6 0.0 copy-done.3
  11.6 0.0 collective-permute-done
  11.6 0.9 pad_maximum_fusion.rest_0_
  12.5 1.3 collective-permute-start.1
  13.8 0.3 collective-permute-start.8
  14.0 0.0 collective-permute-done.3.refs_1_
  14.0 1.8 %collective-permute-start.9 = (bf16[2,64,512]{2,1,0:T(8,128)(2,1)S(1)}, bf16[2,64,512]{2,1,0:T(8,128)(2,1)S(1)}, u32[]{:S(2)}, u32[]{:S(2)}) collective-permute-start(bf16[2,64,512]{2,1,0:T(8,128)(2,1)S(1)} %pad_maximum_fusion.rest_0_), channel_id=1, source_target_pairs={{0,64},{8,72},{16,80},{24,88},{32,96},{40,104},{48,112},{56,120},{... | collective-permute-start | bytes 393224 | tf_op jit(solution)/shard_map/ppermute | solution.py:459
  15.9 0.0 copy-start
  15.9 1.0 copy-done
  16.9 1.0 shard_map.83
  18.0 0.0 copy-start.1
  18.0 0.7 copy-done.1
  18.7 17.3 %shard_map.84.rest_1_ = bf16[2,72,512]{2,1,0:T(8,128)(2,1)S(1)} custom-call(s32[1]{0:T(128)} %bitcast.1.seq_ref, s32[32,128]{1,0:T(8,128)S(1)} %copy-done.1, f32[1]{0:T(128)} %get-tuple-element.44.norm_ref, s32[32,256]{1,0:T(8,128)S(1)} %reshape.7.pos_ref, bf16[4096,128]{1,0:T(8,128)(2,1)S(1)} %get-tuple-element.45.kv_ref, ...), custom_call_target="tpu_custom_call" | custom-call | flops 6000000000 | bytes 4194304 | tf_op jit(solution)/shard_map/pallas_call | solution.py:358
  36.0 0.0 collective-permute-done.2
  36.0 1.7 collective-permute-start.6
  37.7 0.0 collective-permute-done.1.rest_0_.rest_1_
  37.7 2.2 %collective-permute-start.7 = (bf16[256,1024]{1,0:T(8,128)(2,1)S(1)}, bf16[256,1024]{1,0:T(8,128)(2,1)S(1)}, u32[]{:S(2)}, u32[]{:S(2)}) collective-permute-start(bf16[256,1024]{1,0:T(8,128)(2,1)S(1)} %constant_dynamic-update-slice_fusion.refs_0_), channel_id=1, source_target_pairs={{0,3},{1,0},{2,1},{3,2},{4,7},{5,4},{6,5},{7,6},{8,11},{9,8},{10,9... | collective-permute-start | bytes 1572872 | tf_op jit(solution)/shard_map/ppermute | solution.py:470
  40.0 0.0 collective-permute-done.4.refs_0_
  40.0 1.2 collective-permute-start.13
  41.2 0.0 collective-permute-done.8.rest_1_.rest_2_
  41.2 1.2 collective-permute-start.5
  42.4 0.0 collective-permute-done.9.rest_2_.rest_0_
  42.4 45.5 %shard_map.85 = (bf16[2,72,512]{2,1,0:T(8,128)(2,1)S(1)}, bf16[2,72,512]{2,1,0:T(8,128)(2,1)S(1)}, bf16[2,72,512]{2,1,0:T(8,128)(2,1)S(1)}) custom-call(s32[1]{0:T(128)} %bitcast.1.seq_ref, s32[32,128]{1,0:T(8,128)S(1)} %copy-done.1, f32[1]{0:T(128)} %get-tuple-element.44.norm_ref, s32[32,256]{1,0:T(8,128)S(1)} %reshape.7.pos_ref, ...), custom_call_target="tpu_custom_call" | custom-call | flops 17999998976 | bytes 4194304 | tf_op jit(solution)/shard_map/pallas_call | solution.py:358
  87.9 0.0 collective-permute-done.6.refs_1_
  87.9 0.0 collective-permute-done.7.refs_3_
  87.9 0.0 collective-permute-done.5.refs_1_
  87.9 1.0 shard_map.86
  89.0 46.7 %shard_map.87 = (bf16[2,72,512]{2,1,0:T(8,128)(2,1)S(1)}, bf16[2,72,512]{2,1,0:T(8,128)(2,1)S(1)}, bf16[2,72,512]{2,1,0:T(8,128)(2,1)S(1)}) custom-call(s32[1]{0:T(128)} %bitcast.1.seq_ref, s32[32,128]{1,0:T(8,128)S(1)} %copy-done.1, f32[1]{0:T(128)} %get-tuple-element.54.norm_ref, s32[32,256]{1,0:T(8,128)S(1)} %reshape.7.pos_ref, ...), custom_call_target="tpu_custom_call" | custom-call | flops 17999998976 | bytes 4194304 | tf_op jit(solution)/shard_map/pallas_call | solution.py:358
  135.6 1.4 collective-permute-start.12
  137.0 0.4 collective-permute-start.10
  137.4 2.0 %collective-permute-start.11 = (bf16[2,72,512]{2,1,0:T(8,128)(2,1)S(1)}, bf16[2,72,512]{2,1,0:T(8,128)(2,1)S(1)}, u32[]{:S(2)}, u32[]{:S(2)}) collective-permute-start(bf16[2,72,512]{2,1,0:T(8,128)(2,1)S(1)} %get-tuple-element.61), channel_id=1, source_target_pairs={{0,96},{8,104},{16,112},{24,120},{32,0},{40,8},{48,16},{56,24},{64... | collective-permute-start | bytes 442376 | tf_op jit(solution)/shard_map/ppermute | solution.py:495
  139.4 17.9 %shard_map.88.refs_3_ = bf16[2,72,512]{2,1,0:T(8,128)(2,1)S(1)} custom-call(s32[1]{0:T(128)} %bitcast.1.seq_ref, s32[32,128]{1,0:T(8,128)S(1)} %copy-done.1, f32[1]{0:T(128)} %get-tuple-element.54.norm_ref, s32[32,256]{1,0:T(8,128)S(1)} %reshape.7.pos_ref, bf16[4096,128]{1,0:T(8,128)(2,1)S(1)} %get-tuple-element.55.kv_ref, ...), custom_call_target="tpu_custom_call" | custom-call | flops 6000000000 | bytes 4194304 | tf_op jit(solution)/shard_map/pallas_call | solution.py:358
  157.3 0.0 collective-permute-done.13.refs_2_
  157.3 0.0 collective-permute-done.12.refs_2_
  157.3 0.0 collective-permute-done.10.refs_0_
  157.3 0.0 collective-permute-done.11.refs_1_
  157.3 1.0 shard_map.89
  158.3 6.7 %all-to-all-start = ((bf16[16,32,128]{2,1,0:T(8,128)(2,1)}), bf16[16,32,128]{2,1,0:T(8,128)(2,1)S(1)}, u32[]{:S(2)}, u32[]{:S(2)}) async-start(bf16[16,32,128]{2,1,0:T(8,128)(2,1)} %shard_map.89), calls=%async_computation | async-start | bytes 262144 | tf_op jit(solution)/shard_map/all_to_all | solution.py:499
  165.1 6.4 %all-to-all-done.pieces_ref = bf16[16,32,128]{2,1,0:T(8,128)(2,1)S(1)} async-done(((bf16[16,32,128]{2,1,0:T(8,128)(2,1)}), bf16[16,32,128]{2,1,0:T(8,128)(2,1)S(1)}, u32[]{:S(2)}, u32[]{:S(2)}) %all-to-all-start) | async-done | bytes 131104 | tf_op jit(solution)/shard_map/all_to_all | solution.py:499
  171.4 1.2 shard_map.90
  (3 shorter events, 0.0 us)
Async XLA Ops:
  0.0 11.6 %copy-start.3 = (s32[8192]{0:T(1024)S(1)}, s32[8192]{0:T(1024)}, u32[]{:S(2)}) copy-start(s32[8192]{0:T(1024)} %param.14) | copy-start | bytes 98308
  0.0 7.7 %copy-start.2 = (bf16[128,1024]{1,0:T(8,128)(2,1)S(1)}, bf16[128,1024]{1,0:T(8,128)(2,1)}, u32[]{:S(2)}) copy-start(bf16[128,1024]{1,0:T(8,128)(2,1)} %param.13) | copy-start | bytes 786436
  6.8 7.2 %collective-permute-start.3 = (bf16[2048,128]{1,0:T(8,128)(2,1)}, bf16[2048,128]{1,0:T(8,128)(2,1)S(1)}, u32[]{:S(2)}, u32[]{:S(2)}) collective-permute-start(bf16[2048,128]{1,0:T(8,128)(2,1)} %get-tuple-element.43), channel_id=1, source_target_pairs={{0,8},{8,0},{16,24},{24,16},{32,40},{40,32},{48,56},{56,48},{64,72... | collective-permute-start | bytes 1572872 | tf_op jit(solution)/shard_map/ppermute | solution.py:460
  7.6 4.1 %collective-permute-start = (bf16[64,512]{1,0:T(8,128)(2,1)}, bf16[64,512]{1,0:T(8,128)(2,1)S(1)}, u32[]{:S(2)}, u32[]{:S(2)}) collective-permute-start(bf16[64,512]{1,0:T(8,128)(2,1)} %get-tuple-element.41), channel_id=1, source_target_pairs={{0,8},{8,0},{16,24},{24,16},{32,40},{40,32},{48,56},{56,48},{64,72... | collective-permute-start | bytes 196616 | tf_op jit(solution)/shard_map/ppermute | solution.py:458
  7.7 28.3 %collective-permute-start.2 = (bf16[128,1024]{1,0:T(8,128)(2,1)S(1)}, bf16[128,1024]{1,0:T(8,128)(2,1)S(1)}, u32[]{:S(2)}, u32[]{:S(2)}) collective-permute-start(bf16[128,1024]{1,0:T(8,128)(2,1)S(1)} %copy-done.2), channel_id=1, source_target_pairs={{0,4},{1,5},{2,6},{3,7},{4,0},{5,1},{6,2},{7,3},{8,12},{9,13},{10,... | collective-permute-start | bytes 786440 | tf_op jit(solution)/shard_map/ppermute | solution.py:464
  9.0 31.0 %collective-permute-start.4 = (bf16[2048,128]{1,0:T(8,128)(2,1)}, bf16[2048,128]{1,0:T(8,128)(2,1)S(1)}, u32[]{:S(2)}, u32[]{:S(2)}) collective-permute-start(bf16[2048,128]{1,0:T(8,128)(2,1)} %get-tuple-element.42.refs_0_), channel_id=1, source_target_pairs={{0,16},{8,24},{16,0},{24,8},{32,48},{40,56},{48,32},{56,40},{64,80... | collective-permute-start | bytes 1572872 | tf_op jit(solution)/shard_map/ppermute | solution.py:462
  12.5 25.2 %collective-permute-start.1 = (bf16[2,64,512]{2,1,0:T(8,128)(2,1)S(1)}, bf16[2,64,512]{2,1,0:T(8,128)(2,1)S(1)}, u32[]{:S(2)}, u32[]{:S(2)}) collective-permute-start(bf16[2,64,512]{2,1,0:T(8,128)(2,1)S(1)} %pad_maximum_fusion.rest_0_), channel_id=1, source_target_pairs={{0,32},{8,40},{16,48},{24,56},{32,64},{40,72},{48,80},{56,88},{64,... | collective-permute-start | bytes 393224 | tf_op jit(solution)/shard_map/ppermute | solution.py:459
  13.8 27.4 %collective-permute-start.8 = (bf16[2,64,512]{2,1,0:T(8,128)(2,1)S(1)}, bf16[2,64,512]{2,1,0:T(8,128)(2,1)S(1)}, u32[]{:S(2)}, u32[]{:S(2)}) collective-permute-start(bf16[2,64,512]{2,1,0:T(8,128)(2,1)S(1)} %pad_maximum_fusion.rest_0_), channel_id=1, source_target_pairs={{0,96},{8,104},{16,112},{24,120},{32,0},{40,8},{48,16},{56,24},{64... | collective-permute-start | bytes 393224 | tf_op jit(solution)/shard_map/ppermute | solution.py:459
  14.0 28.3 %collective-permute-start.9 = (bf16[2,64,512]{2,1,0:T(8,128)(2,1)S(1)}, bf16[2,64,512]{2,1,0:T(8,128)(2,1)S(1)}, u32[]{:S(2)}, u32[]{:S(2)}) collective-permute-start(bf16[2,64,512]{2,1,0:T(8,128)(2,1)S(1)} %pad_maximum_fusion.rest_0_), channel_id=1, source_target_pairs={{0,64},{8,72},{16,80},{24,88},{32,96},{40,104},{48,112},{56,120},{... | collective-permute-start | bytes 393224 | tf_op jit(solution)/shard_map/ppermute | solution.py:459
  15.9 1.0 copy-start
  18.0 0.7 copy-start.1
  36.0 51.9 %collective-permute-start.6 = (bf16[256,1024]{1,0:T(8,128)(2,1)S(1)}, bf16[256,1024]{1,0:T(8,128)(2,1)S(1)}, u32[]{:S(2)}, u32[]{:S(2)}) collective-permute-start(bf16[256,1024]{1,0:T(8,128)(2,1)S(1)} %constant_dynamic-update-slice_fusion.refs_0_), channel_id=1, source_target_pairs={{0,1},{1,2},{2,3},{3,0},{4,5},{5,6},{6,7},{7,4},{8,9},{9,10},{10,1... | collective-permute-start | bytes 1572872 | tf_op jit(solution)/shard_map/ppermute | solution.py:470
  37.7 50.2 %collective-permute-start.7 = (bf16[256,1024]{1,0:T(8,128)(2,1)S(1)}, bf16[256,1024]{1,0:T(8,128)(2,1)S(1)}, u32[]{:S(2)}, u32[]{:S(2)}) collective-permute-start(bf16[256,1024]{1,0:T(8,128)(2,1)S(1)} %constant_dynamic-update-slice_fusion.refs_0_), channel_id=1, source_target_pairs={{0,3},{1,0},{2,1},{3,2},{4,7},{5,4},{6,5},{7,6},{8,11},{9,8},{10,9... | collective-permute-start | bytes 1572872 | tf_op jit(solution)/shard_map/ppermute | solution.py:470
  40.0 117.3 %collective-permute-start.13 = (bf16[256,1024]{1,0:T(8,128)(2,1)S(1)}, bf16[256,1024]{1,0:T(8,128)(2,1)S(1)}, u32[]{:S(2)}, u32[]{:S(2)}) collective-permute-start(bf16[256,1024]{1,0:T(8,128)(2,1)S(1)} %constant_dynamic-update-slice_fusion.refs_0_), channel_id=1, source_target_pairs={{0,2},{1,3},{2,0},{3,1},{4,6},{5,7},{6,4},{7,5},{8,10},{9,11},{10,... | collective-permute-start | bytes 1572872 | tf_op jit(solution)/shard_map/ppermute | solution.py:470
  41.2 46.7 %collective-permute-start.5 = (bf16[2048,128]{1,0:T(8,128)(2,1)S(1)}, bf16[2048,128]{1,0:T(8,128)(2,1)S(1)}, u32[]{:S(2)}, u32[]{:S(2)}) collective-permute-start(bf16[2048,128]{1,0:T(8,128)(2,1)S(1)} %collective-permute-done.3.refs_1_), channel_id=1, source_target_pairs={{0,16},{8,24},{16,0},{24,8},{32,48},{40,56},{48,32},{56,40},{64,80... | collective-permute-start | bytes 1572872 | tf_op jit(solution)/shard_map/ppermute | solution.py:462
  135.6 21.7 %collective-permute-start.12 = (bf16[2,72,512]{2,1,0:T(8,128)(2,1)S(1)}, bf16[2,72,512]{2,1,0:T(8,128)(2,1)S(1)}, u32[]{:S(2)}, u32[]{:S(2)}) collective-permute-start(bf16[2,72,512]{2,1,0:T(8,128)(2,1)S(1)} %get-tuple-element.63), channel_id=1, source_target_pairs={{0,32},{8,40},{16,48},{24,56},{32,64},{40,72},{48,80},{56,88},{64,... | collective-permute-start | bytes 442376 | tf_op jit(solution)/shard_map/ppermute | solution.py:495
  137.0 20.3 %collective-permute-start.10 = (bf16[2,72,512]{2,1,0:T(8,128)(2,1)S(1)}, bf16[2,72,512]{2,1,0:T(8,128)(2,1)S(1)}, u32[]{:S(2)}, u32[]{:S(2)}) collective-permute-start(bf16[2,72,512]{2,1,0:T(8,128)(2,1)S(1)} %get-tuple-element.60), channel_id=1, source_target_pairs={{0,64},{8,72},{16,80},{24,88},{32,96},{40,104},{48,112},{56,120},{... | collective-permute-start | bytes 442376 | tf_op jit(solution)/shard_map/ppermute | solution.py:495
  137.4 19.9 %collective-permute-start.11 = (bf16[2,72,512]{2,1,0:T(8,128)(2,1)S(1)}, bf16[2,72,512]{2,1,0:T(8,128)(2,1)S(1)}, u32[]{:S(2)}, u32[]{:S(2)}) collective-permute-start(bf16[2,72,512]{2,1,0:T(8,128)(2,1)S(1)} %get-tuple-element.61), channel_id=1, source_target_pairs={{0,96},{8,104},{16,112},{24,120},{32,0},{40,8},{48,16},{56,24},{64... | collective-permute-start | bytes 442376 | tf_op jit(solution)/shard_map/ppermute | solution.py:495
  158.3 13.1 %all-to-all-start = ((bf16[16,32,128]{2,1,0:T(8,128)(2,1)}), bf16[16,32,128]{2,1,0:T(8,128)(2,1)S(1)}, u32[]{:S(2)}, u32[]{:S(2)}) async-start(bf16[16,32,128]{2,1,0:T(8,128)(2,1)} %shard_map.89), calls=%async_computation | async-start | bytes 262144 | tf_op jit(solution)/shard_map/all_to_all | solution.py:499

commit v7 on v6

--- a/solution.py
+++ b/solution.py
@@ -21,6 +21,10 @@
 lowest_max = -1e29
 SMEM = pl.BlockSpec(memory_space=pltpu.SMEM)
 VMEM = pl.BlockSpec(memory_space=pltpu.VMEM)
+
+
+def in_hbm(*arrays):
+    return [pltpu.with_memory_space_constraint(a, pltpu.HBM) for a in arrays]
 
 
 def list_work(me, pos_ref, mask_ref, code_ref):
@@ -172,8 +176,8 @@
         in_specs=[VMEM] * len(sources),
         out_specs=[VMEM, VMEM, SMEM],
         out_shape=[
-            jax.ShapeDtypeStruct((keys, 2 * HS), jnp.bfloat16),
-            jax.ShapeDtypeStruct((ACC_ROWS, keys), jnp.bfloat16),
+            pltpu.HBM((keys, 2 * HS), jnp.bfloat16),
+            pltpu.HBM((ACC_ROWS, keys), jnp.bfloat16),
             jax.ShapeDtypeStruct((1,), jnp.float32),
         ],
         compiler_params=pltpu.CompilerParams(vmem_limit_bytes=24 * 2**20),
@@ -353,6 +357,7 @@
 
 def attend(steps, seq, codes, spots, held, queries, before=()):
     kv, vt, norm = held
+    kv, vt, codes = in_hbm(kv, vt, codes)
     chips = len(steps)
     out = jax.ShapeDtypeStruct((2, ACC_ROWS, queries[0].shape[2]), jnp.bfloat16)
     return pl.pallas_call(
@@ -458,7 +463,7 @@
     q_chip = jnp.stack([mine, lax.ppermute(theirs, "seq", CORE_SWAP)])
     queries = {by: q_chip if by == 0 else lax.ppermute(q_chip, "seq", along_x(by)) for by in (0, 1, 3, 2)}
     kv_partner = lax.ppermute(kv_other, "seq", CORE_SWAP)
-    near = prepare(kv_own, kv_partner)
+    near = prepare(*in_hbm(kv_own), kv_partner)
     kv_far = [lax.ppermute(kv, "seq", Y_SWAP) for kv in (kv_own, kv_partner)]
 
     w_other = lax.ppermute(w_out, "grp", [(g, g ^ 4) for g in range(8)])
@@ -478,9 +483,7 @@
         )
         near_parts.update(zip(call, attend(call, seq, codes, spots, near, [queries[by] for by in call])))
         last = call[-1]
-    w_early = w_turns[1], w_turns[3]
-    kv_far, w_early, near_parts[last] = lax.optimization_barrier((kv_far, w_early, near_parts[last]))
-    w_turns[1], w_turns[3] = w_early
+    kv_far, near_parts[last] = lax.optimization_barrier((kv_far, near_parts[last]))
     far = prepare(*kv_far)
     last = None
     for call in FAR_CALLS:
@@ -493,7 +496,7 @@
         last = call[-1]
 
     parts = [part if by == 0 else lax.ppermute(part, "seq", along_x(-by)) for by, part in parts.items()]
-    parts, w_turns[2] = lax.optimization_barrier((parts, w_turns[2]))
+    parts, w_turns = lax.optimization_barrier((parts, w_turns))
     pieces = combine(core, parts)
     owners = [[(4 * x + 2 * y + c) * 8 + g for c in range(2) for g in range(8)] for x in range(4) for y in range(2)]
     pieces = lax.all_to_all(pieces, ("seq", "grp"), 0, 0, axis_index_groups=owners)

time: 172 us -> 176 us (1.023); the launches traced: 173 us -> 174 us
  Pallas kernels: 138 us -> 142 us
    pallas_call x2, Pallas kernels: 2.05 us -> 4.01 us  [prepare(): pl.pallas_call(prepare_kernel, in_specs=[VMEM] * len(sources), out_specs=...]
  transfers between devices with their start and end apart: 15 -> 15, of which waited for: 1 -> 1; matrix products, arithmetic and copies ran while one was open for 1% -> 1% of each run, Pallas kernels for 75% -> 76%
where the time goes in v7:
time: 176 us; the launch traced here: 174 us
  Pallas kernels  142 us (81%)
  starting transfers between devices  25.2 us (14%)
  waiting for transfers between devices  6.39 us (4%)
    pallas_call x4, Pallas kernels, attend(): pl.pallas_call(functools.partial(attention_kernel, steps, bool(before)),...  129 us
    pallas_call x1, Pallas kernels, front(): pl.pallas_call(front_kernel, in_specs=[SMEM] + [pl.BlockSpec(memory_space...  6.8 us
    all_to_all x1, starting transfers between devices, body(): lax.all_to_all(pieces, ('seq', 'grp'), 0, 0, axis_index_groups=owners)  6.5 us
    all_to_all x1, waiting for transfers between devices, body(): lax.all_to_all(pieces, ('seq', 'grp'), 0, 0, axis_index_groups=owners)  6.35 us
    ppermute x3, starting transfers between devices, body(): lax.ppermute(w_pair, 'grp', [(g, g & 4 | g + k & 3) for g in range(8)])  5.74 us
    ppermute x3, starting transfers between devices, body(): lax.ppermute(part, 'seq', along_x(-by))  4.16 us
    pallas_call x2, Pallas kernels, prepare(): pl.pallas_call(prepare_kernel, in_specs=[VMEM] * len(sources), out_specs=...  4.01 us
  transfers between devices with their start and end apart: 15, of which 1 were waited for; matrix products, arithmetic and copies ran while one was open for 1% of the time, Pallas kernels for 76%

profile of v7, /device:TPU:3, one launch (start us, length us, event | category | flops | bytes accessed | tf_op | source)
XLA Modules:
  0.0 174.3 jit_solution(10978734817259629379)
XLA Ops:
  0.0 0.0 copy-start.1
  0.0 0.0 copy-start
  0.0 6.8 %shard_map.82 = (bf16[64,512]{1,0:T(8,128)(2,1)}, bf16[64,512]{1,0:T(8,128)(2,1)}, bf16[2048,128]{1,0:T(8,128)(2,1)}, bf16[2048,128]{1,0:T(8,128)(2,1)}, s32[32,128]{1,0:T(8,128)}) custom-call(s32[1]{0:T(128)} %bitcast.1.seq_ref, bf16[512,1024]{1,0:T(8,128)(2,1)} %lat_hbm.1, bf16[2048,1024]{1,0:T(8,128)(2,1)} %x_hbm.1, bf16[1024,128]{1,0:T(8,128)(2,1)} %wq_hbm.1, ...), custom_call_target="tpu_custom_call" | custom-call | flops 1207959552 | bytes 6291456 | tf_op jit(solution)/shard_map/pallas_call | solution.py:137
  6.8 0.8 collective-permute-start.3
  7.6 0.1 collective-permute-start
  7.7 0.0 copy-done
  7.7 1.3 collective-permute-start.2
  9.0 2.6 %collective-permute-start.4 = (bf16[2048,128]{1,0:T(8,128)(2,1)}, bf16[2048,128]{1,0:T(8,128)(2,1)S(1)}, u32[]{:S(2)}, u32[]{:S(2)}) collective-permute-start(bf16[2048,128]{1,0:T(8,128)(2,1)} %get-tuple-element.43.refs_0_), channel_id=1, source_target_pairs={{0,16},{8,24},{16,0},{24,8},{32,48},{40,56},{48,32},{56,40},{64,80... | collective-permute-start | bytes 1572872 | tf_op jit(solution)/shard_map/ppermute | solution.py:467
  11.6 0.0 copy-done.1
  11.6 0.0 collective-permute-done
  11.6 0.9 pad_maximum_fusion.rest_0_
  12.5 1.3 collective-permute-start.1
  13.8 0.3 collective-permute-start.6
  14.0 0.0 collective-permute-done.3.refs_1_
  14.0 1.8 %collective-permute-start.7 = (bf16[2,64,512]{2,1,0:T(8,128)(2,1)S(1)}, bf16[2,64,512]{2,1,0:T(8,128)(2,1)S(1)}, u32[]{:S(2)}, u32[]{:S(2)}) collective-permute-start(bf16[2,64,512]{2,1,0:T(8,128)(2,1)S(1)} %pad_maximum_fusion.rest_0_), channel_id=1, source_target_pairs={{0,64},{8,72},{16,80},{24,88},{32,96},{40,104},{48,112},{56,120},{... | collective-permute-start | bytes 393224 | tf_op jit(solution)/shard_map/ppermute | solution.py:464
  15.9 2.5 %shard_map.83 = (bf16[4096,128]{1,0:T(8,128)(2,1)}, bf16[72,4096]{1,0:T(8,128)(2,1)}, f32[1]{0:T(128)}) custom-call(bf16[2048,128]{1,0:T(8,128)(2,1)} %get-tuple-element.43.refs_0_, bf16[2048,128]{1,0:T(8,128)(2,1)S(1)} %collective-permute-done.3.refs_1_), custom_call_target="tpu_custom_call" | custom-call | tf_op jit(solution)/shard_map/pallas_call | solution.py:174
  18.4 18.4 %shard_map.84.rest_1_ = bf16[2,72,512]{2,1,0:T(8,128)(2,1)S(1)} custom-call(s32[1]{0:T(128)} %bitcast.1.seq_ref, s32[32,128]{1,0:T(8,128)} %get-tuple-element.40.code_ref, f32[1]{0:T(128)} %get-tuple-element.45.norm_ref, s32[32,256]{1,0:T(8,128)S(1)} %reshape.7.pos_ref, bf16[4096,128]{1,0:T(8,128)(2,1)} %get-tuple-element.46.kv_ref, ...), custom_call_target="tpu_custom_call" | custom-call | flops 6000000000 | bytes 4194304 | tf_op jit(solution)/shard_map/pallas_call | solution.py:363
  36.9 0.0 collective-permute-done.2
  36.9 1.7 collective-permute-start.11
  38.6 0.0 collective-permute-done.1.rest_0_.rest_1_
  38.6 3.3 %collective-permute-start.12 = (bf16[256,1024]{1,0:T(8,128)(2,1)S(1)}, bf16[256,1024]{1,0:T(8,128)(2,1)S(1)}, u32[]{:S(2)}, u32[]{:S(2)}) collective-permute-start(bf16[256,1024]{1,0:T(8,128)(2,1)S(1)} %constant_dynamic-update-slice_fusion.refs_0_), channel_id=1, source_target_pairs={{0,2},{1,3},{2,0},{3,1},{4,6},{5,7},{6,4},{7,5},{8,10},{9,11},{10,... | collective-permute-start | bytes 1572872 | tf_op jit(solution)/shard_map/ppermute | solution.py:475
  41.9 0.0 collective-permute-done.4.refs_0_
  41.9 0.7 collective-permute-start.13
  42.7 0.0 collective-permute-done.6.rest_1_.rest_2_
  42.7 0.7 collective-permute-start.5
  43.3 0.0 collective-permute-done.7.rest_2_.rest_0_
  43.3 45.5 %shard_map.85 = (bf16[2,72,512]{2,1,0:T(8,128)(2,1)S(1)}, bf16[2,72,512]{2,1,0:T(8,128)(2,1)S(1)}, bf16[2,72,512]{2,1,0:T(8,128)(2,1)S(1)}) custom-call(s32[1]{0:T(128)} %bitcast.1.seq_ref, s32[32,128]{1,0:T(8,128)} %get-tuple-element.40.code_ref, f32[1]{0:T(128)} %get-tuple-element.45.norm_ref, s32[32,256]{1,0:T(8,128)S(1)} %reshape.7.pos_ref, ...), custom_call_target="tpu_custom_call" | custom-call | flops 17999998976 | bytes 4194304 | tf_op jit(solution)/shard_map/pallas_call | solution.py:363
  88.8 0.0 collective-permute-done.5.refs_1_
  88.8 1.5 shard_map.86
  90.3 47.3 %shard_map.87 = (bf16[2,72,512]{2,1,0:T(8,128)(2,1)S(1)}, bf16[2,72,512]{2,1,0:T(8,128)(2,1)S(1)}, bf16[2,72,512]{2,1,0:T(8,128)(2,1)S(1)}) custom-call(s32[1]{0:T(128)} %bitcast.1.seq_ref, s32[32,128]{1,0:T(8,128)} %get-tuple-element.40.code_ref, f32[1]{0:T(128)} %get-tuple-element.54.norm_ref, s32[32,256]{1,0:T(8,128)S(1)} %reshape.7.pos_ref, ...), custom_call_target="tpu_custom_call" | custom-call | flops 17999998976 | bytes 4194304 | tf_op jit(solution)/shard_map/pallas_call | solution.py:363
  137.6 2.3 %collective-permute-start.10 = (bf16[2,72,512]{2,1,0:T(8,128)(2,1)S(1)}, bf16[2,72,512]{2,1,0:T(8,128)(2,1)S(1)}, u32[]{:S(2)}, u32[]{:S(2)}) collective-permute-start(bf16[2,72,512]{2,1,0:T(8,128)(2,1)S(1)} %get-tuple-element.63), channel_id=1, source_target_pairs={{0,32},{8,40},{16,48},{24,56},{32,64},{40,72},{48,80},{56,88},{64,... | collective-permute-start | bytes 442376 | tf_op jit(solution)/shard_map/ppermute | solution.py:498
  139.9 0.0 collective-permute-start.8
  139.9 0.0 collective-permute-done.11.refs_1_
  139.9 1.9 %collective-permute-start.9 = (bf16[2,72,512]{2,1,0:T(8,128)(2,1)S(1)}, bf16[2,72,512]{2,1,0:T(8,128)(2,1)S(1)}, u32[]{:S(2)}, u32[]{:S(2)}) collective-permute-start(bf16[2,72,512]{2,1,0:T(8,128)(2,1)S(1)} %get-tuple-element.61), channel_id=1, source_target_pairs={{0,96},{8,104},{16,112},{24,120},{32,0},{40,8},{48,16},{56,24},{64... | collective-permute-start | bytes 442376 | tf_op jit(solution)/shard_map/ppermute | solution.py:498
  141.8 17.4 %shard_map.88.refs_3_ = bf16[2,72,512]{2,1,0:T(8,128)(2,1)S(1)} custom-call(s32[1]{0:T(128)} %bitcast.1.seq_ref, s32[32,128]{1,0:T(8,128)} %get-tuple-element.40.code_ref, f32[1]{0:T(128)} %get-tuple-element.54.norm_ref, s32[32,256]{1,0:T(8,128)S(1)} %reshape.7.pos_ref, bf16[4096,128]{1,0:T(8,128)(2,1)} %get-tuple-element.55.kv_ref, ...), custom_call_target="tpu_custom_call" | custom-call | flops 6000000000 | bytes 4194304 | tf_op jit(solution)/shard_map/pallas_call | solution.py:363
  159.2 0.0 collective-permute-done.12.refs_2_
  159.2 0.0 collective-permute-done.13.refs_3_
  159.2 0.0 collective-permute-done.10.refs_2_
  159.2 0.0 collective-permute-done.8.refs_0_
  159.2 0.0 collective-permute-done.9.refs_1_
  159.3 1.0 shard_map.89
  160.2 6.5 %all-to-all-start = ((bf16[16,32,128]{2,1,0:T(8,128)(2,1)}), bf16[16,32,128]{2,1,0:T(8,128)(2,1)S(1)}, u32[]{:S(2)}, u32[]{:S(2)}) async-start(bf16[16,32,128]{2,1,0:T(8,128)(2,1)} %shard_map.89), calls=%async_computation | async-start | bytes 262144 | tf_op jit(solution)/shard_map/all_to_all | solution.py:502
  166.7 6.4 %all-to-all-done.pieces_ref = bf16[16,32,128]{2,1,0:T(8,128)(2,1)S(1)} async-done(((bf16[16,32,128]{2,1,0:T(8,128)(2,1)}), bf16[16,32,128]{2,1,0:T(8,128)(2,1)S(1)}, u32[]{:S(2)}, u32[]{:S(2)}) %all-to-all-start) | async-done | bytes 131104 | tf_op jit(solution)/shard_map/all_to_all | solution.py:502
  173.1 1.2 shard_map.90
  (3 shorter events, 0.0 us)
Async XLA Ops:
  0.0 11.6 %copy-start.1 = (s32[8192]{0:T(1024)S(1)}, s32[8192]{0:T(1024)}, u32[]{:S(2)}) copy-start(s32[8192]{0:T(1024)} %param.14) | copy-start | bytes 98308
  0.0 7.7 %copy-start = (bf16[128,1024]{1,0:T(8,128)(2,1)S(1)}, bf16[128,1024]{1,0:T(8,128)(2,1)}, u32[]{:S(2)}) copy-start(bf16[128,1024]{1,0:T(8,128)(2,1)} %param.13) | copy-start | bytes 786436
  6.8 7.2 %collective-permute-start.3 = (bf16[2048,128]{1,0:T(8,128)(2,1)}, bf16[2048,128]{1,0:T(8,128)(2,1)S(1)}, u32[]{:S(2)}, u32[]{:S(2)}) collective-permute-start(bf16[2048,128]{1,0:T(8,128)(2,1)} %get-tuple-element.44), channel_id=1, source_target_pairs={{0,8},{8,0},{16,24},{24,16},{32,40},{40,32},{48,56},{56,48},{64,72... | collective-permute-start | bytes 1572872 | tf_op jit(solution)/shard_map/ppermute | solution.py:465
  7.6 4.1 %collective-permute-start = (bf16[64,512]{1,0:T(8,128)(2,1)}, bf16[64,512]{1,0:T(8,128)(2,1)S(1)}, u32[]{:S(2)}, u32[]{:S(2)}) collective-permute-start(bf16[64,512]{1,0:T(8,128)(2,1)} %get-tuple-element.42), channel_id=1, source_target_pairs={{0,8},{8,0},{16,24},{24,16},{32,40},{40,32},{48,56},{56,48},{64,72... | collective-permute-start | bytes 196616 | tf_op jit(solution)/shard_map/ppermute | solution.py:463
  7.7 29.2 %collective-permute-start.2 = (bf16[128,1024]{1,0:T(8,128)(2,1)S(1)}, bf16[128,1024]{1,0:T(8,128)(2,1)S(1)}, u32[]{:S(2)}, u32[]{:S(2)}) collective-permute-start(bf16[128,1024]{1,0:T(8,128)(2,1)S(1)} %copy-done), channel_id=1, source_target_pairs={{0,4},{1,5},{2,6},{3,7},{4,0},{5,1},{6,2},{7,3},{8,12},{9,13},{10,... | collective-permute-start | bytes 786440 | tf_op jit(solution)/shard_map/ppermute | solution.py:469
  9.0 33.0 %collective-permute-start.4 = (bf16[2048,128]{1,0:T(8,128)(2,1)}, bf16[2048,128]{1,0:T(8,128)(2,1)S(1)}, u32[]{:S(2)}, u32[]{:S(2)}) collective-permute-start(bf16[2048,128]{1,0:T(8,128)(2,1)} %get-tuple-element.43.refs_0_), channel_id=1, source_target_pairs={{0,16},{8,24},{16,0},{24,8},{32,48},{40,56},{48,32},{56,40},{64,80... | collective-permute-start | bytes 1572872 | tf_op jit(solution)/shard_map/ppermute | solution.py:467
  12.5 26.1 %collective-permute-start.1 = (bf16[2,64,512]{2,1,0:T(8,128)(2,1)S(1)}, bf16[2,64,512]{2,1,0:T(8,128)(2,1)S(1)}, u32[]{:S(2)}, u32[]{:S(2)}) collective-permute-start(bf16[2,64,512]{2,1,0:T(8,128)(2,1)S(1)} %pad_maximum_fusion.rest_0_), channel_id=1, source_target_pairs={{0,32},{8,40},{16,48},{24,56},{32,64},{40,72},{48,80},{56,88},{64,... | collective-permute-start | bytes 393224 | tf_op jit(solution)/shard_map/ppermute | solution.py:464
  13.8 28.9 %collective-permute-start.6 = (bf16[2,64,512]{2,1,0:T(8,128)(2,1)S(1)}, bf16[2,64,512]{2,1,0:T(8,128)(2,1)S(1)}, u32[]{:S(2)}, u32[]{:S(2)}) collective-permute-start(bf16[2,64,512]{2,1,0:T(8,128)(2,1)S(1)} %pad_maximum_fusion.rest_0_), channel_id=1, source_target_pairs={{0,96},{8,104},{16,112},{24,120},{32,0},{40,8},{48,16},{56,24},{64... | collective-permute-start | bytes 393224 | tf_op jit(solution)/shard_map/ppermute | solution.py:464
  14.0 29.3 %collective-permute-start.7 = (bf16[2,64,512]{2,1,0:T(8,128)(2,1)S(1)}, bf16[2,64,512]{2,1,0:T(8,128)(2,1)S(1)}, u32[]{:S(2)}, u32[]{:S(2)}) collective-permute-start(bf16[2,64,512]{2,1,0:T(8,128)(2,1)S(1)} %pad_maximum_fusion.rest_0_), channel_id=1, source_target_pairs={{0,64},{8,72},{16,80},{24,88},{32,96},{40,104},{48,112},{56,120},{... | collective-permute-start | bytes 393224 | tf_op jit(solution)/shard_map/ppermute | solution.py:464
  36.9 103.0 %collective-permute-start.11 = (bf16[256,1024]{1,0:T(8,128)(2,1)S(1)}, bf16[256,1024]{1,0:T(8,128)(2,1)S(1)}, u32[]{:S(2)}, u32[]{:S(2)}) collective-permute-start(bf16[256,1024]{1,0:T(8,128)(2,1)S(1)} %constant_dynamic-update-slice_fusion.refs_0_), channel_id=1, source_target_pairs={{0,1},{1,2},{2,3},{3,0},{4,5},{5,6},{6,7},{7,4},{8,9},{9,10},{10,1... | collective-permute-start | bytes 1572872 | tf_op jit(solution)/shard_map/ppermute | solution.py:475
  38.6 120.6 %collective-permute-start.12 = (bf16[256,1024]{1,0:T(8,128)(2,1)S(1)}, bf16[256,1024]{1,0:T(8,128)(2,1)S(1)}, u32[]{:S(2)}, u32[]{:S(2)}) collective-permute-start(bf16[256,1024]{1,0:T(8,128)(2,1)S(1)} %constant_dynamic-update-slice_fusion.refs_0_), channel_id=1, source_target_pairs={{0,2},{1,3},{2,0},{3,1},{4,6},{5,7},{6,4},{7,5},{8,10},{9,11},{10,... | collective-permute-start | bytes 1572872 | tf_op jit(solution)/shard_map/ppermute | solution.py:475
  41.9 117.3 %collective-permute-start.13 = (bf16[256,1024]{1,0:T(8,128)(2,1)S(1)}, bf16[256,1024]{1,0:T(8,128)(2,1)S(1)}, u32[]{:S(2)}, u32[]{:S(2)}) collective-permute-start(bf16[256,1024]{1,0:T(8,128)(2,1)S(1)} %constant_dynamic-update-slice_fusion.refs_0_), channel_id=1, source_target_pairs={{0,3},{1,0},{2,1},{3,2},{4,7},{5,4},{6,5},{7,6},{8,11},{9,8},{10,9... | collective-permute-start | bytes 1572872 | tf_op jit(solution)/shard_map/ppermute | solution.py:475
  42.7 46.2 %collective-permute-start.5 = (bf16[2048,128]{1,0:T(8,128)(2,1)S(1)}, bf16[2048,128]{1,0:T(8,128)(2,1)S(1)}, u32[]{:S(2)}, u32[]{:S(2)}) collective-permute-start(bf16[2048,128]{1,0:T(8,128)(2,1)S(1)} %collective-permute-done.3.refs_1_), channel_id=1, source_target_pairs={{0,16},{8,24},{16,0},{24,8},{32,48},{40,56},{48,32},{56,40},{64,80... | collective-permute-start | bytes 1572872 | tf_op jit(solution)/shard_map/ppermute | solution.py:467
  137.6 21.6 %collective-permute-start.10 = (bf16[2,72,512]{2,1,0:T(8,128)(2,1)S(1)}, bf16[2,72,512]{2,1,0:T(8,128)(2,1)S(1)}, u32[]{:S(2)}, u32[]{:S(2)}) collective-permute-start(bf16[2,72,512]{2,1,0:T(8,128)(2,1)S(1)} %get-tuple-element.63), channel_id=1, source_target_pairs={{0,32},{8,40},{16,48},{24,56},{32,64},{40,72},{48,80},{56,88},{64,... | collective-permute-start | bytes 442376 | tf_op jit(solution)/shard_map/ppermute | solution.py:498
  139.9 19.3 %collective-permute-start.8 = (bf16[2,72,512]{2,1,0:T(8,128)(2,1)S(1)}, bf16[2,72,512]{2,1,0:T(8,128)(2,1)S(1)}, u32[]{:S(2)}, u32[]{:S(2)}) collective-permute-start(bf16[2,72,512]{2,1,0:T(8,128)(2,1)S(1)} %get-tuple-element.60), channel_id=1, source_target_pairs={{0,64},{8,72},{16,80},{24,88},{32,96},{40,104},{48,112},{56,120},{... | collective-permute-start | bytes 442376 | tf_op jit(solution)/shard_map/ppermute | solution.py:498
  139.9 19.3 %collective-permute-start.9 = (bf16[2,72,512]{2,1,0:T(8,128)(2,1)S(1)}, bf16[2,72,512]{2,1,0:T(8,128)(2,1)S(1)}, u32[]{:S(2)}, u32[]{:S(2)}) collective-permute-start(bf16[2,72,512]{2,1,0:T(8,128)(2,1)S(1)} %get-tuple-element.61), channel_id=1, source_target_pairs={{0,96},{8,104},{16,112},{24,120},{32,0},{40,8},{48,16},{56,24},{64... | collective-permute-start | bytes 442376 | tf_op jit(solution)/shard_map/ppermute | solution.py:498
  160.2 12.8 %all-to-all-start = ((bf16[16,32,128]{2,1,0:T(8,128)(2,1)}), bf16[16,32,128]{2,1,0:T(8,128)(2,1)S(1)}, u32[]{:S(2)}, u32[]{:S(2)}) async-start(bf16[16,32,128]{2,1,0:T(8,128)(2,1)} %shard_map.89), calls=%async_computation | async-start | bytes 262144 | tf_op jit(solution)/shard_map/all_to_all | solution.py:502

commit v8 on v7

--- a/solution.py
+++ b/solution.py
@@ -86,8 +86,15 @@
 
 
 def front_kernel(seq_ref, lat_hbm, x_hbm, wq_hbm, wk_hbm, wv_hbm, pos_hbm, mask_hbm, *rest):
-    mine_ref, theirs_ref, own_ref, other_ref, code_ref = rest[:5]
-    lat, x, wq, wk, wv, pos, mask, w_all, sems, x_sems = rest[5:]
+    mine_hbm, theirs_hbm, own_hbm, other_hbm, code_hbm = rest[:5]
+    lat, x, wq, wk, wv, pos, mask, mine_ref, theirs_ref, own_ref, other_ref, code_ref = rest[5:17]
+    w_all, sems, x_sems, out_sems = rest[17:]
+    sent = []
+
+    def send(source, target):
+        sent.append(pltpu.make_async_copy(source, target, out_sems.at[len(sent)]))
+        sent[-1].start()
+
     small = [
         pltpu.make_async_copy(source, target, sems.at[i])
         for i, (source, target) in enumerate(
@@ -105,6 +112,7 @@
     got_pos.wait()
     got_mask.wait()
     list_work(seq_ref[0], pos, mask, code_ref)
+    send(code_ref, code_hbm)
 
     got_wq.wait()
     got_lat.wait()
@@ -112,6 +120,8 @@
     q = q.astype(jnp.bfloat16) * jnp.bfloat16(HS ** -0.5)
     mine_ref[...] = jnp.where(first, q[:HS], q[HS:])
     theirs_ref[...] = jnp.where(first, q[HS:], q[:HS])
+    send(mine_ref, mine_hbm)
+    send(theirs_ref, theirs_hbm)
 
     got_wk.wait()
     got_wv.wait()
@@ -125,6 +135,10 @@
         both = jnp.dot(x[part, :], w_all[...], preferred_element_type=jnp.float32).astype(jnp.bfloat16)
         own_ref[part, :] = both[:, : 2 * HS]
         other_ref[part, :] = both[:, 2 * HS :]
+        send(own_ref.at[part], own_hbm.at[part])
+        send(other_ref.at[part], other_hbm.at[part])
+    for copy in sent:
+        copy.wait()
 
 
 def front(seq, latents, inputs, w_query, w_key, w_value, positions, block_mask):
@@ -134,16 +148,18 @@
     operands = (latents, inputs, w_query, w_key, w_value, spots, block_mask)
     q = jax.ShapeDtypeStruct((HS, rows), jnp.bfloat16)
     kv = jax.ShapeDtypeStruct((keys, 2 * HS), jnp.bfloat16)
+    results = [q, q, kv, kv, jax.ShapeDtypeStruct((spots.shape[0] // 2, BLOCK), jnp.int32)]
     return pl.pallas_call(
         front_kernel,
         in_specs=[SMEM] + [pl.BlockSpec(memory_space=pl.ANY)] * len(operands),
-        out_specs=[VMEM] * 5,
-        out_shape=[q, q, kv, kv, jax.ShapeDtypeStruct((spots.shape[0] // 2, BLOCK), jnp.int32)],
-        scratch_shapes=[pltpu.VMEM(a.shape, a.dtype) for a in operands]
+        out_specs=[pl.BlockSpec(memory_space=pl.ANY)] * 5,
+        out_shape=results,
+        scratch_shapes=[pltpu.VMEM(a.shape, a.dtype) for a in (*operands, *results)]
         + [
             pltpu.VMEM((width, 4 * HS), jnp.bfloat16),
             pltpu.SemaphoreType.DMA((6,)),
             pltpu.SemaphoreType.DMA((4,)),
+            pltpu.SemaphoreType.DMA((11,)),
         ],
         compiler_params=pltpu.CompilerParams(vmem_limit_bytes=61 * 2**20),
         cost_estimate=pl.CostEstimate(
@@ -176,8 +192,8 @@
         in_specs=[VMEM] * len(sources),
         out_specs=[VMEM, VMEM, SMEM],
         out_shape=[
-            pltpu.HBM((keys, 2 * HS), jnp.bfloat16),
-            pltpu.HBM((ACC_ROWS, keys), jnp.bfloat16),
+            jax.ShapeDtypeStruct((keys, 2 * HS), jnp.bfloat16),
+            jax.ShapeDtypeStruct((ACC_ROWS, keys), jnp.bfloat16),
             jax.ShapeDtypeStruct((1,), jnp.float32),
         ],
         compiler_params=pltpu.CompilerParams(vmem_limit_bytes=24 * 2**20),
@@ -357,7 +373,7 @@
 
 def attend(steps, seq, codes, spots, held, queries, before=()):
     kv, vt, norm = held
-    kv, vt, codes = in_hbm(kv, vt, codes)
+    codes, = in_hbm(codes)
     chips = len(steps)
     out = jax.ShapeDtypeStruct((2, ACC_ROWS, queries[0].shape[2]), jnp.bfloat16)
     return pl.pallas_call(

time: 176 us -> 173 us (0.983)
  Pallas kernels: 142 us -> 140 us
where the time goes in v8:
time: 173 us; the launch traced here: 172 us
  Pallas kernels  140 us (81%)
  starting transfers between devices  24.7 us (14%)
  waiting for transfers between devices  6.39 us (4%)
    pallas_call x4, Pallas kernels, attend(): pl.pallas_call(functools.partial(attention_kernel, steps, bool(before)),...  128 us
    pallas_call x1, Pallas kernels, front(): pl.pallas_call(front_kernel, in_specs=[SMEM] + [pl.BlockSpec(memory_space...  6.64 us
    all_to_all x1, starting transfers between devices, body(): lax.all_to_all(pieces, ('seq', 'grp'), 0, 0, axis_index_groups=owners)  6.49 us
    all_to_all x1, waiting for transfers between devices, body(): lax.all_to_all(pieces, ('seq', 'grp'), 0, 0, axis_index_groups=owners)  6.35 us
    ppermute x3, starting transfers between devices, body(): lax.ppermute(w_pair, 'grp', [(g, g & 4 | g + k & 3) for g in range(8)])  5.74 us
    ppermute x3, starting transfers between devices, body(): lax.ppermute(part, 'seq', along_x(-by))  4.17 us
  transfers between devices with their start and end apart: 15, of which 1 were waited for; matrix products, arithmetic and copies ran while one was open for 1% of the time, Pallas kernels for 76%

profile of v8, /device:TPU:3, one launch (start us, length us, event | category | flops | bytes accessed | tf_op | source)
XLA Modules:
  0.0 172.0 jit_solution(9935152306680204680)
XLA Ops:
  0.0 0.0 copy-start.1
  0.0 0.0 copy-start
  0.0 6.6 %shard_map.82 = (bf16[64,512]{1,0:T(8,128)(2,1)}, bf16[64,512]{1,0:T(8,128)(2,1)}, bf16[2048,128]{1,0:T(8,128)(2,1)}, bf16[2048,128]{1,0:T(8,128)(2,1)}, s32[32,128]{1,0:T(8,128)}) custom-call(s32[1]{0:T(128)} %bitcast.1.seq_ref, bf16[512,1024]{1,0:T(8,128)(2,1)} %lat_hbm.1, bf16[2048,1024]{1,0:T(8,128)(2,1)} %x_hbm.1, bf16[1024,128]{1,0:T(8,128)(2,1)} %wq_hbm.1, ...), custom_call_target="tpu_custom_call" | custom-call | flops 1207959552 | bytes 6291456 | tf_op jit(solution)/shard_map/pallas_call | solution.py:152
  6.7 0.8 collective-permute-start.3
  7.4 0.1 collective-permute-start
  7.5 0.0 copy-done
  7.5 1.3 collective-permute-start.2
  8.8 2.6 %collective-permute-start.4 = (bf16[2048,128]{1,0:T(8,128)(2,1)}, bf16[2048,128]{1,0:T(8,128)(2,1)S(1)}, u32[]{:S(2)}, u32[]{:S(2)}) collective-permute-start(bf16[2048,128]{1,0:T(8,128)(2,1)} %get-tuple-element.43.refs_0_), channel_id=1, source_target_pairs={{0,16},{8,24},{16,0},{24,8},{32,48},{40,56},{48,32},{56,40},{64,80... | collective-permute-start | bytes 1572872 | tf_op jit(solution)/shard_map/ppermute | solution.py:483
  11.4 0.0 copy-done.1
  11.5 0.0 collective-permute-done
  11.5 0.9 pad_maximum_fusion.rest_0_
  12.3 1.3 collective-permute-start.1
  13.6 0.3 collective-permute-start.6
  13.9 0.0 collective-permute-done.3.refs_1_
  13.9 1.8 %collective-permute-start.7 = (bf16[2,64,512]{2,1,0:T(8,128)(2,1)S(1)}, bf16[2,64,512]{2,1,0:T(8,128)(2,1)S(1)}, u32[]{:S(2)}, u32[]{:S(2)}) collective-permute-start(bf16[2,64,512]{2,1,0:T(8,128)(2,1)S(1)} %pad_maximum_fusion.rest_0_), channel_id=1, source_target_pairs={{0,64},{8,72},{16,80},{24,88},{32,96},{40,104},{48,112},{56,120},{... | collective-permute-start | bytes 393224 | tf_op jit(solution)/shard_map/ppermute | solution.py:480
  15.7 2.1 %shard_map.83 = (bf16[4096,128]{1,0:T(8,128)(2,1)S(1)}, bf16[72,4096]{1,0:T(8,128)(2,1)S(1)}, f32[1]{0:T(128)}) custom-call(bf16[2048,128]{1,0:T(8,128)(2,1)} %get-tuple-element.43.refs_0_, bf16[2048,128]{1,0:T(8,128)(2,1)S(1)} %collective-permute-done.3.refs_1_), custom_call_target="tpu_custom_call" | custom-call | tf_op jit(solution)/shard_map/pallas_call | solution.py:190
  17.8 17.9 %shard_map.84.rest_1_ = bf16[2,72,512]{2,1,0:T(8,128)(2,1)S(1)} custom-call(s32[1]{0:T(128)} %bitcast.1.seq_ref, s32[32,128]{1,0:T(8,128)} %get-tuple-element.40.code_ref, f32[1]{0:T(128)} %get-tuple-element.45.norm_ref, s32[32,256]{1,0:T(8,128)S(1)} %reshape.7.pos_ref, bf16[4096,128]{1,0:T(8,128)(2,1)S(1)} %get-tuple-element.46.kv_ref, ...), custom_call_target="tpu_custom_call" | custom-call | flops 6000000000 | bytes 4194304 | tf_op jit(solution)/shard_map/pallas_call | solution.py:379
  35.7 0.0 collective-permute-done.2
  35.8 1.7 collective-permute-start.11
  37.5 0.0 collective-permute-done.1.rest_0_.rest_1_
  37.5 3.3 %collective-permute-start.12 = (bf16[256,1024]{1,0:T(8,128)(2,1)S(1)}, bf16[256,1024]{1,0:T(8,128)(2,1)S(1)}, u32[]{:S(2)}, u32[]{:S(2)}) collective-permute-start(bf16[256,1024]{1,0:T(8,128)(2,1)S(1)} %constant_dynamic-update-slice_fusion.refs_0_), channel_id=1, source_target_pairs={{0,2},{1,3},{2,0},{3,1},{4,6},{5,7},{6,4},{7,5},{8,10},{9,11},{10,... | collective-permute-start | bytes 1572872 | tf_op jit(solution)/shard_map/ppermute | solution.py:491
  40.8 0.0 collective-permute-done.4.refs_0_
  40.8 0.7 collective-permute-start.13
  41.5 0.0 collective-permute-done.6.rest_1_.rest_2_
  41.5 0.2 collective-permute-start.5
  41.7 0.0 collective-permute-done.7.rest_2_.rest_0_
  41.7 45.6 %shard_map.85 = (bf16[2,72,512]{2,1,0:T(8,128)(2,1)S(1)}, bf16[2,72,512]{2,1,0:T(8,128)(2,1)S(1)}, bf16[2,72,512]{2,1,0:T(8,128)(2,1)S(1)}) custom-call(s32[1]{0:T(128)} %bitcast.1.seq_ref, s32[32,128]{1,0:T(8,128)} %get-tuple-element.40.code_ref, f32[1]{0:T(128)} %get-tuple-element.45.norm_ref, s32[32,256]{1,0:T(8,128)S(1)} %reshape.7.pos_ref, ...), custom_call_target="tpu_custom_call" | custom-call | flops 17999998976 | bytes 4194304 | tf_op jit(solution)/shard_map/pallas_call | solution.py:379
  87.3 0.0 collective-permute-done.5.refs_1_
  87.4 1.0 shard_map.86
  88.4 46.3 %shard_map.87 = (bf16[2,72,512]{2,1,0:T(8,128)(2,1)S(1)}, bf16[2,72,512]{2,1,0:T(8,128)(2,1)S(1)}, bf16[2,72,512]{2,1,0:T(8,128)(2,1)S(1)}) custom-call(s32[1]{0:T(128)} %bitcast.1.seq_ref, s32[32,128]{1,0:T(8,128)} %get-tuple-element.40.code_ref, f32[1]{0:T(128)} %get-tuple-element.54.norm_ref, s32[32,256]{1,0:T(8,128)S(1)} %reshape.7.pos_ref, ...), custom_call_target="tpu_custom_call" | custom-call | flops 17999998976 | bytes 4194304 | tf_op jit(solution)/shard_map/pallas_call | solution.py:379
  134.8 2.3 %collective-permute-start.10 = (bf16[2,72,512]{2,1,0:T(8,128)(2,1)S(1)}, bf16[2,72,512]{2,1,0:T(8,128)(2,1)S(1)}, u32[]{:S(2)}, u32[]{:S(2)}) collective-permute-start(bf16[2,72,512]{2,1,0:T(8,128)(2,1)S(1)} %get-tuple-element.63), channel_id=1, source_target_pairs={{0,32},{8,40},{16,48},{24,56},{32,64},{40,72},{48,80},{56,88},{64,... | collective-permute-start | bytes 442376 | tf_op jit(solution)/shard_map/ppermute | solution.py:514
  137.0 0.0 collective-permute-start.8
  137.0 0.0 collective-permute-done.11.refs_1_
  137.0 1.9 %collective-permute-start.9 = (bf16[2,72,512]{2,1,0:T(8,128)(2,1)S(1)}, bf16[2,72,512]{2,1,0:T(8,128)(2,1)S(1)}, u32[]{:S(2)}, u32[]{:S(2)}) collective-permute-start(bf16[2,72,512]{2,1,0:T(8,128)(2,1)S(1)} %get-tuple-element.61), channel_id=1, source_target_pairs={{0,96},{8,104},{16,112},{24,120},{32,0},{40,8},{48,16},{56,24},{64... | collective-permute-start | bytes 442376 | tf_op jit(solution)/shard_map/ppermute | solution.py:514
  138.9 18.0 %shard_map.88.refs_3_ = bf16[2,72,512]{2,1,0:T(8,128)(2,1)S(1)} custom-call(s32[1]{0:T(128)} %bitcast.1.seq_ref, s32[32,128]{1,0:T(8,128)} %get-tuple-element.40.code_ref, f32[1]{0:T(128)} %get-tuple-element.54.norm_ref, s32[32,256]{1,0:T(8,128)S(1)} %reshape.7.pos_ref, bf16[4096,128]{1,0:T(8,128)(2,1)S(1)} %get-tuple-element.55.kv_ref, ...), custom_call_target="tpu_custom_call" | custom-call | flops 6000000000 | bytes 4194304 | tf_op jit(solution)/shard_map/pallas_call | solution.py:379
  157.0 0.0 collective-permute-done.12.refs_2_
  157.0 0.0 collective-permute-done.13.refs_3_
  157.0 0.0 collective-permute-done.10.refs_2_
  157.0 0.0 collective-permute-done.8.refs_0_
  157.0 0.0 collective-permute-done.9.refs_1_
  157.0 1.0 shard_map.89
  158.0 6.5 %all-to-all-start = ((bf16[16,32,128]{2,1,0:T(8,128)(2,1)}), bf16[16,32,128]{2,1,0:T(8,128)(2,1)S(1)}, u32[]{:S(2)}, u32[]{:S(2)}) async-start(bf16[16,32,128]{2,1,0:T(8,128)(2,1)} %shard_map.89), calls=%async_computation | async-start | bytes 262144 | tf_op jit(solution)/shard_map/all_to_all | solution.py:518
  164.5 6.4 %all-to-all-done.pieces_ref = bf16[16,32,128]{2,1,0:T(8,128)(2,1)S(1)} async-done(((bf16[16,32,128]{2,1,0:T(8,128)(2,1)}), bf16[16,32,128]{2,1,0:T(8,128)(2,1)S(1)}, u32[]{:S(2)}, u32[]{:S(2)}) %all-to-all-start) | async-done | bytes 131104 | tf_op jit(solution)/shard_map/all_to_all | solution.py:518
  170.9 1.2 shard_map.90
  (3 shorter events, 0.0 us)
Async XLA Ops:
  0.0 11.4 %copy-start.1 = (s32[8192]{0:T(1024)S(1)}, s32[8192]{0:T(1024)}, u32[]{:S(2)}) copy-start(s32[8192]{0:T(1024)} %param.14) | copy-start | bytes 98308
  0.0 7.5 %copy-start = (bf16[128,1024]{1,0:T(8,128)(2,1)S(1)}, bf16[128,1024]{1,0:T(8,128)(2,1)}, u32[]{:S(2)}) copy-start(bf16[128,1024]{1,0:T(8,128)(2,1)} %param.13) | copy-start | bytes 786436
  6.7 7.2 %collective-permute-start.3 = (bf16[2048,128]{1,0:T(8,128)(2,1)}, bf16[2048,128]{1,0:T(8,128)(2,1)S(1)}, u32[]{:S(2)}, u32[]{:S(2)}) collective-permute-start(bf16[2048,128]{1,0:T(8,128)(2,1)} %get-tuple-element.44), channel_id=1, source_target_pairs={{0,8},{8,0},{16,24},{24,16},{32,40},{40,32},{48,56},{56,48},{64,72... | collective-permute-start | bytes 1572872 | tf_op jit(solution)/shard_map/ppermute | solution.py:481
  7.4 4.1 %collective-permute-start = (bf16[64,512]{1,0:T(8,128)(2,1)}, bf16[64,512]{1,0:T(8,128)(2,1)S(1)}, u32[]{:S(2)}, u32[]{:S(2)}) collective-permute-start(bf16[64,512]{1,0:T(8,128)(2,1)} %get-tuple-element.42), channel_id=1, source_target_pairs={{0,8},{8,0},{16,24},{24,16},{32,40},{40,32},{48,56},{56,48},{64,72... | collective-permute-start | bytes 196616 | tf_op jit(solution)/shard_map/ppermute | solution.py:479
  7.5 28.2 %collective-permute-start.2 = (bf16[128,1024]{1,0:T(8,128)(2,1)S(1)}, bf16[128,1024]{1,0:T(8,128)(2,1)S(1)}, u32[]{:S(2)}, u32[]{:S(2)}) collective-permute-start(bf16[128,1024]{1,0:T(8,128)(2,1)S(1)} %copy-done), channel_id=1, source_target_pairs={{0,4},{1,5},{2,6},{3,7},{4,0},{5,1},{6,2},{7,3},{8,12},{9,13},{10,... | collective-permute-start | bytes 786440 | tf_op jit(solution)/shard_map/ppermute | solution.py:485
  8.8 32.0 %collective-permute-start.4 = (bf16[2048,128]{1,0:T(8,128)(2,1)}, bf16[2048,128]{1,0:T(8,128)(2,1)S(1)}, u32[]{:S(2)}, u32[]{:S(2)}) collective-permute-start(bf16[2048,128]{1,0:T(8,128)(2,1)} %get-tuple-element.43.refs_0_), channel_id=1, source_target_pairs={{0,16},{8,24},{16,0},{24,8},{32,48},{40,56},{48,32},{56,40},{64,80... | collective-permute-start | bytes 1572872 | tf_op jit(solution)/shard_map/ppermute | solution.py:483
  12.3 25.2 %collective-permute-start.1 = (bf16[2,64,512]{2,1,0:T(8,128)(2,1)S(1)}, bf16[2,64,512]{2,1,0:T(8,128)(2,1)S(1)}, u32[]{:S(2)}, u32[]{:S(2)}) collective-permute-start(bf16[2,64,512]{2,1,0:T(8,128)(2,1)S(1)} %pad_maximum_fusion.rest_0_), channel_id=1, source_target_pairs={{0,32},{8,40},{16,48},{24,56},{32,64},{40,72},{48,80},{56,88},{64,... | collective-permute-start | bytes 393224 | tf_op jit(solution)/shard_map/ppermute | solution.py:480
  13.6 27.9 %collective-permute-start.6 = (bf16[2,64,512]{2,1,0:T(8,128)(2,1)S(1)}, bf16[2,64,512]{2,1,0:T(8,128)(2,1)S(1)}, u32[]{:S(2)}, u32[]{:S(2)}) collective-permute-start(bf16[2,64,512]{2,1,0:T(8,128)(2,1)S(1)} %pad_maximum_fusion.rest_0_), channel_id=1, source_target_pairs={{0,96},{8,104},{16,112},{24,120},{32,0},{40,8},{48,16},{56,24},{64... | collective-permute-start | bytes 393224 | tf_op jit(solution)/shard_map/ppermute | solution.py:480
  13.9 27.9 %collective-permute-start.7 = (bf16[2,64,512]{2,1,0:T(8,128)(2,1)S(1)}, bf16[2,64,512]{2,1,0:T(8,128)(2,1)S(1)}, u32[]{:S(2)}, u32[]{:S(2)}) collective-permute-start(bf16[2,64,512]{2,1,0:T(8,128)(2,1)S(1)} %pad_maximum_fusion.rest_0_), channel_id=1, source_target_pairs={{0,64},{8,72},{16,80},{24,88},{32,96},{40,104},{48,112},{56,120},{... | collective-permute-start | bytes 393224 | tf_op jit(solution)/shard_map/ppermute | solution.py:480
  35.8 101.3 %collective-permute-start.11 = (bf16[256,1024]{1,0:T(8,128)(2,1)S(1)}, bf16[256,1024]{1,0:T(8,128)(2,1)S(1)}, u32[]{:S(2)}, u32[]{:S(2)}) collective-permute-start(bf16[256,1024]{1,0:T(8,128)(2,1)S(1)} %constant_dynamic-update-slice_fusion.refs_0_), channel_id=1, source_target_pairs={{0,1},{1,2},{2,3},{3,0},{4,5},{5,6},{6,7},{7,4},{8,9},{9,10},{10,1... | collective-permute-start | bytes 1572872 | tf_op jit(solution)/shard_map/ppermute | solution.py:491
  37.5 119.5 %collective-permute-start.12 = (bf16[256,1024]{1,0:T(8,128)(2,1)S(1)}, bf16[256,1024]{1,0:T(8,128)(2,1)S(1)}, u32[]{:S(2)}, u32[]{:S(2)}) collective-permute-start(bf16[256,1024]{1,0:T(8,128)(2,1)S(1)} %constant_dynamic-update-slice_fusion.refs_0_), channel_id=1, source_target_pairs={{0,2},{1,3},{2,0},{3,1},{4,6},{5,7},{6,4},{7,5},{8,10},{9,11},{10,... | collective-permute-start | bytes 1572872 | tf_op jit(solution)/shard_map/ppermute | solution.py:491
  40.8 116.2 %collective-permute-start.13 = (bf16[256,1024]{1,0:T(8,128)(2,1)S(1)}, bf16[256,1024]{1,0:T(8,128)(2,1)S(1)}, u32[]{:S(2)}, u32[]{:S(2)}) collective-permute-start(bf16[256,1024]{1,0:T(8,128)(2,1)S(1)} %constant_dynamic-update-slice_fusion.refs_0_), channel_id=1, source_target_pairs={{0,3},{1,0},{2,1},{3,2},{4,7},{5,4},{6,5},{7,6},{8,11},{9,8},{10,9... | collective-permute-start | bytes 1572872 | tf_op jit(solution)/shard_map/ppermute | solution.py:491
  41.5 45.8 %collective-permute-start.5 = (bf16[2048,128]{1,0:T(8,128)(2,1)S(1)}, bf16[2048,128]{1,0:T(8,128)(2,1)S(1)}, u32[]{:S(2)}, u32[]{:S(2)}) collective-permute-start(bf16[2048,128]{1,0:T(8,128)(2,1)S(1)} %collective-permute-done.3.refs_1_), channel_id=1, source_target_pairs={{0,16},{8,24},{16,0},{24,8},{32,48},{40,56},{48,32},{56,40},{64,80... | collective-permute-start | bytes 1572872 | tf_op jit(solution)/shard_map/ppermute | solution.py:483
  134.8 22.2 %collective-permute-start.10 = (bf16[2,72,512]{2,1,0:T(8,128)(2,1)S(1)}, bf16[2,72,512]{2,1,0:T(8,128)(2,1)S(1)}, u32[]{:S(2)}, u32[]{:S(2)}) collective-permute-start(bf16[2,72,512]{2,1,0:T(8,128)(2,1)S(1)} %get-tuple-element.63), channel_id=1, source_target_pairs={{0,32},{8,40},{16,48},{24,56},{32,64},{40,72},{48,80},{56,88},{64,... | collective-permute-start | bytes 442376 | tf_op jit(solution)/shard_map/ppermute | solution.py:514
  137.0 20.0 %collective-permute-start.8 = (bf16[2,72,512]{2,1,0:T(8,128)(2,1)S(1)}, bf16[2,72,512]{2,1,0:T(8,128)(2,1)S(1)}, u32[]{:S(2)}, u32[]{:S(2)}) collective-permute-start(bf16[2,72,512]{2,1,0:T(8,128)(2,1)S(1)} %get-tuple-element.60), channel_id=1, source_target_pairs={{0,64},{8,72},{16,80},{24,88},{32,96},{40,104},{48,112},{56,120},{... | collective-permute-start | bytes 442376 | tf_op jit(solution)/shard_map/ppermute | solution.py:514
  137.0 20.0 %collective-permute-start.9 = (bf16[2,72,512]{2,1,0:T(8,128)(2,1)S(1)}, bf16[2,72,512]{2,1,0:T(8,128)(2,1)S(1)}, u32[]{:S(2)}, u32[]{:S(2)}) collective-permute-start(bf16[2,72,512]{2,1,0:T(8,128)(2,1)S(1)} %get-tuple-element.61), channel_id=1, source_target_pairs={{0,96},{8,104},{16,112},{24,120},{32,0},{40,8},{48,16},{56,24},{64... | collective-permute-start | bytes 442376 | tf_op jit(solution)/shard_map/ppermute | solution.py:514
  158.0 12.8 %all-to-all-start = ((bf16[16,32,128]{2,1,0:T(8,128)(2,1)}), bf16[16,32,128]{2,1,0:T(8,128)(2,1)S(1)}, u32[]{:S(2)}, u32[]{:S(2)}) async-start(bf16[16,32,128]{2,1,0:T(8,128)(2,1)} %shard_map.89), calls=%async_computation | async-start | bytes 262144 | tf_op jit(solution)/shard_map/all_to_all | solution.py:518

commit v9 on v8

--- a/solution.py
+++ b/solution.py
@@ -86,8 +86,8 @@
 
 
 def front_kernel(seq_ref, lat_hbm, x_hbm, wq_hbm, wk_hbm, wv_hbm, pos_hbm, mask_hbm, *rest):
-    mine_hbm, theirs_hbm, own_hbm, other_hbm, code_hbm = rest[:5]
-    lat, x, wq, wk, wv, pos, mask, mine_ref, theirs_ref, own_ref, other_ref, code_ref = rest[5:17]
+    pair_hbm, theirs_hbm, own_hbm, other_hbm, code_hbm = rest[:5]
+    lat, x, wq, wk, wv, pos, mask, pair_ref, theirs_ref, own_ref, other_ref, code_ref = rest[5:17]
     w_all, sems, x_sems, out_sems = rest[17:]
     sent = []
 
@@ -118,9 +118,11 @@
     got_lat.wait()
     q = jnp.dot(lat[...], wq[...], preferred_element_type=jnp.float32).T
     q = q.astype(jnp.bfloat16) * jnp.bfloat16(HS ** -0.5)
-    mine_ref[...] = jnp.where(first, q[:HS], q[HS:])
+    mine = jnp.where(first, q[:HS], q[HS:])
+    pair_ref[0] = mine
+    pair_ref[1] = mine
     theirs_ref[...] = jnp.where(first, q[HS:], q[:HS])
-    send(mine_ref, mine_hbm)
+    send(pair_ref, pair_hbm)
     send(theirs_ref, theirs_hbm)
 
     got_wk.wait()
@@ -148,7 +150,7 @@
     operands = (latents, inputs, w_query, w_key, w_value, spots, block_mask)
     q = jax.ShapeDtypeStruct((HS, rows), jnp.bfloat16)
     kv = jax.ShapeDtypeStruct((keys, 2 * HS), jnp.bfloat16)
-    results = [q, q, kv, kv, jax.ShapeDtypeStruct((spots.shape[0] // 2, BLOCK), jnp.int32)]
+    results = [jax.ShapeDtypeStruct((2, HS, rows), jnp.bfloat16), q, kv, kv, jax.ShapeDtypeStruct((spots.shape[0] // 2, BLOCK), jnp.int32)]
     return pl.pallas_call(
         front_kernel,
         in_specs=[SMEM] + [pl.BlockSpec(memory_space=pl.ANY)] * len(operands),
@@ -433,7 +435,7 @@
     me = grp_ref[0]
     result = None
     for k, w_ref in enumerate(w_refs):
-        near = jnp.bitwise_or(jnp.bitwise_and(me, 4), jnp.bitwise_and(me - k, 3))
+        near = jnp.bitwise_xor(me, k)
         order = [c * groups + g for g in (near, jnp.bitwise_xor(near, 4)) for c in range(2)]
         blocks = [pieces_ref[i] for i in order]
         upper = jnp.concatenate([p[:, :HS] for p in blocks], 1)
@@ -455,11 +457,11 @@
 
 
 def along_x(by):
-    return [(s, (s + 4 * by) % 16) for s in range(16)]
+    return [(s, s ^ (4 * by)) for s in range(16)]
 
 
 def came_from(s, by):
-    return jnp.bitwise_and(s - 4 * by, 15)
+    return jnp.bitwise_xor(s, 4 * by)
 
 
 NEAR_CALLS = ((0,), (1, 3, 2))
@@ -473,10 +475,10 @@
     grp = lax.axis_index("grp")[None]
     core = jnp.bitwise_and(seq, 1)
 
-    mine, theirs, kv_own, kv_other, codes = front(
+    q_chip, theirs, kv_own, kv_other, codes = front(
         seq, latents, inputs, w_query, w_key, w_value, positions, block_mask
     )
-    q_chip = jnp.stack([mine, lax.ppermute(theirs, "seq", CORE_SWAP)])
+    q_chip = q_chip.at[1].set(lax.ppermute(theirs, "seq", CORE_SWAP))
     queries = {by: q_chip if by == 0 else lax.ppermute(q_chip, "seq", along_x(by)) for by in (0, 1, 3, 2)}
     kv_partner = lax.ppermute(kv_other, "seq", CORE_SWAP)
     near = prepare(*in_hbm(kv_own), kv_partner)
@@ -484,11 +486,12 @@
 
     w_other = lax.ppermute(w_out, "grp", [(g, g ^ 4) for g in range(8)])
     spots = positions.reshape(-1, ROWS)
-    near_parts = dict(zip(NEAR_CALLS[0], attend(NEAR_CALLS[0], seq, codes, spots, near, [q_chip])))
+    queries[0], = in_hbm(q_chip)
+    near_parts = dict(zip(NEAR_CALLS[0], attend(NEAR_CALLS[0], seq, codes, spots, near, [queries[0]])))
     w_other, near_parts[0] = lax.optimization_barrier((w_other, near_parts[0]))
     w_pair = jnp.concatenate([w_out, w_other], 0)
     w_turns = [w_pair] + [
-        lax.ppermute(w_pair, "grp", [(g, (g & 4) | ((g + k) & 3)) for g in range(8)]) for k in (1, 2, 3)
+        lax.ppermute(w_pair, "grp", [(g, g ^ k) for g in range(8)]) for k in (1, 2, 3)
     ]
 
     parts = {}
@@ -511,7 +514,7 @@
         parts.update(zip(call, done))
         last = call[-1]
 
-    parts = [part if by == 0 else lax.ppermute(part, "seq", along_x(-by)) for by, part in parts.items()]
+    parts = [part if by == 0 else lax.ppermute(part, "seq", along_x(by)) for by, part in parts.items()]
     parts, w_turns = lax.optimization_barrier((parts, w_turns))
     pieces = combine(core, parts)
     owners = [[(4 * x + 2 * y + c) * 8 + g for c in range(2) for g in range(8)] for x in range(4) for y in range(2)]

time: 173 us -> 172 us (level)
  transfers between devices with their start and end apart: 15 -> 15, of which waited for: 1 -> 1; matrix products, arithmetic and copies ran while one was open for 1% -> 0% of each run, Pallas kernels for 76% -> 76%
where the time goes in v9:
time: 172 us
  Pallas kernels  140 us (81%)
  starting transfers between devices  24.7 us (14%)
  waiting for transfers between devices  6.38 us (4%)
    pallas_call x4, Pallas kernels, attend(): pl.pallas_call(functools.partial(attention_kernel, steps, bool(before)),...  128 us
    all_to_all x1, starting transfers between devices, body(): lax.all_to_all(pieces, ('seq', 'grp'), 0, 0, axis_index_groups=owners)  7.63 us
    pallas_call x1, Pallas kernels, front(): pl.pallas_call(front_kernel, in_specs=[SMEM] + [pl.BlockSpec(memory_space...  6.64 us
    all_to_all x1, waiting for transfers between devices, body(): lax.all_to_all(pieces, ('seq', 'grp'), 0, 0, axis_index_groups=owners)  6.34 us
    ppermute x3, starting transfers between devices, body(): lax.ppermute(w_pair, 'grp', [(g, g ^ k) for g in range(8)])  5.02 us
  transfers between devices with their start and end apart: 15, of which 1 were waited for; matrix products, arithmetic and copies ran while one was open for 0% of the time, Pallas kernels for 76%

profile of v9, /device:TPU:3, one launch (start us, length us, event | category | flops | bytes accessed | tf_op | source)
XLA Modules:
  0.0 171.7 jit_solution(4027559875536508646)
XLA Ops:
  0.0 0.0 copy-start.1
  0.0 0.0 copy-start
  0.0 6.6 %shard_map.82 = (bf16[2,64,512]{2,1,0:T(8,128)(2,1)}, bf16[64,512]{1,0:T(8,128)(2,1)}, bf16[2048,128]{1,0:T(8,128)(2,1)}, bf16[2048,128]{1,0:T(8,128)(2,1)}, s32[32,128]{1,0:T(8,128)}) custom-call(s32[1]{0:T(128)} %bitcast.1.seq_ref, bf16[512,1024]{1,0:T(8,128)(2,1)} %lat_hbm.1, bf16[2048,1024]{1,0:T(8,128)(2,1)} %x_hbm.1, bf16[1024,128]{1,0:T(8,128)(2,1)} %wq_hbm.1, ...), custom_call_target="tpu_custom_call" | custom-call | flops 1207959552 | bytes 6291456 | tf_op jit(solution)/shard_map/pallas_call | solution.py:154
  6.7 0.8 collective-permute-start.3
  7.4 0.1 collective-permute-start
  7.5 0.0 copy-done
  7.5 1.3 collective-permute-start.2
  8.8 2.6 %collective-permute-start.4 = (bf16[2048,128]{1,0:T(8,128)(2,1)}, bf16[2048,128]{1,0:T(8,128)(2,1)S(1)}, u32[]{:S(2)}, u32[]{:S(2)}) collective-permute-start(bf16[2048,128]{1,0:T(8,128)(2,1)} %get-tuple-element.55.refs_0_), channel_id=1, source_target_pairs={{0,16},{8,24},{16,0},{24,8},{32,48},{40,56},{48,32},{56,40},{64,80... | collective-permute-start | bytes 1572872 | tf_op jit(solution)/shard_map/ppermute | solution.py:485
  11.4 0.0 copy-done.1
  11.5 0.0 collective-permute-done
  11.5 0.6 bitcast_dynamic-update-slice_fusion.rest_0_
  12.1 0.3 collective-permute-start.1
  12.4 1.9 %collective-permute-start.6 = (bf16[2,64,512]{2,1,0:T(8,128)(2,1)}, bf16[2,64,512]{2,1,0:T(8,128)(2,1)S(1)}, u32[]{:S(2)}, u32[]{:S(2)}) collective-permute-start(bf16[2,64,512]{2,1,0:T(8,128)(2,1)} %bitcast_dynamic-update-slice_fusion.rest_0_), channel_id=1, source_target_pairs={{0,96},{8,104},{16,112},{24,120},{32,64},{40,72},{48,80},{56,88},{... | collective-permute-start | bytes 393224 | tf_op jit(solution)/shard_map/ppermute | solution.py:482
  14.2 0.0 collective-permute-done.3.refs_1_
  14.2 1.1 collective-permute-start.7
  15.4 2.1 %shard_map.83 = (bf16[4096,128]{1,0:T(8,128)(2,1)S(1)}, bf16[72,4096]{1,0:T(8,128)(2,1)S(1)}, f32[1]{0:T(128)}) custom-call(bf16[2048,128]{1,0:T(8,128)(2,1)} %get-tuple-element.55.refs_0_, bf16[2048,128]{1,0:T(8,128)(2,1)S(1)} %collective-permute-done.3.refs_1_), custom_call_target="tpu_custom_call" | custom-call | tf_op jit(solution)/shard_map/pallas_call | solution.py:192
  17.4 18.0 %shard_map.84.rest_1_ = bf16[2,72,512]{2,1,0:T(8,128)(2,1)S(1)} custom-call(s32[1]{0:T(128)} %bitcast.1.seq_ref, s32[32,128]{1,0:T(8,128)} %get-tuple-element.52.code_ref, f32[1]{0:T(128)} %get-tuple-element.57.norm_ref, s32[32,256]{1,0:T(8,128)S(1)} %reshape.40.pos_ref, bf16[4096,128]{1,0:T(8,128)(2,1)S(1)} %get-tuple-element.58.kv_ref, ...), custom_call_target="tpu_custom_call" | custom-call | flops 6000000000 | bytes 4194304 | tf_op jit(solution)/shard_map/pallas_call | solution.py:381
  35.4 0.0 collective-permute-done.2
  35.5 1.7 collective-permute-start.11
  37.2 0.0 collective-permute-done.1.rest_0_.rest_1_
  37.2 3.3 %collective-permute-start.12 = (bf16[256,1024]{1,0:T(8,128)(2,1)S(1)}, bf16[256,1024]{1,0:T(8,128)(2,1)S(1)}, u32[]{:S(2)}, u32[]{:S(2)}) collective-permute-start(bf16[256,1024]{1,0:T(8,128)(2,1)S(1)} %constant_dynamic-update-slice_fusion.refs_0_), channel_id=1, source_target_pairs={{0,2},{1,3},{2,0},{3,1},{4,6},{5,7},{6,4},{7,5},{8,10},{9,11},{10,... | collective-permute-start | bytes 1572872 | tf_op jit(solution)/shard_map/ppermute | solution.py:494
  40.5 0.0 collective-permute-done.4.refs_0_
  40.5 0.0 collective-permute-start.13
  40.5 0.0 collective-permute-done.6.rest_1_.rest_2_
  40.5 0.7 collective-permute-start.5
  41.3 0.0 collective-permute-done.7.rest_2_.rest_0_
  41.3 46.5 %shard_map.85 = (bf16[2,72,512]{2,1,0:T(8,128)(2,1)S(1)}, bf16[2,72,512]{2,1,0:T(8,128)(2,1)S(1)}, bf16[2,72,512]{2,1,0:T(8,128)(2,1)S(1)}) custom-call(s32[1]{0:T(128)} %bitcast.1.seq_ref, s32[32,128]{1,0:T(8,128)} %get-tuple-element.52.code_ref, f32[1]{0:T(128)} %get-tuple-element.57.norm_ref, s32[32,256]{1,0:T(8,128)S(1)} %reshape.40.pos_ref, ...), custom_call_target="tpu_custom_call" | custom-call | flops 17999998976 | bytes 4194304 | tf_op jit(solution)/shard_map/pallas_call | solution.py:381
  87.8 0.0 collective-permute-done.5.refs_1_
  87.8 1.0 shard_map.86
  88.8 46.3 %shard_map.87 = (bf16[2,72,512]{2,1,0:T(8,128)(2,1)S(1)}, bf16[2,72,512]{2,1,0:T(8,128)(2,1)S(1)}, bf16[2,72,512]{2,1,0:T(8,128)(2,1)S(1)}) custom-call(s32[1]{0:T(128)} %bitcast.1.seq_ref, s32[32,128]{1,0:T(8,128)} %get-tuple-element.52.code_ref, f32[1]{0:T(128)} %get-tuple-element.66.norm_ref, s32[32,256]{1,0:T(8,128)S(1)} %reshape.40.pos_ref, ...), custom_call_target="tpu_custom_call" | custom-call | flops 17999998976 | bytes 4194304 | tf_op jit(solution)/shard_map/pallas_call | solution.py:381
  135.1 0.9 collective-permute-start.10
  136.0 0.7 collective-permute-start.8
  136.7 0.0 collective-permute-done.11.refs_1_
  136.7 1.7 %collective-permute-start.9 = (bf16[2,72,512]{2,1,0:T(8,128)(2,1)S(1)}, bf16[2,72,512]{2,1,0:T(8,128)(2,1)S(1)}, u32[]{:S(2)}, u32[]{:S(2)}) collective-permute-start(bf16[2,72,512]{2,1,0:T(8,128)(2,1)S(1)} %get-tuple-element.73), channel_id=1, source_target_pairs={{0,32},{8,40},{16,48},{24,56},{32,0},{40,8},{48,16},{56,24},{64,96... | collective-permute-start | bytes 442376 | tf_op jit(solution)/shard_map/ppermute | solution.py:517
  138.4 17.0 %shard_map.88.refs_3_ = bf16[2,72,512]{2,1,0:T(8,128)(2,1)S(1)} custom-call(s32[1]{0:T(128)} %bitcast.1.seq_ref, s32[32,128]{1,0:T(8,128)} %get-tuple-element.52.code_ref, f32[1]{0:T(128)} %get-tuple-element.66.norm_ref, s32[32,256]{1,0:T(8,128)S(1)} %reshape.40.pos_ref, bf16[4096,128]{1,0:T(8,128)(2,1)S(1)} %get-tuple-element.67.kv_ref, ...), custom_call_target="tpu_custom_call" | custom-call | flops 6000000000 | bytes 4194304 | tf_op jit(solution)/shard_map/pallas_call | solution.py:381
  155.5 0.0 collective-permute-done.12.refs_2_
  155.5 0.0 collective-permute-done.13.refs_3_
  155.5 0.0 collective-permute-done.10.refs_2_
  155.5 0.0 collective-permute-done.8.refs_0_
  155.5 0.0 collective-permute-done.9.refs_1_
  155.5 1.0 shard_map.89
  156.5 7.6 %all-to-all-start = ((bf16[16,32,128]{2,1,0:T(8,128)(2,1)}), bf16[16,32,128]{2,1,0:T(8,128)(2,1)S(1)}, u32[]{:S(2)}, u32[]{:S(2)}) async-start(bf16[16,32,128]{2,1,0:T(8,128)(2,1)} %shard_map.89), calls=%async_computation | async-start | bytes 262144 | tf_op jit(solution)/shard_map/all_to_all | solution.py:521
  164.1 6.3 %all-to-all-done.pieces_ref = bf16[16,32,128]{2,1,0:T(8,128)(2,1)S(1)} async-done(((bf16[16,32,128]{2,1,0:T(8,128)(2,1)}), bf16[16,32,128]{2,1,0:T(8,128)(2,1)S(1)}, u32[]{:S(2)}, u32[]{:S(2)}) %all-to-all-start) | async-done | bytes 131104 | tf_op jit(solution)/shard_map/all_to_all | solution.py:521
  170.5 1.2 shard_map.90
  (3 shorter events, 0.0 us)
Async XLA Ops:
  0.0 11.4 %copy-start.1 = (s32[8192]{0:T(1024)S(1)}, s32[8192]{0:T(1024)}, u32[]{:S(2)}) copy-start(s32[8192]{0:T(1024)} %param.16) | copy-start | bytes 98308
  0.0 7.5 %copy-start = (bf16[128,1024]{1,0:T(8,128)(2,1)S(1)}, bf16[128,1024]{1,0:T(8,128)(2,1)}, u32[]{:S(2)}) copy-start(bf16[128,1024]{1,0:T(8,128)(2,1)} %param.15) | copy-start | bytes 786436
  6.7 7.6 %collective-permute-start.3 = (bf16[2048,128]{1,0:T(8,128)(2,1)}, bf16[2048,128]{1,0:T(8,128)(2,1)S(1)}, u32[]{:S(2)}, u32[]{:S(2)}) collective-permute-start(bf16[2048,128]{1,0:T(8,128)(2,1)} %get-tuple-element.56), channel_id=1, source_target_pairs={{0,8},{8,0},{16,24},{24,16},{32,40},{40,32},{48,56},{56,48},{64,72... | collective-permute-start | bytes 1572872 | tf_op jit(solution)/shard_map/ppermute | solution.py:483
  7.4 4.1 %collective-permute-start = (bf16[64,512]{1,0:T(8,128)(2,1)}, bf16[64,512]{1,0:T(8,128)(2,1)S(1)}, u32[]{:S(2)}, u32[]{:S(2)}) collective-permute-start(bf16[64,512]{1,0:T(8,128)(2,1)} %get-tuple-element.54), channel_id=1, source_target_pairs={{0,8},{8,0},{16,24},{24,16},{32,40},{40,32},{48,56},{56,48},{64,72... | collective-permute-start | bytes 196616 | tf_op jit(solution)/shard_map/ppermute | solution.py:481
  7.5 27.9 %collective-permute-start.2 = (bf16[128,1024]{1,0:T(8,128)(2,1)S(1)}, bf16[128,1024]{1,0:T(8,128)(2,1)S(1)}, u32[]{:S(2)}, u32[]{:S(2)}) collective-permute-start(bf16[128,1024]{1,0:T(8,128)(2,1)S(1)} %copy-done), channel_id=1, source_target_pairs={{0,4},{1,5},{2,6},{3,7},{4,0},{5,1},{6,2},{7,3},{8,12},{9,13},{10,... | collective-permute-start | bytes 786440 | tf_op jit(solution)/shard_map/ppermute | solution.py:487
  8.8 31.7 %collective-permute-start.4 = (bf16[2048,128]{1,0:T(8,128)(2,1)}, bf16[2048,128]{1,0:T(8,128)(2,1)S(1)}, u32[]{:S(2)}, u32[]{:S(2)}) collective-permute-start(bf16[2048,128]{1,0:T(8,128)(2,1)} %get-tuple-element.55.refs_0_), channel_id=1, source_target_pairs={{0,16},{8,24},{16,0},{24,8},{32,48},{40,56},{48,32},{56,40},{64,80... | collective-permute-start | bytes 1572872 | tf_op jit(solution)/shard_map/ppermute | solution.py:485
  12.1 25.1 %collective-permute-start.1 = (bf16[2,64,512]{2,1,0:T(8,128)(2,1)}, bf16[2,64,512]{2,1,0:T(8,128)(2,1)S(1)}, u32[]{:S(2)}, u32[]{:S(2)}) collective-permute-start(bf16[2,64,512]{2,1,0:T(8,128)(2,1)} %bitcast_dynamic-update-slice_fusion.rest_0_), channel_id=1, source_target_pairs={{0,32},{8,40},{16,48},{24,56},{32,0},{40,8},{48,16},{56,24},{64,96... | collective-permute-start | bytes 393224 | tf_op jit(solution)/shard_map/ppermute | solution.py:482
  12.4 28.1 %collective-permute-start.6 = (bf16[2,64,512]{2,1,0:T(8,128)(2,1)}, bf16[2,64,512]{2,1,0:T(8,128)(2,1)S(1)}, u32[]{:S(2)}, u32[]{:S(2)}) collective-permute-start(bf16[2,64,512]{2,1,0:T(8,128)(2,1)} %bitcast_dynamic-update-slice_fusion.rest_0_), channel_id=1, source_target_pairs={{0,96},{8,104},{16,112},{24,120},{32,64},{40,72},{48,80},{56,88},{... | collective-permute-start | bytes 393224 | tf_op jit(solution)/shard_map/ppermute | solution.py:482
  14.2 27.0 %collective-permute-start.7 = (bf16[2,64,512]{2,1,0:T(8,128)(2,1)}, bf16[2,64,512]{2,1,0:T(8,128)(2,1)S(1)}, u32[]{:S(2)}, u32[]{:S(2)}) collective-permute-start(bf16[2,64,512]{2,1,0:T(8,128)(2,1)} %bitcast_dynamic-update-slice_fusion.rest_0_), channel_id=1, source_target_pairs={{0,64},{8,72},{16,80},{24,88},{32,96},{40,104},{48,112},{56,120},{... | collective-permute-start | bytes 393224 | tf_op jit(solution)/shard_map/ppermute | solution.py:482
  35.5 101.2 %collective-permute-start.11 = (bf16[256,1024]{1,0:T(8,128)(2,1)S(1)}, bf16[256,1024]{1,0:T(8,128)(2,1)S(1)}, u32[]{:S(2)}, u32[]{:S(2)}) collective-permute-start(bf16[256,1024]{1,0:T(8,128)(2,1)S(1)} %constant_dynamic-update-slice_fusion.refs_0_), channel_id=1, source_target_pairs={{0,1},{1,0},{2,3},{3,2},{4,5},{5,4},{6,7},{7,6},{8,9},{9,8},{10,11... | collective-permute-start | bytes 1572872 | tf_op jit(solution)/shard_map/ppermute | solution.py:494
  37.2 118.3 %collective-permute-start.12 = (bf16[256,1024]{1,0:T(8,128)(2,1)S(1)}, bf16[256,1024]{1,0:T(8,128)(2,1)S(1)}, u32[]{:S(2)}, u32[]{:S(2)}) collective-permute-start(bf16[256,1024]{1,0:T(8,128)(2,1)S(1)} %constant_dynamic-update-slice_fusion.refs_0_), channel_id=1, source_target_pairs={{0,2},{1,3},{2,0},{3,1},{4,6},{5,7},{6,4},{7,5},{8,10},{9,11},{10,... | collective-permute-start | bytes 1572872 | tf_op jit(solution)/shard_map/ppermute | solution.py:494
  40.5 115.0 %collective-permute-start.13 = (bf16[256,1024]{1,0:T(8,128)(2,1)S(1)}, bf16[256,1024]{1,0:T(8,128)(2,1)S(1)}, u32[]{:S(2)}, u32[]{:S(2)}) collective-permute-start(bf16[256,1024]{1,0:T(8,128)(2,1)S(1)} %constant_dynamic-update-slice_fusion.refs_0_), channel_id=1, source_target_pairs={{0,3},{1,2},{2,1},{3,0},{4,7},{5,6},{6,5},{7,4},{8,11},{9,10},{10,... | collective-permute-start | bytes 1572872 | tf_op jit(solution)/shard_map/ppermute | solution.py:494
  40.5 47.3 %collective-permute-start.5 = (bf16[2048,128]{1,0:T(8,128)(2,1)S(1)}, bf16[2048,128]{1,0:T(8,128)(2,1)S(1)}, u32[]{:S(2)}, u32[]{:S(2)}) collective-permute-start(bf16[2048,128]{1,0:T(8,128)(2,1)S(1)} %collective-permute-done.3.refs_1_), channel_id=1, source_target_pairs={{0,16},{8,24},{16,0},{24,8},{32,48},{40,56},{48,32},{56,40},{64,80... | collective-permute-start | bytes 1572872 | tf_op jit(solution)/shard_map/ppermute | solution.py:485
  135.1 20.4 %collective-permute-start.10 = (bf16[2,72,512]{2,1,0:T(8,128)(2,1)S(1)}, bf16[2,72,512]{2,1,0:T(8,128)(2,1)S(1)}, u32[]{:S(2)}, u32[]{:S(2)}) collective-permute-start(bf16[2,72,512]{2,1,0:T(8,128)(2,1)S(1)} %get-tuple-element.75), channel_id=1, source_target_pairs={{0,96},{8,104},{16,112},{24,120},{32,64},{40,72},{48,80},{56,88},{... | collective-permute-start | bytes 442376 | tf_op jit(solution)/shard_map/ppermute | solution.py:517
  136.0 19.5 %collective-permute-start.8 = (bf16[2,72,512]{2,1,0:T(8,128)(2,1)S(1)}, bf16[2,72,512]{2,1,0:T(8,128)(2,1)S(1)}, u32[]{:S(2)}, u32[]{:S(2)}) collective-permute-start(bf16[2,72,512]{2,1,0:T(8,128)(2,1)S(1)} %get-tuple-element.72), channel_id=1, source_target_pairs={{0,64},{8,72},{16,80},{24,88},{32,96},{40,104},{48,112},{56,120},{... | collective-permute-start | bytes 442376 | tf_op jit(solution)/shard_map/ppermute | solution.py:517
  136.7 18.8 %collective-permute-start.9 = (bf16[2,72,512]{2,1,0:T(8,128)(2,1)S(1)}, bf16[2,72,512]{2,1,0:T(8,128)(2,1)S(1)}, u32[]{:S(2)}, u32[]{:S(2)}) collective-permute-start(bf16[2,72,512]{2,1,0:T(8,128)(2,1)S(1)} %get-tuple-element.73), channel_id=1, source_target_pairs={{0,32},{8,40},{16,48},{24,56},{32,0},{40,8},{48,16},{56,24},{64,96... | collective-permute-start | bytes 442376 | tf_op jit(solution)/shard_map/ppermute | solution.py:517
  156.5 14.0 %all-to-all-start = ((bf16[16,32,128]{2,1,0:T(8,128)(2,1)}), bf16[16,32,128]{2,1,0:T(8,128)(2,1)S(1)}, u32[]{:S(2)}, u32[]{:S(2)}) async-start(bf16[16,32,128]{2,1,0:T(8,128)(2,1)} %shard_map.89), calls=%async_computation | async-start | bytes 262144 | tf_op jit(solution)/shard_map/all_to_all | solution.py:521

commit v10 on v9

--- a/solution.py
+++ b/solution.py
@@ -429,31 +429,23 @@
     )(core, *parts)
 
 
-def finish_kernel(grp_ref, pieces_ref, *refs):
-    w_refs, out_ref = refs[:-1], refs[-1]
+def finish_kernel(pieces_ref, w_ref, out_ref):
     groups = pieces_ref.shape[0] // 2
-    me = grp_ref[0]
-    result = None
-    for k, w_ref in enumerate(w_refs):
-        near = jnp.bitwise_xor(me, k)
-        order = [c * groups + g for g in (near, jnp.bitwise_xor(near, 4)) for c in range(2)]
-        blocks = [pieces_ref[i] for i in order]
-        upper = jnp.concatenate([p[:, :HS] for p in blocks], 1)
-        lower = jnp.concatenate([p[:, HS:] for p in blocks], 1)
-        attention = jnp.concatenate([upper, lower], 0)
-        term = jnp.dot(attention, w_ref[...], preferred_element_type=jnp.float32)
-        result = term if result is None else result + term
-    out_ref[...] = result.astype(jnp.bfloat16)
-
-
-def finish(grp, pieces, w_turns):
+    order = [c * groups + g for g in range(groups) for c in range(2)]
+    upper = jnp.concatenate([pieces_ref[i][:, :HS] for i in order], 1)
+    lower = jnp.concatenate([pieces_ref[i][:, HS:] for i in order], 1)
+    attention = jnp.concatenate([upper, lower], 0)
+    out_ref[...] = jnp.dot(attention, w_ref[...], preferred_element_type=jnp.float32).astype(jnp.bfloat16)
+
+
+def finish(pieces, w_all):
     return pl.pallas_call(
         finish_kernel,
-        in_specs=[SMEM] + [VMEM] * (1 + len(w_turns)),
+        in_specs=[VMEM, VMEM],
         out_specs=VMEM,
-        out_shape=jax.ShapeDtypeStruct((2 * pieces.shape[1], w_turns[0].shape[1]), jnp.bfloat16),
+        out_shape=jax.ShapeDtypeStruct((2 * pieces.shape[1], w_all.shape[1]), jnp.bfloat16),
         compiler_params=pltpu.CompilerParams(vmem_limit_bytes=24 * 2**20),
-    )(grp, pieces, *w_turns)
+    )(pieces, w_all)
 
 
 def along_x(by):
@@ -472,7 +464,6 @@
 
 def body(inputs, latents, w_query, w_key, w_value, w_out, positions, block_mask):
     seq = lax.axis_index("seq")[None]
-    grp = lax.axis_index("grp")[None]
     core = jnp.bitwise_and(seq, 1)
 
     q_chip, theirs, kv_own, kv_other, codes = front(
@@ -484,15 +475,11 @@
     near = prepare(*in_hbm(kv_own), kv_partner)
     kv_far = [lax.ppermute(kv, "seq", Y_SWAP) for kv in (kv_own, kv_partner)]
 
-    w_other = lax.ppermute(w_out, "grp", [(g, g ^ 4) for g in range(8)])
     spots = positions.reshape(-1, ROWS)
     queries[0], = in_hbm(q_chip)
     near_parts = dict(zip(NEAR_CALLS[0], attend(NEAR_CALLS[0], seq, codes, spots, near, [queries[0]])))
-    w_other, near_parts[0] = lax.optimization_barrier((w_other, near_parts[0]))
-    w_pair = jnp.concatenate([w_out, w_other], 0)
-    w_turns = [w_pair] + [
-        lax.ppermute(w_pair, "grp", [(g, g ^ k) for g in range(8)]) for k in (1, 2, 3)
-    ]
+    w_mine, near_parts[0] = lax.optimization_barrier((w_out, near_parts[0]))
+    w_all = lax.all_to_all(jnp.broadcast_to(w_mine, (8, *w_out.shape)), "grp", 0, 0)
 
     parts = {}
     last = 0
@@ -515,11 +502,11 @@
         last = call[-1]
 
     parts = [part if by == 0 else lax.ppermute(part, "seq", along_x(by)) for by, part in parts.items()]
-    parts, w_turns = lax.optimization_barrier((parts, w_turns))
+    parts, w_all = lax.optimization_barrier((parts, w_all))
     pieces = combine(core, parts)
     owners = [[(4 * x + 2 * y + c) * 8 + g for c in range(2) for g in range(8)] for x in range(4) for y in range(2)]
     pieces = lax.all_to_all(pieces, ("seq", "grp"), 0, 0, axis_index_groups=owners)
-    return finish(grp, pieces, w_turns)
+    return finish(pieces, w_all.reshape(-1, w_out.shape[1]))
 
 
 def solution(mesh):

time: 172 us -> 180 us (1.047); the launches traced: 172 us -> 177 us
  blocking collectives: 0 us -> 13.6 us
  waiting for transfers between devices: 6.38 us -> 0.03 us
  local copies, waits for them, and re-layouts: 0.69 us -> 6.73 us
  starting transfers between devices: 24.7 us -> 19.9 us
  Pallas kernels: 140 us -> 137 us
    all_to_all x0 -> x1, blocking collectives: none -> 13.6 us  [body(): lax.all_to_all(pieces, ('seq', 'grp'), 0, 0, axis_index_groups=owners)]
    all_to_all x1, waiting for transfers between devices: 6.34 us -> 0.01 us  [body(): lax.all_to_all(jnp.broadcast_to(w_mine, (8, *w_out.shape)), 'grp', 0, 0)]
    ppermute x4 -> x0, starting transfers between devices: 6.32 us -> none  [the longest x3 5.02 us: body(): lax.ppermute(w_pair, 'grp', [(g, g ^ k) for g in range(8)])]
    unnamed x5 -> x20, local copies, waits for them, and re-layouts: 0.03 us -> 4.49 us
    all_to_all x1, starting transfers between devices: 7.63 us -> 5.14 us  [body(): lax.all_to_all(jnp.broadcast_to(w_mine, (8, *w_out.shape)), 'grp', 0, 0)]
    ppermute x2, starting transfers between devices: 3.37 us -> 5.75 us  [body(): kv_far = [lax.ppermute(kv, 'seq', Y_SWAP) for kv in (kv_own, kv_partner)]]
    pallas_call x4, Pallas kernels: 128 us -> 126 us  [attend(): pl.pallas_call(functools.partial(attention_kernel, steps, bool(before)),...]
  transfers between devices with their start and end apart: 15 -> 11, of which waited for: 1 -> 0; matrix products, arithmetic and copies ran while one was open for 0% -> 1% of each run, Pallas kernels for 76% -> 73%
where the time goes in v10:
time: 180 us; the launch traced here: 177 us
  Pallas kernels  137 us (76%)
  starting transfers between devices  19.9 us (11%)
  blocking collectives  13.6 us (8%)
  local copies, waits for them, and re-layouts  6.73 us (4%)
    pallas_call x4, Pallas kernels, attend(): pl.pallas_call(functools.partial(attention_kernel, steps, bool(before)),...  126 us
    all_to_all x1, blocking collectives, body(): lax.all_to_all(pieces, ('seq', 'grp'), 0, 0, axis_index_groups=owners)  13.6 us
    pallas_call x1, Pallas kernels, front(): pl.pallas_call(front_kernel, in_specs=[SMEM] + [pl.BlockSpec(memory_space...  6.62 us
    ppermute x2, starting transfers between devices, body(): kv_far = [lax.ppermute(kv, 'seq', Y_SWAP) for kv in (kv_own, kv_partner)]  5.75 us
    all_to_all x1, starting transfers between devices, body(): lax.all_to_all(jnp.broadcast_to(w_mine, (8, *w_out.shape)), 'grp', 0, 0)  5.14 us
    unnamed x20, local copies, waits for them, and re-layouts  4.49 us
    ppermute x3, starting transfers between devices, body(): lax.ppermute(part, 'seq', along_x(by))  4.3 us
    ppermute x3, starting transfers between devices, body(): lax.ppermute(q_chip, 'seq', along_x(by))  3.86 us
  transfers between devices with their start and end apart: 11, of which 0 were waited for; matrix products, arithmetic and copies ran while one was open for 1% of the time, Pallas kernels for 73%

profile of v10, /device:TPU:3, one launch (start us, length us, event | category | flops | bytes accessed | tf_op | source)
XLA Modules:
  0.0 177.5 jit_solution(1232021300499208192)
XLA Ops:
  0.0 0.0 copy-start.9
  0.0 6.6 %shard_map.82 = (bf16[2,64,512]{2,1,0:T(8,128)(2,1)}, bf16[64,512]{1,0:T(8,128)(2,1)}, bf16[2048,128]{1,0:T(8,128)(2,1)}, bf16[2048,128]{1,0:T(8,128)(2,1)}, s32[32,128]{1,0:T(8,128)}) custom-call(s32[1]{0:T(128)} %bitcast.seq_ref, bf16[512,1024]{1,0:T(8,128)(2,1)} %lat_hbm.1, bf16[2048,1024]{1,0:T(8,128)(2,1)} %x_hbm.1, bf16[1024,128]{1,0:T(8,128)(2,1)} %wq_hbm.1, ...), custom_call_target="tpu_custom_call" | custom-call | flops 1207959552 | bytes 6291456 | tf_op jit(solution)/shard_map/pallas_call | solution.py:154
  6.6 0.8 collective-permute-start.2
  7.4 0.1 collective-permute-start
  7.5 2.9 %collective-permute-start.3 = (bf16[2048,128]{1,0:T(8,128)(2,1)}, bf16[2048,128]{1,0:T(8,128)(2,1)S(1)}, u32[]{:S(2)}, u32[]{:S(2)}) collective-permute-start(bf16[2048,128]{1,0:T(8,128)(2,1)} %get-tuple-element.52.refs_0_), channel_id=1, source_target_pairs={{0,16},{8,24},{16,0},{24,8},{32,48},{40,56},{48,32},{56,40},{64,80... | collective-permute-start | bytes 1572872 | tf_op jit(solution)/shard_map/ppermute | solution.py:476
  10.4 0.0 copy-done.9
  10.4 0.0 collective-permute-done
  10.4 0.6 bitcast_dynamic-update-slice_fusion.rest_0_
  11.1 1.8 %collective-permute-start.6 = (bf16[2,64,512]{2,1,0:T(8,128)(2,1)}, bf16[2,64,512]{2,1,0:T(8,128)(2,1)S(1)}, u32[]{:S(2)}, u32[]{:S(2)}) collective-permute-start(bf16[2,64,512]{2,1,0:T(8,128)(2,1)} %bitcast_dynamic-update-slice_fusion.rest_0_), channel_id=1, source_target_pairs={{0,64},{8,72},{16,80},{24,88},{32,96},{40,104},{48,112},{56,120},{... | collective-permute-start | bytes 393224 | tf_op jit(solution)/shard_map/ppermute | solution.py:473
  12.9 0.0 collective-permute-start.5
  12.9 2.0 %collective-permute-start.1 = (bf16[2,64,512]{2,1,0:T(8,128)(2,1)}, bf16[2,64,512]{2,1,0:T(8,128)(2,1)S(1)}, u32[]{:S(2)}, u32[]{:S(2)}) collective-permute-start(bf16[2,64,512]{2,1,0:T(8,128)(2,1)} %bitcast_dynamic-update-slice_fusion.rest_0_), channel_id=1, source_target_pairs={{0,32},{8,40},{16,48},{24,56},{32,0},{40,8},{48,16},{56,24},{64,96... | collective-permute-start | bytes 393224 | tf_op jit(solution)/shard_map/ppermute | solution.py:473
  14.9 0.0 collective-permute-done.2.refs_1_
  14.9 2.1 %shard_map.83 = (bf16[4096,128]{1,0:T(8,128)(2,1)S(1)}, bf16[72,4096]{1,0:T(8,128)(2,1)S(1)}, f32[1]{0:T(128)}) custom-call(bf16[2048,128]{1,0:T(8,128)(2,1)} %get-tuple-element.52.refs_0_, bf16[2048,128]{1,0:T(8,128)(2,1)S(1)} %collective-permute-done.2.refs_1_), custom_call_target="tpu_custom_call" | custom-call | tf_op jit(solution)/shard_map/pallas_call | solution.py:192
  17.0 0.0 copy-start
  17.0 0.0 copy-start.2
  17.0 0.0 copy-start.8
  17.0 17.5 %shard_map.84.rest_1_ = bf16[2,72,512]{2,1,0:T(8,128)(2,1)S(1)} custom-call(s32[1]{0:T(128)} %bitcast.seq_ref, s32[32,128]{1,0:T(8,128)} %get-tuple-element.49.code_ref, f32[1]{0:T(128)} %get-tuple-element.54.norm_ref, s32[32,256]{1,0:T(8,128)S(1)} %reshape.43.pos_ref, bf16[4096,128]{1,0:T(8,128)(2,1)S(1)} %get-tuple-element.55.kv_ref, ...), custom_call_target="tpu_custom_call" | custom-call | flops 6000000000 | bytes 4194304 | tf_op jit(solution)/shard_map/pallas_call | solution.py:381
  34.5 0.0 copy-done
  34.5 0.0 copy-done.2
  34.6 0.0 copy-start.6
  34.6 0.6 copy-done.6
  35.2 0.0 collective-permute-done.1.rest_0_.rest_1_
  35.2 0.0 copy-start.4
  35.2 0.6 copy-done.4
  35.8 0.0 collective-permute-done.3.refs_0_
  35.9 0.0 copy-done.8
  35.9 1.6 broadcast_in_dim.7
  37.5 5.1 %all-to-all-start = ((bf16[8,128,1024]{2,1,0:T(8,128)(2,1)}), bf16[8,128,1024]{2,1,0:T(8,128)(2,1)S(1)}, u32[]{:S(2)}, u32[]{:S(2)}) async-start(bf16[8,128,1024]{2,1,0:T(8,128)(2,1)} %broadcast_in_dim.7), calls=%async_computation | async-start | bytes 4194304 | tf_op jit(solution)/shard_map/all_to_all | solution.py:482
  42.6 2.8 %collective-permute-start.4 = (bf16[2048,128]{1,0:T(8,128)(2,1)S(1)}, bf16[2048,128]{1,0:T(8,128)(2,1)S(1)}, u32[]{:S(2)}, u32[]{:S(2)}) collective-permute-start(bf16[2048,128]{1,0:T(8,128)(2,1)S(1)} %collective-permute-done.2.refs_1_), channel_id=1, source_target_pairs={{0,16},{8,24},{16,0},{24,8},{32,48},{40,56},{48,32},{56,40},{64,80... | collective-permute-start | bytes 1572872 | tf_op jit(solution)/shard_map/ppermute | solution.py:476
  45.4 0.0 collective-permute-done.6.rest_2_.rest_0_
  45.4 0.0 collective-permute-done.5.rest_1_.rest_2_
  45.4 0.0 copy-start.1
  45.4 1.2 copy-done.1
  46.7 0.0 copy-start.3
  46.7 1.1 copy-done.3
  47.7 0.0 copy-start.5
  47.7 0.9 copy-done.5
  48.6 45.1 %shard_map.85 = (bf16[2,72,512]{2,1,0:T(8,128)(2,1)S(1)}, bf16[2,72,512]{2,1,0:T(8,128)(2,1)S(1)}, bf16[2,72,512]{2,1,0:T(8,128)(2,1)S(1)}) custom-call(s32[1]{0:T(128)} %bitcast.seq_ref, s32[32,128]{1,0:T(8,128)} %get-tuple-element.49.code_ref, f32[1]{0:T(128)} %get-tuple-element.54.norm_ref, s32[32,256]{1,0:T(8,128)S(1)} %reshape.43.pos_ref, ...), custom_call_target="tpu_custom_call" | custom-call | flops 17999998976 | bytes 4194304 | tf_op jit(solution)/shard_map/pallas_call | solution.py:381
  93.8 0.0 collective-permute-done.4.refs_1_
  93.8 1.0 shard_map.86
  94.8 0.0 copy-start.7
  94.8 45.7 %shard_map.87 = (bf16[2,72,512]{2,1,0:T(8,128)(2,1)S(1)}, bf16[2,72,512]{2,1,0:T(8,128)(2,1)S(1)}, bf16[2,72,512]{2,1,0:T(8,128)(2,1)S(1)}) custom-call(s32[1]{0:T(128)} %bitcast.seq_ref, s32[32,128]{1,0:T(8,128)} %get-tuple-element.49.code_ref, f32[1]{0:T(128)} %get-tuple-element.63.norm_ref, s32[32,256]{1,0:T(8,128)S(1)} %reshape.43.pos_ref, ...), custom_call_target="tpu_custom_call" | custom-call | flops 17999998976 | bytes 4194304 | tf_op jit(solution)/shard_map/pallas_call | solution.py:381
  140.5 2.4 %collective-permute-start.9 = (bf16[2,72,512]{2,1,0:T(8,128)(2,1)S(1)}, bf16[2,72,512]{2,1,0:T(8,128)(2,1)S(1)}, u32[]{:S(2)}, u32[]{:S(2)}) collective-permute-start(bf16[2,72,512]{2,1,0:T(8,128)(2,1)S(1)} %get-tuple-element.72), channel_id=1, source_target_pairs={{0,96},{8,104},{16,112},{24,120},{32,64},{40,72},{48,80},{56,88},{... | collective-permute-start | bytes 442376 | tf_op jit(solution)/shard_map/ppermute | solution.py:504
  142.9 0.0 collective-permute-start.7
  142.9 1.9 %collective-permute-start.8 = (bf16[2,72,512]{2,1,0:T(8,128)(2,1)S(1)}, bf16[2,72,512]{2,1,0:T(8,128)(2,1)S(1)}, u32[]{:S(2)}, u32[]{:S(2)}) collective-permute-start(bf16[2,72,512]{2,1,0:T(8,128)(2,1)S(1)} %get-tuple-element.70), channel_id=1, source_target_pairs={{0,32},{8,40},{16,48},{24,56},{32,0},{40,8},{48,16},{56,24},{64,96... | collective-permute-start | bytes 442376 | tf_op jit(solution)/shard_map/ppermute | solution.py:504
  144.8 0.0 copy-done.7
  144.8 17.5 %shard_map.88.refs_3_ = bf16[2,72,512]{2,1,0:T(8,128)(2,1)S(1)} custom-call(s32[1]{0:T(128)} %bitcast.seq_ref, s32[32,128]{1,0:T(8,128)} %get-tuple-element.49.code_ref, f32[1]{0:T(128)} %get-tuple-element.63.norm_ref, s32[32,256]{1,0:T(8,128)S(1)} %reshape.43.pos_ref, bf16[4096,128]{1,0:T(8,128)(2,1)S(1)} %get-tuple-element.64.kv_ref, ...), custom_call_target="tpu_custom_call" | custom-call | flops 6000000000 | bytes 4194304 | tf_op jit(solution)/shard_map/pallas_call | solution.py:381
  162.3 0.0 collective-permute-done.9.refs_2_
  162.3 0.0 collective-permute-done.7.refs_0_
  162.3 0.0 collective-permute-done.8.refs_1_
  162.4 0.0 all-to-all-done
  162.4 0.3 shard_map.89
  162.7 13.6 %all_to_all.10.pieces_ref = bf16[16,32,128]{2,1,0:T(8,128)(2,1)S(1)} all-to-all(bf16[16,32,128]{2,1,0:T(8,128)(2,1)S(1)} %shard_map.89), channel_id=1, replica_groups={{0,1,2,3,4,5,6,7,8,9,10,11,12,13,14,15},{16,17,18,19,20,21,22,23,24,25,..., dimensions={0} | all-to-all | bytes 262144 | tf_op jit(solution)/shard_map/all_to_all | solution.py:508
  176.3 1.2 shard_map.90
  (1 shorter events, 0.0 us)
Async XLA Ops:
  0.0 10.4 %copy-start.9 = (s32[8192]{0:T(1024)S(1)}, s32[8192]{0:T(1024)}, u32[]{:S(2)}) copy-start(s32[8192]{0:T(1024)} %param.16) | copy-start | bytes 98308
  6.6 8.3 %collective-permute-start.2 = (bf16[2048,128]{1,0:T(8,128)(2,1)}, bf16[2048,128]{1,0:T(8,128)(2,1)S(1)}, u32[]{:S(2)}, u32[]{:S(2)}) collective-permute-start(bf16[2048,128]{1,0:T(8,128)(2,1)} %get-tuple-element.53), channel_id=1, source_target_pairs={{0,8},{8,0},{16,24},{24,16},{32,40},{40,32},{48,56},{56,48},{64,72... | collective-permute-start | bytes 1572872 | tf_op jit(solution)/shard_map/ppermute | solution.py:474
  7.4 3.0 %collective-permute-start = (bf16[64,512]{1,0:T(8,128)(2,1)}, bf16[64,512]{1,0:T(8,128)(2,1)S(1)}, u32[]{:S(2)}, u32[]{:S(2)}) collective-permute-start(bf16[64,512]{1,0:T(8,128)(2,1)} %get-tuple-element.51), channel_id=1, source_target_pairs={{0,8},{8,0},{16,24},{24,16},{32,40},{40,32},{48,56},{56,48},{64,72... | collective-permute-start | bytes 196616 | tf_op jit(solution)/shard_map/ppermute | solution.py:472
  7.5 28.4 %collective-permute-start.3 = (bf16[2048,128]{1,0:T(8,128)(2,1)}, bf16[2048,128]{1,0:T(8,128)(2,1)S(1)}, u32[]{:S(2)}, u32[]{:S(2)}) collective-permute-start(bf16[2048,128]{1,0:T(8,128)(2,1)} %get-tuple-element.52.refs_0_), channel_id=1, source_target_pairs={{0,16},{8,24},{16,0},{24,8},{32,48},{40,56},{48,32},{56,40},{64,80... | collective-permute-start | bytes 1572872 | tf_op jit(solution)/shard_map/ppermute | solution.py:476
  11.1 34.4 %collective-permute-start.6 = (bf16[2,64,512]{2,1,0:T(8,128)(2,1)}, bf16[2,64,512]{2,1,0:T(8,128)(2,1)S(1)}, u32[]{:S(2)}, u32[]{:S(2)}) collective-permute-start(bf16[2,64,512]{2,1,0:T(8,128)(2,1)} %bitcast_dynamic-update-slice_fusion.rest_0_), channel_id=1, source_target_pairs={{0,64},{8,72},{16,80},{24,88},{32,96},{40,104},{48,112},{56,120},{... | collective-permute-start | bytes 393224 | tf_op jit(solution)/shard_map/ppermute | solution.py:473
  12.9 32.5 %collective-permute-start.5 = (bf16[2,64,512]{2,1,0:T(8,128)(2,1)}, bf16[2,64,512]{2,1,0:T(8,128)(2,1)S(1)}, u32[]{:S(2)}, u32[]{:S(2)}) collective-permute-start(bf16[2,64,512]{2,1,0:T(8,128)(2,1)} %bitcast_dynamic-update-slice_fusion.rest_0_), channel_id=1, source_target_pairs={{0,96},{8,104},{16,112},{24,120},{32,64},{40,72},{48,80},{56,88},{... | collective-permute-start | bytes 393224 | tf_op jit(solution)/shard_map/ppermute | solution.py:473
  12.9 22.3 %collective-permute-start.1 = (bf16[2,64,512]{2,1,0:T(8,128)(2,1)}, bf16[2,64,512]{2,1,0:T(8,128)(2,1)S(1)}, u32[]{:S(2)}, u32[]{:S(2)}) collective-permute-start(bf16[2,64,512]{2,1,0:T(8,128)(2,1)} %bitcast_dynamic-update-slice_fusion.rest_0_), channel_id=1, source_target_pairs={{0,32},{8,40},{16,48},{24,56},{32,0},{40,8},{48,16},{56,24},{64,96... | collective-permute-start | bytes 393224 | tf_op jit(solution)/shard_map/ppermute | solution.py:473
  17.0 17.6 %copy-start = (bf16[4096,128]{1,0:T(8,128)(2,1)}, bf16[4096,128]{1,0:T(8,128)(2,1)S(1)}, u32[]{:S(2)}) copy-start(bf16[4096,128]{1,0:T(8,128)(2,1)S(1)} %get-tuple-element.55.kv_ref) | copy-start | bytes 3145732
  17.0 17.6 %copy-start.2 = (bf16[72,4096]{1,0:T(8,128)(2,1)}, bf16[72,4096]{1,0:T(8,128)(2,1)S(1)}, u32[]{:S(2)}) copy-start(bf16[72,4096]{1,0:T(8,128)(2,1)S(1)} %get-tuple-element.56.vt_ref) | copy-start | bytes 1769476
  17.0 18.8 %copy-start.8 = (bf16[128,1024]{1,0:T(8,128)(2,1)S(1)}, bf16[128,1024]{1,0:T(8,128)(2,1)}, u32[]{:S(2)}) copy-start(bf16[128,1024]{1,0:T(8,128)(2,1)} %param.15) | copy-start | bytes 786436
  34.6 0.6 copy-start.6
  35.2 0.6 copy-start.4
  37.5 124.9 %all-to-all-start = ((bf16[8,128,1024]{2,1,0:T(8,128)(2,1)}), bf16[8,128,1024]{2,1,0:T(8,128)(2,1)S(1)}, u32[]{:S(2)}, u32[]{:S(2)}) async-start(bf16[8,128,1024]{2,1,0:T(8,128)(2,1)} %broadcast_in_dim.7), calls=%async_computation | async-start | bytes 4194304 | tf_op jit(solution)/shard_map/all_to_all | solution.py:482
  42.6 51.2 %collective-permute-start.4 = (bf16[2048,128]{1,0:T(8,128)(2,1)S(1)}, bf16[2048,128]{1,0:T(8,128)(2,1)S(1)}, u32[]{:S(2)}, u32[]{:S(2)}) collective-permute-start(bf16[2048,128]{1,0:T(8,128)(2,1)S(1)} %collective-permute-done.2.refs_1_), channel_id=1, source_target_pairs={{0,16},{8,24},{16,0},{24,8},{32,48},{40,56},{48,32},{56,40},{64,80... | collective-permute-start | bytes 1572872 | tf_op jit(solution)/shard_map/ppermute | solution.py:476
  45.4 1.2 copy-start.1
  46.7 1.1 copy-start.3
  47.7 0.9 copy-start.5
  94.8 50.0 %copy-start.7 = (bf16[2,72,512]{2,1,0:T(8,128)(2,1)S(1)}, bf16[2,72,512]{2,1,0:T(8,128)(2,1)}, u32[]{:S(2)}) copy-start(bf16[2,72,512]{2,1,0:T(8,128)(2,1)} %copy-done.6) | copy-start | bytes 442372
  140.5 21.8 %collective-permute-start.9 = (bf16[2,72,512]{2,1,0:T(8,128)(2,1)S(1)}, bf16[2,72,512]{2,1,0:T(8,128)(2,1)S(1)}, u32[]{:S(2)}, u32[]{:S(2)}) collective-permute-start(bf16[2,72,512]{2,1,0:T(8,128)(2,1)S(1)} %get-tuple-element.72), channel_id=1, source_target_pairs={{0,96},{8,104},{16,112},{24,120},{32,64},{40,72},{48,80},{56,88},{... | collective-permute-start | bytes 442376 | tf_op jit(solution)/shard_map/ppermute | solution.py:504
  142.9 19.4 %collective-permute-start.7 = (bf16[2,72,512]{2,1,0:T(8,128)(2,1)S(1)}, bf16[2,72,512]{2,1,0:T(8,128)(2,1)S(1)}, u32[]{:S(2)}, u32[]{:S(2)}) collective-permute-start(bf16[2,72,512]{2,1,0:T(8,128)(2,1)S(1)} %get-tuple-element.69), channel_id=1, source_target_pairs={{0,64},{8,72},{16,80},{24,88},{32,96},{40,104},{48,112},{56,120},{... | collective-permute-start | bytes 442376 | tf_op jit(solution)/shard_map/ppermute | solution.py:504
  142.9 19.4 %collective-permute-start.8 = (bf16[2,72,512]{2,1,0:T(8,128)(2,1)S(1)}, bf16[2,72,512]{2,1,0:T(8,128)(2,1)S(1)}, u32[]{:S(2)}, u32[]{:S(2)}) collective-permute-start(bf16[2,72,512]{2,1,0:T(8,128)(2,1)S(1)} %get-tuple-element.70), channel_id=1, source_target_pairs={{0,32},{8,40},{16,48},{24,56},{32,0},{40,8},{48,16},{56,24},{64,96... | collective-permute-start | bytes 442376 | tf_op jit(solution)/shard_map/ppermute | solution.py:504

commit v11 on v9

--- a/solution.py
+++ b/solution.py
@@ -163,11 +163,11 @@
             pltpu.SemaphoreType.DMA((4,)),
             pltpu.SemaphoreType.DMA((11,)),
         ],
-        compiler_params=pltpu.CompilerParams(vmem_limit_bytes=61 * 2**20),
+        compiler_params=pltpu.CompilerParams(vmem_limit_bytes=24 * 2**20),
         cost_estimate=pl.CostEstimate(
             flops=2 * (keys * 4 + rows * 2) * width * HS, bytes_accessed=6 * 2**20, transcendentals=0
         ),
-    )(seq, *operands)
+    )(seq, *in_hbm(*operands))
 
 
 def prepare_kernel(*refs):
@@ -375,7 +375,6 @@
 
 def attend(steps, seq, codes, spots, held, queries, before=()):
     kv, vt, norm = held
-    codes, = in_hbm(codes)
     chips = len(steps)
     out = jax.ShapeDtypeStruct((2, ACC_ROWS, queries[0].shape[2]), jnp.bfloat16)
     return pl.pallas_call(
@@ -481,13 +480,12 @@
     q_chip = q_chip.at[1].set(lax.ppermute(theirs, "seq", CORE_SWAP))
     queries = {by: q_chip if by == 0 else lax.ppermute(q_chip, "seq", along_x(by)) for by in (0, 1, 3, 2)}
     kv_partner = lax.ppermute(kv_other, "seq", CORE_SWAP)
-    near = prepare(*in_hbm(kv_own), kv_partner)
+    near = prepare(kv_own, kv_partner)
     kv_far = [lax.ppermute(kv, "seq", Y_SWAP) for kv in (kv_own, kv_partner)]
 
     w_other = lax.ppermute(w_out, "grp", [(g, g ^ 4) for g in range(8)])
     spots = positions.reshape(-1, ROWS)
-    queries[0], = in_hbm(q_chip)
-    near_parts = dict(zip(NEAR_CALLS[0], attend(NEAR_CALLS[0], seq, codes, spots, near, [queries[0]])))
+    near_parts = dict(zip(NEAR_CALLS[0], attend(NEAR_CALLS[0], seq, codes, spots, near, [q_chip])))
     w_other, near_parts[0] = lax.optimization_barrier((w_other, near_parts[0]))
     w_pair = jnp.concatenate([w_out, w_other], 0)
     w_turns = [w_pair] + [

time: 172 us -> 171 us (level)
  Pallas kernels: 140 us -> 136 us
  starting transfers between devices: 24.7 us -> 27.2 us
    pallas_call x4, Pallas kernels: 128 us -> 124 us  [attend(): pl.pallas_call(functools.partial(attention_kernel, steps, bool(before)),...]
    ppermute x3, starting transfers between devices: 3.33 us -> 5.07 us  [body(): lax.ppermute(part, 'seq', along_x(by))]
  transfers between devices with their start and end apart: 15 -> 15, of which waited for: 1 -> 1; matrix products, arithmetic and copies ran while one was open for 0% -> 1% of each run, Pallas kernels for 76% -> 74%
where the time goes in v11:
time: 171 us
  Pallas kernels  136 us (80%)
  starting transfers between devices  27.2 us (16%)
  waiting for transfers between devices  6.38 us (4%)
    pallas_call x4, Pallas kernels, attend(): pl.pallas_call(functools.partial(attention_kernel, steps, bool(before)),...  124 us
    all_to_all x1, starting transfers between devices, body(): lax.all_to_all(pieces, ('seq', 'grp'), 0, 0, axis_index_groups=owners)  7.53 us
    pallas_call x1, Pallas kernels, front(): pl.pallas_call(front_kernel, in_specs=[SMEM] + [pl.BlockSpec(memory_space...  7.51 us
    all_to_all x1, waiting for transfers between devices, body(): lax.all_to_all(pieces, ('seq', 'grp'), 0, 0, axis_index_groups=owners)  6.34 us
    ppermute x3, starting transfers between devices, body(): lax.ppermute(part, 'seq', along_x(by))  5.07 us
    ppermute x3, starting transfers between devices, body(): lax.ppermute(w_pair, 'grp', [(g, g ^ k) for g in range(8)])  5.02 us
    ppermute x2, starting transfers between devices, body(): kv_far = [lax.ppermute(kv, 'seq', Y_SWAP) for kv in (kv_own, kv_partner)]  4.09 us
  transfers between devices with their start and end apart: 15, of which 1 were waited for; matrix products, arithmetic and copies ran while one was open for 1% of the time, Pallas kernels for 74%

profile of v11, /device:TPU:3, one launch (start us, length us, event | category | flops | bytes accessed | tf_op | source)
XLA Modules:
  0.0 170.8 jit_solution(4813043968827335340)
XLA Ops:
  0.0 0.0 copy-start.1
  0.0 0.0 copy-start
  0.0 7.5 %shard_map.82 = (bf16[2,64,512]{2,1,0:T(8,128)(2,1)S(1)}, bf16[64,512]{1,0:T(8,128)(2,1)S(1)}, bf16[2048,128]{1,0:T(8,128)(2,1)S(1)}, bf16[2048,128]{1,0:T(8,128)(2,1)S(1)}, s32[32,128]{1,0:T(8,128)S(1)}) custom-call(s32[1]{0:T(128)} %bitcast.1.seq_ref, bf16[512,1024]{1,0:T(8,128)(2,1)} %lat_hbm.1, bf16[2048,1024]{1,0:T(8,128)(2,1)} %x_hbm.1, ...), custom_call_target="tpu_custom_call" | custom-call | flops 1207959552 | bytes 6291456 | tf_op jit(solution)/shard_map/pallas_call | solution.py:154
  7.5 0.8 collective-permute-start.3
  8.3 0.1 collective-permute-start
  8.4 0.0 copy-done
  8.4 1.3 collective-permute-start.2
  9.7 2.6 %collective-permute-start.4 = (bf16[2048,128]{1,0:T(8,128)(2,1)S(1)}, bf16[2048,128]{1,0:T(8,128)(2,1)S(1)}, u32[]{:S(2)}, u32[]{:S(2)}) collective-permute-start(bf16[2048,128]{1,0:T(8,128)(2,1)S(1)} %get-tuple-element.55.refs_0_), channel_id=1, source_target_pairs={{0,16},{8,24},{16,0},{24,8},{32,48},{40,56},{48,32},{56,40},{64,80... | collective-permute-start | bytes 1572872 | tf_op jit(solution)/shard_map/ppermute | solution.py:484
  12.3 0.0 copy-done.1
  12.3 0.0 collective-permute-done
  12.4 0.3 collective-permute-start.1
  12.7 1.9 %collective-permute-start.6 = (bf16[2,64,512]{2,1,0:T(8,128)(2,1)S(1)}, bf16[2,64,512]{2,1,0:T(8,128)(2,1)S(1)}, u32[]{:S(2)}, u32[]{:S(2)}) collective-permute-start(bf16[2,64,512]{2,1,0:T(8,128)(2,1)S(1)} %bitcast_dynamic-update-slice_fusion.rest_0_), channel_id=1, source_target_pairs={{0,96},{8,104},{16,112},{24,120},{32,64},{40,72},{48,80},{56,88},{... | collective-permute-start | bytes 393224 | tf_op jit(solution)/shard_map/ppermute | solution.py:481
  14.6 0.0 collective-permute-done.3.refs_1_
  14.6 1.1 collective-permute-start.7
  15.7 1.0 shard_map.83
  16.7 16.7 %shard_map.84.rest_1_ = bf16[2,72,512]{2,1,0:T(8,128)(2,1)S(1)} custom-call(s32[1]{0:T(128)} %bitcast.1.seq_ref, s32[32,128]{1,0:T(8,128)S(1)} %get-tuple-element.52.code_ref, f32[1]{0:T(128)} %get-tuple-element.57.norm_ref, s32[32,256]{1,0:T(8,128)S(1)} %reshape.40.pos_ref, bf16[4096,128]{1,0:T(8,128)(2,1)S(1)} %get-tuple-element.58.kv_ref, ...), custom_call_target="tpu_custom_call" | custom-call | flops 6000000000 | bytes 4194304 | tf_op jit(solution)/shard_map/pallas_call | solution.py:380
  33.5 0.0 collective-permute-done.2
  33.5 1.0 constant_dynamic-update-slice_fusion.refs_0_
  34.5 1.7 %collective-permute-start.11 = (bf16[256,1024]{1,0:T(8,128)(2,1)S(1)}, bf16[256,1024]{1,0:T(8,128)(2,1)S(1)}, u32[]{:S(2)}, u32[]{:S(2)}) collective-permute-start(bf16[256,1024]{1,0:T(8,128)(2,1)S(1)} %constant_dynamic-update-slice_fusion.refs_0_), channel_id=1, source_target_pairs={{0,1},{1,0},{2,3},{3,2},{4,5},{5,4},{6,7},{7,6},{8,9},{9,8},{10,11... | collective-permute-start | bytes 1572872 | tf_op jit(solution)/shard_map/ppermute | solution.py:492
  36.2 0.0 collective-permute-done.1.rest_0_.rest_1_
  36.2 3.3 %collective-permute-start.12 = (bf16[256,1024]{1,0:T(8,128)(2,1)S(1)}, bf16[256,1024]{1,0:T(8,128)(2,1)S(1)}, u32[]{:S(2)}, u32[]{:S(2)}) collective-permute-start(bf16[256,1024]{1,0:T(8,128)(2,1)S(1)} %constant_dynamic-update-slice_fusion.refs_0_), channel_id=1, source_target_pairs={{0,2},{1,3},{2,0},{3,1},{4,6},{5,7},{6,4},{7,5},{8,10},{9,11},{10,... | collective-permute-start | bytes 1572872 | tf_op jit(solution)/shard_map/ppermute | solution.py:492
  39.5 0.0 collective-permute-done.4.refs_0_
  39.5 0.0 collective-permute-start.13
  39.5 0.0 collective-permute-done.6.rest_1_.rest_2_
  39.5 1.5 collective-permute-start.5
  41.0 0.0 collective-permute-done.7.rest_2_.rest_0_
  41.0 45.0 %shard_map.85 = (bf16[2,72,512]{2,1,0:T(8,128)(2,1)S(1)}, bf16[2,72,512]{2,1,0:T(8,128)(2,1)S(1)}, bf16[2,72,512]{2,1,0:T(8,128)(2,1)S(1)}) custom-call(s32[1]{0:T(128)} %bitcast.1.seq_ref, s32[32,128]{1,0:T(8,128)S(1)} %get-tuple-element.52.code_ref, f32[1]{0:T(128)} %get-tuple-element.57.norm_ref, s32[32,256]{1,0:T(8,128)S(1)} %reshape.40.pos_ref, ...), custom_call_target="tpu_custom_call" | custom-call | flops 17999998976 | bytes 4194304 | tf_op jit(solution)/shard_map/pallas_call | solution.py:380
  85.9 0.0 collective-permute-done.5.refs_1_
  86.0 1.0 shard_map.86
  87.0 45.3 %shard_map.87 = (bf16[2,72,512]{2,1,0:T(8,128)(2,1)S(1)}, bf16[2,72,512]{2,1,0:T(8,128)(2,1)S(1)}, bf16[2,72,512]{2,1,0:T(8,128)(2,1)S(1)}) custom-call(s32[1]{0:T(128)} %bitcast.1.seq_ref, s32[32,128]{1,0:T(8,128)S(1)} %get-tuple-element.52.code_ref, f32[1]{0:T(128)} %get-tuple-element.66.norm_ref, s32[32,256]{1,0:T(8,128)S(1)} %reshape.40.pos_ref, ...), custom_call_target="tpu_custom_call" | custom-call | flops 17999998976 | bytes 4194304 | tf_op jit(solution)/shard_map/pallas_call | solution.py:380
  132.3 3.2 %collective-permute-start.10 = (bf16[2,72,512]{2,1,0:T(8,128)(2,1)S(1)}, bf16[2,72,512]{2,1,0:T(8,128)(2,1)S(1)}, u32[]{:S(2)}, u32[]{:S(2)}) collective-permute-start(bf16[2,72,512]{2,1,0:T(8,128)(2,1)S(1)} %get-tuple-element.75), channel_id=1, source_target_pairs={{0,96},{8,104},{16,112},{24,120},{32,64},{40,72},{48,80},{56,88},{... | collective-permute-start | bytes 442376 | tf_op jit(solution)/shard_map/ppermute | solution.py:515
  135.4 0.2 collective-permute-start.8
  135.7 0.0 collective-permute-done.11.refs_1_
  135.7 1.6 collective-permute-start.9
  137.3 17.4 %shard_map.88.refs_3_ = bf16[2,72,512]{2,1,0:T(8,128)(2,1)S(1)} custom-call(s32[1]{0:T(128)} %bitcast.1.seq_ref, s32[32,128]{1,0:T(8,128)S(1)} %get-tuple-element.52.code_ref, f32[1]{0:T(128)} %get-tuple-element.66.norm_ref, s32[32,256]{1,0:T(8,128)S(1)} %reshape.40.pos_ref, bf16[4096,128]{1,0:T(8,128)(2,1)S(1)} %get-tuple-element.67.kv_ref, ...), custom_call_target="tpu_custom_call" | custom-call | flops 6000000000 | bytes 4194304 | tf_op jit(solution)/shard_map/pallas_call | solution.py:380
  154.7 0.0 collective-permute-done.12.refs_2_
  154.7 0.0 collective-permute-done.13.refs_3_
  154.8 0.0 collective-permute-done.10.refs_2_
  154.8 0.0 collective-permute-done.8.refs_0_
  154.8 0.0 collective-permute-done.9.refs_1_
  154.8 1.0 shard_map.89
  155.8 7.5 %all-to-all-start = ((bf16[16,32,128]{2,1,0:T(8,128)(2,1)}), bf16[16,32,128]{2,1,0:T(8,128)(2,1)S(1)}, u32[]{:S(2)}, u32[]{:S(2)}) async-start(bf16[16,32,128]{2,1,0:T(8,128)(2,1)} %shard_map.89), calls=%async_computation | async-start | bytes 262144 | tf_op jit(solution)/shard_map/all_to_all | solution.py:519
  163.3 6.3 %all-to-all-done.pieces_ref = bf16[16,32,128]{2,1,0:T(8,128)(2,1)S(1)} async-done(((bf16[16,32,128]{2,1,0:T(8,128)(2,1)}), bf16[16,32,128]{2,1,0:T(8,128)(2,1)S(1)}, u32[]{:S(2)}, u32[]{:S(2)}) %all-to-all-start) | async-done | bytes 131104 | tf_op jit(solution)/shard_map/all_to_all | solution.py:519
  169.6 1.2 shard_map.90
  (3 shorter events, 0.0 us)
Async XLA Ops:
  0.0 12.3 %copy-start.1 = (s32[8192]{0:T(1024)S(1)}, s32[8192]{0:T(1024)}, u32[]{:S(2)}) copy-start(s32[8192]{0:T(1024)} %param.16) | copy-start | bytes 98308
  0.0 8.4 %copy-start = (bf16[128,1024]{1,0:T(8,128)(2,1)S(1)}, bf16[128,1024]{1,0:T(8,128)(2,1)}, u32[]{:S(2)}) copy-start(bf16[128,1024]{1,0:T(8,128)(2,1)} %param.15) | copy-start | bytes 786436
  7.5 7.0 %collective-permute-start.3 = (bf16[2048,128]{1,0:T(8,128)(2,1)S(1)}, bf16[2048,128]{1,0:T(8,128)(2,1)S(1)}, u32[]{:S(2)}, u32[]{:S(2)}) collective-permute-start(bf16[2048,128]{1,0:T(8,128)(2,1)S(1)} %get-tuple-element.56), channel_id=1, source_target_pairs={{0,8},{8,0},{16,24},{24,16},{32,40},{40,32},{48,56},{56,48},{64,72... | collective-permute-start | bytes 1572872 | tf_op jit(solution)/shard_map/ppermute | solution.py:482
  8.3 4.1 %collective-permute-start = (bf16[64,512]{1,0:T(8,128)(2,1)S(1)}, bf16[64,512]{1,0:T(8,128)(2,1)S(1)}, u32[]{:S(2)}, u32[]{:S(2)}) collective-permute-start(bf16[64,512]{1,0:T(8,128)(2,1)S(1)} %get-tuple-element.54), channel_id=1, source_target_pairs={{0,8},{8,0},{16,24},{24,16},{32,40},{40,32},{48,56},{56,48},{64,72... | collective-permute-start | bytes 196616 | tf_op jit(solution)/shard_map/ppermute | solution.py:480
  8.4 25.1 %collective-permute-start.2 = (bf16[128,1024]{1,0:T(8,128)(2,1)S(1)}, bf16[128,1024]{1,0:T(8,128)(2,1)}, u32[]{:S(2)}, u32[]{:S(2)}) collective-permute-start(bf16[128,1024]{1,0:T(8,128)(2,1)S(1)} %copy-done), channel_id=1, source_target_pairs={{0,4},{1,5},{2,6},{3,7},{4,0},{5,1},{6,2},{7,3},{8,12},{9,13},{10,... | collective-permute-start | bytes 786440 | tf_op jit(solution)/shard_map/ppermute | solution.py:486
  9.7 29.8 %collective-permute-start.4 = (bf16[2048,128]{1,0:T(8,128)(2,1)S(1)}, bf16[2048,128]{1,0:T(8,128)(2,1)S(1)}, u32[]{:S(2)}, u32[]{:S(2)}) collective-permute-start(bf16[2048,128]{1,0:T(8,128)(2,1)S(1)} %get-tuple-element.55.refs_0_), channel_id=1, source_target_pairs={{0,16},{8,24},{16,0},{24,8},{32,48},{40,56},{48,32},{56,40},{64,80... | collective-permute-start | bytes 1572872 | tf_op jit(solution)/shard_map/ppermute | solution.py:484
  12.4 23.8 %collective-permute-start.1 = (bf16[2,64,512]{2,1,0:T(8,128)(2,1)S(1)}, bf16[2,64,512]{2,1,0:T(8,128)(2,1)S(1)}, u32[]{:S(2)}, u32[]{:S(2)}) collective-permute-start(bf16[2,64,512]{2,1,0:T(8,128)(2,1)S(1)} %bitcast_dynamic-update-slice_fusion.rest_0_), channel_id=1, source_target_pairs={{0,32},{8,40},{16,48},{24,56},{32,0},{40,8},{48,16},{56,24},{64,96... | collective-permute-start | bytes 393224 | tf_op jit(solution)/shard_map/ppermute | solution.py:481
  12.7 26.8 %collective-permute-start.6 = (bf16[2,64,512]{2,1,0:T(8,128)(2,1)S(1)}, bf16[2,64,512]{2,1,0:T(8,128)(2,1)S(1)}, u32[]{:S(2)}, u32[]{:S(2)}) collective-permute-start(bf16[2,64,512]{2,1,0:T(8,128)(2,1)S(1)} %bitcast_dynamic-update-slice_fusion.rest_0_), channel_id=1, source_target_pairs={{0,96},{8,104},{16,112},{24,120},{32,64},{40,72},{48,80},{56,88},{... | collective-permute-start | bytes 393224 | tf_op jit(solution)/shard_map/ppermute | solution.py:481
  14.6 26.4 %collective-permute-start.7 = (bf16[2,64,512]{2,1,0:T(8,128)(2,1)S(1)}, bf16[2,64,512]{2,1,0:T(8,128)(2,1)S(1)}, u32[]{:S(2)}, u32[]{:S(2)}) collective-permute-start(bf16[2,64,512]{2,1,0:T(8,128)(2,1)S(1)} %bitcast_dynamic-update-slice_fusion.rest_0_), channel_id=1, source_target_pairs={{0,64},{8,72},{16,80},{24,88},{32,96},{40,104},{48,112},{56,120},{... | collective-permute-start | bytes 393224 | tf_op jit(solution)/shard_map/ppermute | solution.py:481
  34.5 101.2 %collective-permute-start.11 = (bf16[256,1024]{1,0:T(8,128)(2,1)S(1)}, bf16[256,1024]{1,0:T(8,128)(2,1)S(1)}, u32[]{:S(2)}, u32[]{:S(2)}) collective-permute-start(bf16[256,1024]{1,0:T(8,128)(2,1)S(1)} %constant_dynamic-update-slice_fusion.refs_0_), channel_id=1, source_target_pairs={{0,1},{1,0},{2,3},{3,2},{4,5},{5,4},{6,7},{7,6},{8,9},{9,8},{10,11... | collective-permute-start | bytes 1572872 | tf_op jit(solution)/shard_map/ppermute | solution.py:492
  36.2 118.6 %collective-permute-start.12 = (bf16[256,1024]{1,0:T(8,128)(2,1)S(1)}, bf16[256,1024]{1,0:T(8,128)(2,1)S(1)}, u32[]{:S(2)}, u32[]{:S(2)}) collective-permute-start(bf16[256,1024]{1,0:T(8,128)(2,1)S(1)} %constant_dynamic-update-slice_fusion.refs_0_), channel_id=1, source_target_pairs={{0,2},{1,3},{2,0},{3,1},{4,6},{5,7},{6,4},{7,5},{8,10},{9,11},{10,... | collective-permute-start | bytes 1572872 | tf_op jit(solution)/shard_map/ppermute | solution.py:492
  39.5 115.3 %collective-permute-start.13 = (bf16[256,1024]{1,0:T(8,128)(2,1)S(1)}, bf16[256,1024]{1,0:T(8,128)(2,1)S(1)}, u32[]{:S(2)}, u32[]{:S(2)}) collective-permute-start(bf16[256,1024]{1,0:T(8,128)(2,1)S(1)} %constant_dynamic-update-slice_fusion.refs_0_), channel_id=1, source_target_pairs={{0,3},{1,2},{2,1},{3,0},{4,7},{5,6},{6,5},{7,4},{8,11},{9,10},{10,... | collective-permute-start | bytes 1572872 | tf_op jit(solution)/shard_map/ppermute | solution.py:492
  39.5 46.5 %collective-permute-start.5 = (bf16[2048,128]{1,0:T(8,128)(2,1)S(1)}, bf16[2048,128]{1,0:T(8,128)(2,1)S(1)}, u32[]{:S(2)}, u32[]{:S(2)}) collective-permute-start(bf16[2048,128]{1,0:T(8,128)(2,1)S(1)} %collective-permute-done.3.refs_1_), channel_id=1, source_target_pairs={{0,16},{8,24},{16,0},{24,8},{32,48},{40,56},{48,32},{56,40},{64,80... | collective-permute-start | bytes 1572872 | tf_op jit(solution)/shard_map/ppermute | solution.py:484
  132.3 22.5 %collective-permute-start.10 = (bf16[2,72,512]{2,1,0:T(8,128)(2,1)S(1)}, bf16[2,72,512]{2,1,0:T(8,128)(2,1)S(1)}, u32[]{:S(2)}, u32[]{:S(2)}) collective-permute-start(bf16[2,72,512]{2,1,0:T(8,128)(2,1)S(1)} %get-tuple-element.75), channel_id=1, source_target_pairs={{0,96},{8,104},{16,112},{24,120},{32,64},{40,72},{48,80},{56,88},{... | collective-permute-start | bytes 442376 | tf_op jit(solution)/shard_map/ppermute | solution.py:515
  135.4 19.3 %collective-permute-start.8 = (bf16[2,72,512]{2,1,0:T(8,128)(2,1)S(1)}, bf16[2,72,512]{2,1,0:T(8,128)(2,1)S(1)}, u32[]{:S(2)}, u32[]{:S(2)}) collective-permute-start(bf16[2,72,512]{2,1,0:T(8,128)(2,1)S(1)} %get-tuple-element.72), channel_id=1, source_target_pairs={{0,64},{8,72},{16,80},{24,88},{32,96},{40,104},{48,112},{56,120},{... | collective-permute-start | bytes 442376 | tf_op jit(solution)/shard_map/ppermute | solution.py:515
  135.7 19.1 %collective-permute-start.9 = (bf16[2,72,512]{2,1,0:T(8,128)(2,1)S(1)}, bf16[2,72,512]{2,1,0:T(8,128)(2,1)S(1)}, u32[]{:S(2)}, u32[]{:S(2)}) collective-permute-start(bf16[2,72,512]{2,1,0:T(8,128)(2,1)S(1)} %get-tuple-element.73), channel_id=1, source_target_pairs={{0,32},{8,40},{16,48},{24,56},{32,0},{40,8},{48,16},{56,24},{64,96... | collective-permute-start | bytes 442376 | tf_op jit(solution)/shard_map/ppermute | solution.py:515
  155.8 13.9 %all-to-all-start = ((bf16[16,32,128]{2,1,0:T(8,128)(2,1)}), bf16[16,32,128]{2,1,0:T(8,128)(2,1)S(1)}, u32[]{:S(2)}, u32[]{:S(2)}) async-start(bf16[16,32,128]{2,1,0:T(8,128)(2,1)} %shard_map.89), calls=%async_computation | async-start | bytes 262144 | tf_op jit(solution)/shard_map/all_to_all | solution.py:519

commit v12 on v11

--- a/solution.py
+++ b/solution.py
@@ -474,16 +474,17 @@
     grp = lax.axis_index("grp")[None]
     core = jnp.bitwise_and(seq, 1)
 
+    w_other = lax.ppermute(w_out, "grp", [(g, g ^ 4) for g in range(8)])
     q_chip, theirs, kv_own, kv_other, codes = front(
         seq, latents, inputs, w_query, w_key, w_value, positions, block_mask
     )
+    theirs, kv_other, kv_own, w_other = lax.optimization_barrier((theirs, kv_other, kv_own, w_other))
     q_chip = q_chip.at[1].set(lax.ppermute(theirs, "seq", CORE_SWAP))
     queries = {by: q_chip if by == 0 else lax.ppermute(q_chip, "seq", along_x(by)) for by in (0, 1, 3, 2)}
     kv_partner = lax.ppermute(kv_other, "seq", CORE_SWAP)
     near = prepare(kv_own, kv_partner)
     kv_far = [lax.ppermute(kv, "seq", Y_SWAP) for kv in (kv_own, kv_partner)]
 
-    w_other = lax.ppermute(w_out, "grp", [(g, g ^ 4) for g in range(8)])
     spots = positions.reshape(-1, ROWS)
     near_parts = dict(zip(NEAR_CALLS[0], attend(NEAR_CALLS[0], seq, codes, spots, near, [q_chip])))
     w_other, near_parts[0] = lax.optimization_barrier((w_other, near_parts[0]))

time: 171 us -> 172 us (level)
  Pallas kernels: 136 us -> 139 us
    pallas_call x4, Pallas kernels: 124 us -> 127 us  [attend(): pl.pallas_call(functools.partial(attention_kernel, steps, bool(before)),...]
    ppermute x3, starting transfers between devices: 5.07 us -> 3.33 us  [body(): lax.ppermute(part, 'seq', along_x(by))]
  transfers between devices with their start and end apart: 15 -> 15, of which waited for: 1 -> 1; matrix products, arithmetic and copies ran while one was open for 1% -> 0% of each run, Pallas kernels for 74% -> 80%
where the time goes in v12:
time: 172 us
  Pallas kernels  139 us (81%)
  starting transfers between devices  26 us (15%)
  waiting for transfers between devices  6.38 us (4%)
    pallas_call x4, Pallas kernels, attend(): pl.pallas_call(functools.partial(attention_kernel, steps, bool(before)),...  127 us
    pallas_call x1, Pallas kernels, front(): pl.pallas_call(front_kernel, in_specs=[SMEM] + [pl.BlockSpec(memory_space...  7.47 us
    all_to_all x1, starting transfers between devices, body(): lax.all_to_all(pieces, ('seq', 'grp'), 0, 0, axis_index_groups=owners)  7.31 us
    all_to_all x1, waiting for transfers between devices, body(): lax.all_to_all(pieces, ('seq', 'grp'), 0, 0, axis_index_groups=owners)  6.34 us
    ppermute x3, starting transfers between devices, body(): lax.ppermute(w_pair, 'grp', [(g, g ^ k) for g in range(8)])  5.02 us
    ppermute x2, starting transfers between devices, body(): kv_far = [lax.ppermute(kv, 'seq', Y_SWAP) for kv in (kv_own, kv_partner)]  4.6 us
  transfers between devices with their start and end apart: 15, of which 1 were waited for; matrix products, arithmetic and copies ran while one was open for 0% of the time, Pallas kernels for 80%

profile of v12, /device:TPU:3, one launch (start us, length us, event | category | flops | bytes accessed | tf_op | source)
XLA Modules:
  0.0 171.6 jit_solution(5892800761891680096)
XLA Ops:
  0.0 0.0 copy-start
  0.0 0.0 copy-start.1
  0.0 1.3 collective-permute-start
  1.3 7.5 %shard_map.82 = (bf16[2,64,512]{2,1,0:T(8,128)(2,1)S(1)}, bf16[64,512]{1,0:T(8,128)(2,1)S(1)}, bf16[2048,128]{1,0:T(8,128)(2,1)S(1)}, bf16[2048,128]{1,0:T(8,128)(2,1)S(1)}, s32[32,128]{1,0:T(8,128)S(1)}) custom-call(s32[1]{0:T(128)} %bitcast.1.seq_ref, bf16[512,1024]{1,0:T(8,128)(2,1)} %lat_hbm.1, bf16[2048,1024]{1,0:T(8,128)(2,1)} %x_hbm.1, ...), custom_call_target="tpu_custom_call" | custom-call | flops 1207959552 | bytes 6291456 | tf_op jit(solution)/shard_map/pallas_call | solution.py:154
  8.8 0.0 collective-permute-done
  8.8 1.0 collective-permute-start.3
  9.8 0.0 copy-done.1
  9.8 0.1 collective-permute-start.1
  9.9 0.0 copy-done
  10.0 2.7 %collective-permute-start.4 = (bf16[2048,128]{1,0:T(8,128)(2,1)S(1)}, bf16[2048,128]{1,0:T(8,128)(2,1)S(1)}, u32[]{:S(2)}, u32[]{:S(2)}) collective-permute-start(bf16[2048,128]{1,0:T(8,128)(2,1)S(1)} %get-tuple-element.63.refs_0_), channel_id=1, source_target_pairs={{0,16},{8,24},{16,0},{24,8},{32,48},{40,56},{48,32},{56,40},{64,80... | collective-permute-start | bytes 1572872 | tf_op jit(solution)/shard_map/ppermute | solution.py:486
  12.7 0.0 collective-permute-done.1
  12.7 0.3 collective-permute-start.2
  13.0 1.9 %collective-permute-start.6 = (bf16[2,64,512]{2,1,0:T(8,128)(2,1)S(1)}, bf16[2,64,512]{2,1,0:T(8,128)(2,1)S(1)}, u32[]{:S(2)}, u32[]{:S(2)}) collective-permute-start(bf16[2,64,512]{2,1,0:T(8,128)(2,1)S(1)} %bitcast_dynamic-update-slice_fusion.rest_0_), channel_id=1, source_target_pairs={{0,96},{8,104},{16,112},{24,120},{32,64},{40,72},{48,80},{56,88},{... | collective-permute-start | bytes 393224 | tf_op jit(solution)/shard_map/ppermute | solution.py:483
  14.9 1.1 collective-permute-start.7
  16.0 0.0 collective-permute-done.3.refs_1_
  16.0 1.0 shard_map.83
  17.0 16.8 %shard_map.84.rest_1_ = bf16[2,72,512]{2,1,0:T(8,128)(2,1)S(1)} custom-call(s32[1]{0:T(128)} %bitcast.1.seq_ref, s32[32,128]{1,0:T(8,128)S(1)} %get-tuple-element.56.code_ref, f32[1]{0:T(128)} %get-tuple-element.65.norm_ref, s32[32,256]{1,0:T(8,128)S(1)} %reshape.40.pos_ref, bf16[4096,128]{1,0:T(8,128)(2,1)S(1)} %get-tuple-element.66.kv_ref, ...), custom_call_target="tpu_custom_call" | custom-call | flops 6000000000 | bytes 4194304 | tf_op jit(solution)/shard_map/pallas_call | solution.py:380
  33.9 1.7 collective-permute-start.11
  35.6 0.0 collective-permute-done.2.rest_0_.rest_1_
  35.6 3.3 %collective-permute-start.12 = (bf16[256,1024]{1,0:T(8,128)(2,1)S(1)}, bf16[256,1024]{1,0:T(8,128)(2,1)S(1)}, u32[]{:S(2)}, u32[]{:S(2)}) collective-permute-start(bf16[256,1024]{1,0:T(8,128)(2,1)S(1)} %constant_dynamic-update-slice_fusion.refs_0_), channel_id=1, source_target_pairs={{0,2},{1,3},{2,0},{3,1},{4,6},{5,7},{6,4},{7,5},{8,10},{9,11},{10,... | collective-permute-start | bytes 1572872 | tf_op jit(solution)/shard_map/ppermute | solution.py:493
  38.9 0.0 collective-permute-done.4.refs_0_
  38.9 0.0 collective-permute-start.13
  38.9 0.0 collective-permute-done.6.rest_1_.rest_2_
  38.9 1.9 %collective-permute-start.5 = (bf16[2048,128]{1,0:T(8,128)(2,1)S(1)}, bf16[2048,128]{1,0:T(8,128)(2,1)S(1)}, u32[]{:S(2)}, u32[]{:S(2)}) collective-permute-start(bf16[2048,128]{1,0:T(8,128)(2,1)S(1)} %collective-permute-done.3.refs_1_), channel_id=1, source_target_pairs={{0,16},{8,24},{16,0},{24,8},{32,48},{40,56},{48,32},{56,40},{64,80... | collective-permute-start | bytes 1572872 | tf_op jit(solution)/shard_map/ppermute | solution.py:486
  40.8 0.0 collective-permute-done.7.rest_2_.rest_0_
  40.8 45.5 %shard_map.85 = (bf16[2,72,512]{2,1,0:T(8,128)(2,1)S(1)}, bf16[2,72,512]{2,1,0:T(8,128)(2,1)S(1)}, bf16[2,72,512]{2,1,0:T(8,128)(2,1)S(1)}) custom-call(s32[1]{0:T(128)} %bitcast.1.seq_ref, s32[32,128]{1,0:T(8,128)S(1)} %get-tuple-element.56.code_ref, f32[1]{0:T(128)} %get-tuple-element.65.norm_ref, s32[32,256]{1,0:T(8,128)S(1)} %reshape.40.pos_ref, ...), custom_call_target="tpu_custom_call" | custom-call | flops 17999998976 | bytes 4194304 | tf_op jit(solution)/shard_map/pallas_call | solution.py:380
  86.3 0.0 collective-permute-done.5.refs_1_
  86.3 1.0 shard_map.86
  87.4 47.1 %shard_map.87 = (bf16[2,72,512]{2,1,0:T(8,128)(2,1)S(1)}, bf16[2,72,512]{2,1,0:T(8,128)(2,1)S(1)}, bf16[2,72,512]{2,1,0:T(8,128)(2,1)S(1)}) custom-call(s32[1]{0:T(128)} %bitcast.1.seq_ref, s32[32,128]{1,0:T(8,128)S(1)} %get-tuple-element.56.code_ref, f32[1]{0:T(128)} %get-tuple-element.74.norm_ref, s32[32,256]{1,0:T(8,128)S(1)} %reshape.40.pos_ref, ...), custom_call_target="tpu_custom_call" | custom-call | flops 17999998976 | bytes 4194304 | tf_op jit(solution)/shard_map/pallas_call | solution.py:380
  134.5 1.3 collective-permute-start.10
  135.8 0.0 collective-permute-start.8
  135.8 0.0 collective-permute-done.11.refs_1_
  135.8 2.0 %collective-permute-start.9 = (bf16[2,72,512]{2,1,0:T(8,128)(2,1)S(1)}, bf16[2,72,512]{2,1,0:T(8,128)(2,1)S(1)}, u32[]{:S(2)}, u32[]{:S(2)}) collective-permute-start(bf16[2,72,512]{2,1,0:T(8,128)(2,1)S(1)} %get-tuple-element.81), channel_id=1, source_target_pairs={{0,32},{8,40},{16,48},{24,56},{32,0},{40,8},{48,16},{56,24},{64,96... | collective-permute-start | bytes 442376 | tf_op jit(solution)/shard_map/ppermute | solution.py:516
  137.8 17.9 %shard_map.88.refs_3_ = bf16[2,72,512]{2,1,0:T(8,128)(2,1)S(1)} custom-call(s32[1]{0:T(128)} %bitcast.1.seq_ref, s32[32,128]{1,0:T(8,128)S(1)} %get-tuple-element.56.code_ref, f32[1]{0:T(128)} %get-tuple-element.74.norm_ref, s32[32,256]{1,0:T(8,128)S(1)} %reshape.40.pos_ref, bf16[4096,128]{1,0:T(8,128)(2,1)S(1)} %get-tuple-element.75.kv_ref, ...), custom_call_target="tpu_custom_call" | custom-call | flops 6000000000 | bytes 4194304 | tf_op jit(solution)/shard_map/pallas_call | solution.py:380
  155.7 0.0 collective-permute-done.12.refs_2_
  155.7 0.0 collective-permute-done.13.refs_3_
  155.8 0.0 collective-permute-done.10.refs_2_
  155.8 0.0 collective-permute-done.8.refs_0_
  155.8 0.0 collective-permute-done.9.refs_1_
  155.8 1.0 shard_map.89
  156.8 7.3 %all-to-all-start = ((bf16[16,32,128]{2,1,0:T(8,128)(2,1)}), bf16[16,32,128]{2,1,0:T(8,128)(2,1)S(1)}, u32[]{:S(2)}, u32[]{:S(2)}) async-start(bf16[16,32,128]{2,1,0:T(8,128)(2,1)} %shard_map.89), calls=%async_computation | async-start | bytes 262144 | tf_op jit(solution)/shard_map/all_to_all | solution.py:520
  164.1 6.3 %all-to-all-done.pieces_ref = bf16[16,32,128]{2,1,0:T(8,128)(2,1)S(1)} async-done(((bf16[16,32,128]{2,1,0:T(8,128)(2,1)}), bf16[16,32,128]{2,1,0:T(8,128)(2,1)S(1)}, u32[]{:S(2)}, u32[]{:S(2)}) %all-to-all-start) | async-done | bytes 131104 | tf_op jit(solution)/shard_map/all_to_all | solution.py:520
  170.4 1.2 shard_map.90
  (4 shorter events, 0.1 us)
Async XLA Ops:
  0.0 10.0 %copy-start = (bf16[128,1024]{1,0:T(8,128)(2,1)S(1)}, bf16[128,1024]{1,0:T(8,128)(2,1)}, u32[]{:S(2)}) copy-start(bf16[128,1024]{1,0:T(8,128)(2,1)} %param.15) | copy-start | bytes 786436
  0.0 9.8 %copy-start.1 = (s32[8192]{0:T(1024)S(1)}, s32[8192]{0:T(1024)}, u32[]{:S(2)}) copy-start(s32[8192]{0:T(1024)} %param.16) | copy-start | bytes 98308
  0.0 8.8 %collective-permute-start = (bf16[128,1024]{1,0:T(8,128)(2,1)}, bf16[128,1024]{1,0:T(8,128)(2,1)S(1)}, u32[]{:S(2)}, u32[]{:S(2)}) collective-permute-start(bf16[128,1024]{1,0:T(8,128)(2,1)} %param.15), channel_id=1, source_target_pairs={{0,4},{1,5},{2,6},{3,7},{4,0},{5,1},{6,2},{7,3},{8,12},{9,13},{10,... | collective-permute-start | bytes 786440 | tf_op jit(solution)/shard_map/ppermute | solution.py:477
  8.8 7.2 %collective-permute-start.3 = (bf16[2048,128]{1,0:T(8,128)(2,1)S(1)}, bf16[2048,128]{1,0:T(8,128)(2,1)S(1)}, u32[]{:S(2)}, u32[]{:S(2)}) collective-permute-start(bf16[2048,128]{1,0:T(8,128)(2,1)S(1)} %get-tuple-element.64), channel_id=1, source_target_pairs={{0,8},{8,0},{16,24},{24,16},{32,40},{40,32},{48,56},{56,48},{64,72... | collective-permute-start | bytes 1572872 | tf_op jit(solution)/shard_map/ppermute | solution.py:484
  9.8 2.8 %collective-permute-start.1 = (bf16[64,512]{1,0:T(8,128)(2,1)S(1)}, bf16[64,512]{1,0:T(8,128)(2,1)S(1)}, u32[]{:S(2)}, u32[]{:S(2)}) collective-permute-start(bf16[64,512]{1,0:T(8,128)(2,1)S(1)} %get-tuple-element.61), channel_id=1, source_target_pairs={{0,8},{8,0},{16,24},{24,16},{32,40},{40,32},{48,56},{56,48},{64,72... | collective-permute-start | bytes 196616 | tf_op jit(solution)/shard_map/ppermute | solution.py:482
  10.0 28.9 %collective-permute-start.4 = (bf16[2048,128]{1,0:T(8,128)(2,1)S(1)}, bf16[2048,128]{1,0:T(8,128)(2,1)S(1)}, u32[]{:S(2)}, u32[]{:S(2)}) collective-permute-start(bf16[2048,128]{1,0:T(8,128)(2,1)S(1)} %get-tuple-element.63.refs_0_), channel_id=1, source_target_pairs={{0,16},{8,24},{16,0},{24,8},{32,48},{40,56},{48,32},{56,40},{64,80... | collective-permute-start | bytes 1572872 | tf_op jit(solution)/shard_map/ppermute | solution.py:486
  12.7 22.9 %collective-permute-start.2 = (bf16[2,64,512]{2,1,0:T(8,128)(2,1)S(1)}, bf16[2,64,512]{2,1,0:T(8,128)(2,1)S(1)}, u32[]{:S(2)}, u32[]{:S(2)}) collective-permute-start(bf16[2,64,512]{2,1,0:T(8,128)(2,1)S(1)} %bitcast_dynamic-update-slice_fusion.rest_0_), channel_id=1, source_target_pairs={{0,32},{8,40},{16,48},{24,56},{32,0},{40,8},{48,16},{56,24},{64,96... | collective-permute-start | bytes 393224 | tf_op jit(solution)/shard_map/ppermute | solution.py:483
  13.0 25.9 %collective-permute-start.6 = (bf16[2,64,512]{2,1,0:T(8,128)(2,1)S(1)}, bf16[2,64,512]{2,1,0:T(8,128)(2,1)S(1)}, u32[]{:S(2)}, u32[]{:S(2)}) collective-permute-start(bf16[2,64,512]{2,1,0:T(8,128)(2,1)S(1)} %bitcast_dynamic-update-slice_fusion.rest_0_), channel_id=1, source_target_pairs={{0,96},{8,104},{16,112},{24,120},{32,64},{40,72},{48,80},{56,88},{... | collective-permute-start | bytes 393224 | tf_op jit(solution)/shard_map/ppermute | solution.py:483
  14.9 25.9 %collective-permute-start.7 = (bf16[2,64,512]{2,1,0:T(8,128)(2,1)S(1)}, bf16[2,64,512]{2,1,0:T(8,128)(2,1)S(1)}, u32[]{:S(2)}, u32[]{:S(2)}) collective-permute-start(bf16[2,64,512]{2,1,0:T(8,128)(2,1)S(1)} %bitcast_dynamic-update-slice_fusion.rest_0_), channel_id=1, source_target_pairs={{0,64},{8,72},{16,80},{24,88},{32,96},{40,104},{48,112},{56,120},{... | collective-permute-start | bytes 393224 | tf_op jit(solution)/shard_map/ppermute | solution.py:483
  33.9 102.0 %collective-permute-start.11 = (bf16[256,1024]{1,0:T(8,128)(2,1)S(1)}, bf16[256,1024]{1,0:T(8,128)(2,1)S(1)}, u32[]{:S(2)}, u32[]{:S(2)}) collective-permute-start(bf16[256,1024]{1,0:T(8,128)(2,1)S(1)} %constant_dynamic-update-slice_fusion.refs_0_), channel_id=1, source_target_pairs={{0,1},{1,0},{2,3},{3,2},{4,5},{5,4},{6,7},{7,6},{8,9},{9,8},{10,11... | collective-permute-start | bytes 1572872 | tf_op jit(solution)/shard_map/ppermute | solution.py:493
  35.6 120.1 %collective-permute-start.12 = (bf16[256,1024]{1,0:T(8,128)(2,1)S(1)}, bf16[256,1024]{1,0:T(8,128)(2,1)S(1)}, u32[]{:S(2)}, u32[]{:S(2)}) collective-permute-start(bf16[256,1024]{1,0:T(8,128)(2,1)S(1)} %constant_dynamic-update-slice_fusion.refs_0_), channel_id=1, source_target_pairs={{0,2},{1,3},{2,0},{3,1},{4,6},{5,7},{6,4},{7,5},{8,10},{9,11},{10,... | collective-permute-start | bytes 1572872 | tf_op jit(solution)/shard_map/ppermute | solution.py:493
  38.9 116.8 %collective-permute-start.13 = (bf16[256,1024]{1,0:T(8,128)(2,1)S(1)}, bf16[256,1024]{1,0:T(8,128)(2,1)S(1)}, u32[]{:S(2)}, u32[]{:S(2)}) collective-permute-start(bf16[256,1024]{1,0:T(8,128)(2,1)S(1)} %constant_dynamic-update-slice_fusion.refs_0_), channel_id=1, source_target_pairs={{0,3},{1,2},{2,1},{3,0},{4,7},{5,6},{6,5},{7,4},{8,11},{9,10},{10,... | collective-permute-start | bytes 1572872 | tf_op jit(solution)/shard_map/ppermute | solution.py:493
  38.9 47.4 %collective-permute-start.5 = (bf16[2048,128]{1,0:T(8,128)(2,1)S(1)}, bf16[2048,128]{1,0:T(8,128)(2,1)S(1)}, u32[]{:S(2)}, u32[]{:S(2)}) collective-permute-start(bf16[2048,128]{1,0:T(8,128)(2,1)S(1)} %collective-permute-done.3.refs_1_), channel_id=1, source_target_pairs={{0,16},{8,24},{16,0},{24,8},{32,48},{40,56},{48,32},{56,40},{64,80... | collective-permute-start | bytes 1572872 | tf_op jit(solution)/shard_map/ppermute | solution.py:486
  134.5 21.3 %collective-permute-start.10 = (bf16[2,72,512]{2,1,0:T(8,128)(2,1)S(1)}, bf16[2,72,512]{2,1,0:T(8,128)(2,1)S(1)}, u32[]{:S(2)}, u32[]{:S(2)}) collective-permute-start(bf16[2,72,512]{2,1,0:T(8,128)(2,1)S(1)} %get-tuple-element.83), channel_id=1, source_target_pairs={{0,96},{8,104},{16,112},{24,120},{32,64},{40,72},{48,80},{56,88},{... | collective-permute-start | bytes 442376 | tf_op jit(solution)/shard_map/ppermute | solution.py:516
  135.8 19.9 %collective-permute-start.8 = (bf16[2,72,512]{2,1,0:T(8,128)(2,1)S(1)}, bf16[2,72,512]{2,1,0:T(8,128)(2,1)S(1)}, u32[]{:S(2)}, u32[]{:S(2)}) collective-permute-start(bf16[2,72,512]{2,1,0:T(8,128)(2,1)S(1)} %get-tuple-element.80), channel_id=1, source_target_pairs={{0,64},{8,72},{16,80},{24,88},{32,96},{40,104},{48,112},{56,120},{... | collective-permute-start | bytes 442376 | tf_op jit(solution)/shard_map/ppermute | solution.py:516
  135.8 19.9 %collective-permute-start.9 = (bf16[2,72,512]{2,1,0:T(8,128)(2,1)S(1)}, bf16[2,72,512]{2,1,0:T(8,128)(2,1)S(1)}, u32[]{:S(2)}, u32[]{:S(2)}) collective-permute-start(bf16[2,72,512]{2,1,0:T(8,128)(2,1)S(1)} %get-tuple-element.81), channel_id=1, source_target_pairs={{0,32},{8,40},{16,48},{24,56},{32,0},{40,8},{48,16},{56,24},{64,96... | collective-permute-start | bytes 442376 | tf_op jit(solution)/shard_map/ppermute | solution.py:516
  156.8 13.7 %all-to-all-start = ((bf16[16,32,128]{2,1,0:T(8,128)(2,1)}), bf16[16,32,128]{2,1,0:T(8,128)(2,1)S(1)}, u32[]{:S(2)}, u32[]{:S(2)}) async-start(bf16[16,32,128]{2,1,0:T(8,128)(2,1)} %shard_map.89), calls=%async_computation | async-start | bytes 262144 | tf_op jit(solution)/shard_map/all_to_all | solution.py:520

commit v13 on v12

--- a/solution.py
+++ b/solution.py
@@ -160,8 +160,8 @@
         + [
             pltpu.VMEM((width, 4 * HS), jnp.bfloat16),
             pltpu.SemaphoreType.DMA((6,)),
-            pltpu.SemaphoreType.DMA((4,)),
-            pltpu.SemaphoreType.DMA((11,)),
+            pltpu.SemaphoreType.DMA((1,)),
+            pltpu.SemaphoreType.DMA((5,)),
         ],
         compiler_params=pltpu.CompilerParams(vmem_limit_bytes=24 * 2**20),
         cost_estimate=pl.CostEstimate(

time: 172 us -> 171 us (level)
  Pallas kernels: 139 us -> 136 us
    pallas_call x1, Pallas kernels: 7.47 us -> 5.16 us  [front(): pl.pallas_call(front_kernel, in_specs=[SMEM] + [pl.BlockSpec(memory_space...]
  transfers between devices with their start and end apart: 15 -> 15, of which waited for: 1 -> 2; matrix products, arithmetic and copies ran while one was open for 0% -> 0% of each run, Pallas kernels for 80% -> 79%
where the time goes in v13:
time: 171 us; the launch traced here: 169 us
  Pallas kernels  136 us (80%)
  starting transfers between devices  25.2 us (15%)
  waiting for transfers between devices  7.3 us (4%)
    pallas_call x4, Pallas kernels, attend(): pl.pallas_call(functools.partial(attention_kernel, steps, bool(before)),...  127 us
    all_to_all x1, starting transfers between devices, body(): lax.all_to_all(pieces, ('seq', 'grp'), 0, 0, axis_index_groups=owners)  7.21 us
    all_to_all x1, waiting for transfers between devices, body(): lax.all_to_all(pieces, ('seq', 'grp'), 0, 0, axis_index_groups=owners)  6.34 us
    pallas_call x1, Pallas kernels, front(): pl.pallas_call(front_kernel, in_specs=[SMEM] + [pl.BlockSpec(memory_space...  5.16 us
    ppermute x3, starting transfers between devices, body(): lax.ppermute(w_pair, 'grp', [(g, g ^ k) for g in range(8)])  5.02 us
  transfers between devices with their start and end apart: 15, of which 2 were waited for; matrix products, arithmetic and copies ran while one was open for 0% of the time, Pallas kernels for 79%

profile of v13, /device:TPU:3, one launch (start us, length us, event | category | flops | bytes accessed | tf_op | source)
XLA Modules:
  0.0 169.0 jit_solution(15686690109259187652)
XLA Ops:
  0.0 0.0 copy-start
  0.0 0.0 copy-start.1
  0.0 1.3 collective-permute-start
  1.3 5.2 %shard_map.82 = (bf16[2,64,512]{2,1,0:T(8,128)(2,1)S(1)}, bf16[64,512]{1,0:T(8,128)(2,1)S(1)}, bf16[2048,128]{1,0:T(8,128)(2,1)S(1)}, bf16[2048,128]{1,0:T(8,128)(2,1)S(1)}, s32[32,128]{1,0:T(8,128)S(1)}) custom-call(s32[1]{0:T(128)} %bitcast.1.seq_ref, bf16[512,1024]{1,0:T(8,128)(2,1)} %lat_hbm.1, bf16[2048,1024]{1,0:T(8,128)(2,1)} %x_hbm.1, ...), custom_call_target="tpu_custom_call" | custom-call | flops 1207959552 | bytes 6291456 | tf_op jit(solution)/shard_map/pallas_call | solution.py:154
  6.5 0.9 collective-permute-done
  7.4 1.5 collective-permute-start.3
  8.9 0.0 copy-done.1
  9.0 0.1 collective-permute-start.1
  9.0 0.0 copy-done
  9.1 3.0 %collective-permute-start.4 = (bf16[2048,128]{1,0:T(8,128)(2,1)S(1)}, bf16[2048,128]{1,0:T(8,128)(2,1)S(1)}, u32[]{:S(2)}, u32[]{:S(2)}) collective-permute-start(bf16[2048,128]{1,0:T(8,128)(2,1)S(1)} %get-tuple-element.63.refs_0_), channel_id=1, source_target_pairs={{0,16},{8,24},{16,0},{24,8},{32,48},{40,56},{48,32},{56,40},{64,80... | collective-permute-start | bytes 1572872 | tf_op jit(solution)/shard_map/ppermute | solution.py:486
  12.1 0.0 collective-permute-done.1
  12.1 0.3 collective-permute-start.2
  12.4 1.9 %collective-permute-start.6 = (bf16[2,64,512]{2,1,0:T(8,128)(2,1)S(1)}, bf16[2,64,512]{2,1,0:T(8,128)(2,1)S(1)}, u32[]{:S(2)}, u32[]{:S(2)}) collective-permute-start(bf16[2,64,512]{2,1,0:T(8,128)(2,1)S(1)} %bitcast_dynamic-update-slice_fusion.rest_0_), channel_id=1, source_target_pairs={{0,96},{8,104},{16,112},{24,120},{32,64},{40,72},{48,80},{56,88},{... | collective-permute-start | bytes 393224 | tf_op jit(solution)/shard_map/ppermute | solution.py:483
  14.3 1.1 collective-permute-start.7
  15.4 0.0 collective-permute-done.3.refs_1_
  15.4 1.0 shard_map.83
  16.5 17.8 %shard_map.84.rest_1_ = bf16[2,72,512]{2,1,0:T(8,128)(2,1)S(1)} custom-call(s32[1]{0:T(128)} %bitcast.1.seq_ref, s32[32,128]{1,0:T(8,128)S(1)} %get-tuple-element.56.code_ref, f32[1]{0:T(128)} %get-tuple-element.65.norm_ref, s32[32,256]{1,0:T(8,128)S(1)} %reshape.40.pos_ref, bf16[4096,128]{1,0:T(8,128)(2,1)S(1)} %get-tuple-element.66.kv_ref, ...), custom_call_target="tpu_custom_call" | custom-call | flops 6000000000 | bytes 4194304 | tf_op jit(solution)/shard_map/pallas_call | solution.py:380
  34.3 1.7 %collective-permute-start.11 = (bf16[256,1024]{1,0:T(8,128)(2,1)S(1)}, bf16[256,1024]{1,0:T(8,128)(2,1)S(1)}, u32[]{:S(2)}, u32[]{:S(2)}) collective-permute-start(bf16[256,1024]{1,0:T(8,128)(2,1)S(1)} %constant_dynamic-update-slice_fusion.refs_0_), channel_id=1, source_target_pairs={{0,1},{1,0},{2,3},{3,2},{4,5},{5,4},{6,7},{7,6},{8,9},{9,8},{10,11... | collective-permute-start | bytes 1572872 | tf_op jit(solution)/shard_map/ppermute | solution.py:493
  36.0 0.0 collective-permute-done.2.rest_0_.rest_1_
  36.0 3.3 %collective-permute-start.12 = (bf16[256,1024]{1,0:T(8,128)(2,1)S(1)}, bf16[256,1024]{1,0:T(8,128)(2,1)S(1)}, u32[]{:S(2)}, u32[]{:S(2)}) collective-permute-start(bf16[256,1024]{1,0:T(8,128)(2,1)S(1)} %constant_dynamic-update-slice_fusion.refs_0_), channel_id=1, source_target_pairs={{0,2},{1,3},{2,0},{3,1},{4,6},{5,7},{6,4},{7,5},{8,10},{9,11},{10,... | collective-permute-start | bytes 1572872 | tf_op jit(solution)/shard_map/ppermute | solution.py:493
  39.3 0.0 collective-permute-done.4.refs_0_
  39.3 0.0 collective-permute-start.13
  39.3 0.0 collective-permute-done.6.rest_1_.rest_2_
  39.3 0.4 collective-permute-start.5
  39.7 0.0 collective-permute-done.7.rest_2_.rest_0_
  39.7 45.1 %shard_map.85 = (bf16[2,72,512]{2,1,0:T(8,128)(2,1)S(1)}, bf16[2,72,512]{2,1,0:T(8,128)(2,1)S(1)}, bf16[2,72,512]{2,1,0:T(8,128)(2,1)S(1)}) custom-call(s32[1]{0:T(128)} %bitcast.1.seq_ref, s32[32,128]{1,0:T(8,128)S(1)} %get-tuple-element.56.code_ref, f32[1]{0:T(128)} %get-tuple-element.65.norm_ref, s32[32,256]{1,0:T(8,128)S(1)} %reshape.40.pos_ref, ...), custom_call_target="tpu_custom_call" | custom-call | flops 17999998976 | bytes 4194304 | tf_op jit(solution)/shard_map/pallas_call | solution.py:380
  84.8 0.0 collective-permute-done.5.refs_1_
  84.8 1.0 shard_map.86
  85.8 46.7 %shard_map.87 = (bf16[2,72,512]{2,1,0:T(8,128)(2,1)S(1)}, bf16[2,72,512]{2,1,0:T(8,128)(2,1)S(1)}, bf16[2,72,512]{2,1,0:T(8,128)(2,1)S(1)}) custom-call(s32[1]{0:T(128)} %bitcast.1.seq_ref, s32[32,128]{1,0:T(8,128)S(1)} %get-tuple-element.56.code_ref, f32[1]{0:T(128)} %get-tuple-element.74.norm_ref, s32[32,256]{1,0:T(8,128)S(1)} %reshape.40.pos_ref, ...), custom_call_target="tpu_custom_call" | custom-call | flops 17999998976 | bytes 4194304 | tf_op jit(solution)/shard_map/pallas_call | solution.py:380
  132.5 0.8 collective-permute-start.10
  133.3 1.7 collective-permute-start.8
  134.9 0.0 collective-permute-done.11.refs_1_
  134.9 0.9 collective-permute-start.9
  135.8 17.4 %shard_map.88.refs_3_ = bf16[2,72,512]{2,1,0:T(8,128)(2,1)S(1)} custom-call(s32[1]{0:T(128)} %bitcast.1.seq_ref, s32[32,128]{1,0:T(8,128)S(1)} %get-tuple-element.56.code_ref, f32[1]{0:T(128)} %get-tuple-element.74.norm_ref, s32[32,256]{1,0:T(8,128)S(1)} %reshape.40.pos_ref, bf16[4096,128]{1,0:T(8,128)(2,1)S(1)} %get-tuple-element.75.kv_ref, ...), custom_call_target="tpu_custom_call" | custom-call | flops 6000000000 | bytes 4194304 | tf_op jit(solution)/shard_map/pallas_call | solution.py:380
  153.2 0.0 collective-permute-done.12.refs_2_
  153.3 0.0 collective-permute-done.13.refs_3_
  153.3 0.0 collective-permute-done.10.refs_2_
  153.3 0.0 collective-permute-done.8.refs_0_
  153.3 0.0 collective-permute-done.9.refs_1_
  153.3 1.0 shard_map.89
  154.3 7.2 %all-to-all-start = ((bf16[16,32,128]{2,1,0:T(8,128)(2,1)}), bf16[16,32,128]{2,1,0:T(8,128)(2,1)S(1)}, u32[]{:S(2)}, u32[]{:S(2)}) async-start(bf16[16,32,128]{2,1,0:T(8,128)(2,1)} %shard_map.89), calls=%async_computation | async-start | bytes 262144 | tf_op jit(solution)/shard_map/all_to_all | solution.py:520
  161.5 6.3 %all-to-all-done.pieces_ref = bf16[16,32,128]{2,1,0:T(8,128)(2,1)S(1)} async-done(((bf16[16,32,128]{2,1,0:T(8,128)(2,1)}), bf16[16,32,128]{2,1,0:T(8,128)(2,1)S(1)}, u32[]{:S(2)}, u32[]{:S(2)}) %all-to-all-start) | async-done | bytes 131104 | tf_op jit(solution)/shard_map/all_to_all | solution.py:520
  167.8 1.2 shard_map.90
  (4 shorter events, 0.1 us)
Async XLA Ops:
  0.0 9.0 %copy-start = (bf16[128,1024]{1,0:T(8,128)(2,1)S(1)}, bf16[128,1024]{1,0:T(8,128)(2,1)}, u32[]{:S(2)}) copy-start(bf16[128,1024]{1,0:T(8,128)(2,1)} %param.15) | copy-start | bytes 786436
  0.0 8.9 %copy-start.1 = (s32[8192]{0:T(1024)S(1)}, s32[8192]{0:T(1024)}, u32[]{:S(2)}) copy-start(s32[8192]{0:T(1024)} %param.16) | copy-start | bytes 98308
  0.0 7.4 %collective-permute-start = (bf16[128,1024]{1,0:T(8,128)(2,1)}, bf16[128,1024]{1,0:T(8,128)(2,1)S(1)}, u32[]{:S(2)}, u32[]{:S(2)}) collective-permute-start(bf16[128,1024]{1,0:T(8,128)(2,1)} %param.15), channel_id=1, source_target_pairs={{0,4},{1,5},{2,6},{3,7},{4,0},{5,1},{6,2},{7,3},{8,12},{9,13},{10,... | collective-permute-start | bytes 786440 | tf_op jit(solution)/shard_map/ppermute | solution.py:477
  7.4 8.0 %collective-permute-start.3 = (bf16[2048,128]{1,0:T(8,128)(2,1)S(1)}, bf16[2048,128]{1,0:T(8,128)(2,1)S(1)}, u32[]{:S(2)}, u32[]{:S(2)}) collective-permute-start(bf16[2048,128]{1,0:T(8,128)(2,1)S(1)} %get-tuple-element.64), channel_id=1, source_target_pairs={{0,8},{8,0},{16,24},{24,16},{32,40},{40,32},{48,56},{56,48},{64,72... | collective-permute-start | bytes 1572872 | tf_op jit(solution)/shard_map/ppermute | solution.py:484
  9.0 3.1 %collective-permute-start.1 = (bf16[64,512]{1,0:T(8,128)(2,1)S(1)}, bf16[64,512]{1,0:T(8,128)(2,1)S(1)}, u32[]{:S(2)}, u32[]{:S(2)}) collective-permute-start(bf16[64,512]{1,0:T(8,128)(2,1)S(1)} %get-tuple-element.61), channel_id=1, source_target_pairs={{0,8},{8,0},{16,24},{24,16},{32,40},{40,32},{48,56},{56,48},{64,72... | collective-permute-start | bytes 196616 | tf_op jit(solution)/shard_map/ppermute | solution.py:482
  9.1 30.2 %collective-permute-start.4 = (bf16[2048,128]{1,0:T(8,128)(2,1)S(1)}, bf16[2048,128]{1,0:T(8,128)(2,1)S(1)}, u32[]{:S(2)}, u32[]{:S(2)}) collective-permute-start(bf16[2048,128]{1,0:T(8,128)(2,1)S(1)} %get-tuple-element.63.refs_0_), channel_id=1, source_target_pairs={{0,16},{8,24},{16,0},{24,8},{32,48},{40,56},{48,32},{56,40},{64,80... | collective-permute-start | bytes 1572872 | tf_op jit(solution)/shard_map/ppermute | solution.py:486
  12.1 23.9 %collective-permute-start.2 = (bf16[2,64,512]{2,1,0:T(8,128)(2,1)S(1)}, bf16[2,64,512]{2,1,0:T(8,128)(2,1)S(1)}, u32[]{:S(2)}, u32[]{:S(2)}) collective-permute-start(bf16[2,64,512]{2,1,0:T(8,128)(2,1)S(1)} %bitcast_dynamic-update-slice_fusion.rest_0_), channel_id=1, source_target_pairs={{0,32},{8,40},{16,48},{24,56},{32,0},{40,8},{48,16},{56,24},{64,96... | collective-permute-start | bytes 393224 | tf_op jit(solution)/shard_map/ppermute | solution.py:483
  12.4 26.9 %collective-permute-start.6 = (bf16[2,64,512]{2,1,0:T(8,128)(2,1)S(1)}, bf16[2,64,512]{2,1,0:T(8,128)(2,1)S(1)}, u32[]{:S(2)}, u32[]{:S(2)}) collective-permute-start(bf16[2,64,512]{2,1,0:T(8,128)(2,1)S(1)} %bitcast_dynamic-update-slice_fusion.rest_0_), channel_id=1, source_target_pairs={{0,96},{8,104},{16,112},{24,120},{32,64},{40,72},{48,80},{56,88},{... | collective-permute-start | bytes 393224 | tf_op jit(solution)/shard_map/ppermute | solution.py:483
  14.3 25.4 %collective-permute-start.7 = (bf16[2,64,512]{2,1,0:T(8,128)(2,1)S(1)}, bf16[2,64,512]{2,1,0:T(8,128)(2,1)S(1)}, u32[]{:S(2)}, u32[]{:S(2)}) collective-permute-start(bf16[2,64,512]{2,1,0:T(8,128)(2,1)S(1)} %bitcast_dynamic-update-slice_fusion.rest_0_), channel_id=1, source_target_pairs={{0,64},{8,72},{16,80},{24,88},{32,96},{40,104},{48,112},{56,120},{... | collective-permute-start | bytes 393224 | tf_op jit(solution)/shard_map/ppermute | solution.py:483
  34.3 100.6 %collective-permute-start.11 = (bf16[256,1024]{1,0:T(8,128)(2,1)S(1)}, bf16[256,1024]{1,0:T(8,128)(2,1)S(1)}, u32[]{:S(2)}, u32[]{:S(2)}) collective-permute-start(bf16[256,1024]{1,0:T(8,128)(2,1)S(1)} %constant_dynamic-update-slice_fusion.refs_0_), channel_id=1, source_target_pairs={{0,1},{1,0},{2,3},{3,2},{4,5},{5,4},{6,7},{7,6},{8,9},{9,8},{10,11... | collective-permute-start | bytes 1572872 | tf_op jit(solution)/shard_map/ppermute | solution.py:493
  36.0 117.2 %collective-permute-start.12 = (bf16[256,1024]{1,0:T(8,128)(2,1)S(1)}, bf16[256,1024]{1,0:T(8,128)(2,1)S(1)}, u32[]{:S(2)}, u32[]{:S(2)}) collective-permute-start(bf16[256,1024]{1,0:T(8,128)(2,1)S(1)} %constant_dynamic-update-slice_fusion.refs_0_), channel_id=1, source_target_pairs={{0,2},{1,3},{2,0},{3,1},{4,6},{5,7},{6,4},{7,5},{8,10},{9,11},{10,... | collective-permute-start | bytes 1572872 | tf_op jit(solution)/shard_map/ppermute | solution.py:493
  39.3 113.9 %collective-permute-start.13 = (bf16[256,1024]{1,0:T(8,128)(2,1)S(1)}, bf16[256,1024]{1,0:T(8,128)(2,1)S(1)}, u32[]{:S(2)}, u32[]{:S(2)}) collective-permute-start(bf16[256,1024]{1,0:T(8,128)(2,1)S(1)} %constant_dynamic-update-slice_fusion.refs_0_), channel_id=1, source_target_pairs={{0,3},{1,2},{2,1},{3,0},{4,7},{5,6},{6,5},{7,4},{8,11},{9,10},{10,... | collective-permute-start | bytes 1572872 | tf_op jit(solution)/shard_map/ppermute | solution.py:493
  39.3 45.5 %collective-permute-start.5 = (bf16[2048,128]{1,0:T(8,128)(2,1)S(1)}, bf16[2048,128]{1,0:T(8,128)(2,1)S(1)}, u32[]{:S(2)}, u32[]{:S(2)}) collective-permute-start(bf16[2048,128]{1,0:T(8,128)(2,1)S(1)} %collective-permute-done.3.refs_1_), channel_id=1, source_target_pairs={{0,16},{8,24},{16,0},{24,8},{32,48},{40,56},{48,32},{56,40},{64,80... | collective-permute-start | bytes 1572872 | tf_op jit(solution)/shard_map/ppermute | solution.py:486
  132.5 20.8 %collective-permute-start.10 = (bf16[2,72,512]{2,1,0:T(8,128)(2,1)S(1)}, bf16[2,72,512]{2,1,0:T(8,128)(2,1)S(1)}, u32[]{:S(2)}, u32[]{:S(2)}) collective-permute-start(bf16[2,72,512]{2,1,0:T(8,128)(2,1)S(1)} %get-tuple-element.83), channel_id=1, source_target_pairs={{0,96},{8,104},{16,112},{24,120},{32,64},{40,72},{48,80},{56,88},{... | collective-permute-start | bytes 442376 | tf_op jit(solution)/shard_map/ppermute | solution.py:516
  133.3 20.0 %collective-permute-start.8 = (bf16[2,72,512]{2,1,0:T(8,128)(2,1)S(1)}, bf16[2,72,512]{2,1,0:T(8,128)(2,1)S(1)}, u32[]{:S(2)}, u32[]{:S(2)}) collective-permute-start(bf16[2,72,512]{2,1,0:T(8,128)(2,1)S(1)} %get-tuple-element.80), channel_id=1, source_target_pairs={{0,64},{8,72},{16,80},{24,88},{32,96},{40,104},{48,112},{56,120},{... | collective-permute-start | bytes 442376 | tf_op jit(solution)/shard_map/ppermute | solution.py:516
  134.9 18.3 %collective-permute-start.9 = (bf16[2,72,512]{2,1,0:T(8,128)(2,1)S(1)}, bf16[2,72,512]{2,1,0:T(8,128)(2,1)S(1)}, u32[]{:S(2)}, u32[]{:S(2)}) collective-permute-start(bf16[2,72,512]{2,1,0:T(8,128)(2,1)S(1)} %get-tuple-element.81), channel_id=1, source_target_pairs={{0,32},{8,40},{16,48},{24,56},{32,0},{40,8},{48,16},{56,24},{64,96... | collective-permute-start | bytes 442376 | tf_op jit(solution)/shard_map/ppermute | solution.py:516
  154.3 13.6 %all-to-all-start = ((bf16[16,32,128]{2,1,0:T(8,128)(2,1)}), bf16[16,32,128]{2,1,0:T(8,128)(2,1)S(1)}, u32[]{:S(2)}, u32[]{:S(2)}) async-start(bf16[16,32,128]{2,1,0:T(8,128)(2,1)} %shard_map.89), calls=%async_computation | async-start | bytes 262144 | tf_op jit(solution)/shard_map/all_to_all | solution.py:520

commit v14 on v13

--- a/solution.py
+++ b/solution.py
@@ -12,6 +12,7 @@
 TILES = 4
 SLOTS = 2
 ROWS = 2 * BLOCK
+DEVICE = 40
 FAR = 64
 KEY_BLOCKS = 32
 ACC_ROWS = 72
@@ -82,7 +83,8 @@
         count = jnp.sum(ones[n * KEY_BLOCKS : (n + 1) * KEY_BLOCKS], axis=0, keepdims=True)
         slots = jnp.maximum(lax.shift_right_logical(count + (TILES - 1), 2), 1)
         tables += [codes, jnp.broadcast_to(slots, (FAR - KEY_BLOCKS, BLOCK))]
-    code_ref[...] = jnp.concatenate(tables, 0).T[: code_ref.shape[0]]
+    table = jnp.concatenate(tables, 0).T[: code_ref.shape[0]]
+    code_ref[...] = jnp.where(lax.broadcasted_iota(jnp.int32, table.shape, 1) == DEVICE, me, table)
 
 
 def front_kernel(seq_ref, lat_hbm, x_hbm, wq_hbm, wk_hbm, wv_hbm, pos_hbm, mask_hbm, *rest):
@@ -184,7 +186,7 @@
         squares = jnp.sum(k * k, axis=0, keepdims=True)
         most = squares if most is None else jnp.maximum(most, squares)
     vt_ref[HS:, :] = jnp.ones((ACC_ROWS - HS, KEY_BLOCKS * BLOCK), jnp.bfloat16)
-    norm_ref[0] = jnp.max(most)
+    norm_ref[...] = most
 
 
 def prepare(*sources):
@@ -192,28 +194,25 @@
     return pl.pallas_call(
         prepare_kernel,
         in_specs=[VMEM] * len(sources),
-        out_specs=[VMEM, VMEM, SMEM],
+        out_specs=[VMEM] * 3,
         out_shape=[
             jax.ShapeDtypeStruct((keys, 2 * HS), jnp.bfloat16),
             jax.ShapeDtypeStruct((ACC_ROWS, keys), jnp.bfloat16),
-            jax.ShapeDtypeStruct((1,), jnp.float32),
+            jax.ShapeDtypeStruct((1, BLOCK), jnp.float32),
         ],
         compiler_params=pltpu.CompilerParams(vmem_limit_bytes=24 * 2**20),
     )(*sources)
 
 
-def attention_kernel(steps, far, seq_ref, code_ref, norm_ref, pos_ref, kv_ref, vt_ref, *rest):
+def attention_kernel(steps, far, code_any, norm_ref, pos_ref, kv_ref, vt_ref, *rest):
     chips = len(steps)
     q_refs, rest = rest[:chips], rest[chips:]
     before_refs, rest = (rest[:chips], rest[chips:]) if far else (None, rest)
-    o_refs, (q_all, p_a, p_b, s_all, acc) = rest[:chips], rest[chips:]
+    o_refs, (q_all, p_a, p_b, s_all, acc, code_ref, sem) = rest[:chips], rest[chips:]
     table = FAR if far else 0
+    got_codes = pltpu.make_async_copy(code_any, code_ref, sem)
+    got_codes.start()
     blocks = 4 * chips
-    me = seq_ref[0]
-    keys_of = jnp.bitwise_xor(me, 2) if far else me
-    own_base = keys_of * (KEY_BLOCKS // 2 * BLOCK)
-    partner_base = jnp.bitwise_xor(keys_of, 1) * (KEY_BLOCKS // 2 * BLOCK)
-    sources = [came_from(me, step) for step in steps]
     iota = lax.broadcasted_iota(jnp.int32, (BLOCK, ROWS), 0)
     in_first = lax.broadcasted_iota(jnp.int32, (1, ROWS), 1) < BLOCK
     iota_half = iota.astype(jnp.float32).astype(jnp.bfloat16)
@@ -226,7 +225,13 @@
             q = q.astype(jnp.float32)
             squares = jnp.sum(q * q, axis=0, keepdims=True)
             most = squares if most is None else jnp.maximum(most, squares)
-    safe = jnp.max(most) * norm_ref[0] <= SAFE_SCORE * SAFE_SCORE
+    safe = jnp.max(most) * jnp.max(norm_ref[...]) <= SAFE_SCORE * SAFE_SCORE
+    got_codes.wait()
+    me = code_ref[0, DEVICE]
+    keys_of = jnp.bitwise_xor(me, 2) if far else me
+    own_base = keys_of * (KEY_BLOCKS // 2 * BLOCK)
+    partner_base = jnp.bitwise_xor(keys_of, 1) * (KEY_BLOCKS // 2 * BLOCK)
+    sources = [came_from(me, step) for step in steps]
 
     def clamp(r):
         return jnp.minimum(r, blocks - 1)
@@ -373,13 +378,13 @@
             lax.fori_loop(0, 4, one_block, 0)
 
 
-def attend(steps, seq, codes, spots, held, queries, before=()):
+def attend(steps, codes, spots, held, queries, before=()):
     kv, vt, norm = held
     chips = len(steps)
     out = jax.ShapeDtypeStruct((2, ACC_ROWS, queries[0].shape[2]), jnp.bfloat16)
     return pl.pallas_call(
         functools.partial(attention_kernel, steps, bool(before)),
-        in_specs=[SMEM] * 3 + [VMEM] * (3 + len(queries) + len(before)),
+        in_specs=[pl.BlockSpec(memory_space=pl.ANY)] + [VMEM] * (4 + len(queries) + len(before)),
         out_specs=[VMEM] * chips,
         out_shape=[out] * chips,
         scratch_shapes=[
@@ -388,12 +393,14 @@
             pltpu.VMEM((SLOTS * TILES * BLOCK, ROWS), jnp.bfloat16),
             pltpu.VMEM((TILES * BLOCK, ROWS), jnp.float32),
             pltpu.VMEM((4 * chips + 1, ACC_ROWS, ROWS), jnp.float32),
+            pltpu.SMEM(codes.shape, jnp.int32),
+            pltpu.SemaphoreType.DMA,
         ],
         compiler_params=pltpu.CompilerParams(vmem_limit_bytes=32 * 2**20),
         cost_estimate=pl.CostEstimate(
             flops=chips * 6 * 10**9, bytes_accessed=4 * 2**20, transcendentals=chips * 2**20
         ),
-    )(seq, codes, norm, spots, kv, vt, *queries, *before)
+    )(codes, norm, spots, kv, vt, *queries, *before)
 
 
 def combine_kernel(core_ref, *refs):
@@ -478,7 +485,7 @@
     q_chip, theirs, kv_own, kv_other, codes = front(
         seq, latents, inputs, w_query, w_key, w_value, positions, block_mask
     )
-    theirs, kv_other, kv_own, w_other = lax.optimization_barrier((theirs, kv_other, kv_own, w_other))
+    kv_other, kv_own, w_other = lax.optimization_barrier((kv_other, kv_own, w_other))
     q_chip = q_chip.at[1].set(lax.ppermute(theirs, "seq", CORE_SWAP))
     queries = {by: q_chip if by == 0 else lax.ppermute(q_chip, "seq", along_x(by)) for by in (0, 1, 3, 2)}
     kv_partner = lax.ppermute(kv_other, "seq", CORE_SWAP)
@@ -486,7 +493,7 @@
     kv_far = [lax.ppermute(kv, "seq", Y_SWAP) for kv in (kv_own, kv_partner)]
 
     spots = positions.reshape(-1, ROWS)
-    near_parts = dict(zip(NEAR_CALLS[0], attend(NEAR_CALLS[0], seq, codes, spots, near, [q_chip])))
+    near_parts = dict(zip(NEAR_CALLS[0], attend(NEAR_CALLS[0], codes, spots, near, [q_chip])))
     w_other, near_parts[0] = lax.optimization_barrier((w_other, near_parts[0]))
     w_pair = jnp.concatenate([w_out, w_other], 0)
     w_turns = [w_pair] + [
@@ -499,7 +506,7 @@
         queries[call[0]], near_parts[last], kv_far[0] = lax.optimization_barrier(
             (queries[call[0]], near_parts[last], kv_far[0])
         )
-        near_parts.update(zip(call, attend(call, seq, codes, spots, near, [queries[by] for by in call])))
+        near_parts.update(zip(call, attend(call, codes, spots, near, [queries[by] for by in call])))
         last = call[-1]
     kv_far, near_parts[last] = lax.optimization_barrier((kv_far, near_parts[last]))
     far = prepare(*kv_far)
@@ -508,7 +515,7 @@
         if last is not None:
             queries[call[0]], parts[last] = lax.optimization_barrier((queries[call[0]], parts[last]))
         done = attend(
-            call, seq, codes, spots, far, [queries[by] for by in call], [near_parts[by] for by in call]
+            call, codes, spots, far, [queries[by] for by in call], [near_parts[by] for by in call]
         )
         parts.update(zip(call, done))
         last = call[-1]

time: 171 us -> 167 us (0.977)
  Pallas kernels: 136 us -> 131 us
    pallas_call x4, Pallas kernels: 127 us -> 123 us  [attend(): pl.pallas_call(functools.partial(attention_kernel, steps, bool(before)),...]
  transfers between devices with their start and end apart: 15 -> 15, of which waited for: 2 -> 3; matrix products, arithmetic and copies ran while one was open for 0% -> 0% of each run, Pallas kernels for 79% -> 78%
where the time goes in v14:
time: 167 us; the launch traced here: 166 us
  Pallas kernels  131 us (78%)
  starting transfers between devices  26.1 us (16%)
  waiting for transfers between devices  8.87 us (5%)
    pallas_call x4, Pallas kernels, attend(): pl.pallas_call(functools.partial(attention_kernel, steps, bool(before)),...  123 us
    all_to_all x1, starting transfers between devices, body(): lax.all_to_all(pieces, ('seq', 'grp'), 0, 0, axis_index_groups=owners)  8.61 us
    all_to_all x1, waiting for transfers between devices, body(): lax.all_to_all(pieces, ('seq', 'grp'), 0, 0, axis_index_groups=owners)  6.34 us
    pallas_call x1, Pallas kernels, front(): pl.pallas_call(front_kernel, in_specs=[SMEM] + [pl.BlockSpec(memory_space...  5.16 us
    ppermute x3, starting transfers between devices, body(): lax.ppermute(w_pair, 'grp', [(g, g ^ k) for g in range(8)])  5.02 us
  transfers between devices with their start and end apart: 15, of which 3 were waited for; matrix products, arithmetic and copies ran while one was open for 0% of the time, Pallas kernels for 78%

profile of v14, /device:TPU:3, one launch (start us, length us, event | category | flops | bytes accessed | tf_op | source)
XLA Modules:
  0.0 166.4 jit_solution(18083606143657085910)
XLA Ops:
  0.0 0.0 copy-start
  0.0 0.0 copy-start.1
  0.0 1.3 collective-permute-start.2
  1.3 5.2 %shard_map.82 = (bf16[2,64,512]{2,1,0:T(8,128)(2,1)S(1)}, bf16[64,512]{1,0:T(8,128)(2,1)S(1)}, bf16[2048,128]{1,0:T(8,128)(2,1)S(1)}, bf16[2048,128]{1,0:T(8,128)(2,1)S(1)}, s32[32,128]{1,0:T(8,128)S(1)}) custom-call(s32[1]{0:T(128)} %bitcast.1.seq_ref, bf16[512,1024]{1,0:T(8,128)(2,1)} %lat_hbm.1, bf16[2048,1024]{1,0:T(8,128)(2,1)} %x_hbm.1, ...), custom_call_target="tpu_custom_call" | custom-call | flops 1207959552 | bytes 6291456 | tf_op jit(solution)/shard_map/pallas_call | solution.py:156
  6.5 0.9 collective-permute-done.2
  7.4 1.5 collective-permute-start.3
  8.9 0.0 collective-permute-start
  8.9 0.0 copy-done.1
  9.0 0.0 copy-done
  9.0 1.6 collective-permute-done
  10.6 0.2 collective-permute-start.1
  10.7 2.0 %collective-permute-start.6 = (bf16[2,64,512]{2,1,0:T(8,128)(2,1)S(1)}, bf16[2,64,512]{2,1,0:T(8,128)(2,1)S(1)}, u32[]{:S(2)}, u32[]{:S(2)}) collective-permute-start(bf16[2,64,512]{2,1,0:T(8,128)(2,1)S(1)} %bitcast_dynamic-update-slice_fusion.rest_0_), channel_id=1, source_target_pairs={{0,96},{8,104},{16,112},{24,120},{32,64},{40,72},{48,80},{56,88},{... | collective-permute-start | bytes 393224 | tf_op jit(solution)/shard_map/ppermute | solution.py:490
  12.7 1.1 collective-permute-start.7
  13.8 2.9 %collective-permute-start.4 = (bf16[2048,128]{1,0:T(8,128)(2,1)S(1)}, bf16[2048,128]{1,0:T(8,128)(2,1)S(1)}, u32[]{:S(2)}, u32[]{:S(2)}) collective-permute-start(bf16[2048,128]{1,0:T(8,128)(2,1)S(1)} %get-tuple-element.61.refs_0_), channel_id=1, source_target_pairs={{0,16},{8,24},{16,0},{24,8},{32,48},{40,56},{48,32},{56,40},{64,80... | collective-permute-start | bytes 1572872 | tf_op jit(solution)/shard_map/ppermute | solution.py:493
  16.7 0.0 collective-permute-done.3.refs_1_
  16.7 0.4 shard_map.83
  17.1 16.5 %shard_map.84.rest_1_ = bf16[2,72,512]{2,1,0:T(8,128)(2,1)S(1)} custom-call(s32[32,128]{1,0:T(8,128)S(1)} %get-tuple-element.55.code_any, f32[1,128]{1,0:T(1,128)S(1)} %get-tuple-element.63.norm_ref, s32[32,256]{1,0:T(8,128)S(1)} %reshape.40.pos_ref, bf16[4096,128]{1,0:T(8,128)(2,1)S(1)} %get-tuple-element.64.kv_ref, ...), custom_call_target="tpu_custom_call" | custom-call | flops 6000000000 | bytes 4194304 | tf_op jit(solution)/shard_map/pallas_call | solution.py:385
  33.7 1.7 %collective-permute-start.11 = (bf16[256,1024]{1,0:T(8,128)(2,1)S(1)}, bf16[256,1024]{1,0:T(8,128)(2,1)S(1)}, u32[]{:S(2)}, u32[]{:S(2)}) collective-permute-start(bf16[256,1024]{1,0:T(8,128)(2,1)S(1)} %constant_dynamic-update-slice_fusion.refs_0_), channel_id=1, source_target_pairs={{0,1},{1,0},{2,3},{3,2},{4,5},{5,4},{6,7},{7,6},{8,9},{9,8},{10,11... | collective-permute-start | bytes 1572872 | tf_op jit(solution)/shard_map/ppermute | solution.py:500
  35.4 0.0 collective-permute-done.1.rest_0_.rest_1_
  35.4 3.3 %collective-permute-start.12 = (bf16[256,1024]{1,0:T(8,128)(2,1)S(1)}, bf16[256,1024]{1,0:T(8,128)(2,1)S(1)}, u32[]{:S(2)}, u32[]{:S(2)}) collective-permute-start(bf16[256,1024]{1,0:T(8,128)(2,1)S(1)} %constant_dynamic-update-slice_fusion.refs_0_), channel_id=1, source_target_pairs={{0,2},{1,3},{2,0},{3,1},{4,6},{5,7},{6,4},{7,5},{8,10},{9,11},{10,... | collective-permute-start | bytes 1572872 | tf_op jit(solution)/shard_map/ppermute | solution.py:500
  38.7 0.0 collective-permute-done.4.refs_0_
  38.7 0.0 collective-permute-start.13
  38.7 0.0 collective-permute-done.6.rest_1_.rest_2_
  38.7 0.1 collective-permute-start.5
  38.8 0.0 collective-permute-done.7.rest_2_.rest_0_
  38.8 45.1 %shard_map.85 = (bf16[2,72,512]{2,1,0:T(8,128)(2,1)S(1)}, bf16[2,72,512]{2,1,0:T(8,128)(2,1)S(1)}, bf16[2,72,512]{2,1,0:T(8,128)(2,1)S(1)}) custom-call(s32[32,128]{1,0:T(8,128)S(1)} %get-tuple-element.55.code_any, f32[1,128]{1,0:T(1,128)S(1)} %get-tuple-element.63.norm_ref, s32[32,256]{1,0:T(8,128)S(1)} %reshape.40.pos_ref, ...), custom_call_target="tpu_custom_call" | custom-call | flops 17999998976 | bytes 4194304 | tf_op jit(solution)/shard_map/pallas_call | solution.py:385
  84.0 0.0 collective-permute-done.5.refs_1_
  84.0 0.4 shard_map.86
  84.4 44.4 %shard_map.87 = (bf16[2,72,512]{2,1,0:T(8,128)(2,1)S(1)}, bf16[2,72,512]{2,1,0:T(8,128)(2,1)S(1)}, bf16[2,72,512]{2,1,0:T(8,128)(2,1)S(1)}) custom-call(s32[32,128]{1,0:T(8,128)S(1)} %get-tuple-element.55.code_any, f32[1,128]{1,0:T(1,128)S(1)} %get-tuple-element.72.norm_ref, s32[32,256]{1,0:T(8,128)S(1)} %reshape.40.pos_ref, ...), custom_call_target="tpu_custom_call" | custom-call | flops 17999998976 | bytes 4194304 | tf_op jit(solution)/shard_map/pallas_call | solution.py:385
  128.8 1.4 collective-permute-start.10
  130.2 1.1 collective-permute-start.8
  131.3 0.0 collective-permute-done.11.refs_1_
  131.3 0.8 collective-permute-start.9
  132.2 17.1 %shard_map.88.refs_3_ = bf16[2,72,512]{2,1,0:T(8,128)(2,1)S(1)} custom-call(s32[32,128]{1,0:T(8,128)S(1)} %get-tuple-element.55.code_any, f32[1,128]{1,0:T(1,128)S(1)} %get-tuple-element.72.norm_ref, s32[32,256]{1,0:T(8,128)S(1)} %reshape.40.pos_ref, bf16[4096,128]{1,0:T(8,128)(2,1)S(1)} %get-tuple-element.73.kv_ref, ...), custom_call_target="tpu_custom_call" | custom-call | flops 6000000000 | bytes 4194304 | tf_op jit(solution)/shard_map/pallas_call | solution.py:385
  149.2 0.0 collective-permute-done.12.refs_2_
  149.3 0.0 collective-permute-done.13.refs_3_
  149.3 0.0 collective-permute-done.10.refs_2_
  149.3 0.0 collective-permute-done.8.refs_0_
  149.3 0.0 collective-permute-done.9.refs_1_
  149.3 1.0 shard_map.89
  150.3 8.6 %all-to-all-start = ((bf16[16,32,128]{2,1,0:T(8,128)(2,1)}), bf16[16,32,128]{2,1,0:T(8,128)(2,1)S(1)}, u32[]{:S(2)}, u32[]{:S(2)}) async-start(bf16[16,32,128]{2,1,0:T(8,128)(2,1)} %shard_map.89), calls=%async_computation | async-start | bytes 262144 | tf_op jit(solution)/shard_map/all_to_all | solution.py:527
  158.9 6.3 %all-to-all-done.pieces_ref = bf16[16,32,128]{2,1,0:T(8,128)(2,1)S(1)} async-done(((bf16[16,32,128]{2,1,0:T(8,128)(2,1)}), bf16[16,32,128]{2,1,0:T(8,128)(2,1)S(1)}, u32[]{:S(2)}, u32[]{:S(2)}) %all-to-all-start) | async-done | bytes 131104 | tf_op jit(solution)/shard_map/all_to_all | solution.py:527
  165.2 1.2 shard_map.90
  (4 shorter events, 0.1 us)
Async XLA Ops:
  0.0 9.0 %copy-start = (bf16[128,1024]{1,0:T(8,128)(2,1)S(1)}, bf16[128,1024]{1,0:T(8,128)(2,1)}, u32[]{:S(2)}) copy-start(bf16[128,1024]{1,0:T(8,128)(2,1)} %param.15) | copy-start | bytes 786436
  0.0 8.9 %copy-start.1 = (s32[8192]{0:T(1024)S(1)}, s32[8192]{0:T(1024)}, u32[]{:S(2)}) copy-start(s32[8192]{0:T(1024)} %param.16) | copy-start | bytes 98308
  0.0 7.4 %collective-permute-start.2 = (bf16[128,1024]{1,0:T(8,128)(2,1)}, bf16[128,1024]{1,0:T(8,128)(2,1)S(1)}, u32[]{:S(2)}, u32[]{:S(2)}) collective-permute-start(bf16[128,1024]{1,0:T(8,128)(2,1)} %param.15), channel_id=1, source_target_pairs={{0,4},{1,5},{2,6},{3,7},{4,0},{5,1},{6,2},{7,3},{8,12},{9,13},{10,... | collective-permute-start | bytes 786440 | tf_op jit(solution)/shard_map/ppermute | solution.py:484
  7.4 9.4 %collective-permute-start.3 = (bf16[2048,128]{1,0:T(8,128)(2,1)S(1)}, bf16[2048,128]{1,0:T(8,128)(2,1)S(1)}, u32[]{:S(2)}, u32[]{:S(2)}) collective-permute-start(bf16[2048,128]{1,0:T(8,128)(2,1)S(1)} %get-tuple-element.62), channel_id=1, source_target_pairs={{0,8},{8,0},{16,24},{24,16},{32,40},{40,32},{48,56},{56,48},{64,72... | collective-permute-start | bytes 1572872 | tf_op jit(solution)/shard_map/ppermute | solution.py:491
  8.9 1.6 collective-permute-start
  10.6 24.8 %collective-permute-start.1 = (bf16[2,64,512]{2,1,0:T(8,128)(2,1)S(1)}, bf16[2,64,512]{2,1,0:T(8,128)(2,1)S(1)}, u32[]{:S(2)}, u32[]{:S(2)}) collective-permute-start(bf16[2,64,512]{2,1,0:T(8,128)(2,1)S(1)} %bitcast_dynamic-update-slice_fusion.rest_0_), channel_id=1, source_target_pairs={{0,32},{8,40},{16,48},{24,56},{32,0},{40,8},{48,16},{56,24},{64,96... | collective-permute-start | bytes 393224 | tf_op jit(solution)/shard_map/ppermute | solution.py:490
  10.7 28.0 %collective-permute-start.6 = (bf16[2,64,512]{2,1,0:T(8,128)(2,1)S(1)}, bf16[2,64,512]{2,1,0:T(8,128)(2,1)S(1)}, u32[]{:S(2)}, u32[]{:S(2)}) collective-permute-start(bf16[2,64,512]{2,1,0:T(8,128)(2,1)S(1)} %bitcast_dynamic-update-slice_fusion.rest_0_), channel_id=1, source_target_pairs={{0,96},{8,104},{16,112},{24,120},{32,64},{40,72},{48,80},{56,88},{... | collective-permute-start | bytes 393224 | tf_op jit(solution)/shard_map/ppermute | solution.py:490
  12.7 26.1 %collective-permute-start.7 = (bf16[2,64,512]{2,1,0:T(8,128)(2,1)S(1)}, bf16[2,64,512]{2,1,0:T(8,128)(2,1)S(1)}, u32[]{:S(2)}, u32[]{:S(2)}) collective-permute-start(bf16[2,64,512]{2,1,0:T(8,128)(2,1)S(1)} %bitcast_dynamic-update-slice_fusion.rest_0_), channel_id=1, source_target_pairs={{0,64},{8,72},{16,80},{24,88},{32,96},{40,104},{48,112},{56,120},{... | collective-permute-start | bytes 393224 | tf_op jit(solution)/shard_map/ppermute | solution.py:490
  13.8 24.8 %collective-permute-start.4 = (bf16[2048,128]{1,0:T(8,128)(2,1)S(1)}, bf16[2048,128]{1,0:T(8,128)(2,1)S(1)}, u32[]{:S(2)}, u32[]{:S(2)}) collective-permute-start(bf16[2048,128]{1,0:T(8,128)(2,1)S(1)} %get-tuple-element.61.refs_0_), channel_id=1, source_target_pairs={{0,16},{8,24},{16,0},{24,8},{32,48},{40,56},{48,32},{56,40},{64,80... | collective-permute-start | bytes 1572872 | tf_op jit(solution)/shard_map/ppermute | solution.py:493
  33.7 97.7 %collective-permute-start.11 = (bf16[256,1024]{1,0:T(8,128)(2,1)S(1)}, bf16[256,1024]{1,0:T(8,128)(2,1)S(1)}, u32[]{:S(2)}, u32[]{:S(2)}) collective-permute-start(bf16[256,1024]{1,0:T(8,128)(2,1)S(1)} %constant_dynamic-update-slice_fusion.refs_0_), channel_id=1, source_target_pairs={{0,1},{1,0},{2,3},{3,2},{4,5},{5,4},{6,7},{7,6},{8,9},{9,8},{10,11... | collective-permute-start | bytes 1572872 | tf_op jit(solution)/shard_map/ppermute | solution.py:500
  35.4 113.9 %collective-permute-start.12 = (bf16[256,1024]{1,0:T(8,128)(2,1)S(1)}, bf16[256,1024]{1,0:T(8,128)(2,1)S(1)}, u32[]{:S(2)}, u32[]{:S(2)}) collective-permute-start(bf16[256,1024]{1,0:T(8,128)(2,1)S(1)} %constant_dynamic-update-slice_fusion.refs_0_), channel_id=1, source_target_pairs={{0,2},{1,3},{2,0},{3,1},{4,6},{5,7},{6,4},{7,5},{8,10},{9,11},{10,... | collective-permute-start | bytes 1572872 | tf_op jit(solution)/shard_map/ppermute | solution.py:500
  38.7 110.6 %collective-permute-start.13 = (bf16[256,1024]{1,0:T(8,128)(2,1)S(1)}, bf16[256,1024]{1,0:T(8,128)(2,1)S(1)}, u32[]{:S(2)}, u32[]{:S(2)}) collective-permute-start(bf16[256,1024]{1,0:T(8,128)(2,1)S(1)} %constant_dynamic-update-slice_fusion.refs_0_), channel_id=1, source_target_pairs={{0,3},{1,2},{2,1},{3,0},{4,7},{5,6},{6,5},{7,4},{8,11},{9,10},{10,... | collective-permute-start | bytes 1572872 | tf_op jit(solution)/shard_map/ppermute | solution.py:500
  38.7 45.3 %collective-permute-start.5 = (bf16[2048,128]{1,0:T(8,128)(2,1)S(1)}, bf16[2048,128]{1,0:T(8,128)(2,1)S(1)}, u32[]{:S(2)}, u32[]{:S(2)}) collective-permute-start(bf16[2048,128]{1,0:T(8,128)(2,1)S(1)} %collective-permute-done.3.refs_1_), channel_id=1, source_target_pairs={{0,16},{8,24},{16,0},{24,8},{32,48},{40,56},{48,32},{56,40},{64,80... | collective-permute-start | bytes 1572872 | tf_op jit(solution)/shard_map/ppermute | solution.py:493
  128.8 20.4 %collective-permute-start.10 = (bf16[2,72,512]{2,1,0:T(8,128)(2,1)S(1)}, bf16[2,72,512]{2,1,0:T(8,128)(2,1)S(1)}, u32[]{:S(2)}, u32[]{:S(2)}) collective-permute-start(bf16[2,72,512]{2,1,0:T(8,128)(2,1)S(1)} %get-tuple-element.81), channel_id=1, source_target_pairs={{0,96},{8,104},{16,112},{24,120},{32,64},{40,72},{48,80},{56,88},{... | collective-permute-start | bytes 442376 | tf_op jit(solution)/shard_map/ppermute | solution.py:523
  130.2 19.1 %collective-permute-start.8 = (bf16[2,72,512]{2,1,0:T(8,128)(2,1)S(1)}, bf16[2,72,512]{2,1,0:T(8,128)(2,1)S(1)}, u32[]{:S(2)}, u32[]{:S(2)}) collective-permute-start(bf16[2,72,512]{2,1,0:T(8,128)(2,1)S(1)} %get-tuple-element.78), channel_id=1, source_target_pairs={{0,64},{8,72},{16,80},{24,88},{32,96},{40,104},{48,112},{56,120},{... | collective-permute-start | bytes 442376 | tf_op jit(solution)/shard_map/ppermute | solution.py:523
  131.3 18.0 %collective-permute-start.9 = (bf16[2,72,512]{2,1,0:T(8,128)(2,1)S(1)}, bf16[2,72,512]{2,1,0:T(8,128)(2,1)S(1)}, u32[]{:S(2)}, u32[]{:S(2)}) collective-permute-start(bf16[2,72,512]{2,1,0:T(8,128)(2,1)S(1)} %get-tuple-element.79), channel_id=1, source_target_pairs={{0,32},{8,40},{16,48},{24,56},{32,0},{40,8},{48,16},{56,24},{64,96... | collective-permute-start | bytes 442376 | tf_op jit(solution)/shard_map/ppermute | solution.py:523
  150.3 15.0 %all-to-all-start = ((bf16[16,32,128]{2,1,0:T(8,128)(2,1)}), bf16[16,32,128]{2,1,0:T(8,128)(2,1)S(1)}, u32[]{:S(2)}, u32[]{:S(2)}) async-start(bf16[16,32,128]{2,1,0:T(8,128)(2,1)} %shard_map.89), calls=%async_computation | async-start | bytes 262144 | tf_op jit(solution)/shard_map/all_to_all | solution.py:527

commit v15 on v14

--- a/solution.py
+++ b/solution.py
@@ -485,7 +485,7 @@
     q_chip, theirs, kv_own, kv_other, codes = front(
         seq, latents, inputs, w_query, w_key, w_value, positions, block_mask
     )
-    kv_other, kv_own, w_other = lax.optimization_barrier((kv_other, kv_own, w_other))
+    theirs, kv_other, kv_own, w_other = lax.optimization_barrier((theirs, kv_other, kv_own, w_other))
     q_chip = q_chip.at[1].set(lax.ppermute(theirs, "seq", CORE_SWAP))
     queries = {by: q_chip if by == 0 else lax.ppermute(q_chip, "seq", along_x(by)) for by in (0, 1, 3, 2)}
     kv_partner = lax.ppermute(kv_other, "seq", CORE_SWAP)

time: 167 us -> 167 us (level); the launches traced: 166 us -> 165 us
  transfers between devices with their start and end apart: 15 -> 15, of which waited for: 3 -> 2; matrix products, arithmetic and copies ran while one was open for 0% -> 0% of each run, Pallas kernels for 78% -> 77%
where the time goes in v15:
time: 167 us; the launch traced here: 165 us
  Pallas kernels  130 us (78%)
  starting transfers between devices  27.5 us (16%)
  waiting for transfers between devices  7.29 us (4%)
    pallas_call x4, Pallas kernels, attend(): pl.pallas_call(functools.partial(attention_kernel, steps, bool(before)),...  122 us
    all_to_all x1, starting transfers between devices, body(): lax.all_to_all(pieces, ('seq', 'grp'), 0, 0, axis_index_groups=owners)  7.21 us
    all_to_all x1, waiting for transfers between devices, body(): lax.all_to_all(pieces, ('seq', 'grp'), 0, 0, axis_index_groups=owners)  6.34 us
    pallas_call x1, Pallas kernels, front(): pl.pallas_call(front_kernel, in_specs=[SMEM] + [pl.BlockSpec(memory_space...  5.16 us
    ppermute x3, starting transfers between devices, body(): lax.ppermute(w_pair, 'grp', [(g, g ^ k) for g in range(8)])  5.02 us
    ppermute x3, starting transfers between devices, body(): lax.ppermute(part, 'seq', along_x(by))  4.59 us
    ppermute x2, starting transfers between devices, body(): kv_far = [lax.ppermute(kv, 'seq', Y_SWAP) for kv in (kv_own, kv_partner)]  4.39 us
  transfers between devices with their start and end apart: 15, of which 2 were waited for; matrix products, arithmetic and copies ran while one was open for 0% of the time, Pallas kernels for 77%

profile of v15, /device:TPU:3, one launch (start us, length us, event | category | flops | bytes accessed | tf_op | source)
XLA Modules:
  0.0 164.7 jit_solution(1781382373904360907)
XLA Ops:
  0.0 0.0 copy-start
  0.0 0.0 copy-start.1
  0.0 1.3 collective-permute-start
  1.3 5.2 %shard_map.82 = (bf16[2,64,512]{2,1,0:T(8,128)(2,1)S(1)}, bf16[64,512]{1,0:T(8,128)(2,1)S(1)}, bf16[2048,128]{1,0:T(8,128)(2,1)S(1)}, bf16[2048,128]{1,0:T(8,128)(2,1)S(1)}, s32[32,128]{1,0:T(8,128)S(1)}) custom-call(s32[1]{0:T(128)} %bitcast.1.seq_ref, bf16[512,1024]{1,0:T(8,128)(2,1)} %lat_hbm.1, bf16[2048,1024]{1,0:T(8,128)(2,1)} %x_hbm.1, ...), custom_call_target="tpu_custom_call" | custom-call | flops 1207959552 | bytes 6291456 | tf_op jit(solution)/shard_map/pallas_call | solution.py:156
  6.5 0.9 collective-permute-done
  7.4 1.5 collective-permute-start.3
  8.9 0.0 copy-done.1
  9.0 0.1 collective-permute-start.1
  9.0 0.0 copy-done
  9.1 3.0 %collective-permute-start.4 = (bf16[2048,128]{1,0:T(8,128)(2,1)S(1)}, bf16[2048,128]{1,0:T(8,128)(2,1)S(1)}, u32[]{:S(2)}, u32[]{:S(2)}) collective-permute-start(bf16[2048,128]{1,0:T(8,128)(2,1)S(1)} %get-tuple-element.63.refs_0_), channel_id=1, source_target_pairs={{0,16},{8,24},{16,0},{24,8},{32,48},{40,56},{48,32},{56,40},{64,80... | collective-permute-start | bytes 1572872 | tf_op jit(solution)/shard_map/ppermute | solution.py:493
  12.1 0.0 collective-permute-done.1
  12.1 0.3 collective-permute-start.2
  12.4 1.9 %collective-permute-start.6 = (bf16[2,64,512]{2,1,0:T(8,128)(2,1)S(1)}, bf16[2,64,512]{2,1,0:T(8,128)(2,1)S(1)}, u32[]{:S(2)}, u32[]{:S(2)}) collective-permute-start(bf16[2,64,512]{2,1,0:T(8,128)(2,1)S(1)} %bitcast_dynamic-update-slice_fusion.rest_0_), channel_id=1, source_target_pairs={{0,96},{8,104},{16,112},{24,120},{32,64},{40,72},{48,80},{56,88},{... | collective-permute-start | bytes 393224 | tf_op jit(solution)/shard_map/ppermute | solution.py:490
  14.3 1.1 collective-permute-start.7
  15.4 0.0 collective-permute-done.3.refs_1_
  15.4 0.4 shard_map.83
  15.8 16.5 %shard_map.84.rest_1_ = bf16[2,72,512]{2,1,0:T(8,128)(2,1)S(1)} custom-call(s32[32,128]{1,0:T(8,128)S(1)} %get-tuple-element.56.code_any, f32[1,128]{1,0:T(1,128)S(1)} %get-tuple-element.65.norm_ref, s32[32,256]{1,0:T(8,128)S(1)} %reshape.40.pos_ref, bf16[4096,128]{1,0:T(8,128)(2,1)S(1)} %get-tuple-element.66.kv_ref, ...), custom_call_target="tpu_custom_call" | custom-call | flops 6000000000 | bytes 4194304 | tf_op jit(solution)/shard_map/pallas_call | solution.py:385
  32.3 1.7 %collective-permute-start.11 = (bf16[256,1024]{1,0:T(8,128)(2,1)S(1)}, bf16[256,1024]{1,0:T(8,128)(2,1)S(1)}, u32[]{:S(2)}, u32[]{:S(2)}) collective-permute-start(bf16[256,1024]{1,0:T(8,128)(2,1)S(1)} %constant_dynamic-update-slice_fusion.refs_0_), channel_id=1, source_target_pairs={{0,1},{1,0},{2,3},{3,2},{4,5},{5,4},{6,7},{7,6},{8,9},{9,8},{10,11... | collective-permute-start | bytes 1572872 | tf_op jit(solution)/shard_map/ppermute | solution.py:500
  34.0 0.0 collective-permute-done.2.rest_0_.rest_1_
  34.0 3.3 %collective-permute-start.12 = (bf16[256,1024]{1,0:T(8,128)(2,1)S(1)}, bf16[256,1024]{1,0:T(8,128)(2,1)S(1)}, u32[]{:S(2)}, u32[]{:S(2)}) collective-permute-start(bf16[256,1024]{1,0:T(8,128)(2,1)S(1)} %constant_dynamic-update-slice_fusion.refs_0_), channel_id=1, source_target_pairs={{0,2},{1,3},{2,0},{3,1},{4,6},{5,7},{6,4},{7,5},{8,10},{9,11},{10,... | collective-permute-start | bytes 1572872 | tf_op jit(solution)/shard_map/ppermute | solution.py:500
  37.4 0.0 collective-permute-done.4.refs_0_
  37.4 0.0 collective-permute-start.13
  37.4 0.0 collective-permute-done.6.rest_1_.rest_2_
  37.4 1.4 collective-permute-start.5
  38.8 0.0 collective-permute-done.7.rest_2_.rest_0_
  38.8 44.2 %shard_map.85 = (bf16[2,72,512]{2,1,0:T(8,128)(2,1)S(1)}, bf16[2,72,512]{2,1,0:T(8,128)(2,1)S(1)}, bf16[2,72,512]{2,1,0:T(8,128)(2,1)S(1)}) custom-call(s32[32,128]{1,0:T(8,128)S(1)} %get-tuple-element.56.code_any, f32[1,128]{1,0:T(1,128)S(1)} %get-tuple-element.65.norm_ref, s32[32,256]{1,0:T(8,128)S(1)} %reshape.40.pos_ref, ...), custom_call_target="tpu_custom_call" | custom-call | flops 17999998976 | bytes 4194304 | tf_op jit(solution)/shard_map/pallas_call | solution.py:385
  83.0 0.0 collective-permute-done.5.refs_1_
  83.0 0.4 shard_map.86
  83.4 45.4 %shard_map.87 = (bf16[2,72,512]{2,1,0:T(8,128)(2,1)S(1)}, bf16[2,72,512]{2,1,0:T(8,128)(2,1)S(1)}, bf16[2,72,512]{2,1,0:T(8,128)(2,1)S(1)}) custom-call(s32[32,128]{1,0:T(8,128)S(1)} %get-tuple-element.56.code_any, f32[1,128]{1,0:T(1,128)S(1)} %get-tuple-element.74.norm_ref, s32[32,256]{1,0:T(8,128)S(1)} %reshape.40.pos_ref, ...), custom_call_target="tpu_custom_call" | custom-call | flops 17999998976 | bytes 4194304 | tf_op jit(solution)/shard_map/pallas_call | solution.py:385
  128.8 2.7 %collective-permute-start.10 = (bf16[2,72,512]{2,1,0:T(8,128)(2,1)S(1)}, bf16[2,72,512]{2,1,0:T(8,128)(2,1)S(1)}, u32[]{:S(2)}, u32[]{:S(2)}) collective-permute-start(bf16[2,72,512]{2,1,0:T(8,128)(2,1)S(1)} %get-tuple-element.83), channel_id=1, source_target_pairs={{0,96},{8,104},{16,112},{24,120},{32,64},{40,72},{48,80},{56,88},{... | collective-permute-start | bytes 442376 | tf_op jit(solution)/shard_map/ppermute | solution.py:523
  131.5 0.7 collective-permute-start.8
  132.2 0.0 collective-permute-done.11.refs_1_
  132.2 1.2 collective-permute-start.9
  133.4 15.5 %shard_map.88.refs_3_ = bf16[2,72,512]{2,1,0:T(8,128)(2,1)S(1)} custom-call(s32[32,128]{1,0:T(8,128)S(1)} %get-tuple-element.56.code_any, f32[1,128]{1,0:T(1,128)S(1)} %get-tuple-element.74.norm_ref, s32[32,256]{1,0:T(8,128)S(1)} %reshape.40.pos_ref, bf16[4096,128]{1,0:T(8,128)(2,1)S(1)} %get-tuple-element.75.kv_ref, ...), custom_call_target="tpu_custom_call" | custom-call | flops 6000000000 | bytes 4194304 | tf_op jit(solution)/shard_map/pallas_call | solution.py:385
  148.9 0.0 collective-permute-done.12.refs_2_
  148.9 0.0 collective-permute-done.13.refs_3_
  149.0 0.0 collective-permute-done.10.refs_2_
  149.0 0.0 collective-permute-done.8.refs_0_
  149.0 0.0 collective-permute-done.9.refs_1_
  149.0 1.0 shard_map.89
  150.0 7.2 %all-to-all-start = ((bf16[16,32,128]{2,1,0:T(8,128)(2,1)}), bf16[16,32,128]{2,1,0:T(8,128)(2,1)S(1)}, u32[]{:S(2)}, u32[]{:S(2)}) async-start(bf16[16,32,128]{2,1,0:T(8,128)(2,1)} %shard_map.89), calls=%async_computation | async-start | bytes 262144 | tf_op jit(solution)/shard_map/all_to_all | solution.py:527
  157.2 6.3 %all-to-all-done.pieces_ref = bf16[16,32,128]{2,1,0:T(8,128)(2,1)S(1)} async-done(((bf16[16,32,128]{2,1,0:T(8,128)(2,1)}), bf16[16,32,128]{2,1,0:T(8,128)(2,1)S(1)}, u32[]{:S(2)}, u32[]{:S(2)}) %all-to-all-start) | async-done | bytes 131104 | tf_op jit(solution)/shard_map/all_to_all | solution.py:527
  163.5 1.2 shard_map.90
  (4 shorter events, 0.1 us)
Async XLA Ops:
  0.0 9.0 %copy-start = (bf16[128,1024]{1,0:T(8,128)(2,1)S(1)}, bf16[128,1024]{1,0:T(8,128)(2,1)}, u32[]{:S(2)}) copy-start(bf16[128,1024]{1,0:T(8,128)(2,1)} %param.15) | copy-start | bytes 786436
  0.0 8.9 %copy-start.1 = (s32[8192]{0:T(1024)S(1)}, s32[8192]{0:T(1024)}, u32[]{:S(2)}) copy-start(s32[8192]{0:T(1024)} %param.16) | copy-start | bytes 98308
  0.0 7.4 %collective-permute-start = (bf16[128,1024]{1,0:T(8,128)(2,1)}, bf16[128,1024]{1,0:T(8,128)(2,1)S(1)}, u32[]{:S(2)}, u32[]{:S(2)}) collective-permute-start(bf16[128,1024]{1,0:T(8,128)(2,1)} %param.15), channel_id=1, source_target_pairs={{0,4},{1,5},{2,6},{3,7},{4,0},{5,1},{6,2},{7,3},{8,12},{9,13},{10,... | collective-permute-start | bytes 786440 | tf_op jit(solution)/shard_map/ppermute | solution.py:484
  7.4 8.0 %collective-permute-start.3 = (bf16[2048,128]{1,0:T(8,128)(2,1)S(1)}, bf16[2048,128]{1,0:T(8,128)(2,1)S(1)}, u32[]{:S(2)}, u32[]{:S(2)}) collective-permute-start(bf16[2048,128]{1,0:T(8,128)(2,1)S(1)} %get-tuple-element.64), channel_id=1, source_target_pairs={{0,8},{8,0},{16,24},{24,16},{32,40},{40,32},{48,56},{56,48},{64,72... | collective-permute-start | bytes 1572872 | tf_op jit(solution)/shard_map/ppermute | solution.py:491
  9.0 3.1 %collective-permute-start.1 = (bf16[64,512]{1,0:T(8,128)(2,1)S(1)}, bf16[64,512]{1,0:T(8,128)(2,1)S(1)}, u32[]{:S(2)}, u32[]{:S(2)}) collective-permute-start(bf16[64,512]{1,0:T(8,128)(2,1)S(1)} %get-tuple-element.61), channel_id=1, source_target_pairs={{0,8},{8,0},{16,24},{24,16},{32,40},{40,32},{48,56},{56,48},{64,72... | collective-permute-start | bytes 196616 | tf_op jit(solution)/shard_map/ppermute | solution.py:489
  9.1 28.3 %collective-permute-start.4 = (bf16[2048,128]{1,0:T(8,128)(2,1)S(1)}, bf16[2048,128]{1,0:T(8,128)(2,1)S(1)}, u32[]{:S(2)}, u32[]{:S(2)}) collective-permute-start(bf16[2048,128]{1,0:T(8,128)(2,1)S(1)} %get-tuple-element.63.refs_0_), channel_id=1, source_target_pairs={{0,16},{8,24},{16,0},{24,8},{32,48},{40,56},{48,32},{56,40},{64,80... | collective-permute-start | bytes 1572872 | tf_op jit(solution)/shard_map/ppermute | solution.py:493
  12.1 22.0 %collective-permute-start.2 = (bf16[2,64,512]{2,1,0:T(8,128)(2,1)S(1)}, bf16[2,64,512]{2,1,0:T(8,128)(2,1)S(1)}, u32[]{:S(2)}, u32[]{:S(2)}) collective-permute-start(bf16[2,64,512]{2,1,0:T(8,128)(2,1)S(1)} %bitcast_dynamic-update-slice_fusion.rest_0_), channel_id=1, source_target_pairs={{0,32},{8,40},{16,48},{24,56},{32,0},{40,8},{48,16},{56,24},{64,96... | collective-permute-start | bytes 393224 | tf_op jit(solution)/shard_map/ppermute | solution.py:490
  12.4 24.9 %collective-permute-start.6 = (bf16[2,64,512]{2,1,0:T(8,128)(2,1)S(1)}, bf16[2,64,512]{2,1,0:T(8,128)(2,1)S(1)}, u32[]{:S(2)}, u32[]{:S(2)}) collective-permute-start(bf16[2,64,512]{2,1,0:T(8,128)(2,1)S(1)} %bitcast_dynamic-update-slice_fusion.rest_0_), channel_id=1, source_target_pairs={{0,96},{8,104},{16,112},{24,120},{32,64},{40,72},{48,80},{56,88},{... | collective-permute-start | bytes 393224 | tf_op jit(solution)/shard_map/ppermute | solution.py:490
  14.3 24.5 %collective-permute-start.7 = (bf16[2,64,512]{2,1,0:T(8,128)(2,1)S(1)}, bf16[2,64,512]{2,1,0:T(8,128)(2,1)S(1)}, u32[]{:S(2)}, u32[]{:S(2)}) collective-permute-start(bf16[2,64,512]{2,1,0:T(8,128)(2,1)S(1)} %bitcast_dynamic-update-slice_fusion.rest_0_), channel_id=1, source_target_pairs={{0,64},{8,72},{16,80},{24,88},{32,96},{40,104},{48,112},{56,120},{... | collective-permute-start | bytes 393224 | tf_op jit(solution)/shard_map/ppermute | solution.py:490
  32.3 99.9 %collective-permute-start.11 = (bf16[256,1024]{1,0:T(8,128)(2,1)S(1)}, bf16[256,1024]{1,0:T(8,128)(2,1)S(1)}, u32[]{:S(2)}, u32[]{:S(2)}) collective-permute-start(bf16[256,1024]{1,0:T(8,128)(2,1)S(1)} %constant_dynamic-update-slice_fusion.refs_0_), channel_id=1, source_target_pairs={{0,1},{1,0},{2,3},{3,2},{4,5},{5,4},{6,7},{7,6},{8,9},{9,8},{10,11... | collective-permute-start | bytes 1572872 | tf_op jit(solution)/shard_map/ppermute | solution.py:500
  34.0 114.9 %collective-permute-start.12 = (bf16[256,1024]{1,0:T(8,128)(2,1)S(1)}, bf16[256,1024]{1,0:T(8,128)(2,1)S(1)}, u32[]{:S(2)}, u32[]{:S(2)}) collective-permute-start(bf16[256,1024]{1,0:T(8,128)(2,1)S(1)} %constant_dynamic-update-slice_fusion.refs_0_), channel_id=1, source_target_pairs={{0,2},{1,3},{2,0},{3,1},{4,6},{5,7},{6,4},{7,5},{8,10},{9,11},{10,... | collective-permute-start | bytes 1572872 | tf_op jit(solution)/shard_map/ppermute | solution.py:500
  37.4 111.6 %collective-permute-start.13 = (bf16[256,1024]{1,0:T(8,128)(2,1)S(1)}, bf16[256,1024]{1,0:T(8,128)(2,1)S(1)}, u32[]{:S(2)}, u32[]{:S(2)}) collective-permute-start(bf16[256,1024]{1,0:T(8,128)(2,1)S(1)} %constant_dynamic-update-slice_fusion.refs_0_), channel_id=1, source_target_pairs={{0,3},{1,2},{2,1},{3,0},{4,7},{5,6},{6,5},{7,4},{8,11},{9,10},{10,... | collective-permute-start | bytes 1572872 | tf_op jit(solution)/shard_map/ppermute | solution.py:500
  37.4 45.6 %collective-permute-start.5 = (bf16[2048,128]{1,0:T(8,128)(2,1)S(1)}, bf16[2048,128]{1,0:T(8,128)(2,1)S(1)}, u32[]{:S(2)}, u32[]{:S(2)}) collective-permute-start(bf16[2048,128]{1,0:T(8,128)(2,1)S(1)} %collective-permute-done.3.refs_1_), channel_id=1, source_target_pairs={{0,16},{8,24},{16,0},{24,8},{32,48},{40,56},{48,32},{56,40},{64,80... | collective-permute-start | bytes 1572872 | tf_op jit(solution)/shard_map/ppermute | solution.py:493
  128.8 20.2 %collective-permute-start.10 = (bf16[2,72,512]{2,1,0:T(8,128)(2,1)S(1)}, bf16[2,72,512]{2,1,0:T(8,128)(2,1)S(1)}, u32[]{:S(2)}, u32[]{:S(2)}) collective-permute-start(bf16[2,72,512]{2,1,0:T(8,128)(2,1)S(1)} %get-tuple-element.83), channel_id=1, source_target_pairs={{0,96},{8,104},{16,112},{24,120},{32,64},{40,72},{48,80},{56,88},{... | collective-permute-start | bytes 442376 | tf_op jit(solution)/shard_map/ppermute | solution.py:523
  131.5 17.5 %collective-permute-start.8 = (bf16[2,72,512]{2,1,0:T(8,128)(2,1)S(1)}, bf16[2,72,512]{2,1,0:T(8,128)(2,1)S(1)}, u32[]{:S(2)}, u32[]{:S(2)}) collective-permute-start(bf16[2,72,512]{2,1,0:T(8,128)(2,1)S(1)} %get-tuple-element.80), channel_id=1, source_target_pairs={{0,64},{8,72},{16,80},{24,88},{32,96},{40,104},{48,112},{56,120},{... | collective-permute-start | bytes 442376 | tf_op jit(solution)/shard_map/ppermute | solution.py:523
  132.2 16.8 %collective-permute-start.9 = (bf16[2,72,512]{2,1,0:T(8,128)(2,1)S(1)}, bf16[2,72,512]{2,1,0:T(8,128)(2,1)S(1)}, u32[]{:S(2)}, u32[]{:S(2)}) collective-permute-start(bf16[2,72,512]{2,1,0:T(8,128)(2,1)S(1)} %get-tuple-element.81), channel_id=1, source_target_pairs={{0,32},{8,40},{16,48},{24,56},{32,0},{40,8},{48,16},{56,24},{64,96... | collective-permute-start | bytes 442376 | tf_op jit(solution)/shard_map/ppermute | solution.py:523
  150.0 13.6 %all-to-all-start = ((bf16[16,32,128]{2,1,0:T(8,128)(2,1)}), bf16[16,32,128]{2,1,0:T(8,128)(2,1)S(1)}, u32[]{:S(2)}, u32[]{:S(2)}) async-start(bf16[16,32,128]{2,1,0:T(8,128)(2,1)} %shard_map.89), calls=%async_computation | async-start | bytes 262144 | tf_op jit(solution)/shard_map/all_to_all | solution.py:527

commit v16 on v15

--- a/solution.py
+++ b/solution.py
@@ -20,7 +20,6 @@
 SAFE_SCORE = 60.0
 masked_score = -1e30
 lowest_max = -1e29
-SMEM = pl.BlockSpec(memory_space=pltpu.SMEM)
 VMEM = pl.BlockSpec(memory_space=pltpu.VMEM)
 
 
@@ -87,7 +86,7 @@
     code_ref[...] = jnp.where(lax.broadcasted_iota(jnp.int32, table.shape, 1) == DEVICE, me, table)
 
 
-def front_kernel(seq_ref, lat_hbm, x_hbm, wq_hbm, wk_hbm, wv_hbm, pos_hbm, mask_hbm, *rest):
+def front_kernel(lat_hbm, x_hbm, wq_hbm, wk_hbm, wv_hbm, pos_hbm, mask_hbm, *rest):
     pair_hbm, theirs_hbm, own_hbm, other_hbm, code_hbm = rest[:5]
     lat, x, wq, wk, wv, pos, mask, pair_ref, theirs_ref, own_ref, other_ref, code_ref = rest[5:17]
     w_all, sems, x_sems, out_sems = rest[17:]
@@ -109,11 +108,12 @@
     for copy in small + large:
         copy.start()
     got_pos, got_mask, got_wq, got_lat, got_wk, got_wv = small
-    first = jnp.bitwise_and(seq_ref[0], 1) == 0
+    me = lax.axis_index("seq")
+    first = jnp.bitwise_and(me, 1) == 0
 
     got_pos.wait()
     got_mask.wait()
-    list_work(seq_ref[0], pos, mask, code_ref)
+    list_work(me, pos, mask, code_ref)
     send(code_ref, code_hbm)
 
     got_wq.wait()
@@ -145,7 +145,7 @@
         copy.wait()
 
 
-def front(seq, latents, inputs, w_query, w_key, w_value, positions, block_mask):
+def front(latents, inputs, w_query, w_key, w_value, positions, block_mask):
     rows, width = latents.shape
     keys = inputs.shape[0]
     spots = positions.reshape(-1, BLOCK)
@@ -155,7 +155,7 @@
     results = [jax.ShapeDtypeStruct((2, HS, rows), jnp.bfloat16), q, kv, kv, jax.ShapeDtypeStruct((spots.shape[0] // 2, BLOCK), jnp.int32)]
     return pl.pallas_call(
         front_kernel,
-        in_specs=[SMEM] + [pl.BlockSpec(memory_space=pl.ANY)] * len(operands),
+        in_specs=[pl.BlockSpec(memory_space=pl.ANY)] * len(operands),
         out_specs=[pl.BlockSpec(memory_space=pl.ANY)] * 5,
         out_shape=results,
         scratch_shapes=[pltpu.VMEM(a.shape, a.dtype) for a in (*operands, *results)]
@@ -169,7 +169,7 @@
         cost_estimate=pl.CostEstimate(
             flops=2 * (keys * 4 + rows * 2) * width * HS, bytes_accessed=6 * 2**20, transcendentals=0
         ),
-    )(seq, *in_hbm(*operands))
+    )(*in_hbm(*operands))
 
 
 def prepare_kernel(*refs):
@@ -403,7 +403,8 @@
     )(codes, norm, spots, kv, vt, *queries, *before)
 
 
-def combine_kernel(core_ref, *refs):
+def combine_kernel(*refs):
+    core = jnp.bitwise_and(lax.axis_index("seq"), 1)
     parts, out_ref = refs[:-1], refs[-1]
     groups = out_ref.shape[0] // 2
     half = out_ref.shape[1]
@@ -417,28 +418,28 @@
         )
         summed = sum(p[j, :HS, :].astype(jnp.float32) * scale for p, scale in zip(parts, scales))
         rows = (summed / total).T.astype(jnp.bfloat16)
-        first = jnp.bitwise_xor(core_ref[0], j) * groups
+        first = jnp.bitwise_xor(core, j) * groups
         for g in range(groups):
             upper = rows[2 * g * half : (2 * g + 1) * half]
             lower = rows[(2 * g + 1) * half : (2 * g + 2) * half]
             out_ref[first + g] = jnp.concatenate([upper, lower], 1)
 
 
-def combine(core, parts):
+def combine(parts):
     half = parts[0].shape[2] // 16
     return pl.pallas_call(
         combine_kernel,
-        in_specs=[SMEM] + [VMEM] * len(parts),
+        in_specs=[VMEM] * len(parts),
         out_specs=VMEM,
         out_shape=jax.ShapeDtypeStruct((16, half, 2 * HS), jnp.bfloat16),
         compiler_params=pltpu.CompilerParams(vmem_limit_bytes=32 * 2**20),
-    )(core, *parts)
-
-
-def finish_kernel(grp_ref, pieces_ref, *refs):
+    )(*parts)
+
+
+def finish_kernel(pieces_ref, *refs):
     w_refs, out_ref = refs[:-1], refs[-1]
     groups = pieces_ref.shape[0] // 2
-    me = grp_ref[0]
+    me = lax.axis_index("grp")
     result = None
     for k, w_ref in enumerate(w_refs):
         near = jnp.bitwise_xor(me, k)
@@ -452,14 +453,14 @@
     out_ref[...] = result.astype(jnp.bfloat16)
 
 
-def finish(grp, pieces, w_turns):
+def finish(pieces, w_turns):
     return pl.pallas_call(
         finish_kernel,
-        in_specs=[SMEM] + [VMEM] * (1 + len(w_turns)),
+        in_specs=[VMEM] * (1 + len(w_turns)),
         out_specs=VMEM,
         out_shape=jax.ShapeDtypeStruct((2 * pieces.shape[1], w_turns[0].shape[1]), jnp.bfloat16),
         compiler_params=pltpu.CompilerParams(vmem_limit_bytes=24 * 2**20),
-    )(grp, pieces, *w_turns)
+    )(pieces, *w_turns)
 
 
 def along_x(by):
@@ -477,13 +478,9 @@
 
 
 def body(inputs, latents, w_query, w_key, w_value, w_out, positions, block_mask):
-    seq = lax.axis_index("seq")[None]
-    grp = lax.axis_index("grp")[None]
-    core = jnp.bitwise_and(seq, 1)
-
     w_other = lax.ppermute(w_out, "grp", [(g, g ^ 4) for g in range(8)])
     q_chip, theirs, kv_own, kv_other, codes = front(
-        seq, latents, inputs, w_query, w_key, w_value, positions, block_mask
+        latents, inputs, w_query, w_key, w_value, positions, block_mask
     )
     theirs, kv_other, kv_own, w_other = lax.optimization_barrier((theirs, kv_other, kv_own, w_other))
     q_chip = q_chip.at[1].set(lax.ppermute(theirs, "seq", CORE_SWAP))
@@ -522,10 +519,10 @@
 
     parts = [part if by == 0 else lax.ppermute(part, "seq", along_x(by)) for by, part in parts.items()]
     parts, w_turns = lax.optimization_barrier((parts, w_turns))
-    pieces = combine(core, parts)
+    pieces = combine(parts)
     owners = [[(4 * x + 2 * y + c) * 8 + g for c in range(2) for g in range(8)] for x in range(4) for y in range(2)]
     pieces = lax.all_to_all(pieces, ("seq", "grp"), 0, 0, axis_index_groups=owners)
-    return finish(grp, pieces, w_turns)
+    return finish(pieces, w_turns)
 
 
 def solution(mesh):

time: 167 us -> 166 us (level)
  blocking collectives: 0 us -> 13.3 us
  starting transfers between devices: 27.5 us -> 19.8 us
  waiting for transfers between devices: 7.29 us -> 0.95 us
    all_to_all x0 -> x1, blocking collectives: none -> 13.3 us  [body(): lax.all_to_all(pieces, ('seq', 'grp'), 0, 0, axis_index_groups=owners)]
    all_to_all x1 -> x0, starting transfers between devices: 7.21 us -> none  [body(): lax.all_to_all(pieces, ('seq', 'grp'), 0, 0, axis_index_groups=owners)]
    all_to_all x1 -> x0, waiting for transfers between devices: 6.34 us -> none  [body(): lax.all_to_all(pieces, ('seq', 'grp'), 0, 0, axis_index_groups=owners)]
    pallas_call x4, Pallas kernels: 122 us -> 124 us  [attend(): pl.pallas_call(functools.partial(attention_kernel, steps, bool(before)),...]
  transfers between devices with their start and end apart: 15 -> 14, of which waited for: 2 -> 1; matrix products, arithmetic and copies ran while one was open for 0% -> 0% of each run, Pallas kernels for 77% -> 78%
where the time goes in v16:
time: 166 us; the launch traced here: 165 us
  Pallas kernels  131 us (79%)
  starting transfers between devices  19.8 us (12%)
  blocking collectives  13.3 us (8%)
    pallas_call x4, Pallas kernels, attend(): pl.pallas_call(functools.partial(attention_kernel, steps, bool(before)),...  124 us
    all_to_all x1, blocking collectives, body(): lax.all_to_all(pieces, ('seq', 'grp'), 0, 0, axis_index_groups=owners)  13.3 us
    pallas_call x1, Pallas kernels, front(): pl.pallas_call(front_kernel, in_specs=[pl.BlockSpec(memory_space=pl.ANY)]...  5.16 us
    ppermute x3, starting transfers between devices, body(): lax.ppermute(w_pair, 'grp', [(g, g ^ k) for g in range(8)])  5.02 us
    ppermute x2, starting transfers between devices, body(): kv_far = [lax.ppermute(kv, 'seq', Y_SWAP) for kv in (kv_own, kv_partner)]  4.88 us
    ppermute x3, starting transfers between devices, body(): lax.ppermute(part, 'seq', along_x(by))  3.62 us
    ppermute x3, starting transfers between devices, body(): lax.ppermute(q_chip, 'seq', along_x(by))  3.33 us
  transfers between devices with their start and end apart: 14, of which 1 were waited for; matrix products, arithmetic and copies ran while one was open for 0% of the time, Pallas kernels for 78%

profile of v16, /device:TPU:3, one launch (start us, length us, event | category | flops | bytes accessed | tf_op | source)
XLA Modules:
  0.0 165.3 jit_solution(10859627056581541502)
XLA Ops:
  0.0 0.0 copy-start
  0.0 0.0 copy-start.1
  0.0 1.3 collective-permute-start
  1.3 5.2 %shard_map.82 = (bf16[2,64,512]{2,1,0:T(8,128)(2,1)S(1)}, bf16[64,512]{1,0:T(8,128)(2,1)S(1)}, bf16[2048,128]{1,0:T(8,128)(2,1)S(1)}, bf16[2048,128]{1,0:T(8,128)(2,1)S(1)}, s32[32,128]{1,0:T(8,128)S(1)}) custom-call(bf16[512,1024]{1,0:T(8,128)(2,1)} %lat_hbm.1, bf16[2048,1024]{1,0:T(8,128)(2,1)} %x_hbm.1, bf16[1024,128]{1,0:T(8,128)(2,1)} %wq_hbm.1, ...), custom_call_target="tpu_custom_call" | custom-call | flops 1207959552 | bytes 6291456 | tf_op jit(solution)/shard_map/pallas_call | solution.py:156
  6.5 0.9 collective-permute-done
  7.4 1.5 collective-permute-start.3
  8.9 0.0 copy-done.1
  9.0 0.1 collective-permute-start.1
  9.0 0.0 copy-done
  9.1 3.0 %collective-permute-start.4 = (bf16[2048,128]{1,0:T(8,128)(2,1)S(1)}, bf16[2048,128]{1,0:T(8,128)(2,1)S(1)}, u32[]{:S(2)}, u32[]{:S(2)}) collective-permute-start(bf16[2048,128]{1,0:T(8,128)(2,1)S(1)} %get-tuple-element.63.refs_0_), channel_id=1, source_target_pairs={{0,16},{8,24},{16,0},{24,8},{32,48},{40,56},{48,32},{56,40},{64,80... | collective-permute-start | bytes 1572872 | tf_op jit(solution)/shard_map/ppermute | solution.py:490
  12.1 0.0 collective-permute-done.1
  12.1 0.3 collective-permute-start.2
  12.4 1.9 %collective-permute-start.6 = (bf16[2,64,512]{2,1,0:T(8,128)(2,1)S(1)}, bf16[2,64,512]{2,1,0:T(8,128)(2,1)S(1)}, u32[]{:S(2)}, u32[]{:S(2)}) collective-permute-start(bf16[2,64,512]{2,1,0:T(8,128)(2,1)S(1)} %bitcast_dynamic-update-slice_fusion.rest_0_), channel_id=1, source_target_pairs={{0,96},{8,104},{16,112},{24,120},{32,64},{40,72},{48,80},{56,88},{... | collective-permute-start | bytes 393224 | tf_op jit(solution)/shard_map/ppermute | solution.py:487
  14.3 1.1 collective-permute-start.7
  15.4 0.0 collective-permute-done.3.refs_1_
  15.4 0.4 shard_map.83
  15.8 16.5 %shard_map.84.rest_1_ = bf16[2,72,512]{2,1,0:T(8,128)(2,1)S(1)} custom-call(s32[32,128]{1,0:T(8,128)S(1)} %get-tuple-element.56.code_any, f32[1,128]{1,0:T(1,128)S(1)} %get-tuple-element.65.norm_ref, s32[32,256]{1,0:T(8,128)S(1)} %reshape.40.pos_ref, bf16[4096,128]{1,0:T(8,128)(2,1)S(1)} %get-tuple-element.66.kv_ref, ...), custom_call_target="tpu_custom_call" | custom-call | flops 6000000000 | bytes 4194304 | tf_op jit(solution)/shard_map/pallas_call | solution.py:385
  32.3 1.7 %collective-permute-start.11 = (bf16[256,1024]{1,0:T(8,128)(2,1)S(1)}, bf16[256,1024]{1,0:T(8,128)(2,1)S(1)}, u32[]{:S(2)}, u32[]{:S(2)}) collective-permute-start(bf16[256,1024]{1,0:T(8,128)(2,1)S(1)} %constant_dynamic-update-slice_fusion.refs_0_), channel_id=1, source_target_pairs={{0,1},{1,0},{2,3},{3,2},{4,5},{5,4},{6,7},{7,6},{8,9},{9,8},{10,11... | collective-permute-start | bytes 1572872 | tf_op jit(solution)/shard_map/ppermute | solution.py:497
  34.1 0.0 collective-permute-done.2.rest_0_.rest_1_
  34.1 3.3 %collective-permute-start.12 = (bf16[256,1024]{1,0:T(8,128)(2,1)S(1)}, bf16[256,1024]{1,0:T(8,128)(2,1)S(1)}, u32[]{:S(2)}, u32[]{:S(2)}) collective-permute-start(bf16[256,1024]{1,0:T(8,128)(2,1)S(1)} %constant_dynamic-update-slice_fusion.refs_0_), channel_id=1, source_target_pairs={{0,2},{1,3},{2,0},{3,1},{4,6},{5,7},{6,4},{7,5},{8,10},{9,11},{10,... | collective-permute-start | bytes 1572872 | tf_op jit(solution)/shard_map/ppermute | solution.py:497
  37.4 0.0 collective-permute-done.4.refs_0_
  37.4 0.0 collective-permute-start.13
  37.4 0.0 collective-permute-done.6.rest_1_.rest_2_
  37.4 1.9 %collective-permute-start.5 = (bf16[2048,128]{1,0:T(8,128)(2,1)S(1)}, bf16[2048,128]{1,0:T(8,128)(2,1)S(1)}, u32[]{:S(2)}, u32[]{:S(2)}) collective-permute-start(bf16[2048,128]{1,0:T(8,128)(2,1)S(1)} %collective-permute-done.3.refs_1_), channel_id=1, source_target_pairs={{0,16},{8,24},{16,0},{24,8},{32,48},{40,56},{48,32},{56,40},{64,80... | collective-permute-start | bytes 1572872 | tf_op jit(solution)/shard_map/ppermute | solution.py:490
  39.3 0.0 collective-permute-done.7.rest_2_.rest_0_
  39.3 44.7 %shard_map.85 = (bf16[2,72,512]{2,1,0:T(8,128)(2,1)S(1)}, bf16[2,72,512]{2,1,0:T(8,128)(2,1)S(1)}, bf16[2,72,512]{2,1,0:T(8,128)(2,1)S(1)}) custom-call(s32[32,128]{1,0:T(8,128)S(1)} %get-tuple-element.56.code_any, f32[1,128]{1,0:T(1,128)S(1)} %get-tuple-element.65.norm_ref, s32[32,256]{1,0:T(8,128)S(1)} %reshape.40.pos_ref, ...), custom_call_target="tpu_custom_call" | custom-call | flops 17999998976 | bytes 4194304 | tf_op jit(solution)/shard_map/pallas_call | solution.py:385
  83.9 0.0 collective-permute-done.5.refs_1_
  83.9 0.4 shard_map.86
  84.4 45.4 %shard_map.87 = (bf16[2,72,512]{2,1,0:T(8,128)(2,1)S(1)}, bf16[2,72,512]{2,1,0:T(8,128)(2,1)S(1)}, bf16[2,72,512]{2,1,0:T(8,128)(2,1)S(1)}) custom-call(s32[32,128]{1,0:T(8,128)S(1)} %get-tuple-element.56.code_any, f32[1,128]{1,0:T(1,128)S(1)} %get-tuple-element.74.norm_ref, s32[32,256]{1,0:T(8,128)S(1)} %reshape.40.pos_ref, ...), custom_call_target="tpu_custom_call" | custom-call | flops 17999998976 | bytes 4194304 | tf_op jit(solution)/shard_map/pallas_call | solution.py:385
  129.7 1.7 %collective-permute-start.10 = (bf16[2,72,512]{2,1,0:T(8,128)(2,1)S(1)}, bf16[2,72,512]{2,1,0:T(8,128)(2,1)S(1)}, u32[]{:S(2)}, u32[]{:S(2)}) collective-permute-start(bf16[2,72,512]{2,1,0:T(8,128)(2,1)S(1)} %get-tuple-element.83), channel_id=1, source_target_pairs={{0,96},{8,104},{16,112},{24,120},{32,64},{40,72},{48,80},{56,88},{... | collective-permute-start | bytes 442376 | tf_op jit(solution)/shard_map/ppermute | solution.py:520
  131.5 0.0 collective-permute-start.8
  131.5 0.0 collective-permute-done.11.refs_1_
  131.5 1.9 %collective-permute-start.9 = (bf16[2,72,512]{2,1,0:T(8,128)(2,1)S(1)}, bf16[2,72,512]{2,1,0:T(8,128)(2,1)S(1)}, u32[]{:S(2)}, u32[]{:S(2)}) collective-permute-start(bf16[2,72,512]{2,1,0:T(8,128)(2,1)S(1)} %get-tuple-element.81), channel_id=1, source_target_pairs={{0,32},{8,40},{16,48},{24,56},{32,0},{40,8},{48,16},{56,24},{64,96... | collective-permute-start | bytes 442376 | tf_op jit(solution)/shard_map/ppermute | solution.py:520
  133.4 17.0 %shard_map.88.refs_3_ = bf16[2,72,512]{2,1,0:T(8,128)(2,1)S(1)} custom-call(s32[32,128]{1,0:T(8,128)S(1)} %get-tuple-element.56.code_any, f32[1,128]{1,0:T(1,128)S(1)} %get-tuple-element.74.norm_ref, s32[32,256]{1,0:T(8,128)S(1)} %reshape.40.pos_ref, bf16[4096,128]{1,0:T(8,128)(2,1)S(1)} %get-tuple-element.75.kv_ref, ...), custom_call_target="tpu_custom_call" | custom-call | flops 6000000000 | bytes 4194304 | tf_op jit(solution)/shard_map/pallas_call | solution.py:385
  150.4 0.0 collective-permute-done.12.refs_2_
  150.4 0.0 collective-permute-done.13.refs_3_
  150.4 0.0 collective-permute-done.10.refs_2_
  150.4 0.0 collective-permute-done.8.refs_0_
  150.5 0.0 collective-permute-done.9.refs_1_
  150.5 0.3 shard_map.89
  150.8 13.3 %all_to_all.5.pieces_ref = bf16[16,32,128]{2,1,0:T(8,128)(2,1)S(1)} all-to-all(bf16[16,32,128]{2,1,0:T(8,128)(2,1)S(1)} %shard_map.89), channel_id=1, replica_groups={{0,1,2,3,4,5,6,7,8,9,10,11,12,13,14,15},{16,17,18,19,20,21,22,23,24,25,..., dimensions={0} | all-to-all | bytes 262144 | tf_op jit(solution)/shard_map/all_to_all | solution.py:524
  164.1 1.2 shard_map.90
  (4 shorter events, 0.1 us)
Async XLA Ops:
  0.0 9.0 %copy-start = (bf16[128,1024]{1,0:T(8,128)(2,1)S(1)}, bf16[128,1024]{1,0:T(8,128)(2,1)}, u32[]{:S(2)}) copy-start(bf16[128,1024]{1,0:T(8,128)(2,1)} %param.15) | copy-start | bytes 786436
  0.0 8.9 %copy-start.1 = (s32[8192]{0:T(1024)S(1)}, s32[8192]{0:T(1024)}, u32[]{:S(2)}) copy-start(s32[8192]{0:T(1024)} %param.16) | copy-start | bytes 98308
  0.0 7.4 %collective-permute-start = (bf16[128,1024]{1,0:T(8,128)(2,1)}, bf16[128,1024]{1,0:T(8,128)(2,1)S(1)}, u32[]{:S(2)}, u32[]{:S(2)}) collective-permute-start(bf16[128,1024]{1,0:T(8,128)(2,1)} %param.15), channel_id=1, source_target_pairs={{0,4},{1,5},{2,6},{3,7},{4,0},{5,1},{6,2},{7,3},{8,12},{9,13},{10,... | collective-permute-start | bytes 786440 | tf_op jit(solution)/shard_map/ppermute | solution.py:481
  7.4 8.0 %collective-permute-start.3 = (bf16[2048,128]{1,0:T(8,128)(2,1)S(1)}, bf16[2048,128]{1,0:T(8,128)(2,1)S(1)}, u32[]{:S(2)}, u32[]{:S(2)}) collective-permute-start(bf16[2048,128]{1,0:T(8,128)(2,1)S(1)} %get-tuple-element.64), channel_id=1, source_target_pairs={{0,8},{8,0},{16,24},{24,16},{32,40},{40,32},{48,56},{56,48},{64,72... | collective-permute-start | bytes 1572872 | tf_op jit(solution)/shard_map/ppermute | solution.py:488
  9.0 3.1 %collective-permute-start.1 = (bf16[64,512]{1,0:T(8,128)(2,1)S(1)}, bf16[64,512]{1,0:T(8,128)(2,1)S(1)}, u32[]{:S(2)}, u32[]{:S(2)}) collective-permute-start(bf16[64,512]{1,0:T(8,128)(2,1)S(1)} %get-tuple-element.61), channel_id=1, source_target_pairs={{0,8},{8,0},{16,24},{24,16},{32,40},{40,32},{48,56},{56,48},{64,72... | collective-permute-start | bytes 196616 | tf_op jit(solution)/shard_map/ppermute | solution.py:486
  9.1 28.3 %collective-permute-start.4 = (bf16[2048,128]{1,0:T(8,128)(2,1)S(1)}, bf16[2048,128]{1,0:T(8,128)(2,1)S(1)}, u32[]{:S(2)}, u32[]{:S(2)}) collective-permute-start(bf16[2048,128]{1,0:T(8,128)(2,1)S(1)} %get-tuple-element.63.refs_0_), channel_id=1, source_target_pairs={{0,16},{8,24},{16,0},{24,8},{32,48},{40,56},{48,32},{56,40},{64,80... | collective-permute-start | bytes 1572872 | tf_op jit(solution)/shard_map/ppermute | solution.py:490
  12.1 22.0 %collective-permute-start.2 = (bf16[2,64,512]{2,1,0:T(8,128)(2,1)S(1)}, bf16[2,64,512]{2,1,0:T(8,128)(2,1)S(1)}, u32[]{:S(2)}, u32[]{:S(2)}) collective-permute-start(bf16[2,64,512]{2,1,0:T(8,128)(2,1)S(1)} %bitcast_dynamic-update-slice_fusion.rest_0_), channel_id=1, source_target_pairs={{0,32},{8,40},{16,48},{24,56},{32,0},{40,8},{48,16},{56,24},{64,96... | collective-permute-start | bytes 393224 | tf_op jit(solution)/shard_map/ppermute | solution.py:487
  12.4 24.9 %collective-permute-start.6 = (bf16[2,64,512]{2,1,0:T(8,128)(2,1)S(1)}, bf16[2,64,512]{2,1,0:T(8,128)(2,1)S(1)}, u32[]{:S(2)}, u32[]{:S(2)}) collective-permute-start(bf16[2,64,512]{2,1,0:T(8,128)(2,1)S(1)} %bitcast_dynamic-update-slice_fusion.rest_0_), channel_id=1, source_target_pairs={{0,96},{8,104},{16,112},{24,120},{32,64},{40,72},{48,80},{56,88},{... | collective-permute-start | bytes 393224 | tf_op jit(solution)/shard_map/ppermute | solution.py:487
  14.3 25.0 %collective-permute-start.7 = (bf16[2,64,512]{2,1,0:T(8,128)(2,1)S(1)}, bf16[2,64,512]{2,1,0:T(8,128)(2,1)S(1)}, u32[]{:S(2)}, u32[]{:S(2)}) collective-permute-start(bf16[2,64,512]{2,1,0:T(8,128)(2,1)S(1)} %bitcast_dynamic-update-slice_fusion.rest_0_), channel_id=1, source_target_pairs={{0,64},{8,72},{16,80},{24,88},{32,96},{40,104},{48,112},{56,120},{... | collective-permute-start | bytes 393224 | tf_op jit(solution)/shard_map/ppermute | solution.py:487
  32.3 99.2 %collective-permute-start.11 = (bf16[256,1024]{1,0:T(8,128)(2,1)S(1)}, bf16[256,1024]{1,0:T(8,128)(2,1)S(1)}, u32[]{:S(2)}, u32[]{:S(2)}) collective-permute-start(bf16[256,1024]{1,0:T(8,128)(2,1)S(1)} %constant_dynamic-update-slice_fusion.refs_0_), channel_id=1, source_target_pairs={{0,1},{1,0},{2,3},{3,2},{4,5},{5,4},{6,7},{7,6},{8,9},{9,8},{10,11... | collective-permute-start | bytes 1572872 | tf_op jit(solution)/shard_map/ppermute | solution.py:497
  34.1 116.4 %collective-permute-start.12 = (bf16[256,1024]{1,0:T(8,128)(2,1)S(1)}, bf16[256,1024]{1,0:T(8,128)(2,1)S(1)}, u32[]{:S(2)}, u32[]{:S(2)}) collective-permute-start(bf16[256,1024]{1,0:T(8,128)(2,1)S(1)} %constant_dynamic-update-slice_fusion.refs_0_), channel_id=1, source_target_pairs={{0,2},{1,3},{2,0},{3,1},{4,6},{5,7},{6,4},{7,5},{8,10},{9,11},{10,... | collective-permute-start | bytes 1572872 | tf_op jit(solution)/shard_map/ppermute | solution.py:497
  37.4 113.1 %collective-permute-start.13 = (bf16[256,1024]{1,0:T(8,128)(2,1)S(1)}, bf16[256,1024]{1,0:T(8,128)(2,1)S(1)}, u32[]{:S(2)}, u32[]{:S(2)}) collective-permute-start(bf16[256,1024]{1,0:T(8,128)(2,1)S(1)} %constant_dynamic-update-slice_fusion.refs_0_), channel_id=1, source_target_pairs={{0,3},{1,2},{2,1},{3,0},{4,7},{5,6},{6,5},{7,4},{8,11},{9,10},{10,... | collective-permute-start | bytes 1572872 | tf_op jit(solution)/shard_map/ppermute | solution.py:497
  37.4 46.6 %collective-permute-start.5 = (bf16[2048,128]{1,0:T(8,128)(2,1)S(1)}, bf16[2048,128]{1,0:T(8,128)(2,1)S(1)}, u32[]{:S(2)}, u32[]{:S(2)}) collective-permute-start(bf16[2048,128]{1,0:T(8,128)(2,1)S(1)} %collective-permute-done.3.refs_1_), channel_id=1, source_target_pairs={{0,16},{8,24},{16,0},{24,8},{32,48},{40,56},{48,32},{56,40},{64,80... | collective-permute-start | bytes 1572872 | tf_op jit(solution)/shard_map/ppermute | solution.py:490
  129.7 20.7 %collective-permute-start.10 = (bf16[2,72,512]{2,1,0:T(8,128)(2,1)S(1)}, bf16[2,72,512]{2,1,0:T(8,128)(2,1)S(1)}, u32[]{:S(2)}, u32[]{:S(2)}) collective-permute-start(bf16[2,72,512]{2,1,0:T(8,128)(2,1)S(1)} %get-tuple-element.83), channel_id=1, source_target_pairs={{0,96},{8,104},{16,112},{24,120},{32,64},{40,72},{48,80},{56,88},{... | collective-permute-start | bytes 442376 | tf_op jit(solution)/shard_map/ppermute | solution.py:520
  131.5 19.0 %collective-permute-start.8 = (bf16[2,72,512]{2,1,0:T(8,128)(2,1)S(1)}, bf16[2,72,512]{2,1,0:T(8,128)(2,1)S(1)}, u32[]{:S(2)}, u32[]{:S(2)}) collective-permute-start(bf16[2,72,512]{2,1,0:T(8,128)(2,1)S(1)} %get-tuple-element.80), channel_id=1, source_target_pairs={{0,64},{8,72},{16,80},{24,88},{32,96},{40,104},{48,112},{56,120},{... | collective-permute-start | bytes 442376 | tf_op jit(solution)/shard_map/ppermute | solution.py:520
  131.5 19.0 %collective-permute-start.9 = (bf16[2,72,512]{2,1,0:T(8,128)(2,1)S(1)}, bf16[2,72,512]{2,1,0:T(8,128)(2,1)S(1)}, u32[]{:S(2)}, u32[]{:S(2)}) collective-permute-start(bf16[2,72,512]{2,1,0:T(8,128)(2,1)S(1)} %get-tuple-element.81), channel_id=1, source_target_pairs={{0,32},{8,40},{16,48},{24,56},{32,0},{40,8},{48,16},{56,24},{64,96... | collective-permute-start | bytes 442376 | tf_op jit(solution)/shard_map/ppermute | solution.py:520

commit v17 on v16

--- a/solution.py
+++ b/solution.py
@@ -271,7 +271,7 @@
         reach = [jnp.where(jnp.bitwise_and(code, n * KEY_BLOCKS) > 0, 1 << 30, BLOCK) for n in (1, 2)]
         reach = jnp.where(in_first, *[jnp.where(real, n, -(1 << 30)) for n in reach])
         ahead = pos - base
-        return jnp.where(ahead < reach, jnp.minimum(ahead, BLOCK - 1), -1)
+        return jnp.where(ahead < reach, ahead, -1)
 
     def put(i, rr, a, top):
         at = (lax.div(rr, 2), slice(None), pl.ds(row_offset(lax.rem(rr, 2)), ROWS))

time: 166 us -> 167 us (level)
  no operation moved by 1% of the time
where the time goes in v17:
time: 167 us; the launch traced here: 166 us
  Pallas kernels  131 us (78%)
  starting transfers between devices  19.5 us (12%)
  blocking collectives  13.6 us (8%)
    pallas_call x4, Pallas kernels, attend(): pl.pallas_call(functools.partial(attention_kernel, steps, bool(before)),...  124 us
    all_to_all x1, blocking collectives, body(): lax.all_to_all(pieces, ('seq', 'grp'), 0, 0, axis_index_groups=owners)  13.6 us
    pallas_call x1, Pallas kernels, front(): pl.pallas_call(front_kernel, in_specs=[pl.BlockSpec(memory_space=pl.ANY)]...  5.16 us
    ppermute x3, starting transfers between devices, body(): lax.ppermute(w_pair, 'grp', [(g, g ^ k) for g in range(8)])  5.02 us
    ppermute x2, starting transfers between devices, body(): kv_far = [lax.ppermute(kv, 'seq', Y_SWAP) for kv in (kv_own, kv_partner)]  4.89 us
  transfers between devices with their start and end apart: 14, of which 1 were waited for; matrix products, arithmetic and copies ran while one was open for 0% of the time, Pallas kernels for 78%

profile of v17, /device:TPU:3, one launch (start us, length us, event | category | flops | bytes accessed | tf_op | source)
XLA Modules:
  0.0 165.6 jit_solution(6153385750080739533)
XLA Ops:
  0.0 0.0 copy-start
  0.0 0.0 copy-start.1
  0.0 1.3 collective-permute-start
  1.3 5.2 %shard_map.82 = (bf16[2,64,512]{2,1,0:T(8,128)(2,1)S(1)}, bf16[64,512]{1,0:T(8,128)(2,1)S(1)}, bf16[2048,128]{1,0:T(8,128)(2,1)S(1)}, bf16[2048,128]{1,0:T(8,128)(2,1)S(1)}, s32[32,128]{1,0:T(8,128)S(1)}) custom-call(bf16[512,1024]{1,0:T(8,128)(2,1)} %lat_hbm.1, bf16[2048,1024]{1,0:T(8,128)(2,1)} %x_hbm.1, bf16[1024,128]{1,0:T(8,128)(2,1)} %wq_hbm.1, ...), custom_call_target="tpu_custom_call" | custom-call | flops 1207959552 | bytes 6291456 | tf_op jit(solution)/shard_map/pallas_call | solution.py:156
  6.5 0.9 collective-permute-done
  7.4 1.5 collective-permute-start.3
  8.9 0.0 copy-done.1
  9.0 0.1 collective-permute-start.1
  9.0 0.0 copy-done
  9.1 3.0 %collective-permute-start.4 = (bf16[2048,128]{1,0:T(8,128)(2,1)S(1)}, bf16[2048,128]{1,0:T(8,128)(2,1)S(1)}, u32[]{:S(2)}, u32[]{:S(2)}) collective-permute-start(bf16[2048,128]{1,0:T(8,128)(2,1)S(1)} %get-tuple-element.63.refs_0_), channel_id=1, source_target_pairs={{0,16},{8,24},{16,0},{24,8},{32,48},{40,56},{48,32},{56,40},{64,80... | collective-permute-start | bytes 1572872 | tf_op jit(solution)/shard_map/ppermute | solution.py:490
  12.1 0.0 collective-permute-done.1
  12.1 0.3 collective-permute-start.2
  12.4 1.9 %collective-permute-start.6 = (bf16[2,64,512]{2,1,0:T(8,128)(2,1)S(1)}, bf16[2,64,512]{2,1,0:T(8,128)(2,1)S(1)}, u32[]{:S(2)}, u32[]{:S(2)}) collective-permute-start(bf16[2,64,512]{2,1,0:T(8,128)(2,1)S(1)} %bitcast_dynamic-update-slice_fusion.rest_0_), channel_id=1, source_target_pairs={{0,96},{8,104},{16,112},{24,120},{32,64},{40,72},{48,80},{56,88},{... | collective-permute-start | bytes 393224 | tf_op jit(solution)/shard_map/ppermute | solution.py:487
  14.3 1.1 collective-permute-start.7
  15.4 0.0 collective-permute-done.3.refs_1_
  15.4 0.4 shard_map.83
  15.8 16.6 %shard_map.84.rest_1_ = bf16[2,72,512]{2,1,0:T(8,128)(2,1)S(1)} custom-call(s32[32,128]{1,0:T(8,128)S(1)} %get-tuple-element.56.code_any, f32[1,128]{1,0:T(1,128)S(1)} %get-tuple-element.65.norm_ref, s32[32,256]{1,0:T(8,128)S(1)} %reshape.40.pos_ref, bf16[4096,128]{1,0:T(8,128)(2,1)S(1)} %get-tuple-element.66.kv_ref, ...), custom_call_target="tpu_custom_call" | custom-call | flops 6000000000 | bytes 4194304 | tf_op jit(solution)/shard_map/pallas_call | solution.py:385
  32.5 1.7 %collective-permute-start.11 = (bf16[256,1024]{1,0:T(8,128)(2,1)S(1)}, bf16[256,1024]{1,0:T(8,128)(2,1)S(1)}, u32[]{:S(2)}, u32[]{:S(2)}) collective-permute-start(bf16[256,1024]{1,0:T(8,128)(2,1)S(1)} %constant_dynamic-update-slice_fusion.refs_0_), channel_id=1, source_target_pairs={{0,1},{1,0},{2,3},{3,2},{4,5},{5,4},{6,7},{7,6},{8,9},{9,8},{10,11... | collective-permute-start | bytes 1572872 | tf_op jit(solution)/shard_map/ppermute | solution.py:497
  34.2 0.0 collective-permute-done.2.rest_0_.rest_1_
  34.2 3.3 %collective-permute-start.12 = (bf16[256,1024]{1,0:T(8,128)(2,1)S(1)}, bf16[256,1024]{1,0:T(8,128)(2,1)S(1)}, u32[]{:S(2)}, u32[]{:S(2)}) collective-permute-start(bf16[256,1024]{1,0:T(8,128)(2,1)S(1)} %constant_dynamic-update-slice_fusion.refs_0_), channel_id=1, source_target_pairs={{0,2},{1,3},{2,0},{3,1},{4,6},{5,7},{6,4},{7,5},{8,10},{9,11},{10,... | collective-permute-start | bytes 1572872 | tf_op jit(solution)/shard_map/ppermute | solution.py:497
  37.5 0.0 collective-permute-done.4.refs_0_
  37.5 0.0 collective-permute-start.13
  37.5 0.0 collective-permute-done.6.rest_1_.rest_2_
  37.5 1.9 %collective-permute-start.5 = (bf16[2048,128]{1,0:T(8,128)(2,1)S(1)}, bf16[2048,128]{1,0:T(8,128)(2,1)S(1)}, u32[]{:S(2)}, u32[]{:S(2)}) collective-permute-start(bf16[2048,128]{1,0:T(8,128)(2,1)S(1)} %collective-permute-done.3.refs_1_), channel_id=1, source_target_pairs={{0,16},{8,24},{16,0},{24,8},{32,48},{40,56},{48,32},{56,40},{64,80... | collective-permute-start | bytes 1572872 | tf_op jit(solution)/shard_map/ppermute | solution.py:490
  39.4 0.0 collective-permute-done.7.rest_2_.rest_0_
  39.4 44.8 %shard_map.85 = (bf16[2,72,512]{2,1,0:T(8,128)(2,1)S(1)}, bf16[2,72,512]{2,1,0:T(8,128)(2,1)S(1)}, bf16[2,72,512]{2,1,0:T(8,128)(2,1)S(1)}) custom-call(s32[32,128]{1,0:T(8,128)S(1)} %get-tuple-element.56.code_any, f32[1,128]{1,0:T(1,128)S(1)} %get-tuple-element.65.norm_ref, s32[32,256]{1,0:T(8,128)S(1)} %reshape.40.pos_ref, ...), custom_call_target="tpu_custom_call" | custom-call | flops 17999998976 | bytes 4194304 | tf_op jit(solution)/shard_map/pallas_call | solution.py:385
  84.2 0.0 collective-permute-done.5.refs_1_
  84.2 0.4 shard_map.86
  84.6 45.3 %shard_map.87 = (bf16[2,72,512]{2,1,0:T(8,128)(2,1)S(1)}, bf16[2,72,512]{2,1,0:T(8,128)(2,1)S(1)}, bf16[2,72,512]{2,1,0:T(8,128)(2,1)S(1)}) custom-call(s32[32,128]{1,0:T(8,128)S(1)} %get-tuple-element.56.code_any, f32[1,128]{1,0:T(1,128)S(1)} %get-tuple-element.74.norm_ref, s32[32,256]{1,0:T(8,128)S(1)} %reshape.40.pos_ref, ...), custom_call_target="tpu_custom_call" | custom-call | flops 17999998976 | bytes 4194304 | tf_op jit(solution)/shard_map/pallas_call | solution.py:385
  129.9 0.8 collective-permute-start.10
  130.7 0.3 collective-permute-start.8
  131.0 0.0 collective-permute-done.11.refs_1_
  131.0 2.3 %collective-permute-start.9 = (bf16[2,72,512]{2,1,0:T(8,128)(2,1)S(1)}, bf16[2,72,512]{2,1,0:T(8,128)(2,1)S(1)}, u32[]{:S(2)}, u32[]{:S(2)}) collective-permute-start(bf16[2,72,512]{2,1,0:T(8,128)(2,1)S(1)} %get-tuple-element.81), channel_id=1, source_target_pairs={{0,32},{8,40},{16,48},{24,56},{32,0},{40,8},{48,16},{56,24},{64,96... | collective-permute-start | bytes 442376 | tf_op jit(solution)/shard_map/ppermute | solution.py:520
  133.3 17.2 %shard_map.88.refs_3_ = bf16[2,72,512]{2,1,0:T(8,128)(2,1)S(1)} custom-call(s32[32,128]{1,0:T(8,128)S(1)} %get-tuple-element.56.code_any, f32[1,128]{1,0:T(1,128)S(1)} %get-tuple-element.74.norm_ref, s32[32,256]{1,0:T(8,128)S(1)} %reshape.40.pos_ref, bf16[4096,128]{1,0:T(8,128)(2,1)S(1)} %get-tuple-element.75.kv_ref, ...), custom_call_target="tpu_custom_call" | custom-call | flops 6000000000 | bytes 4194304 | tf_op jit(solution)/shard_map/pallas_call | solution.py:385
  150.4 0.0 collective-permute-done.12.refs_2_
  150.4 0.0 collective-permute-done.13.refs_3_
  150.4 0.0 collective-permute-done.10.refs_2_
  150.5 0.0 collective-permute-done.8.refs_0_
  150.5 0.0 collective-permute-done.9.refs_1_
  150.5 0.3 shard_map.89
  150.8 13.6 %all_to_all.5.pieces_ref = bf16[16,32,128]{2,1,0:T(8,128)(2,1)S(1)} all-to-all(bf16[16,32,128]{2,1,0:T(8,128)(2,1)S(1)} %shard_map.89), channel_id=1, replica_groups={{0,1,2,3,4,5,6,7,8,9,10,11,12,13,14,15},{16,17,18,19,20,21,22,23,24,25,..., dimensions={0} | all-to-all | bytes 262144 | tf_op jit(solution)/shard_map/all_to_all | solution.py:524
  164.4 1.2 shard_map.90
  (4 shorter events, 0.1 us)
Async XLA Ops:
  0.0 9.0 %copy-start = (bf16[128,1024]{1,0:T(8,128)(2,1)S(1)}, bf16[128,1024]{1,0:T(8,128)(2,1)}, u32[]{:S(2)}) copy-start(bf16[128,1024]{1,0:T(8,128)(2,1)} %param.15) | copy-start | bytes 786436
  0.0 8.9 %copy-start.1 = (s32[8192]{0:T(1024)S(1)}, s32[8192]{0:T(1024)}, u32[]{:S(2)}) copy-start(s32[8192]{0:T(1024)} %param.16) | copy-start | bytes 98308
  0.0 7.4 %collective-permute-start = (bf16[128,1024]{1,0:T(8,128)(2,1)}, bf16[128,1024]{1,0:T(8,128)(2,1)S(1)}, u32[]{:S(2)}, u32[]{:S(2)}) collective-permute-start(bf16[128,1024]{1,0:T(8,128)(2,1)} %param.15), channel_id=1, source_target_pairs={{0,4},{1,5},{2,6},{3,7},{4,0},{5,1},{6,2},{7,3},{8,12},{9,13},{10,... | collective-permute-start | bytes 786440 | tf_op jit(solution)/shard_map/ppermute | solution.py:481
  7.4 8.0 %collective-permute-start.3 = (bf16[2048,128]{1,0:T(8,128)(2,1)S(1)}, bf16[2048,128]{1,0:T(8,128)(2,1)S(1)}, u32[]{:S(2)}, u32[]{:S(2)}) collective-permute-start(bf16[2048,128]{1,0:T(8,128)(2,1)S(1)} %get-tuple-element.64), channel_id=1, source_target_pairs={{0,8},{8,0},{16,24},{24,16},{32,40},{40,32},{48,56},{56,48},{64,72... | collective-permute-start | bytes 1572872 | tf_op jit(solution)/shard_map/ppermute | solution.py:488
  9.0 3.1 %collective-permute-start.1 = (bf16[64,512]{1,0:T(8,128)(2,1)S(1)}, bf16[64,512]{1,0:T(8,128)(2,1)S(1)}, u32[]{:S(2)}, u32[]{:S(2)}) collective-permute-start(bf16[64,512]{1,0:T(8,128)(2,1)S(1)} %get-tuple-element.61), channel_id=1, source_target_pairs={{0,8},{8,0},{16,24},{24,16},{32,40},{40,32},{48,56},{56,48},{64,72... | collective-permute-start | bytes 196616 | tf_op jit(solution)/shard_map/ppermute | solution.py:486
  9.1 28.4 %collective-permute-start.4 = (bf16[2048,128]{1,0:T(8,128)(2,1)S(1)}, bf16[2048,128]{1,0:T(8,128)(2,1)S(1)}, u32[]{:S(2)}, u32[]{:S(2)}) collective-permute-start(bf16[2048,128]{1,0:T(8,128)(2,1)S(1)} %get-tuple-element.63.refs_0_), channel_id=1, source_target_pairs={{0,16},{8,24},{16,0},{24,8},{32,48},{40,56},{48,32},{56,40},{64,80... | collective-permute-start | bytes 1572872 | tf_op jit(solution)/shard_map/ppermute | solution.py:490
  12.1 22.1 %collective-permute-start.2 = (bf16[2,64,512]{2,1,0:T(8,128)(2,1)S(1)}, bf16[2,64,512]{2,1,0:T(8,128)(2,1)S(1)}, u32[]{:S(2)}, u32[]{:S(2)}) collective-permute-start(bf16[2,64,512]{2,1,0:T(8,128)(2,1)S(1)} %bitcast_dynamic-update-slice_fusion.rest_0_), channel_id=1, source_target_pairs={{0,32},{8,40},{16,48},{24,56},{32,0},{40,8},{48,16},{56,24},{64,96... | collective-permute-start | bytes 393224 | tf_op jit(solution)/shard_map/ppermute | solution.py:487
  12.4 25.1 %collective-permute-start.6 = (bf16[2,64,512]{2,1,0:T(8,128)(2,1)S(1)}, bf16[2,64,512]{2,1,0:T(8,128)(2,1)S(1)}, u32[]{:S(2)}, u32[]{:S(2)}) collective-permute-start(bf16[2,64,512]{2,1,0:T(8,128)(2,1)S(1)} %bitcast_dynamic-update-slice_fusion.rest_0_), channel_id=1, source_target_pairs={{0,96},{8,104},{16,112},{24,120},{32,64},{40,72},{48,80},{56,88},{... | collective-permute-start | bytes 393224 | tf_op jit(solution)/shard_map/ppermute | solution.py:487
  14.3 25.1 %collective-permute-start.7 = (bf16[2,64,512]{2,1,0:T(8,128)(2,1)S(1)}, bf16[2,64,512]{2,1,0:T(8,128)(2,1)S(1)}, u32[]{:S(2)}, u32[]{:S(2)}) collective-permute-start(bf16[2,64,512]{2,1,0:T(8,128)(2,1)S(1)} %bitcast_dynamic-update-slice_fusion.rest_0_), channel_id=1, source_target_pairs={{0,64},{8,72},{16,80},{24,88},{32,96},{40,104},{48,112},{56,120},{... | collective-permute-start | bytes 393224 | tf_op jit(solution)/shard_map/ppermute | solution.py:487
  32.5 98.5 %collective-permute-start.11 = (bf16[256,1024]{1,0:T(8,128)(2,1)S(1)}, bf16[256,1024]{1,0:T(8,128)(2,1)S(1)}, u32[]{:S(2)}, u32[]{:S(2)}) collective-permute-start(bf16[256,1024]{1,0:T(8,128)(2,1)S(1)} %constant_dynamic-update-slice_fusion.refs_0_), channel_id=1, source_target_pairs={{0,1},{1,0},{2,3},{3,2},{4,5},{5,4},{6,7},{7,6},{8,9},{9,8},{10,11... | collective-permute-start | bytes 1572872 | tf_op jit(solution)/shard_map/ppermute | solution.py:497
  34.2 116.3 %collective-permute-start.12 = (bf16[256,1024]{1,0:T(8,128)(2,1)S(1)}, bf16[256,1024]{1,0:T(8,128)(2,1)S(1)}, u32[]{:S(2)}, u32[]{:S(2)}) collective-permute-start(bf16[256,1024]{1,0:T(8,128)(2,1)S(1)} %constant_dynamic-update-slice_fusion.refs_0_), channel_id=1, source_target_pairs={{0,2},{1,3},{2,0},{3,1},{4,6},{5,7},{6,4},{7,5},{8,10},{9,11},{10,... | collective-permute-start | bytes 1572872 | tf_op jit(solution)/shard_map/ppermute | solution.py:497
  37.5 113.0 %collective-permute-start.13 = (bf16[256,1024]{1,0:T(8,128)(2,1)S(1)}, bf16[256,1024]{1,0:T(8,128)(2,1)S(1)}, u32[]{:S(2)}, u32[]{:S(2)}) collective-permute-start(bf16[256,1024]{1,0:T(8,128)(2,1)S(1)} %constant_dynamic-update-slice_fusion.refs_0_), channel_id=1, source_target_pairs={{0,3},{1,2},{2,1},{3,0},{4,7},{5,6},{6,5},{7,4},{8,11},{9,10},{10,... | collective-permute-start | bytes 1572872 | tf_op jit(solution)/shard_map/ppermute | solution.py:497
  37.5 46.7 %collective-permute-start.5 = (bf16[2048,128]{1,0:T(8,128)(2,1)S(1)}, bf16[2048,128]{1,0:T(8,128)(2,1)S(1)}, u32[]{:S(2)}, u32[]{:S(2)}) collective-permute-start(bf16[2048,128]{1,0:T(8,128)(2,1)S(1)} %collective-permute-done.3.refs_1_), channel_id=1, source_target_pairs={{0,16},{8,24},{16,0},{24,8},{32,48},{40,56},{48,32},{56,40},{64,80... | collective-permute-start | bytes 1572872 | tf_op jit(solution)/shard_map/ppermute | solution.py:490
  129.9 20.5 %collective-permute-start.10 = (bf16[2,72,512]{2,1,0:T(8,128)(2,1)S(1)}, bf16[2,72,512]{2,1,0:T(8,128)(2,1)S(1)}, u32[]{:S(2)}, u32[]{:S(2)}) collective-permute-start(bf16[2,72,512]{2,1,0:T(8,128)(2,1)S(1)} %get-tuple-element.83), channel_id=1, source_target_pairs={{0,96},{8,104},{16,112},{24,120},{32,64},{40,72},{48,80},{56,88},{... | collective-permute-start | bytes 442376 | tf_op jit(solution)/shard_map/ppermute | solution.py:520
  130.7 19.7 %collective-permute-start.8 = (bf16[2,72,512]{2,1,0:T(8,128)(2,1)S(1)}, bf16[2,72,512]{2,1,0:T(8,128)(2,1)S(1)}, u32[]{:S(2)}, u32[]{:S(2)}) collective-permute-start(bf16[2,72,512]{2,1,0:T(8,128)(2,1)S(1)} %get-tuple-element.80), channel_id=1, source_target_pairs={{0,64},{8,72},{16,80},{24,88},{32,96},{40,104},{48,112},{56,120},{... | collective-permute-start | bytes 442376 | tf_op jit(solution)/shard_map/ppermute | solution.py:520
  131.0 19.5 %collective-permute-start.9 = (bf16[2,72,512]{2,1,0:T(8,128)(2,1)S(1)}, bf16[2,72,512]{2,1,0:T(8,128)(2,1)S(1)}, u32[]{:S(2)}, u32[]{:S(2)}) collective-permute-start(bf16[2,72,512]{2,1,0:T(8,128)(2,1)S(1)} %get-tuple-element.81), channel_id=1, source_target_pairs={{0,32},{8,40},{16,48},{24,56},{32,0},{40,8},{48,16},{56,24},{64,96... | collective-permute-start | bytes 442376 | tf_op jit(solution)/shard_map/ppermute | solution.py:520
